TPU v7x, 32 devices: a whole 2x2x4 slice. The times are simulated.
32 devices in a mesh: ctx: 8 (over z, x), exp: 4 (over y, core).
Axes of the slice: x: 2, y: 2, z: 4, core: 2. Of those that a mesh axis runs over, the one named last changes fastest.
Arguments:
- queries: bfloat16 [1024, 6144], P('ctx', 'exp'), may hold values from -6 to 6
- keys: bfloat16 [1024, 6144], P('ctx', 'exp'), may hold values from -6 to 6
- values: bfloat16 [1024, 6144], P('ctx', 'exp'), may hold values from -6 to 6
- out_grad: bfloat16 [1024, 6144], P('ctx', 'exp'), may hold values from -6 to 6
- up_weight: bfloat16 [8, 6144, 2304], P('ctx', 'exp'), may hold values from -0.078125 to 0.078125
- down_weight: bfloat16 [8, 2304, 6144], P('ctx', None, 'exp'), may hold values from -0.09375 to 0.09375
- decay_rates: float32 [48], P('exp'), may hold values from 9.765625e-05 to 0.0333333333
- routes: int32 [1024, 2], P('ctx'), may hold values from 0 to 3, all different within a row; in each aligned block of 128 rows (0 to 127, 128 to 255, ...) at most 72 rows name the same one
- gate_weights: float32 [1024, 2], P('ctx'), may hold values from 0.1 to 1
Outputs:
- query_grad: bfloat16 [1024, 6144], P('ctx', 'exp')
- key_grad: bfloat16 [1024, 6144], P('ctx', 'exp')
- value_grad: bfloat16 [1024, 6144], P('ctx', 'exp')
Inputs may be any that keep to these rules, and one draw needn't show every extreme that they name: `routes`: in each aligned block of 128 tokens a token's two experts differ and no expert is named by more than 72 tokens; in every draw some expert is named by exactly 72 tokens of some block.
All inputs are finite; a program needn't handle non-finite values.
Results may differ from a plain program's by a relative error of at most 0.0117.
Values may be sent and summed in bfloat16 or wider, within the bound.
No kernel may reach another device: no remote copies, remote signals or barrier semaphores. Data moves between devices by JAX's collectives and lax.ppermute only.
A program may use at most 128 MiB of HBM per device.

v0:
```python
import jax
import jax.numpy as jnp
from jax import lax
from jax.sharding import PartitionSpec as P

DH = 128


HIGHEST = lax.Precision.HIGHEST


def carried_in(value, axis, join, neutral, backward):
    count, mine = (lax.axis_size(axis), lax.axis_index(axis))
    pieces = jax.tree.map(lambda part: lax.all_gather(part, axis), value)
    if backward:
        pieces = jax.tree.map(lambda part: part[::-1], pieces)
        mine = count - 1 - mine
    so_far = jax.tree.map(
        lambda part, zero: jnp.full_like(part, 0) + jnp.asarray(zero, part.dtype), value, neutral
    )

    def lap(position, so_far):
        longer = join(so_far, jax.tree.map(lambda part: part[position], pieces))
        return jax.tree.map(lambda new, old: jnp.where(position < mine, new, old), longer, so_far)

    return lax.fori_loop(0, count - 1, lap, so_far)


def silu_slope(value):
    sigma = jax.nn.sigmoid(value)
    return sigma * (1.0 + value * (1.0 - sigma))


def decay_tables(rates, block_len):
    offsets = jnp.arange(block_len).astype(jnp.float32)
    distance = offsets[:, None] - offsets[None, :]
    within = jnp.where(
        distance[None] >= 0.0,
        jnp.exp(-rates[:, None, None] * jnp.maximum(distance, 0.0)[None]),
        0.0,
    )
    start_pow = jnp.exp(-rates[None, :] * offsets[:, None])
    end_pow = jnp.exp(-rates[None, :] * (block_len - offsets)[:, None])
    last_pow = jnp.exp(-rates[None, :] * (block_len - 1.0 - offsets)[:, None])
    next_pow = jnp.exp(-rates[None, :] * (offsets + 1.0)[:, None])
    whole_pow = jnp.exp(-rates * block_len)
    return (within, start_pow, end_pow, last_pow, next_pow, whole_pow)


def slot_tables(route_block, gate_block, experts, capacity):
    flat = route_block.reshape(-1)
    hits = (flat[:, None] == jnp.arange(experts, dtype=jnp.int32)[None, :]).astype(jnp.int32)
    before = jnp.cumsum(hits, axis=0) - hits
    placed = jnp.sum(before * hits, axis=1)
    target = flat * capacity + placed
    match = (target[None, :] == jnp.arange(experts * capacity, dtype=jnp.int32)[:, None]).astype(
        jnp.float32
    )
    match = match.reshape(experts * capacity, route_block.shape[0], route_block.shape[1])
    return (jnp.sum(match, axis=2), jnp.sum(match * gate_block[None], axis=2))


def combine_states(earlier, later):
    return (earlier[0] * later[0], later[0] * earlier[1] + later[1])


def forward_states(factor, local):
    result = carried_in(
        (factor, local),
        "ctx",
        combine_states,
        (jnp.ones_like(factor), jnp.zeros_like(local)),
        False,
    )
    return result[1]


def reverse_states(factor, local):
    result = carried_in(
        (factor, local), "ctx", combine_states, (jnp.ones_like(factor), jnp.zeros_like(local)), True
    )
    return result[1]


def contract_last(left, right):
    return lax.dot_general(
        left, right, (((1,), (1,)), ((), ())), preferred_element_type=jnp.float32
    )


def on_device(
    queries, keys, values, out_grad, up_weight, down_weight, decay_rates, routes, gate_weights
):
    block_len = queries.shape[0]
    group = queries.shape[1]
    heads = group // DH
    scale = 1.0 / DH
    within, start_pow, end_pow, last_pow, next_pow, whole_pow = decay_tables(decay_rates, block_len)
    factor = whole_pow[:, None, None]
    query_heads = queries.reshape(block_len, heads, DH)
    key_heads = keys.reshape(block_len, heads, DH)
    value_heads = values.reshape(block_len, heads, DH)
    query_wide = query_heads.astype(jnp.float32)
    key_wide = key_heads.astype(jnp.float32)
    value_wide = value_heads.astype(jnp.float32)
    scores = jnp.einsum("ihd,jhd->hij", query_heads, key_heads, preferred_element_type=jnp.float32)
    weights = (scale * scores * within).astype(jnp.bfloat16)
    intra = jnp.einsum("hij,jhd->ihd", weights, value_heads, preferred_element_type=jnp.float32)
    key_local = jnp.einsum(
        "ihd,ihe->hde", key_wide * end_pow[:, :, None], value_wide, precision=HIGHEST
    )
    entering = forward_states(factor, key_local)
    inter = (
        scale
        * start_pow[:, :, None]
        * jnp.einsum("ihd,hde->ihe", query_wide, entering, precision=HIGHEST)
    )
    attn_out = (intra + inter).astype(jnp.bfloat16).reshape(block_len, group)
    experts = lax.axis_size("ctx") // 2
    capacity = block_len * 9 // (4 * experts)
    choose, weigh = slot_tables(routes, gate_weights, experts, capacity)
    choose_half = choose.astype(jnp.bfloat16)
    send_in = jnp.dot(choose_half, attn_out, preferred_element_type=jnp.float32).astype(
        jnp.bfloat16
    )
    send_grad = jnp.dot(choose_half, out_grad, preferred_element_type=jnp.float32).astype(
        jnp.bfloat16
    )

    def doubled(array):
        spread = jnp.broadcast_to(
            array.reshape(experts, 1, capacity, group), (experts, 2, capacity, group)
        )
        return spread.reshape(2 * experts, capacity, group)

    got_in, got_grad = (
        lax.all_to_all(doubled(send_in), "ctx", split_axis=0, concat_axis=0, tiled=True),
        lax.all_to_all(doubled(send_grad), "ctx", split_axis=0, concat_axis=0, tiled=True),
    )
    in_rows = got_in.reshape(-1, group)
    grad_rows = got_grad.reshape(-1, group)
    up_local = up_weight[0]
    down_local = down_weight[0]
    pre_part = jnp.dot(in_rows, up_local, preferred_element_type=jnp.float32)
    grad_part = contract_last(grad_rows, down_local)
    pre, hidden_grad = (
        lax.psum(pre_part.astype(jnp.bfloat16), "exp").astype(jnp.float32),
        lax.psum(grad_part.astype(jnp.bfloat16), "exp").astype(jnp.float32),
    )
    slope = (hidden_grad * silu_slope(pre)).astype(jnp.bfloat16)
    back = contract_last(slope, up_local)
    back_half = back.astype(jnp.bfloat16).reshape(2 * experts, capacity, group)
    home = lax.all_to_all(back_half, "ctx", split_axis=0, concat_axis=0, tiled=True)
    summed = jnp.sum(home.astype(jnp.float32).reshape(experts, 2, capacity, group), axis=1)
    summed = summed.reshape(experts * capacity, group)
    moe_grad = lax.dot_general(
        weigh,
        summed,
        (((0,), (0,)), ((), ())),
        precision=HIGHEST,
        preferred_element_type=jnp.float32,
    )
    grad_out = (out_grad.astype(jnp.float32) + moe_grad).astype(jnp.bfloat16)
    grad_heads = grad_out.reshape(block_len, heads, DH)
    grad_wide = grad_heads.astype(jnp.float32)
    query_local = jnp.einsum(
        "ihd,ihe->hde", query_wide * next_pow[:, :, None], grad_wide, precision=HIGHEST
    )
    leaving = reverse_states(factor, query_local)
    dscores = jnp.einsum(
        "ihd,jhd->hij", grad_heads, value_heads, preferred_element_type=jnp.float32
    )
    dweights = (scale * dscores * within).astype(jnp.bfloat16)
    query_g = jnp.einsum("hij,jhd->ihd", dweights, key_heads, preferred_element_type=jnp.float32)
    query_g = query_g + scale * start_pow[:, :, None] * jnp.einsum(
        "ihe,hde->ihd", grad_wide, entering, precision=HIGHEST
    )
    key_g = jnp.einsum("hij,ihd->jhd", dweights, query_heads, preferred_element_type=jnp.float32)
    key_g = key_g + scale * last_pow[:, :, None] * jnp.einsum(
        "jhe,hde->jhd", value_wide, leaving, precision=HIGHEST
    )
    value_g = jnp.einsum("hij,ihd->jhd", weights, grad_heads, preferred_element_type=jnp.float32)
    value_g = value_g + scale * last_pow[:, :, None] * jnp.einsum(
        "jhd,hde->jhe", key_wide, leaving, precision=HIGHEST
    )
    return (
        query_g.astype(jnp.bfloat16).reshape(block_len, group),
        key_g.astype(jnp.bfloat16).reshape(block_len, group),
        value_g.astype(jnp.bfloat16).reshape(block_len, group),
    )


def solution(mesh):
    placed = (
        P("ctx", "exp"),
        P("ctx", "exp"),
        P("ctx", "exp"),
        P("ctx", "exp"),
        P("ctx", "exp", None),
        P("ctx", None, "exp"),
        P("exp"),
        P("ctx", None),
        P("ctx", None),
    )
    return jax.shard_map(
        on_device,
        mesh=mesh,
        in_specs=placed,
        out_specs=(P("ctx", "exp"), P("ctx", "exp"), P("ctx", "exp")),
        check_vma=False,
    )
```

profile of v0, /device:TPU:0, one launch (start us, length us, event | category | flops | bytes accessed | tf_op | source)
XLA Modules:
  0.0 505.9 jit_solution(4840898388816468909)
XLA Ops:
  12.5 1.8 fusion.46
  17.1 1.4 broadcast_in_dim.21
  18.6 7.2 %all-to-all-start = ((bf16[8,72,1536]{2,1,0:T(8,128)(2,1)}), bf16[8,72,1536]{2,1,0:T(8,128)(2,1)}, u32[]{:S(2)}, u32[]{:S(2)}) async-start(bf16[8,72,1536]{2,1,0:T(8,128)(2,1)} %bitcast.3), calls=%async_computation | async-start | bytes 3538944 | tf_op jit(solution)/shard_map/all_to_all | solution.py:138
  25.8 69.0 %all-reduce = f32[96]{0:T(128)S(1)} all-reduce(f32[96]{0:T(128)S(1)} %get-tuple-element.323), channel_id=2, replica_groups=mesh['ctx'=8,'exp'=4] {'ctx'}, use_global_device_ids=true, to_apply=%add | all-reduce | flops 96 | bytes 768
  95.8 52.1 %all-gather.6.cloned.1.call-done = f32[96,128,128]{2,1,0:T(8,128)} async-done(((f32[12,128,128]{2,1,0:T(8,128)}), f32[96,128,128]{2,1,0:T(8,128)}) %all-gather.6.cloned.1.call-update) | async-done | bytes 6291472 | tf_op jit(solution)/shard_map/all_gather | solution.py:14
  147.9 9.3 %while.28 = (s32[]{:T(128)}, f32[12,128,128]{2,1,0:T(8,128)S(1)}, s32[]{:T(128)}, f32[8,12,1,1]{1,3,2,0:T(1,128)S(1)}, f32[8,12,128,128]{3,2,1,0:T(8,128)}, /*index=5*/s32[]{:T(128)}, s32[]{:T(128)}) while((s32[]{:T(128)}, f32[12,128,128]{2,1,0:T(8,128)S(1)}, s32[]{:T(128)}, f32[8,12,1,1]{1,3,2,0:T(1,128)S(1)}, ...), condition=%wide.region_7.8_spmd.clone, body=%wide.region_6.7_spmd.clone.sunk | while | flops 786436 | bytes 2359545 | solution.py:26
  149.2 1.3 fusion.90
  150.6 1.3 fusion.90
  151.9 1.3 fusion.90
  154.6 1.3 fusion.90
  155.9 1.3 fusion.90
  158.9 1.3 broadcast_in_dim.25
  160.2 4.3 all-to-all-start.1
  164.6 9.4 %fusion.15 = bf16[576,2304]{1,0:T(8,128)(2,1)} fusion(bf16[576,1536]{1,0:T(8,128)(2,1)} %bitcast.4, bf16[1,2304,1536]{2,1,0:T(8,128)(2,1)} %param.18), kind=kOutput, calls=%fused_computation.21 | convolution fusion | flops 4078190592 | bytes 11501568 | tf_op jit(solution)/shard_map/dot_general | solution.py:86
  174.0 31.7 %all-to-all-done.1 = bf16[8,72,1536]{2,1,0:T(8,128)(2,1)} async-done(((bf16[8,72,1536]{2,1,0:T(8,128)(2,1)}), bf16[8,72,1536]{2,1,0:T(8,128)(2,1)}, u32[]{:S(2)}, u32[]{:S(2)}) %all-to-all-start.1) | async-done | bytes 1769504 | tf_op jit(solution)/shard_map/all_to_all | solution.py:137
  205.7 9.4 %fusion.18 = bf16[576,2304]{1,0:T(8,128)(2,1)} fusion(bf16[576,1536]{1,0:T(8,128)(2,1)} %bitcast.17, bf16[1,1536,2304]{2,1,0:T(8,128)(2,1)} %param.17), kind=kOutput, calls=%fused_computation.22 | convolution fusion | flops 4078190592 | bytes 11501568 | tf_op jit(solution)/shard_map/dot_general | solution.py:144
  215.3 102.7 %all-reduce.4.cloned.1.call-done = (bf16[576,2304]{1,0:T(8,128)(2,1)}, bf16[576,2304]{1,0:T(8,128)(2,1)}) async-done(((bf16[576,2304]{1,0:T(8,128)(2,1)}, bf16[576,2304]{1,0:T(8,128)(2,1)}), (bf16[576,2304]{1,0:T(8,128)(2,1)}, bf16[576,2304]{1,0:T(8,128)(2,1)})) %all-reduce.4.cloned.1.call-update) | async-done | bytes 5308432 | tf_op jit(solution)/shard_map/psum | solution.py:147
  318.1 9.7 %fusion.21 = bf16[576,1536]{1,0:T(8,128)(2,1)S(1)} fusion(bf16[1,1536,2304]{2,1,0:T(8,128)(2,1)} %param.17, bf16[576,2304]{1,0:T(8,128)(2,1)} %get-tuple-element.316, bf16[576,2304]{1,0:T(8,128)(2,1)} %get-tuple-element.317), kind=kOutput, calls=%fused_computation.24 | convolution fusion | flops 4092346368 | bytes 14155776 | tf_op jit(solution)/shard_map/dot_general | solution.py:86
  327.8 46.4 %all_to_all.15 = bf16[8,72,1536]{2,1,0:T(8,128)(2,1)S(1)} all-to-all(bf16[8,72,1536]{2,1,0:T(8,128)(2,1)S(1)} %bitcast.168), channel_id=1, replica_groups=mesh['ctx'=8,'exp'=4] {'ctx'}, dimensions={0} | all-to-all | bytes 3538944 | tf_op jit(solution)/shard_map/all_to_all | solution.py:153
  374.5 1.5 fusion.26
  376.3 1.8 fusion.43
  381.8 94.0 %all-gather.8.cloned.1.call-done = f32[96,128,128]{2,1,0:T(8,128)} async-done(((f32[12,128,128]{2,1,0:T(8,128)}), f32[96,128,128]{2,1,0:T(8,128)}) %all-gather.8.cloned.1.call-update) | async-done | bytes 6291472 | tf_op jit(solution)/shard_map/all_gather | solution.py:14
  475.8 6.3 %rev.7 = f32[8,12,128,128]{3,2,1,0:T(8,128)} reverse(f32[8,12,128,128]{3,2,1,0:T(8,128)} %bitcast.148), dimensions={0} | reverse | bytes 12582912 | tf_op jit(solution)/shard_map/rev | solution.py:16
  482.1 13.6 %while.29 = (s32[]{:T(128)}, f32[12,128,128]{2,1,0:T(8,128)S(1)}, s32[]{:T(128)}, f32[8,12,1,1]{1,3,2,0:T(1,128)}, f32[8,12,128,128]{3,2,1,0:T(8,128)}, /*index=5*/s32[]{:T(128)}, s32[]{:T(128)}) while((s32[]{:T(128)}, f32[12,128,128]{2,1,0:T(8,128)S(1)}, s32[]{:T(128)}, f32[8,12,1,1]{1,3,2,0:T(1,128)}, ...), condition=%wide.region_11.12_spmd.clone, body=%wide.region_10.11_spmd.clone.sunk | while | flops 786436 | bytes 2359545 | solution.py:26
  (101 shorter events, 34.0 us)
Async XLA Ops:
  7.2 7.2 %copy-start.8 = (s32[128,2]{0,1:T(2,128)S(1)}, s32[128,2]{0,1:T(2,128)}, u32[]{:S(2)}) copy-start(s32[128,2]{0,1:T(2,128)} %param.20) | copy-start | bytes 3076
  7.2 9.5 %copy-start.10 = (f32[128,2]{0,1:T(2,128)S(1)}, f32[128,2]{0,1:T(2,128)}, u32[]{:S(2)}) copy-start(f32[128,2]{0,1:T(2,128)} %param.21) | copy-start | bytes 3076
  7.2 9.6 %copy-start = (bf16[128,1536]{1,0:T(8,128)(2,1)S(1)}, bf16[128,1536]{1,0:T(8,128)(2,1)}, u32[]{:S(2)}) copy-start(bf16[128,1536]{1,0:T(8,128)(2,1)} %param.16) | copy-start | bytes 1179652
  7.2 140.7 %all-gather.6.cloned.1.call-start = ((), (), s32[]{:S(2)}) async-start(), calls=%async_computation.3 | async-start | bytes 7077888 | tf_op jit(solution)/shard_map/all_gather | solution.py:14
  12.4 82.9 %copy-start.9 = (f32[12]{0:T(128)}, f32[12]{0:T(128)S(1)}, u32[]{:S(2)}) copy-start(f32[12]{0:T(128)S(1)} %get-tuple-element.322) | copy-start | bytes 148
  17.1 77.8 %copy-start.3 = (bf16[128,1536]{1,0:T(8,128)(2,1)S(1)}, bf16[128,1536]{1,0:T(8,128)(2,1)}, u32[]{:S(2)}) copy-start(bf16[128,1536]{1,0:T(8,128)(2,1)} %param.13) | copy-start | bytes 1179652
  18.6 140.3 %all-to-all-start = ((bf16[8,72,1536]{2,1,0:T(8,128)(2,1)}), bf16[8,72,1536]{2,1,0:T(8,128)(2,1)}, u32[]{:S(2)}, u32[]{:S(2)}) async-start(bf16[8,72,1536]{2,1,0:T(8,128)(2,1)} %bitcast.3), calls=%async_computation | async-start | bytes 3538944 | tf_op jit(solution)/shard_map/all_to_all | solution.py:138
  95.2 52.7 %copy-start.5 = (pred[128,128]{1,0:T(8,128)(4,1)}, pred[128,128]{1,0:T(8,128)(4,1)S(1)}, u32[]{:S(2)}) copy-start(pred[128,128]{1,0:T(8,128)(4,1)S(1)} %subtract_compare_fusion) | copy-start | bytes 49156
  95.3 52.6 %copy-start.4 = (f32[128,128]{1,0:T(8,128)}, f32[128,128]{1,0:T(8,128)S(1)}, u32[]{:S(2)}) copy-start(f32[128,128]{1,0:T(8,128)S(1)} %subtract_maximum_fusion) | copy-start | bytes 196612
  95.8 62.3 %copy-start.1 = (bf16[12,128,128]{2,1,0:T(8,128)(2,1)}, bf16[12,128,128]{2,1,0:T(8,128)(2,1)S(1)}, u32[]{:S(2)}) copy-start(bf16[12,128,128]{2,1,0:T(8,128)(2,1)S(1)} %fusion.38) | copy-start | bytes 1179652
  157.3 1.2 copy-start.6
  160.2 45.5 %all-to-all-start.1 = ((bf16[8,72,1536]{2,1,0:T(8,128)(2,1)}), bf16[8,72,1536]{2,1,0:T(8,128)(2,1)}, u32[]{:S(2)}, u32[]{:S(2)}) async-start(bf16[8,72,1536]{2,1,0:T(8,128)(2,1)} %bitcast.16), calls=%async_computation.1 | async-start | bytes 3538944 | tf_op jit(solution)/shard_map/all_to_all | solution.py:137
  164.6 153.5 %all-reduce.4.cloned.1.call-start = ((), (), s32[]{:S(2)}) async-start(), calls=%async_computation.5 | async-start | bytes 10616832 | tf_op jit(solution)/shard_map/psum | solution.py:147
  215.1 260.7 %all-gather.8.cloned.1.call-start = ((), (), s32[]{:S(2)}) async-start(), calls=%async_computation.4 | async-start | bytes 7077888 | tf_op jit(solution)/shard_map/all_gather | solution.py:14
  374.5 3.6 copy-start.7
  495.7 1.3 copy-start.2
Sparse Core Ops, SparseCore 0:
  14.5 133.3 all-gather.5
  215.2 102.8 all-reduce.3
  378.2 97.5 all-gather.7
where the time goes:
time: 507 us; the launch traced here: 506 us
  waiting for transfers between devices  281 us (55%)
  blocking collectives  115 us (23%)
  matrix products  39.9 us (8%)
  local copies, waits for them, and re-layouts  22 us (4%)
  other arithmetic  20.9 us (4%)
  between operations  14.8 us (3%)
  starting transfers between devices  11.9 us (2%)
    all_gather x2, waiting for transfers between devices, carried_in(): pieces = jax.tree.map(lambda part: lax.all_gather(part, axis), value)  146 us
    psum x1, waiting for transfers between devices, on_device(): lax.psum(pre_part.astype(jnp.bfloat16), 'exp').astype(jnp.float32)  103 us
    unnamed x1, blocking collectives  69 us
    all_to_all x1, blocking collectives, on_device(): lax.all_to_all(back_half, 'ctx', split_axis=0, concat_axis=0, tiled=True)  46.4 us
    all_to_all x1, waiting for transfers between devices, on_device(): lax.all_to_all(doubled(send_in), 'ctx', split_axis=0, concat_axis=0, tile...  31.7 us
    dot_general x2, matrix products, contract_last(): lax.dot_general(left, right, (((1,), (1,)), ((), ())), preferred_element_...  19.1 us
    select_n x14, other arithmetic, lap(): jnp.where(position < mine, new, old)  18.2 us
  transfers between devices with their start and end apart: 5, of which 4 were waited for; matrix products, arithmetic and copies ran while one was open for 6% of the time, Pallas kernels for 0%

commit v1 on v0

v1 whole, which is shorter than its diff:
```python
import functools

import jax
import jax.numpy as jnp
from jax import lax
from jax.experimental import pallas as pl
from jax.experimental.pallas import tpu as pltpu
from jax.sharding import PartitionSpec as P

DH = 128
F32 = jnp.float32
BF16 = jnp.bfloat16
SCALE = 1.0 / DH

SMEM = pl.BlockSpec(memory_space=pltpu.SMEM)
VMEM = pl.BlockSpec(memory_space=pltpu.VMEM)


def dot(left, right, left_dim, right_dim):
    return lax.dot_general(
        left, right, (((left_dim,), (right_dim,)), ((), ())), preferred_element_type=F32
    )


def silu_slope(value):
    sigma = jax.nn.sigmoid(value)
    return sigma * (1.0 + value * (1.0 - sigma))


def lanes_of(place_ref, slot, heads):
    head = lax.rem(place_ref[0] * (heads // 2) + slot, heads)
    return head, pl.ds(pl.multiple_of(head * DH, DH), DH)


def column(block_len):
    return lax.broadcasted_iota(jnp.int32, (block_len, 1), 0).astype(F32)


def decay_within(rate, block_len):
    rows = lax.broadcasted_iota(jnp.int32, (block_len, block_len), 0)
    cols = lax.broadcasted_iota(jnp.int32, (block_len, block_len), 1)
    distance = (rows - cols).astype(F32)
    return jnp.where(distance >= 0.0, jnp.exp(-rate * jnp.maximum(distance, 0.0)), 0.0)


def key_state_kernel(place_ref, rates_ref, k_ref, v_ref, state_ref):
    block_len, heads = k_ref.shape[0], state_ref.shape[0]
    steps = column(block_len)
    for slot in range(heads):
        head, lanes = lanes_of(place_ref, slot, heads)
        power = jnp.exp(-rates_ref[head] * (block_len - steps))
        scaled = (k_ref[:, lanes].astype(F32) * power).astype(BF16)
        state_ref[slot] = dot(scaled, v_ref[:, lanes], 0, 0).astype(BF16)


def route_kernel(place_ref, routes_ref, gates_ref, grad_ref, choose_ref, weigh_ref, *send_refs):
    experts, block_len, capacity = choose_ref.shape
    routes = routes_ref[...]
    gates = gates_ref[...]
    first, second = routes[:, 0:1], routes[:, 1:2]
    wide = lax.broadcasted_iota(jnp.int32, (block_len, 128), 1)
    hit_first = jnp.where(wide == first, 1.0, 0.0)
    hit_second = jnp.where(wide == second, 1.0, 0.0)
    rows = lax.broadcasted_iota(jnp.int32, (block_len, block_len), 0)
    cols = lax.broadcasted_iota(jnp.int32, (block_len, block_len), 1)
    earlier = jnp.where(rows > cols, 1.0, 0.0).astype(BF16)
    before = dot(earlier, (hit_first + hit_second).astype(BF16), 1, 0)
    slot_first = jnp.sum(before * hit_first, axis=1, keepdims=True).astype(jnp.int32)
    slot_second = jnp.sum(before * hit_second, axis=1, keepdims=True).astype(jnp.int32)
    slots = lax.broadcasted_iota(jnp.int32, (block_len, capacity), 1)
    for k in range(experts):
        expert = place_ref[1] ^ k
        one = jnp.where((slots == slot_first) & (first == expert), 1.0, 0.0)
        two = jnp.where((slots == slot_second) & (second == expert), 1.0, 0.0)
        choose = (one + two).astype(BF16)
        choose_ref[k] = choose
        weigh_ref[k] = (one * gates[:, 0:1] + two * gates[:, 1:2]).astype(BF16)
        send_refs[k][...] = dot(choose, grad_ref[...], 0, 0).astype(BF16)


def intra_kernel(place_ref, rates_ref, q_ref, k_ref, v_ref, intra_ref, weights_ref):
    block_len, heads = q_ref.shape[0], weights_ref.shape[0]
    for slot in range(heads):
        head, lanes = lanes_of(place_ref, slot, heads)
        within = decay_within(rates_ref[head], block_len)
        scores = dot(q_ref[:, lanes], k_ref[:, lanes], 1, 1)
        weights = (SCALE * scores * within).astype(BF16)
        weights_ref[slot] = weights
        intra_ref[:, lanes] = dot(weights, v_ref[:, lanes], 1, 0)


def joined_state(far_refs, near_refs, slot, half, rate, block_len, use_near):
    far, near = far_refs[slot // half][slot % half], near_refs[slot // half][slot % half]
    whole = jnp.exp(jnp.full((1, DH), -rate * block_len, F32))
    step = jnp.where(use_near, whole, 1.0)
    return far.astype(F32) * step + jnp.where(use_near, near.astype(F32), 0.0)


def attend_kernel(
    place_ref, rates_ref, q_ref, intra_ref, choose_ref, far0, far1, near0, near1, enter_ref, *send_refs
):
    block_len, heads = q_ref.shape[0], enter_ref.shape[0]
    half = heads // 2
    steps = column(block_len)
    for slot in range(heads):
        head, lanes = lanes_of(place_ref, slot, heads)
        rate = rates_ref[head]
        entering = joined_state(
            (far0, far1), (near0, near1), slot, half, rate, block_len, place_ref[0] == 1
        ).astype(BF16)
        enter_ref[slot] = entering
        inter = SCALE * jnp.exp(-rate * steps) * dot(q_ref[:, lanes], entering, 1, 0)
        attn = (intra_ref[:, lanes] + inter).astype(BF16)
        for k in range(len(send_refs)):
            send_refs[k][:, lanes] = dot(choose_ref[k], attn, 0, 0).astype(BF16)


def grad_kernel(place_ref, rates_ref, q_ref, out_grad_ref, weigh_ref, *refs):
    experts = weigh_ref.shape[0]
    home_refs, (grad_ref, state_ref) = refs[:experts], refs[experts:]
    block_len, heads = q_ref.shape[0], state_ref.shape[0]
    steps = column(block_len)
    for slot in range(heads):
        head, lanes = lanes_of(place_ref, slot, heads)
        total = out_grad_ref[:, lanes].astype(F32)
        for k in range(experts):
            total = total + dot(weigh_ref[k], home_refs[k][:, lanes], 1, 0)
        grad = total.astype(BF16)
        grad_ref[:, lanes] = grad
        power = jnp.exp(-rates_ref[head] * (steps + 1.0))
        scaled = (q_ref[:, lanes].astype(F32) * power).astype(BF16)
        state_ref[slot] = dot(scaled, grad, 0, 0).astype(BF16)


def near_kernel(
    place_ref, rates_ref, q_ref, k_ref, v_ref, grad_ref, enter_ref, weights_ref,
    query_ref, key_ref, value_ref,
):
    block_len, heads = q_ref.shape[0], enter_ref.shape[0]
    steps = column(block_len)
    for slot in range(heads):
        head, lanes = lanes_of(place_ref, slot, heads)
        rate = rates_ref[head]
        grad = grad_ref[:, lanes]
        within = decay_within(rate, block_len)
        dweights = (SCALE * dot(grad, v_ref[:, lanes], 1, 1) * within).astype(BF16)
        query = dot(dweights, k_ref[:, lanes], 1, 0)
        query = query + SCALE * jnp.exp(-rate * steps) * dot(grad, enter_ref[slot], 1, 1)
        query_ref[:, lanes] = query.astype(BF16)
        key_ref[:, lanes] = dot(dweights, q_ref[:, lanes], 0, 0)
        value_ref[:, lanes] = dot(weights_ref[slot], grad, 0, 0)


def far_kernel(
    place_ref, rates_ref, k_ref, v_ref, key_near, value_near, far0, far1, near0, near1, key_ref, value_ref
):
    block_len = k_ref.shape[0]
    half = far0.shape[0]
    heads = 2 * half
    steps = column(block_len)
    for slot in range(heads):
        head, lanes = lanes_of(place_ref, slot, heads)
        rate = rates_ref[head]
        leaving = joined_state(
            (far0, far1), (near0, near1), slot, half, rate, block_len, place_ref[0] == 0
        ).astype(BF16)
        power = SCALE * jnp.exp(-rate * (block_len - 1.0 - steps))
        key_ref[:, lanes] = (
            key_near[:, lanes] + power * dot(v_ref[:, lanes], leaving, 1, 1)
        ).astype(BF16)
        value_ref[:, lanes] = (
            value_near[:, lanes] + power * dot(k_ref[:, lanes], leaving, 1, 0)
        ).astype(BF16)


def call(kernel, out_shapes, scalars, arrays, flops):
    size = sum(leaf.size * leaf.dtype.itemsize for leaf in list(arrays) + list(out_shapes))
    return pl.pallas_call(
        kernel,
        out_shape=list(out_shapes),
        in_specs=[SMEM] * len(scalars) + [VMEM] * len(arrays),
        out_specs=[VMEM] * len(out_shapes),
        compiler_params=pltpu.CompilerParams(vmem_limit_bytes=32 * 1024 * 1024),
        cost_estimate=pl.CostEstimate(flops=flops, bytes_accessed=size, transcendentals=0),
    )(*scalars, *arrays)


def swap(array, axis, distance):
    size = lax.axis_size(axis)
    return lax.ppermute(array, axis, [(i, i ^ distance) for i in range(size)])


def to_pair(array, pairs):
    return lax.ppermute(array, "ctx", [(2 * a + s, 2 * b + s) for a, b in pairs for s in (0, 1)])


def scan_states(state, rates, place, block_len, reverse):
    heads = state.shape[0]
    half = heads // 2
    pairs = lax.axis_size("ctx") // 2
    side, pair = place[0], place[1]
    if reverse:
        side, pair = 1 - side, pairs - 1 - pair
    mine = lax.dynamic_slice(rates, (place[0] * half,), (half,))[:, None, None]
    power = lambda tokens: jnp.exp(-mine * tokens)
    partner = swap(state[half:], "ctx", 1)
    first_end = 1 if reverse else 0
    other = lax.ppermute(
        state[:half], "ctx", [(2 * i + first_end, 2 * i + 1 - first_end) for i in range(pairs)]
    )
    whole = power(float(block_len))
    own_wide, partner_wide = state[:half].astype(F32), partner.astype(F32)
    total = jnp.where(
        side == 0, whole * own_wide + partner_wide, own_wide + whole * partner_wide
    ).astype(BF16)
    before = jnp.zeros_like(total)
    reach = 1
    while reach < pairs:
        if reach == 1:
            upto = total
        else:
            upto = (power(2.0 * block_len) * before.astype(F32) + total.astype(F32)).astype(BF16)
        got = []
        for j in range(reach):
            moves = [(g + reach - 1, g + reach + j) for g in range(0, pairs, 2 * reach)]
            if reverse:
                moves = [(pairs - 1 - a, pairs - 1 - b) for a, b in moves]
            got.append(to_pair(upto, moves))
        got = functools.reduce(lambda a, b: a + b, got)
        steps = lax.rem(pair, reach).astype(F32)
        if reach == 1:
            before = got
        else:
            before = (
                before.astype(F32) + power(2.0 * block_len * steps) * got.astype(F32)
            ).astype(BF16)
        reach *= 2
    return before, swap(before, "ctx", 1), partner, other


def to_experts(sends):
    pairs = len(sends)
    got = [sends[0]] + [swap(sends[k], "ctx", 2 * k) for k in range(1, pairs)]
    chunks = []
    for first in (0, pairs // 2):
        own = jnp.concatenate(got[first : first + pairs // 2], axis=0)
        chunks.append(jnp.concatenate([own, swap(own, "ctx", 1)], axis=0))
    return chunks


def scatter_sum(part, bits):
    for bit in range(bits):
        mine = (lax.axis_index("exp") >> bit) & 1
        halves = part.reshape(2, part.shape[0] // 2, part.shape[1])
        got = swap(lax.dynamic_index_in_dim(halves, 1 - mine, 0, False), "exp", 1 << bit)
        kept = lax.dynamic_index_in_dim(halves, mine, 0, False)
        part = kept.astype(F32) + got.astype(F32)
        if bit < bits - 1:
            part = part.astype(BF16)
    return part


def gather_all(part, bits):
    for bit in reversed(range(bits)):
        mine = (lax.axis_index("exp") >> bit) & 1
        got = swap(part, "exp", 1 << bit)
        part = jnp.concatenate(
            [jnp.where(mine == 0, part, got), jnp.where(mine == 0, got, part)], axis=0
        )
    return part


def on_device(
    queries, keys, values, out_grad, up_weight, down_weight, decay_rates, routes, gate_weights
):
    block_len, group = queries.shape
    heads = group // DH
    half = heads // 2
    experts = lax.axis_size("ctx") // 2
    bits = (lax.axis_size("exp") - 1).bit_length()
    capacity = block_len * 9 // (4 * experts)
    position = lax.axis_index("ctx").astype(jnp.int32)
    place = jnp.stack([position & 1, position >> 1])
    scalars = (place, decay_rates)
    up_local, down_local = up_weight[0], down_weight[0]

    states = jax.ShapeDtypeStruct((heads, DH, DH), BF16)
    weight_sq = jax.ShapeDtypeStruct((heads, block_len, block_len), BF16)
    wide = jax.ShapeDtypeStruct((block_len, group), F32)
    slim = jax.ShapeDtypeStruct((block_len, group), BF16)
    table = jax.ShapeDtypeStruct((experts, block_len, capacity), BF16)
    slots = jax.ShapeDtypeStruct((capacity, group), BF16)
    unit = 2 * block_len * DH * group

    (key_local,) = call(key_state_kernel, [states], scalars, (keys, values), unit)
    choose, weigh, *send_grad = call(
        route_kernel, [table, table] + [slots] * experts, (place,),
        (routes, gate_weights, out_grad), 3 * unit,
    )
    intra, weights = call(intra_kernel, [wide, weight_sq], scalars, (queries, keys, values), 2 * unit)
    enter_states = scan_states(key_local, decay_rates, place, block_len, False)
    entering, *send_in = call(
        attend_kernel, [states] + [slots] * experts, scalars,
        (queries, intra, choose) + enter_states, 4 * unit,
    )

    grad_chunks = to_experts(send_grad)
    in_chunks = to_experts(send_in)
    homes = []
    for in_rows, grad_rows in zip(in_chunks, grad_chunks):
        grad_part = dot(grad_rows, down_local, 1, 1).astype(BF16)
        hidden_grad = scatter_sum(grad_part, bits)
        pre_part = dot(in_rows, up_local, 1, 0).astype(BF16)
        pre = scatter_sum(pre_part, bits)
        slope = (hidden_grad * silu_slope(pre)).astype(BF16)
        slope = gather_all(slope, bits)
        back = dot(slope, up_local, 1, 1).astype(BF16)
        kept = back.shape[0] // 2
        got = swap(back[kept:], "ctx", 1)
        summed = (back[:kept].astype(F32) + got.astype(F32)).astype(BF16)
        for i in range(experts // 2):
            rows = summed[i * capacity : (i + 1) * capacity]
            k = len(homes)
            homes.append(swap(rows, "ctx", 2 * k) if k else rows)

    grad_out, query_local = call(
        grad_kernel, [slim, states], scalars, (queries, out_grad, weigh, *homes), 4 * unit
    )
    leave_states = scan_states(query_local, decay_rates, place, block_len, True)
    query_g, key_near, value_near = call(
        near_kernel, [slim, wide, wide], scalars,
        (queries, keys, values, grad_out, entering, weights), 5 * unit,
    )
    key_g, value_g = call(
        far_kernel, [slim, slim], scalars,
        (keys, values, key_near, value_near) + leave_states, 2 * unit,
    )
    return query_g, key_g, value_g


def solution(mesh):
    placed = (
        P("ctx", "exp"),
        P("ctx", "exp"),
        P("ctx", "exp"),
        P("ctx", "exp"),
        P("ctx", "exp", None),
        P("ctx", None, "exp"),
        P("exp"),
        P("ctx", None),
        P("ctx", None),
    )
    return jax.shard_map(
        on_device,
        mesh=mesh,
        in_specs=placed,
        out_specs=(P("ctx", "exp"), P("ctx", "exp"), P("ctx", "exp")),
        check_vma=False,
    )
```

time: 507 us -> 220 us (0.43)
  waiting for transfers between devices: 281 us -> 111 us
  blocking collectives: 115 us -> 0 us
  starting transfers between devices: 11.9 us -> 58.2 us
  matrix products: 39.9 us -> 17.9 us
  Pallas kernels: 0 us -> 17.8 us
  local copies, waits for them, and re-layouts: 22 us -> 6.25 us
  other arithmetic: 20.9 us -> 6.61 us
  between operations: 14.8 us -> 1.25 us
    all_gather x2 -> x0, waiting for transfers between devices: 146 us -> none  [carried_in(): pieces = jax.tree.map(lambda part: lax.all_gather(part, axis), value)]
    ppermute x0 -> x39, waiting for transfers between devices: none -> 111 us  [the longest x31 96.5 us: swap(): return lax.ppermute(array, axis, [(i, i ^ distance) for i in range(size)])]
    psum x1 -> x0, waiting for transfers between devices: 103 us -> none  [on_device(): lax.psum(pre_part.astype(jnp.bfloat16), 'exp').astype(jnp.float32)]
    unnamed x1 -> x0, blocking collectives: 69 us -> none
    ppermute x0 -> x39, starting transfers between devices: none -> 58.2 us  [the longest x31 46.5 us: swap(): return lax.ppermute(array, axis, [(i, i ^ distance) for i in range(size)])]
    all_to_all x1 -> x0, blocking collectives: 46.4 us -> none  [on_device(): lax.all_to_all(back_half, 'ctx', split_axis=0, concat_axis=0, tiled=True)]
    all_to_all x2 -> x0, waiting for transfers between devices: 31.7 us -> none  [the longest x1 31.7 us: on_device(): lax.all_to_all(doubled(send_in), 'ctx', split_axis=0, concat_axis=0, tile...]
    dot_general x18 -> x6, matrix products: 39.9 us -> 17.9 us  [dot(): lax.dot_general(left, right, (((left_dim,), (right_dim,)), ((), ())), pre...]
  transfers between devices with their start and end apart: 5 -> 39, of which waited for: 4 -> 20; matrix products, arithmetic and copies ran while one was open for 6% -> 11% of each run, Pallas kernels for 0% -> 5%
where the time goes in v1:
time: 220 us; the launch traced here: 219 us
  waiting for transfers between devices  111 us (50%)
  starting transfers between devices  58.2 us (26%)
  matrix products  17.9 us (8%)
  Pallas kernels  17.8 us (8%)
  other arithmetic  6.61 us (3%)
  local copies, waits for them, and re-layouts  6.25 us (3%)
    ppermute x31, waiting for transfers between devices, swap(): return lax.ppermute(array, axis, [(i, i ^ distance) for i in range(size)])  96.5 us
    ppermute x31, starting transfers between devices, swap(): return lax.ppermute(array, axis, [(i, i ^ distance) for i in range(size)])  46.5 us
    dot_general x6, matrix products, dot(): lax.dot_general(left, right, (((left_dim,), (right_dim,)), ((), ())), pre...  17.9 us
    pallas_call x7, Pallas kernels, call(): pl.pallas_call(kernel, out_shape=list(out_shapes), in_specs=[SMEM] * len(...  17.8 us
    ppermute x6, waiting for transfers between devices, to_pair(): lax.ppermute(array, 'ctx', [(2 * a + s, 2 * b + s) for a, b in pairs for...  14.9 us
    ppermute x6, starting transfers between devices, to_pair(): lax.ppermute(array, 'ctx', [(2 * a + s, 2 * b + s) for a, b in pairs for...  8.49 us
    unnamed x48, local copies, waits for them, and re-layouts  4.99 us
  transfers between devices with their start and end apart: 39, of which 20 were waited for; matrix products, arithmetic and copies ran while one was open for 11% of the time, Pallas kernels for 5%

profile of v1, /device:TPU:0, one launch (start us, length us, event | category | flops | bytes accessed | tf_op | source)
XLA Modules:
  0.0 219.4 jit_solution(9291944321986647199)
XLA Ops:
  14.4 3.1 %collective-permute-start.18 = (bf16[72,1536]{1,0:T(8,128)(2,1)}, bf16[72,1536]{1,0:T(8,128)(2,1)}, u32[]{:S(2)}, u32[]{:S(2)}) collective-permute-start(bf16[72,1536]{1,0:T(8,128)(2,1)} %get-tuple-element.30), channel_id=1, source_target_pairs={{0,16},{4,20},{8,24},{12,28},{16,0},{20,4},{24,8},{28,12},{1,17},{... | collective-permute-start | bytes 663560 | tf_op jit(solution)/shard_map/ppermute | solution.py:190
  23.2 3.7 %collective-permute-start.5 = (bf16[6,128,128]{2,1,0:T(8,128)(2,1)S(1)}, bf16[6,128,128]{2,1,0:T(8,128)(2,1)S(1)}, u32[]{:S(2)}, u32[]{:S(2)}) collective-permute-start(bf16[6,128,128]{2,1,0:T(8,128)(2,1)S(1)} %fusion.65), channel_id=1, source_target_pairs={{0,8},{4,12},{16,24},{20,28},{1,9},{5,13},{17,25},{21,29},{2,10},{... | collective-permute-start | bytes 589832 | tf_op jit(solution)/shard_map/ppermute | solution.py:194
  26.9 6.6 %collective-permute-done.18 = bf16[72,1536]{1,0:T(8,128)(2,1)} collective-permute-done((bf16[72,1536]{1,0:T(8,128)(2,1)}, bf16[72,1536]{1,0:T(8,128)(2,1)}, u32[]{:S(2)}, u32[]{:S(2)}) %collective-permute-start.18) | collective-permute-done | bytes 221216 | tf_op jit(solution)/shard_map/ppermute | solution.py:190
  40.6 7.1 %collective-permute-done.20 = bf16[144,1536]{1,0:T(8,128)(2,1)S(1)} collective-permute-done((bf16[144,1536]{1,0:T(8,128)(2,1)S(1)}, bf16[144,1536]{1,0:T(8,128)(2,1)S(1)}, u32[]{:S(2)}, u32[]{:S(2)}) %collective-permute-start.20) | collective-permute-done | bytes 442400 | tf_op jit(solution)/shard_map/ppermute | solution.py:190
  47.7 5.5 %fusion.15 = bf16[288,2304]{1,0:T(8,128)(2,1)S(1)} fusion(bf16[1,2304,1536]{2,1,0:T(8,128)(2,1)} %param.14, bf16[144,1536]{1,0:T(8,128)(2,1)S(1)} %collective-permute-done.20, bf16[72,1536]{1,0:T(8,128)(2,1)} %collective-permute-done.19, bf16[72,1536]{1,0:T(8,128)(2,1)} %collective-permute-done.18), kind=kOutput, calls=%fused_computation.13 | convolution fusion | flops 2041749504 | bytes 9289728 | tf_op jit(solution)/shard_map/dot_general | solution.py:20
  56.0 3.2 %fusion.12 = bf16[288,2304]{1,0:T(8,128)(2,1)S(1)} fusion(bf16[1,2304,1536]{2,1,0:T(8,128)(2,1)S(1)} %bitcast.93, bf16[144,1536]{1,0:T(8,128)(2,1)S(1)} %collective-permute-done.1, bf16[72,1536]{1,0:T(8,128)(2,1)} %collective-permute-done, bf16[72,1536]{1,0:T(8,128)(2,1)S(1)} %copy-done.9), kind=kOutput, calls=%fused_computation.12 | convolution fusion | flops 2041749504 | bytes 9289728 | tf_op jit(solution)/shard_map/dot_general | solution.py:20
  62.3 7.4 %collective-permute-start.23 = (bf16[72,1536]{1,0:T(8,128)(2,1)S(1)}, bf16[72,1536]{1,0:T(8,128)(2,1)S(1)}, u32[]{:S(2)}, u32[]{:S(2)}) collective-permute-start(bf16[72,1536]{1,0:T(8,128)(2,1)S(1)} %get-tuple-element.32), channel_id=1, source_target_pairs={{0,16},{4,20},{8,24},{12,28},{16,0},{20,4},{24,8},{28,12},{1,17},{... | collective-permute-start | bytes 663560 | tf_op jit(solution)/shard_map/ppermute | solution.py:190
  70.6 14.6 %collective-permute-done.23 = bf16[72,1536]{1,0:T(8,128)(2,1)S(1)} collective-permute-done((bf16[72,1536]{1,0:T(8,128)(2,1)S(1)}, bf16[72,1536]{1,0:T(8,128)(2,1)S(1)}, u32[]{:S(2)}, u32[]{:S(2)}) %collective-permute-start.23) | collective-permute-done | bytes 221216 | tf_op jit(solution)/shard_map/ppermute | solution.py:190
  90.1 8.2 %collective-permute-done.25 = bf16[144,1536]{1,0:T(8,128)(2,1)S(1)} collective-permute-done((bf16[144,1536]{1,0:T(8,128)(2,1)S(1)}, bf16[144,1536]{1,0:T(8,128)(2,1)S(1)}, u32[]{:S(2)}, u32[]{:S(2)}) %collective-permute-start.25) | collective-permute-done | bytes 442400 | tf_op jit(solution)/shard_map/ppermute | solution.py:190
  100.8 3.8 %collective-permute-done.11 = bf16[144,1536]{1,0:T(8,128)(2,1)S(1)} collective-permute-done((bf16[144,1536]{1,0:T(8,128)(2,1)S(1)}, bf16[144,1536]{1,0:T(8,128)(2,1)S(1)}, u32[]{:S(2)}, u32[]{:S(2)}) %collective-permute-start.11) | collective-permute-done | bytes 442400 | tf_op jit(solution)/shard_map/ppermute | solution.py:190
  110.9 7.0 %collective-permute-done.27 = bf16[72,2304]{1,0:T(8,128)(2,1)S(1)} collective-permute-done((bf16[72,2304]{1,0:T(8,128)(2,1)S(1)}, bf16[72,2304]{1,0:T(8,128)(2,1)S(1)}, u32[]{:S(2)}, u32[]{:S(2)}) %collective-permute-start.27) | collective-permute-done | bytes 331808 | tf_op jit(solution)/shard_map/ppermute | solution.py:190
  119.8 5.2 %collective-permute-done.13 = bf16[72,2304]{1,0:T(8,128)(2,1)S(1)} collective-permute-done((bf16[72,2304]{1,0:T(8,128)(2,1)S(1)}, bf16[72,2304]{1,0:T(8,128)(2,1)S(1)}, u32[]{:S(2)}, u32[]{:S(2)}) %collective-permute-start.13) | collective-permute-done | bytes 331808 | tf_op jit(solution)/shard_map/ppermute | solution.py:190
  126.9 5.2 %collective-permute-done.28 = bf16[72,2304]{1,0:T(8,128)(2,1)S(1)} collective-permute-done((bf16[72,2304]{1,0:T(8,128)(2,1)S(1)}, bf16[72,2304]{1,0:T(8,128)(2,1)S(1)}, u32[]{:S(2)}, u32[]{:S(2)}) %collective-permute-start.28) | collective-permute-done | bytes 331808 | tf_op jit(solution)/shard_map/ppermute | solution.py:190
  132.3 6.5 %collective-permute-done.14 = bf16[72,2304]{1,0:T(8,128)(2,1)S(1)} collective-permute-done((bf16[72,2304]{1,0:T(8,128)(2,1)S(1)}, bf16[72,2304]{1,0:T(8,128)(2,1)S(1)}, u32[]{:S(2)}, u32[]{:S(2)}) %collective-permute-start.14) | collective-permute-done | bytes 331808 | tf_op jit(solution)/shard_map/ppermute | solution.py:190
  146.4 8.3 %collective-permute-done.30 = bf16[144,1536]{1,0:T(8,128)(2,1)S(1)} collective-permute-done((bf16[144,1536]{1,0:T(8,128)(2,1)S(1)}, bf16[144,1536]{1,0:T(8,128)(2,1)S(1)}, u32[]{:S(2)}, u32[]{:S(2)}) %collective-permute-start.30) | collective-permute-done | bytes 442400 | tf_op jit(solution)/shard_map/ppermute | solution.py:190
  154.9 8.6 %collective-permute-start.31 = (bf16[72,1536]{1,0:T(8,128)(2,1)S(1)}, bf16[72,1536]{1,0:T(8,128)(2,1)S(1)}, u32[]{:S(2)}, u32[]{:S(2)}) collective-permute-start(bf16[72,1536]{1,0:T(8,128)(2,1)S(1)} %get-tuple-element.54), channel_id=1, source_target_pairs={{0,16},{4,20},{8,24},{12,28},{16,0},{20,4},{24,8},{28,12},{1,17},{... | collective-permute-start | bytes 663560 | tf_op jit(solution)/shard_map/ppermute | solution.py:190
  164.1 6.6 %collective-permute-start.17 = (bf16[72,1536]{1,0:T(8,128)(2,1)S(1)}, bf16[72,1536]{1,0:T(8,128)(2,1)S(1)}, u32[]{:S(2)}, u32[]{:S(2)}) collective-permute-start(bf16[72,1536]{1,0:T(8,128)(2,1)S(1)} %get-tuple-element.55), channel_id=1, source_target_pairs={{0,8},{4,12},{8,0},{12,4},{16,24},{20,28},{24,16},{28,20},{1,9},{5... | collective-permute-start | bytes 663560 | tf_op jit(solution)/shard_map/ppermute | solution.py:190
  170.7 7.5 %collective-permute-done.31.refs_2_ = bf16[72,1536]{1,0:T(8,128)(2,1)S(1)} collective-permute-done((bf16[72,1536]{1,0:T(8,128)(2,1)S(1)}, bf16[72,1536]{1,0:T(8,128)(2,1)S(1)}, u32[]{:S(2)}, u32[]{:S(2)}) %collective-permute-start.31) | collective-permute-done | bytes 221216 | tf_op jit(solution)/shard_map/ppermute | solution.py:190
  178.2 4.4 %collective-permute-done.17.refs_1_ = bf16[72,1536]{1,0:T(8,128)(2,1)S(1)} collective-permute-done((bf16[72,1536]{1,0:T(8,128)(2,1)S(1)}, bf16[72,1536]{1,0:T(8,128)(2,1)S(1)}, u32[]{:S(2)}, u32[]{:S(2)}) %collective-permute-start.17) | collective-permute-done | bytes 221216 | tf_op jit(solution)/shard_map/ppermute | solution.py:190
  182.6 3.1 %shard_map.116 = (bf16[128,1536]{1,0:T(8,128)(2,1)S(1)}, bf16[12,128,128]{2,1,0:T(8,128)(2,1)S(1)}) custom-call(s32[2]{0:T(128)S(1)} %pad_add_fusion.place_ref, f32[12]{0:T(128)S(1)} %copy-done.15, bf16[128,1536]{1,0:T(8,128)(2,1)S(1)} %copy-done, bf16[128,1536]{1,0:T(8,128)(2,1)S(1)} %copy-done.5, bf16[4,128,72]{2,1,0:T(8,128)(2,1)S(1)} %copy-done.11, ...), custom_call_target="tpu_custom_call" | custom-call | flops 201326592 | bytes 2531328 | tf_op jit(solution)/shard_map/pallas_call | solution.py:178
  186.2 6.5 %collective-permute-done.33.near0 = bf16[6,128,128]{2,1,0:T(8,128)(2,1)S(1)} collective-permute-done((bf16[6,128,128]{2,1,0:T(8,128)(2,1)S(1)}, bf16[6,128,128]{2,1,0:T(8,128)(2,1)S(1)}, u32[]{:S(2)}, u32[]{:S(2)}) %collective-permute-start.33) | collective-permute-done | bytes 196640 | tf_op jit(solution)/shard_map/ppermute | solution.py:190
  194.2 6.6 %collective-permute-done.34 = bf16[6,128,128]{2,1,0:T(8,128)(2,1)S(1)} collective-permute-done((bf16[6,128,128]{2,1,0:T(8,128)(2,1)S(1)}, bf16[6,128,128]{2,1,0:T(8,128)(2,1)S(1)}, u32[]{:S(2)}, u32[]{:S(2)}) %collective-permute-start.34) | collective-permute-done | bytes 196640 | tf_op jit(solution)/shard_map/ppermute | solution.py:194
  204.2 7.4 %collective-permute-done.36 = bf16[6,128,128]{2,1,0:T(8,128)(2,1)S(1)} collective-permute-done((bf16[6,128,128]{2,1,0:T(8,128)(2,1)S(1)}, bf16[6,128,128]{2,1,0:T(8,128)(2,1)S(1)}, u32[]{:S(2)}, u32[]{:S(2)}) %collective-permute-start.36) | collective-permute-done | bytes 196640 | tf_op jit(solution)/shard_map/ppermute | solution.py:194
  212.1 4.0 %shard_map.117 = (bf16[128,1536]{1,0:T(8,128)(2,1)}, f32[128,1536]{1,0:T(8,128)S(1)}, f32[128,1536]{1,0:T(8,128)S(1)}) custom-call(s32[2]{0:T(128)S(1)} %pad_add_fusion.place_ref, f32[12]{0:T(128)S(1)} %copy-done.15, bf16[128,1536]{1,0:T(8,128)(2,1)S(1)} %copy-done, bf16[128,1536]{1,0:T(8,128)(2,1)S(1)} %copy-done.2, bf16[128,1536]{1,0:T(8,128)(2,1)S(1)} %copy-done.4, ...), custom_call_target="tpu_custom_call" | custom-call | flops 251658240 | bytes 4325376 | tf_op jit(solution)/shard_map/pallas_call | solution.py:178
  (158 shorter events, 67.9 us)
Async XLA Ops:
  5.1 17.8 %collective-permute-start.4 = (bf16[6,128,128]{2,1,0:T(8,128)(2,1)}, bf16[6,128,128]{2,1,0:T(8,128)(2,1)S(1)}, u32[]{:S(2)}, u32[]{:S(2)}) collective-permute-start(bf16[6,128,128]{2,1,0:T(8,128)(2,1)} %get-tuple-element.60), channel_id=1, source_target_pairs={{0,4},{4,0},{8,12},{12,8},{16,20},{20,16},{24,28},{28,24},{1,5},{5... | collective-permute-start | bytes 589832 | tf_op jit(solution)/shard_map/ppermute | solution.py:190
  8.1 51.1 %collective-permute-start.9 = (bf16[6,128,128]{2,1,0:T(8,128)(2,1)}, bf16[6,128,128]{2,1,0:T(8,128)(2,1)S(1)}, u32[]{:S(2)}, u32[]{:S(2)}) collective-permute-start(bf16[6,128,128]{2,1,0:T(8,128)(2,1)} %get-tuple-element.59), channel_id=1, source_target_pairs={{0,4},{8,12},{16,20},{24,28},{1,5},{9,13},{17,21},{25,29},{2,6},{1... | collective-permute-start | bytes 589832 | tf_op jit(solution)/shard_map/ppermute | solution.py:208
  14.4 19.0 %collective-permute-start.18 = (bf16[72,1536]{1,0:T(8,128)(2,1)}, bf16[72,1536]{1,0:T(8,128)(2,1)}, u32[]{:S(2)}, u32[]{:S(2)}) collective-permute-start(bf16[72,1536]{1,0:T(8,128)(2,1)} %get-tuple-element.30), channel_id=1, source_target_pairs={{0,16},{4,20},{8,24},{12,28},{16,0},{20,4},{24,8},{28,12},{1,17},{... | collective-permute-start | bytes 663560 | tf_op jit(solution)/shard_map/ppermute | solution.py:190
  17.6 15.9 %collective-permute-start.19 = (bf16[72,1536]{1,0:T(8,128)(2,1)}, bf16[72,1536]{1,0:T(8,128)(2,1)}, u32[]{:S(2)}, u32[]{:S(2)}) collective-permute-start(bf16[72,1536]{1,0:T(8,128)(2,1)} %get-tuple-element.31), channel_id=1, source_target_pairs={{0,24},{4,28},{8,16},{12,20},{16,8},{20,12},{24,0},{28,4},{1,25},{... | collective-permute-start | bytes 663560 | tf_op jit(solution)/shard_map/ppermute | solution.py:190
  18.9 18.4 %collective-permute-start = (bf16[72,1536]{1,0:T(8,128)(2,1)}, bf16[72,1536]{1,0:T(8,128)(2,1)}, u32[]{:S(2)}, u32[]{:S(2)}) collective-permute-start(bf16[72,1536]{1,0:T(8,128)(2,1)} %get-tuple-element.25), channel_id=1, source_target_pairs={{0,8},{4,12},{8,0},{12,4},{16,24},{20,28},{24,16},{28,20},{1,9},{5... | collective-permute-start | bytes 663560 | tf_op jit(solution)/shard_map/ppermute | solution.py:190
  34.6 13.2 %collective-permute-start.20 = (bf16[144,1536]{1,0:T(8,128)(2,1)S(1)}, bf16[144,1536]{1,0:T(8,128)(2,1)S(1)}, u32[]{:S(2)}, u32[]{:S(2)}) collective-permute-start(bf16[144,1536]{1,0:T(8,128)(2,1)S(1)} %pad_maximum_fusion.4), channel_id=1, source_target_pairs={{0,4},{4,0},{8,12},{12,8},{16,20},{20,16},{24,28},{28,24},{1,5},{5... | collective-permute-start | bytes 1327112 | tf_op jit(solution)/shard_map/ppermute | solution.py:190
  38.3 17.7 %collective-permute-start.1 = (bf16[144,1536]{1,0:T(8,128)(2,1)S(1)}, bf16[144,1536]{1,0:T(8,128)(2,1)S(1)}, u32[]{:S(2)}, u32[]{:S(2)}) collective-permute-start(bf16[144,1536]{1,0:T(8,128)(2,1)S(1)} %pad_maximum_fusion.2), channel_id=1, source_target_pairs={{0,4},{4,0},{8,12},{12,8},{16,20},{20,16},{24,28},{28,24},{1,5},{5... | collective-permute-start | bytes 1327112 | tf_op jit(solution)/shard_map/ppermute | solution.py:190
  39.6 19.6 %collective-permute-start.8 = (bf16[6,128,128]{2,1,0:T(8,128)(2,1)S(1)}, bf16[6,128,128]{2,1,0:T(8,128)(2,1)S(1)}, u32[]{:S(2)}, u32[]{:S(2)}) collective-permute-start(bf16[6,128,128]{2,1,0:T(8,128)(2,1)S(1)} %fusion.68.far0), channel_id=1, source_target_pairs={{0,4},{4,0},{8,12},{12,8},{16,20},{20,16},{24,28},{28,24},{1,5},{5... | collective-permute-start | bytes 589832 | tf_op jit(solution)/shard_map/ppermute | solution.py:190
  53.4 34.2 %collective-permute-start.21 = (bf16[144,2304]{1,0:T(8,128)(2,1)S(1)}, bf16[144,2304]{1,0:T(8,128)(2,1)S(1)}, u32[]{:S(2)}, u32[]{:S(2)}) collective-permute-start(bf16[144,2304]{1,0:T(8,128)(2,1)S(1)} %dynamic-slice_bitcast_fusion.1), channel_id=1, source_target_pairs={{0,1},{1,0},{2,3},{3,2},{4,5},{5,4},{6,7},{7,6},{8,9},{9,8},{10,11... | collective-permute-start | bytes 1990664 | tf_op jit(solution)/shard_map/ppermute | solution.py:190
  62.3 22.9 %collective-permute-start.23 = (bf16[72,1536]{1,0:T(8,128)(2,1)S(1)}, bf16[72,1536]{1,0:T(8,128)(2,1)S(1)}, u32[]{:S(2)}, u32[]{:S(2)}) collective-permute-start(bf16[72,1536]{1,0:T(8,128)(2,1)S(1)} %get-tuple-element.32), channel_id=1, source_target_pairs={{0,16},{4,20},{8,24},{12,28},{16,0},{20,4},{24,8},{28,12},{1,17},{... | collective-permute-start | bytes 663560 | tf_op jit(solution)/shard_map/ppermute | solution.py:190
  69.7 15.5 %collective-permute-start.24 = (bf16[72,1536]{1,0:T(8,128)(2,1)S(1)}, bf16[72,1536]{1,0:T(8,128)(2,1)S(1)}, u32[]{:S(2)}, u32[]{:S(2)}) collective-permute-start(bf16[72,1536]{1,0:T(8,128)(2,1)S(1)} %get-tuple-element.33), channel_id=1, source_target_pairs={{0,24},{4,28},{8,16},{12,20},{16,8},{20,12},{24,0},{28,4},{1,25},{... | collective-permute-start | bytes 663560 | tf_op jit(solution)/shard_map/ppermute | solution.py:190
  70.5 18.9 %collective-permute-start.2 = (bf16[144,2304]{1,0:T(8,128)(2,1)S(1)}, bf16[144,2304]{1,0:T(8,128)(2,1)S(1)}, u32[]{:S(2)}, u32[]{:S(2)}) collective-permute-start(bf16[144,2304]{1,0:T(8,128)(2,1)S(1)} %dynamic-slice_bitcast_fusion.3), channel_id=1, source_target_pairs={{0,1},{1,0},{2,3},{3,2},{4,5},{5,4},{6,7},{7,6},{8,9},{9,8},{10,11... | collective-permute-start | bytes 1990664 | tf_op jit(solution)/shard_map/ppermute | solution.py:190
  70.5 16.2 %collective-permute-start.10 = (bf16[72,1536]{1,0:T(8,128)(2,1)S(1)}, bf16[72,1536]{1,0:T(8,128)(2,1)S(1)}, u32[]{:S(2)}, u32[]{:S(2)}) collective-permute-start(bf16[72,1536]{1,0:T(8,128)(2,1)S(1)} %get-tuple-element.29), channel_id=1, source_target_pairs={{0,8},{4,12},{8,0},{12,4},{16,24},{20,28},{24,16},{28,20},{1,9},{5... | collective-permute-start | bytes 663560 | tf_op jit(solution)/shard_map/ppermute | solution.py:190
  85.2 13.2 %collective-permute-start.25 = (bf16[144,1536]{1,0:T(8,128)(2,1)S(1)}, bf16[144,1536]{1,0:T(8,128)(2,1)S(1)}, u32[]{:S(2)}, u32[]{:S(2)}) collective-permute-start(bf16[144,1536]{1,0:T(8,128)(2,1)S(1)} %pad_maximum_fusion.5), channel_id=1, source_target_pairs={{0,4},{4,0},{8,12},{12,8},{16,20},{20,16},{24,28},{28,24},{1,5},{5... | collective-permute-start | bytes 1327112 | tf_op jit(solution)/shard_map/ppermute | solution.py:190
  86.8 17.8 %collective-permute-start.11 = (bf16[144,1536]{1,0:T(8,128)(2,1)S(1)}, bf16[144,1536]{1,0:T(8,128)(2,1)S(1)}, u32[]{:S(2)}, u32[]{:S(2)}) collective-permute-start(bf16[144,1536]{1,0:T(8,128)(2,1)S(1)} %pad_maximum_fusion.3), channel_id=1, source_target_pairs={{0,4},{4,0},{8,12},{12,8},{16,20},{20,16},{24,28},{28,24},{1,5},{5... | collective-permute-start | bytes 1327112 | tf_op jit(solution)/shard_map/ppermute | solution.py:190
  87.8 23.1 %collective-permute-start.22 = (bf16[72,2304]{1,0:T(8,128)(2,1)S(1)}, bf16[72,2304]{1,0:T(8,128)(2,1)S(1)}, u32[]{:S(2)}, u32[]{:S(2)}) collective-permute-start(bf16[72,2304]{1,0:T(8,128)(2,1)S(1)} %dynamic-slice_bitcast_fusion.5), channel_id=1, source_target_pairs={{0,2},{1,3},{2,0},{3,1},{4,6},{5,7},{6,4},{7,5},{8,10},{9,11},{10,... | collective-permute-start | bytes 995336 | tf_op jit(solution)/shard_map/ppermute | solution.py:190
  89.6 30.2 %collective-permute-start.3 = (bf16[72,2304]{1,0:T(8,128)(2,1)S(1)}, bf16[72,2304]{1,0:T(8,128)(2,1)S(1)}, u32[]{:S(2)}, u32[]{:S(2)}) collective-permute-start(bf16[72,2304]{1,0:T(8,128)(2,1)S(1)} %dynamic-slice_bitcast_fusion.7), channel_id=1, source_target_pairs={{0,2},{1,3},{2,0},{3,1},{4,6},{5,7},{6,4},{7,5},{8,10},{9,11},{10,... | collective-permute-start | bytes 995336 | tf_op jit(solution)/shard_map/ppermute | solution.py:190
  109.3 15.7 %collective-permute-start.13 = (bf16[72,2304]{1,0:T(8,128)(2,1)S(1)}, bf16[72,2304]{1,0:T(8,128)(2,1)S(1)}, u32[]{:S(2)}, u32[]{:S(2)}) collective-permute-start(bf16[72,2304]{1,0:T(8,128)(2,1)S(1)} %dynamic-slice_bitcast_fusion.6), channel_id=1, source_target_pairs={{0,2},{1,3},{2,0},{3,1},{4,6},{5,7},{6,4},{7,5},{8,10},{9,11},{10,... | collective-permute-start | bytes 995336 | tf_op jit(solution)/shard_map/ppermute | solution.py:190
  118.2 13.9 %collective-permute-start.28 = (bf16[72,2304]{1,0:T(8,128)(2,1)S(1)}, bf16[72,2304]{1,0:T(8,128)(2,1)S(1)}, u32[]{:S(2)}, u32[]{:S(2)}) collective-permute-start(bf16[72,2304]{1,0:T(8,128)(2,1)S(1)} %fusion.61), channel_id=1, source_target_pairs={{0,2},{1,3},{2,0},{3,1},{4,6},{5,7},{6,4},{7,5},{8,10},{9,11},{10,... | collective-permute-start | bytes 995336 | tf_op jit(solution)/shard_map/ppermute | solution.py:190
  125.3 13.4 %collective-permute-start.14 = (bf16[72,2304]{1,0:T(8,128)(2,1)S(1)}, bf16[72,2304]{1,0:T(8,128)(2,1)S(1)}, u32[]{:S(2)}, u32[]{:S(2)}) collective-permute-start(bf16[72,2304]{1,0:T(8,128)(2,1)S(1)} %fusion.63), channel_id=1, source_target_pairs={{0,2},{1,3},{2,0},{3,1},{4,6},{5,7},{6,4},{7,5},{8,10},{9,11},{10,... | collective-permute-start | bytes 995336 | tf_op jit(solution)/shard_map/ppermute | solution.py:190
  145.3 18.7 %collective-permute-start.16 = (bf16[144,1536]{1,0:T(8,128)(2,1)S(1)}, bf16[144,1536]{1,0:T(8,128)(2,1)S(1)}, u32[]{:S(2)}, u32[]{:S(2)}) collective-permute-start(bf16[144,1536]{1,0:T(8,128)(2,1)S(1)} %slice.53), channel_id=1, source_target_pairs={{0,4},{4,0},{8,12},{12,8},{16,20},{20,16},{24,28},{28,24},{1,5},{5... | collective-permute-start | bytes 1327112 | tf_op jit(solution)/shard_map/ppermute | solution.py:190
  154.9 23.3 %collective-permute-start.31 = (bf16[72,1536]{1,0:T(8,128)(2,1)S(1)}, bf16[72,1536]{1,0:T(8,128)(2,1)S(1)}, u32[]{:S(2)}, u32[]{:S(2)}) collective-permute-start(bf16[72,1536]{1,0:T(8,128)(2,1)S(1)} %get-tuple-element.54), channel_id=1, source_target_pairs={{0,16},{4,20},{8,24},{12,28},{16,0},{20,4},{24,8},{28,12},{1,17},{... | collective-permute-start | bytes 663560 | tf_op jit(solution)/shard_map/ppermute | solution.py:190
  163.5 14.7 %collective-permute-start.32 = (bf16[72,1536]{1,0:T(8,128)(2,1)S(1)}, bf16[72,1536]{1,0:T(8,128)(2,1)S(1)}, u32[]{:S(2)}, u32[]{:S(2)}) collective-permute-start(bf16[72,1536]{1,0:T(8,128)(2,1)S(1)} %get-tuple-element.53), channel_id=1, source_target_pairs={{0,24},{4,28},{8,16},{12,20},{16,8},{20,12},{24,0},{28,4},{1,25},{... | collective-permute-start | bytes 663560 | tf_op jit(solution)/shard_map/ppermute | solution.py:190
  164.1 18.5 %collective-permute-start.17 = (bf16[72,1536]{1,0:T(8,128)(2,1)S(1)}, bf16[72,1536]{1,0:T(8,128)(2,1)S(1)}, u32[]{:S(2)}, u32[]{:S(2)}) collective-permute-start(bf16[72,1536]{1,0:T(8,128)(2,1)S(1)} %get-tuple-element.55), channel_id=1, source_target_pairs={{0,8},{4,12},{8,0},{12,4},{16,24},{20,28},{24,16},{28,20},{1,9},{5... | collective-permute-start | bytes 663560 | tf_op jit(solution)/shard_map/ppermute | solution.py:190
  (38 other events, 451.7 us)

commit v2 on v1

--- a/solution.py
+++ b/solution.py
@@ -190,80 +190,84 @@
     return lax.ppermute(array, axis, [(i, i ^ distance) for i in range(size)])
 
 
-def to_pair(array, pairs):
-    return lax.ppermute(array, "ctx", [(2 * a + s, 2 * b + s) for a, b in pairs for s in (0, 1)])
-
-
-def scan_states(state, rates, place, block_len, reverse):
-    heads = state.shape[0]
-    half = heads // 2
-    pairs = lax.axis_size("ctx") // 2
-    side, pair = place[0], place[1]
-    if reverse:
-        side, pair = 1 - side, pairs - 1 - pair
-    mine = lax.dynamic_slice(rates, (place[0] * half,), (half,))[:, None, None]
-    power = lambda tokens: jnp.exp(-mine * tokens)
-    partner = swap(state[half:], "ctx", 1)
-    first_end = 1 if reverse else 0
-    other = lax.ppermute(
-        state[:half], "ctx", [(2 * i + first_end, 2 * i + 1 - first_end) for i in range(pairs)]
-    )
-    whole = power(float(block_len))
+def trade(array, pairs, partner):
+    return lax.ppermute(
+        array, "ctx", [(2 * partner(i) + s, 2 * i + s) for i in range(pairs) for s in (0, 1)]
+    )
+
+
+def after(array, *events):
+    return lax.optimization_barrier((array,) + events)[0]
+
+
+def scan_total(state, rates, place, block_len, reverse, *events):
+    half = state.shape[0] // 2
+    side = 1 - place[0] if reverse else place[0]
+    whole = head_power(rates, place, half, block_len)
+    partner = after(swap(state[half:], "ctx", 1), *events)
     own_wide, partner_wide = state[:half].astype(F32), partner.astype(F32)
     total = jnp.where(
         side == 0, whole * own_wide + partner_wide, own_wide + whole * partner_wide
     ).astype(BF16)
-    before = jnp.zeros_like(total)
-    reach = 1
-    while reach < pairs:
-        if reach == 1:
-            upto = total
-        else:
-            upto = (power(2.0 * block_len) * before.astype(F32) + total.astype(F32)).astype(BF16)
-        got = []
-        for j in range(reach):
-            moves = [(g + reach - 1, g + reach + j) for g in range(0, pairs, 2 * reach)]
-            if reverse:
-                moves = [(pairs - 1 - a, pairs - 1 - b) for a, b in moves]
-            got.append(to_pair(upto, moves))
-        got = functools.reduce(lambda a, b: a + b, got)
-        steps = lax.rem(pair, reach).astype(F32)
-        if reach == 1:
-            before = got
-        else:
-            before = (
-                before.astype(F32) + power(2.0 * block_len * steps) * got.astype(F32)
-            ).astype(BF16)
-        reach *= 2
-    return before, swap(before, "ctx", 1), partner, other
-
-
-def to_experts(sends):
-    pairs = len(sends)
-    got = [sends[0]] + [swap(sends[k], "ctx", 2 * k) for k in range(1, pairs)]
-    chunks = []
-    for first in (0, pairs // 2):
-        own = jnp.concatenate(got[first : first + pairs // 2], axis=0)
-        chunks.append(jnp.concatenate([own, swap(own, "ctx", 1)], axis=0))
-    return chunks
-
-
-def scatter_sum(part, bits):
-    for bit in range(bits):
-        mine = (lax.axis_index("exp") >> bit) & 1
-        halves = part.reshape(2, part.shape[0] // 2, part.shape[1])
-        got = swap(lax.dynamic_index_in_dim(halves, 1 - mine, 0, False), "exp", 1 << bit)
-        kept = lax.dynamic_index_in_dim(halves, mine, 0, False)
-        part = kept.astype(F32) + got.astype(F32)
-        if bit < bits - 1:
-            part = part.astype(BF16)
-    return part
-
-
-def gather_all(part, bits):
+    return total, partner
+
+
+def head_power(rates, place, half, tokens):
+    mine = lax.dynamic_slice(rates, (place[0] * half,), (half,))[:, None, None]
+    return jnp.exp(-mine * tokens)
+
+
+def scan_step(before, total, reach, rates, place, block_len, reverse, *events):
+    half = total.shape[0]
+    pairs = lax.axis_size("ctx") // 2
+    pair = pairs - 1 - place[1] if reverse else place[1]
+    if before is None:
+        upto = total
+    else:
+        whole = head_power(rates, place, half, 2.0 * block_len)
+        upto = (whole * before.astype(F32) + total.astype(F32)).astype(BF16)
+    upto = after(upto, *events)
+    lower, offset = (pair & reach) == 0, pair & (reach - 1)
+    got = None
+    for j in range(reach):
+
+        def partner(i, j=j):
+            i = pairs - 1 - i if reverse else i
+            start = i - i % (2 * reach)
+            first, second = start + reach - 1, start + reach + j
+            i = {first: second, second: first}.get(i, i)
+            return pairs - 1 - i if reverse else i
+
+        one = trade(upto, pairs, partner)
+        got = one if got is None else jnp.where(offset == j, one, got)
+    scale = head_power(rates, place, half, 2.0 * block_len * offset.astype(F32))
+    grown = scale * got.astype(F32)
+    if before is not None:
+        grown = grown + before.astype(F32)
+    kept = jnp.zeros_like(total) if before is None else before
+    return jnp.where(lower, kept, grown.astype(BF16)), upto
+
+
+def scatter_part(part, bit):
+    mine = (lax.axis_index("exp") >> bit) & 1
+    halves = part.reshape(2, part.shape[0] // 2, part.shape[1])
+    got = swap(lax.dynamic_index_in_dim(halves, 1 - mine, 0, False), "exp", 1 << bit)
+    kept = lax.dynamic_index_in_dim(halves, mine, 0, False)
+    return (kept.astype(F32) + got.astype(F32)).astype(BF16)
+
+
+def scatter_rest(part, bits):
+    for bit in range(1, bits):
+        part = scatter_part(part, bit)
+    return part.astype(F32)
+
+
+def gather_all(part, bits, *events):
     for bit in reversed(range(bits)):
         mine = (lax.axis_index("exp") >> bit) & 1
         got = swap(part, "exp", 1 << bit)
+        if bit == 0:
+            got = after(got, *events)
         part = jnp.concatenate(
             [jnp.where(mine == 0, part, got), jnp.where(mine == 0, got, part)], axis=0
         )
@@ -292,48 +296,102 @@
     slots = jax.ShapeDtypeStruct((capacity, group), BF16)
     unit = 2 * block_len * DH * group
 
+    reaches = [1 << i for i in range((experts - 1).bit_length())]
     (key_local,) = call(key_state_kernel, [states], scalars, (keys, values), unit)
     choose, weigh, *send_grad = call(
         route_kernel, [table, table] + [slots] * experts, (place,),
         (routes, gate_weights, out_grad), 3 * unit,
     )
+    key_total, near0 = scan_total(
+        key_local, decay_rates, place, block_len, False, send_grad[0]
+    )
     intra, weights = call(intra_kernel, [wide, weight_sq], scalars, (queries, keys, values), 2 * unit)
-    enter_states = scan_states(key_local, decay_rates, place, block_len, False)
+    near1 = swap(after(key_local[:half], key_total), "ctx", 1)
+    half_experts = experts // 2
+    pairs_of = lambda rows, k: swap(rows, "ctx", 2 * k) if k else rows
+
+    grad_own, grad_other = {0: send_grad[0]}, {}
+    for k in range(half_experts, experts - 1):
+        grad_own[k] = pairs_of(send_grad[k], k)
+    before = None
+    for index, reach in enumerate(reaches):
+        events = list(grad_own.values()) if index == 1 else []
+        before, upto = scan_step(
+            before, key_total, reach, decay_rates, place, block_len, False, *events
+        )
+        if index == 0:
+            grad_other[0] = swap(after(grad_own[0], key_total), "ctx", 1)
+    for k in range(half_experts, experts - 1):
+        grad_other[k] = swap(after(grad_own[k], upto), "ctx", 1)
+    for k in range(1, half_experts):
+        grad_own[k] = pairs_of(after(send_grad[k], upto), k)
+    before = after(before, grad_other[0], near1, *[grad_own[k] for k in range(1, half_experts)])
+    grad_own[experts - 1] = pairs_of(after(send_grad[experts - 1], before), experts - 1)
+    far0, far1 = before, swap(before, "ctx", 1)
+    far1 = after(far1, *[grad_other[k] for k in range(half_experts, experts - 1)])
     entering, *send_in = call(
         attend_kernel, [states] + [slots] * experts, scalars,
-        (queries, intra, choose) + enter_states, 4 * unit,
-    )
-
-    grad_chunks = to_experts(send_grad)
-    in_chunks = to_experts(send_in)
-    homes = []
-    for in_rows, grad_rows in zip(in_chunks, grad_chunks):
-        grad_part = dot(grad_rows, down_local, 1, 1).astype(BF16)
-        hidden_grad = scatter_sum(grad_part, bits)
-        pre_part = dot(in_rows, up_local, 1, 0).astype(BF16)
-        pre = scatter_sum(pre_part, bits)
-        slope = (hidden_grad * silu_slope(pre)).astype(BF16)
-        slope = gather_all(slope, bits)
-        back = dot(slope, up_local, 1, 1).astype(BF16)
-        kept = back.shape[0] // 2
-        got = swap(back[kept:], "ctx", 1)
-        summed = (back[:kept].astype(F32) + got.astype(F32)).astype(BF16)
-        for i in range(experts // 2):
-            rows = summed[i * capacity : (i + 1) * capacity]
-            k = len(homes)
-            homes.append(swap(rows, "ctx", 2 * k) if k else rows)
+        (queries, intra, choose, far0, far1, near0, near1), 4 * unit,
+    )
+    for k in [*range(1, half_experts), experts - 1]:
+        grad_other[k] = swap(after(grad_own[k], send_in[0]), "ctx", 1)
+
+    in_own, in_other = {0: send_in[0]}, {}
+    for k in [experts - 1, *range(1, half_experts)]:
+        in_own[k] = pairs_of(send_in[k], k)
+    for k in range(half_experts, experts - 1):
+        in_own[k] = pairs_of(after(send_in[k], in_own[experts - 1]), k)
+    for k in range(experts):
+        in_other[k] = swap(in_own[k], "ctx", 1)
+
+    parts = [range(half_experts), range(half_experts, experts)]
+    gather = lambda own, other, part: jnp.concatenate(
+        [own[k] for k in part] + [other[k] for k in part], axis=0
+    )
+    hidden = []
+    for part in parts:
+        rows = gather(grad_own, grad_other, part)
+        if not hidden:
+            rows = after(rows, in_other[0])
+        hidden.append(scatter_part(dot(rows, down_local, 1, 1).astype(BF16), 0))
+    rows = after(gather(in_own, in_other, parts[0]), *hidden)
+    pre = [scatter_part(dot(rows, up_local, 1, 0).astype(BF16), 0)]
+    hidden = [scatter_rest(rows, bits) for rows in hidden]
+    rows = after(gather(in_own, in_other, parts[1]), hidden[0], pre[0])
+    pre.append(scatter_part(dot(rows, up_local, 1, 0).astype(BF16), 0))
+    pre = [scatter_rest(rows, bits) for rows in pre]
+    slopes = [(h * silu_slope(p)).astype(BF16) for h, p in zip(hidden, pre)]
+    homes = {}
+    slopes = lax.optimization_barrier(slopes)
+    backs = []
+    for part, slope in zip(parts[::-1], slopes[::-1]):
+        back = dot(gather_all(slope, bits, *backs), up_local, 1, 1).astype(BF16)
+        backs.append(back)
+        back = back.reshape(2, len(part), capacity, group)
+        events = []
+        for i in reversed(range(len(part))):
+            got = after(swap(back[1, i], "ctx", 1), *events)
+            summed = (back[0, i].astype(F32) + got.astype(F32)).astype(BF16)
+            events = [summed]
+            homes[part[i]] = pairs_of(summed, part[i])
 
     grad_out, query_local = call(
-        grad_kernel, [slim, states], scalars, (queries, out_grad, weigh, *homes), 4 * unit
-    )
-    leave_states = scan_states(query_local, decay_rates, place, block_len, True)
+        grad_kernel, [slim, states], scalars,
+        (queries, out_grad, weigh, *[homes[k] for k in range(experts)]), 4 * unit,
+    )
+    query_total, near0 = scan_total(query_local, decay_rates, place, block_len, True)
+    near1 = swap(after(query_local[:half], query_total), "ctx", 1)
+    before = None
+    for reach in reaches:
+        before, _ = scan_step(before, query_total, reach, decay_rates, place, block_len, True)
+    far0, far1 = before, swap(before, "ctx", 1)
     query_g, key_near, value_near = call(
         near_kernel, [slim, wide, wide], scalars,
         (queries, keys, values, grad_out, entering, weights), 5 * unit,
     )
     key_g, value_g = call(
         far_kernel, [slim, slim], scalars,
-        (keys, values, key_near, value_near) + leave_states, 2 * unit,
+        (keys, values, key_near, value_near, far0, far1, near0, near1), 2 * unit,
     )
     return query_g, key_g, value_g
 

time: 220 us -> 215 us (0.977)
  waiting for transfers between devices: 111 us -> 94.6 us
  matrix products: 17.9 us -> 24 us
  other arithmetic: 6.61 us -> 10 us
    ppermute x31 -> x39, waiting for transfers between devices: 96.5 us -> 80.3 us  [swap(): return lax.ppermute(array, axis, [(i, i ^ distance) for i in range(size)])]
    dot_general x6, matrix products: 17.9 us -> 24 us  [dot(): lax.dot_general(left, right, (((left_dim,), (right_dim,)), ((), ())), pre...]
    ppermute x8 -> x6, starting transfers between devices: 11.7 us -> 8.2 us  [trade(): lax.ppermute(array, 'ctx', [(2 * partner(i) + s, 2 * i + s) for i in rang...]
    convert_element_type x14, other arithmetic: 2.51 us -> 5.11 us  [the longest x4 2.61 us: scatter_part(): return (kept.astype(F32) + got.astype(F32)).astype(BF16)]
    ppermute x31 -> x39, starting transfers between devices: 46.5 us -> 48.9 us  [swap(): return lax.ppermute(array, axis, [(i, i ^ distance) for i in range(size)])]
    ppermute x8 -> x6, waiting for transfers between devices: 14.9 us -> 14.4 us  [trade(): lax.ppermute(array, 'ctx', [(2 * partner(i) + s, 2 * i + s) for i in rang...]
  transfers between devices with their start and end apart: 39 -> 45, of which waited for: 20 -> 20; matrix products, arithmetic and copies ran while one was open for 11% -> 16% of each run, Pallas kernels for 5% -> 6%
where the time goes in v2:
time: 215 us; the launch traced here: 214 us
  waiting for transfers between devices  94.6 us (44%)
  starting transfers between devices  57.1 us (27%)
  matrix products  24 us (11%)
  Pallas kernels  18.5 us (9%)
  other arithmetic  10 us (5%)
  local copies, waits for them, and re-layouts  8.04 us (4%)
    ppermute x39, waiting for transfers between devices, swap(): return lax.ppermute(array, axis, [(i, i ^ distance) for i in range(size)])  80.3 us
    ppermute x39, starting transfers between devices, swap(): return lax.ppermute(array, axis, [(i, i ^ distance) for i in range(size)])  48.9 us
    dot_general x6, matrix products, dot(): lax.dot_general(left, right, (((left_dim,), (right_dim,)), ((), ())), pre...  24 us
    pallas_call x7, Pallas kernels, call(): pl.pallas_call(kernel, out_shape=list(out_shapes), in_specs=[SMEM] * len(...  18.5 us
    ppermute x6, waiting for transfers between devices, trade(): lax.ppermute(array, 'ctx', [(2 * partner(i) + s, 2 * i + s) for i in rang...  14.4 us
    ppermute x6, starting transfers between devices, trade(): lax.ppermute(array, 'ctx', [(2 * partner(i) + s, 2 * i + s) for i in rang...  8.2 us
    unnamed x48, local copies, waits for them, and re-layouts  6.08 us
  transfers between devices with their start and end apart: 45, of which 20 were waited for; matrix products, arithmetic and copies ran while one was open for 16% of the time, Pallas kernels for 6%

profile of v2, /device:TPU:0, one launch (start us, length us, event | category | flops | bytes accessed | tf_op | source)
XLA Modules:
  0.0 213.6 jit_solution(8951169024647141427)
XLA Ops:
  17.6 5.6 %collective-permute-done.1 = bf16[6,128,128]{2,1,0:T(8,128)(2,1)S(1)} collective-permute-done((bf16[6,128,128]{2,1,0:T(8,128)(2,1)S(1)}, bf16[6,128,128]{2,1,0:T(8,128)(2,1)S(1)}, u32[]{:S(2)}, u32[]{:S(2)}) %collective-permute-start.1) | collective-permute-done | bytes 196640 | tf_op jit(solution)/shard_map/ppermute | solution.py:194
  23.4 3.4 %collective-permute-done.2 = bf16[72,1536]{1,0:T(8,128)(2,1)} collective-permute-done((bf16[72,1536]{1,0:T(8,128)(2,1)S(1)}, bf16[72,1536]{1,0:T(8,128)(2,1)}, u32[]{:S(2)}, u32[]{:S(2)}) %collective-permute-start.2) | collective-permute-done | bytes 221216 | tf_op jit(solution)/shard_map/ppermute | solution.py:190
  31.7 5.5 %collective-permute-start.3 = (bf16[72,1536]{1,0:T(8,128)(2,1)S(1)}, bf16[72,1536]{1,0:T(8,128)(2,1)}, u32[]{:S(2)}, u32[]{:S(2)}) collective-permute-start(bf16[72,1536]{1,0:T(8,128)(2,1)S(1)} %get-tuple-element.50), channel_id=1, source_target_pairs={{0,8},{4,12},{8,0},{12,4},{16,24},{20,28},{24,16},{28,20},{1,9},{5... | collective-permute-start | bytes 663560 | tf_op jit(solution)/shard_map/ppermute | solution.py:190
  37.5 3.8 %collective-permute-done.3 = bf16[72,1536]{1,0:T(8,128)(2,1)} collective-permute-done((bf16[72,1536]{1,0:T(8,128)(2,1)S(1)}, bf16[72,1536]{1,0:T(8,128)(2,1)}, u32[]{:S(2)}, u32[]{:S(2)}) %collective-permute-start.3) | collective-permute-done | bytes 221216 | tf_op jit(solution)/shard_map/ppermute | solution.py:190
  44.6 5.0 %collective-permute-start.16 = (bf16[72,1536]{1,0:T(8,128)(2,1)}, bf16[72,1536]{1,0:T(8,128)(2,1)}, u32[]{:S(2)}, u32[]{:S(2)}) collective-permute-start(bf16[72,1536]{1,0:T(8,128)(2,1)} %get-tuple-element.63), channel_id=1, source_target_pairs={{0,24},{4,28},{8,16},{12,20},{16,8},{20,12},{24,0},{28,4},{1,25},{... | collective-permute-start | bytes 663560 | tf_op jit(solution)/shard_map/ppermute | solution.py:190
  50.4 3.7 %shard_map.115 = (bf16[12,128,128]{2,1,0:T(8,128)(2,1)S(1)}, bf16[72,1536]{1,0:T(8,128)(2,1)S(1)}, bf16[72,1536]{1,0:T(8,128)(2,1)S(1)}, bf16[72,1536]{1,0:T(8,128)(2,1)S(1)}, bf16[72,1536]{1,0:T(8,128)(2,1)}) custom-call(s32[2]{0:T(128)S(1)} %pad_add_fusion.place_ref, f32[12]{0:T(128)S(1)} %copy-done.7, bf16[128,1536]{1,0:T(8,128)(2,1)S(1)} %copy-done, ...), custom_call_target="tpu_custom_call" | custom-call | flops 201326592 | bytes 3317760 | tf_op jit(solution)/shard_map/pallas_call | solution.py:178
  64.6 4.8 %collective-permute-start.23 = (bf16[72,1536]{1,0:T(8,128)(2,1)}, bf16[72,1536]{1,0:T(8,128)(2,1)}, u32[]{:S(2)}, u32[]{:S(2)}) collective-permute-start(bf16[72,1536]{1,0:T(8,128)(2,1)} %copy-done.8), channel_id=1, source_target_pairs={{0,16},{4,20},{8,24},{12,28},{16,0},{20,4},{24,8},{28,12},{1,17},{... | collective-permute-start | bytes 663560 | tf_op jit(solution)/shard_map/ppermute | solution.py:190
  70.8 5.5 %fusion.12 = bf16[288,2304]{1,0:T(8,128)(2,1)S(1)} fusion(bf16[288,1536]{1,0:T(8,128)(2,1)S(1)} %pad_maximum_fusion, bf16[1,2304,1536]{2,1,0:T(8,128)(2,1)} %param.14), kind=kOutput, calls=%fused_computation.12 | convolution fusion | flops 2039095296 | bytes 9289728 | tf_op jit(solution)/shard_map/dot_general | solution.py:20
  78.6 3.3 %fusion.15 = bf16[288,2304]{1,0:T(8,128)(2,1)S(1)} fusion(bf16[1,2304,1536]{2,1,0:T(8,128)(2,1)S(1)} %bitcast.134, bf16[72,1536]{1,0:T(8,128)(2,1)S(1)} %collective-permute-done.17, bf16[72,1536]{1,0:T(8,128)(2,1)S(1)} %copy-done.16, bf16[72,1536]{1,0:T(8,128)(2,1)} %collective-permute-done.16, bf16[72,1536]{1,0:T(8,128)(2,1)} %collective-permute-done.2), kind=kOutput, calls=%fused_computation.13 | convolution fusion | flops 2042634240 | bytes 9289728 | tf_op jit(solution)/shard_map/dot_general | solution.py:20
  82.3 7.2 %collective-permute-done.15 = bf16[72,1536]{1,0:T(8,128)(2,1)S(1)} collective-permute-done((bf16[72,1536]{1,0:T(8,128)(2,1)S(1)}, bf16[72,1536]{1,0:T(8,128)(2,1)S(1)}, u32[]{:S(2)}, u32[]{:S(2)}) %collective-permute-start.15) | collective-permute-done | bytes 221216 | tf_op jit(solution)/shard_map/ppermute | solution.py:190
  99.3 5.3 %fusion.21 = bf16[288,2304]{1,0:T(8,128)(2,1)S(1)} fusion(bf16[288,1536]{1,0:T(8,128)(2,1)S(1)} %pad_maximum_fusion.2, bf16[1,1536,2304]{2,1,0:T(8,128)(2,1)} %param.13), kind=kOutput, calls=%fused_computation.15 | convolution fusion | flops 2039095296 | bytes 9289728 | tf_op jit(solution)/shard_map/dot_general | solution.py:20
  108.3 14.4 %collective-permute-done.20 = bf16[72,2304]{1,0:T(8,128)(2,1)S(1)} collective-permute-done((bf16[72,2304]{1,0:T(8,128)(2,1)S(1)}, bf16[72,2304]{1,0:T(8,128)(2,1)S(1)}, u32[]{:S(2)}, u32[]{:S(2)}) %collective-permute-start.20) | collective-permute-done | bytes 331808 | tf_op jit(solution)/shard_map/ppermute | solution.py:190
  123.1 6.1 %collective-permute-done.27 = bf16[72,2304]{1,0:T(8,128)(2,1)S(1)} collective-permute-done((bf16[72,2304]{1,0:T(8,128)(2,1)S(1)}, bf16[72,2304]{1,0:T(8,128)(2,1)S(1)}, u32[]{:S(2)}, u32[]{:S(2)}) %collective-permute-start.27) | collective-permute-done | bytes 331808 | tf_op jit(solution)/shard_map/ppermute | solution.py:190
  131.8 8.8 %collective-permute-done.30 = bf16[72,2304]{1,0:T(8,128)(2,1)} collective-permute-done((bf16[72,2304]{1,0:T(8,128)(2,1)S(1)}, bf16[72,2304]{1,0:T(8,128)(2,1)}, u32[]{:S(2)}, u32[]{:S(2)}) %collective-permute-start.30) | collective-permute-done | bytes 331808 | tf_op jit(solution)/shard_map/ppermute | solution.py:190
  141.8 4.3 %collective-permute-done.28 = bf16[72,2304]{1,0:T(8,128)(2,1)S(1)} collective-permute-done((bf16[72,2304]{1,0:T(8,128)(2,1)S(1)}, bf16[72,2304]{1,0:T(8,128)(2,1)S(1)}, u32[]{:S(2)}, u32[]{:S(2)}) %collective-permute-start.28) | collective-permute-done | bytes 331808 | tf_op jit(solution)/shard_map/ppermute | solution.py:190
  146.6 5.4 %fusion.24 = bf16[288,1536]{1,0:T(8,128)(2,1)S(1)} fusion(bf16[1,1536,2304]{2,1,0:T(8,128)(2,1)} %param.13, bf16[144,2304]{1,0:T(8,128)(2,1)S(1)} %get-tuple-element.90, bf16[144,2304]{1,0:T(8,128)(2,1)S(1)} %get-tuple-element.89), kind=kOutput, calls=%fused_computation.16 | convolution fusion | flops 2041528320 | bytes 9289728 | tf_op jit(solution)/shard_map/dot_general | solution.py:20
  161.0 4.1 %collective-permute-done.35 = bf16[72,1536]{1,0:T(8,128)(2,1)S(1)} collective-permute-done((bf16[72,1536]{1,0:T(8,128)(2,1)S(1)}, bf16[72,1536]{1,0:T(8,128)(2,1)S(1)}, u32[]{:S(2)}, u32[]{:S(2)}) %collective-permute-start.35) | collective-permute-done | bytes 221216 | tf_op jit(solution)/shard_map/ppermute | solution.py:190
  165.2 4.6 %collective-permute-done.33 = bf16[72,1536]{1,0:T(8,128)(2,1)S(1)} collective-permute-done((bf16[72,1536]{1,0:T(8,128)(2,1)S(1)}, bf16[72,1536]{1,0:T(8,128)(2,1)S(1)}, u32[]{:S(2)}, u32[]{:S(2)}) %collective-permute-start.33) | collective-permute-done | bytes 221216 | tf_op jit(solution)/shard_map/ppermute | solution.py:190
  170.0 4.2 %collective-permute-done.32 = bf16[72,1536]{1,0:T(8,128)(2,1)S(1)} collective-permute-done((bf16[72,1536]{1,0:T(8,128)(2,1)S(1)}, bf16[72,1536]{1,0:T(8,128)(2,1)S(1)}, u32[]{:S(2)}, u32[]{:S(2)}) %collective-permute-start.32) | collective-permute-done | bytes 221216 | tf_op jit(solution)/shard_map/ppermute | solution.py:190
  174.2 6.2 %collective-permute-done.37.refs_2_ = bf16[72,1536]{1,0:T(8,128)(2,1)S(1)} collective-permute-done((bf16[72,1536]{1,0:T(8,128)(2,1)S(1)}, bf16[72,1536]{1,0:T(8,128)(2,1)S(1)}, u32[]{:S(2)}, u32[]{:S(2)}) %collective-permute-start.37) | collective-permute-done | bytes 221216 | tf_op jit(solution)/shard_map/ppermute | solution.py:190
  181.3 3.1 %shard_map.116 = (bf16[128,1536]{1,0:T(8,128)(2,1)S(1)}, bf16[12,128,128]{2,1,0:T(8,128)(2,1)S(1)}) custom-call(s32[2]{0:T(128)S(1)} %pad_add_fusion.place_ref, f32[12]{0:T(128)S(1)} %copy-done.7, bf16[128,1536]{1,0:T(8,128)(2,1)S(1)} %copy-done, bf16[128,1536]{1,0:T(8,128)(2,1)S(1)} %copy-done.5, bf16[4,128,72]{2,1,0:T(8,128)(2,1)S(1)} %get-tuple-element.44.weigh_ref, ...), custom_call_target="tpu_custom_call" | custom-call | flops 201326592 | bytes 2531328 | tf_op jit(solution)/shard_map/pallas_call | solution.py:178
  185.0 5.2 %collective-permute-done.39.near0 = bf16[6,128,128]{2,1,0:T(8,128)(2,1)S(1)} collective-permute-done((bf16[6,128,128]{2,1,0:T(8,128)(2,1)S(1)}, bf16[6,128,128]{2,1,0:T(8,128)(2,1)S(1)}, u32[]{:S(2)}, u32[]{:S(2)}) %collective-permute-start.39) | collective-permute-done | bytes 196640 | tf_op jit(solution)/shard_map/ppermute | solution.py:190
  190.5 5.7 %collective-permute-done.40 = bf16[6,128,128]{2,1,0:T(8,128)(2,1)S(1)} collective-permute-done((bf16[6,128,128]{2,1,0:T(8,128)(2,1)S(1)}, bf16[6,128,128]{2,1,0:T(8,128)(2,1)S(1)}, u32[]{:S(2)}, u32[]{:S(2)}) %collective-permute-start.40) | collective-permute-done | bytes 196640 | tf_op jit(solution)/shard_map/ppermute | solution.py:194
  206.4 4.0 %shard_map.117 = (bf16[128,1536]{1,0:T(8,128)(2,1)}, f32[128,1536]{1,0:T(8,128)S(1)}, f32[128,1536]{1,0:T(8,128)S(1)}) custom-call(s32[2]{0:T(128)S(1)} %pad_add_fusion.place_ref, f32[12]{0:T(128)S(1)} %copy-done.7, bf16[128,1536]{1,0:T(8,128)(2,1)S(1)} %copy-done, bf16[128,1536]{1,0:T(8,128)(2,1)S(1)} %copy-done.2, bf16[128,1536]{1,0:T(8,128)(2,1)S(1)} %copy-done.4, ...), custom_call_target="tpu_custom_call" | custom-call | flops 251658240 | bytes 4325376 | tf_op jit(solution)/shard_map/pallas_call | solution.py:178
  (170 shorter events, 82.9 us)
Async XLA Ops:
  15.0 11.8 %collective-permute-start.2 = (bf16[72,1536]{1,0:T(8,128)(2,1)S(1)}, bf16[72,1536]{1,0:T(8,128)(2,1)}, u32[]{:S(2)}, u32[]{:S(2)}) collective-permute-start(bf16[72,1536]{1,0:T(8,128)(2,1)S(1)} %get-tuple-element.48), channel_id=1, source_target_pairs={{0,16},{4,20},{8,24},{12,28},{16,0},{20,4},{24,8},{28,12},{1,17},{... | collective-permute-start | bytes 663560 | tf_op jit(solution)/shard_map/ppermute | solution.py:190
  30.2 19.4 %collective-permute-start.9 = (bf16[72,1536]{1,0:T(8,128)(2,1)}, bf16[72,1536]{1,0:T(8,128)(2,1)S(1)}, u32[]{:S(2)}, u32[]{:S(2)}) collective-permute-start(bf16[72,1536]{1,0:T(8,128)(2,1)} %collective-permute-done.2), channel_id=1, source_target_pairs={{0,4},{4,0},{8,12},{12,8},{16,20},{20,16},{24,28},{28,24},{1,5},{5... | collective-permute-start | bytes 663560 | tf_op jit(solution)/shard_map/ppermute | solution.py:190
  44.6 16.6 %collective-permute-start.16 = (bf16[72,1536]{1,0:T(8,128)(2,1)}, bf16[72,1536]{1,0:T(8,128)(2,1)}, u32[]{:S(2)}, u32[]{:S(2)}) collective-permute-start(bf16[72,1536]{1,0:T(8,128)(2,1)} %get-tuple-element.63), channel_id=1, source_target_pairs={{0,24},{4,28},{8,16},{12,20},{16,8},{20,12},{24,0},{28,4},{1,25},{... | collective-permute-start | bytes 663560 | tf_op jit(solution)/shard_map/ppermute | solution.py:190
  56.3 13.1 %collective-permute-start.10 = (bf16[72,1536]{1,0:T(8,128)(2,1)}, bf16[72,1536]{1,0:T(8,128)(2,1)}, u32[]{:S(2)}, u32[]{:S(2)}) collective-permute-start(bf16[72,1536]{1,0:T(8,128)(2,1)} %collective-permute-done.3), channel_id=1, source_target_pairs={{0,4},{4,0},{8,12},{12,8},{16,20},{20,16},{24,28},{28,24},{1,5},{5... | collective-permute-start | bytes 663560 | tf_op jit(solution)/shard_map/ppermute | solution.py:190
  57.8 13.0 %collective-permute-start.11 = (bf16[72,1536]{1,0:T(8,128)(2,1)S(1)}, bf16[72,1536]{1,0:T(8,128)(2,1)S(1)}, u32[]{:S(2)}, u32[]{:S(2)}) collective-permute-start(bf16[72,1536]{1,0:T(8,128)(2,1)S(1)} %get-tuple-element.58), channel_id=1, source_target_pairs={{0,4},{4,0},{8,12},{12,8},{16,20},{20,16},{24,28},{28,24},{1,5},{5... | collective-permute-start | bytes 663560 | tf_op jit(solution)/shard_map/ppermute | solution.py:190
  58.3 18.4 %collective-permute-start.14 = (bf16[72,1536]{1,0:T(8,128)(2,1)}, bf16[72,1536]{1,0:T(8,128)(2,1)S(1)}, u32[]{:S(2)}, u32[]{:S(2)}) collective-permute-start(bf16[72,1536]{1,0:T(8,128)(2,1)} %copy-done.9), channel_id=1, source_target_pairs={{0,8},{4,12},{8,0},{12,4},{16,24},{20,28},{24,16},{28,20},{1,9},{5... | collective-permute-start | bytes 663560 | tf_op jit(solution)/shard_map/ppermute | solution.py:190
  61.3 17.3 %collective-permute-start.17 = (bf16[72,1536]{1,0:T(8,128)(2,1)}, bf16[72,1536]{1,0:T(8,128)(2,1)S(1)}, u32[]{:S(2)}, u32[]{:S(2)}) collective-permute-start(bf16[72,1536]{1,0:T(8,128)(2,1)} %collective-permute-done.16), channel_id=1, source_target_pairs={{0,4},{4,0},{8,12},{12,8},{16,20},{20,16},{24,28},{28,24},{1,5},{5... | collective-permute-start | bytes 663560 | tf_op jit(solution)/shard_map/ppermute | solution.py:190
  64.6 17.5 %collective-permute-start.23 = (bf16[72,1536]{1,0:T(8,128)(2,1)}, bf16[72,1536]{1,0:T(8,128)(2,1)}, u32[]{:S(2)}, u32[]{:S(2)}) collective-permute-start(bf16[72,1536]{1,0:T(8,128)(2,1)} %copy-done.8), channel_id=1, source_target_pairs={{0,16},{4,20},{8,24},{12,28},{16,0},{20,4},{24,8},{28,12},{1,17},{... | collective-permute-start | bytes 663560 | tf_op jit(solution)/shard_map/ppermute | solution.py:190
  76.4 13.2 %collective-permute-start.12 = (bf16[144,2304]{1,0:T(8,128)(2,1)S(1)}, bf16[144,2304]{1,0:T(8,128)(2,1)S(1)}, u32[]{:S(2)}, u32[]{:S(2)}) collective-permute-start(bf16[144,2304]{1,0:T(8,128)(2,1)S(1)} %dynamic-slice_bitcast_fusion.3), channel_id=1, source_target_pairs={{0,1},{1,0},{2,3},{3,2},{4,5},{5,4},{6,7},{7,6},{8,9},{9,8},{10,11... | collective-permute-start | bytes 1990664 | tf_op jit(solution)/shard_map/ppermute | solution.py:190
  76.5 18.5 %collective-permute-start.25 = (bf16[72,1536]{1,0:T(8,128)(2,1)S(1)}, bf16[72,1536]{1,0:T(8,128)(2,1)}, u32[]{:S(2)}, u32[]{:S(2)}) collective-permute-start(bf16[72,1536]{1,0:T(8,128)(2,1)S(1)} %collective-permute-done.22), channel_id=1, source_target_pairs={{0,4},{4,0},{8,12},{12,8},{16,20},{20,16},{24,28},{28,24},{1,5},{5... | collective-permute-start | bytes 663560 | tf_op jit(solution)/shard_map/ppermute | solution.py:190
  76.8 12.8 %collective-permute-start.15 = (bf16[72,1536]{1,0:T(8,128)(2,1)S(1)}, bf16[72,1536]{1,0:T(8,128)(2,1)S(1)}, u32[]{:S(2)}, u32[]{:S(2)}) collective-permute-start(bf16[72,1536]{1,0:T(8,128)(2,1)S(1)} %collective-permute-done.14), channel_id=1, source_target_pairs={{0,4},{4,0},{8,12},{12,8},{16,20},{20,16},{24,28},{28,24},{1,5},{5... | collective-permute-start | bytes 663560 | tf_op jit(solution)/shard_map/ppermute | solution.py:190
  82.1 12.9 %collective-permute-start.24 = (bf16[72,1536]{1,0:T(8,128)(2,1)}, bf16[72,1536]{1,0:T(8,128)(2,1)}, u32[]{:S(2)}, u32[]{:S(2)}) collective-permute-start(bf16[72,1536]{1,0:T(8,128)(2,1)} %collective-permute-done.23), channel_id=1, source_target_pairs={{0,4},{4,0},{8,12},{12,8},{16,20},{20,16},{24,28},{28,24},{1,5},{5... | collective-permute-start | bytes 663560 | tf_op jit(solution)/shard_map/ppermute | solution.py:190
  96.4 11.9 %collective-permute-start.13 = (bf16[72,2304]{1,0:T(8,128)(2,1)S(1)}, bf16[72,2304]{1,0:T(8,128)(2,1)S(1)}, u32[]{:S(2)}, u32[]{:S(2)}) collective-permute-start(bf16[72,2304]{1,0:T(8,128)(2,1)S(1)} %dynamic-slice_bitcast_fusion.7), channel_id=1, source_target_pairs={{0,2},{1,3},{2,0},{3,1},{4,6},{5,7},{6,4},{7,5},{8,10},{9,11},{10,... | collective-permute-start | bytes 995336 | tf_op jit(solution)/shard_map/ppermute | solution.py:190
  104.9 18.1 %collective-permute-start.21 = (bf16[72,2304]{1,0:T(8,128)(2,1)S(1)}, bf16[72,2304]{1,0:T(8,128)(2,1)S(1)}, u32[]{:S(2)}, u32[]{:S(2)}) collective-permute-start(bf16[72,2304]{1,0:T(8,128)(2,1)S(1)} %dynamic-slice_bitcast_fusion.5), channel_id=1, source_target_pairs={{0,2},{1,3},{2,0},{3,1},{4,6},{5,7},{6,4},{7,5},{8,10},{9,11},{10,... | collective-permute-start | bytes 995336 | tf_op jit(solution)/shard_map/ppermute | solution.py:190
  105.9 16.8 %collective-permute-start.20 = (bf16[72,2304]{1,0:T(8,128)(2,1)S(1)}, bf16[72,2304]{1,0:T(8,128)(2,1)S(1)}, u32[]{:S(2)}, u32[]{:S(2)}) collective-permute-start(bf16[72,2304]{1,0:T(8,128)(2,1)S(1)} %dynamic-slice_bitcast_fusion.6), channel_id=1, source_target_pairs={{0,2},{1,3},{2,0},{3,1},{4,6},{5,7},{6,4},{7,5},{8,10},{9,11},{10,... | collective-permute-start | bytes 995336 | tf_op jit(solution)/shard_map/ppermute | solution.py:190
  107.3 21.9 %collective-permute-start.27 = (bf16[72,2304]{1,0:T(8,128)(2,1)S(1)}, bf16[72,2304]{1,0:T(8,128)(2,1)S(1)}, u32[]{:S(2)}, u32[]{:S(2)}) collective-permute-start(bf16[72,2304]{1,0:T(8,128)(2,1)S(1)} %dynamic-slice_bitcast_fusion.4), channel_id=1, source_target_pairs={{0,2},{1,3},{2,0},{3,1},{4,6},{5,7},{6,4},{7,5},{8,10},{9,11},{10,... | collective-permute-start | bytes 995336 | tf_op jit(solution)/shard_map/ppermute | solution.py:190
  129.7 10.9 %collective-permute-start.30 = (bf16[72,2304]{1,0:T(8,128)(2,1)S(1)}, bf16[72,2304]{1,0:T(8,128)(2,1)}, u32[]{:S(2)}, u32[]{:S(2)}) collective-permute-start(bf16[72,2304]{1,0:T(8,128)(2,1)S(1)} %fusion.60), channel_id=1, source_target_pairs={{0,2},{1,3},{2,0},{3,1},{4,6},{5,7},{6,4},{7,5},{8,10},{9,11},{10,... | collective-permute-start | bytes 995336 | tf_op jit(solution)/shard_map/ppermute | solution.py:190
  130.9 15.3 %collective-permute-start.28 = (bf16[72,2304]{1,0:T(8,128)(2,1)S(1)}, bf16[72,2304]{1,0:T(8,128)(2,1)S(1)}, u32[]{:S(2)}, u32[]{:S(2)}) collective-permute-start(bf16[72,2304]{1,0:T(8,128)(2,1)S(1)} %fusion.53), channel_id=1, source_target_pairs={{0,2},{1,3},{2,0},{3,1},{4,6},{5,7},{6,4},{7,5},{8,10},{9,11},{10,... | collective-permute-start | bytes 995336 | tf_op jit(solution)/shard_map/ppermute | solution.py:190
  152.3 12.8 %collective-permute-start.35 = (bf16[72,1536]{1,0:T(8,128)(2,1)S(1)}, bf16[72,1536]{1,0:T(8,128)(2,1)S(1)}, u32[]{:S(2)}, u32[]{:S(2)}) collective-permute-start(bf16[72,1536]{1,0:T(8,128)(2,1)S(1)} %get-tuple-element.92), channel_id=1, source_target_pairs={{0,4},{4,0},{8,12},{12,8},{16,20},{20,16},{24,28},{28,24},{1,5},{5... | collective-permute-start | bytes 663560 | tf_op jit(solution)/shard_map/ppermute | solution.py:190
  156.7 13.1 %collective-permute-start.33 = (bf16[72,1536]{1,0:T(8,128)(2,1)S(1)}, bf16[72,1536]{1,0:T(8,128)(2,1)S(1)}, u32[]{:S(2)}, u32[]{:S(2)}) collective-permute-start(bf16[72,1536]{1,0:T(8,128)(2,1)S(1)} %get-tuple-element.93), channel_id=1, source_target_pairs={{0,4},{4,0},{8,12},{12,8},{16,20},{20,16},{24,28},{28,24},{1,5},{5... | collective-permute-start | bytes 663560 | tf_op jit(solution)/shard_map/ppermute | solution.py:190
  156.9 17.2 %collective-permute-start.32 = (bf16[72,1536]{1,0:T(8,128)(2,1)S(1)}, bf16[72,1536]{1,0:T(8,128)(2,1)S(1)}, u32[]{:S(2)}, u32[]{:S(2)}) collective-permute-start(bf16[72,1536]{1,0:T(8,128)(2,1)S(1)} %get-tuple-element.94), channel_id=1, source_target_pairs={{0,4},{4,0},{8,12},{12,8},{16,20},{20,16},{24,28},{28,24},{1,5},{5... | collective-permute-start | bytes 663560 | tf_op jit(solution)/shard_map/ppermute | solution.py:190
  160.4 20.0 %collective-permute-start.38 = (bf16[72,1536]{1,0:T(8,128)(2,1)S(1)}, bf16[72,1536]{1,0:T(8,128)(2,1)S(1)}, u32[]{:S(2)}, u32[]{:S(2)}) collective-permute-start(bf16[72,1536]{1,0:T(8,128)(2,1)S(1)} %fusion.65), channel_id=1, source_target_pairs={{0,24},{4,28},{8,16},{12,20},{16,8},{20,12},{24,0},{28,4},{1,25},{... | collective-permute-start | bytes 663560 | tf_op jit(solution)/shard_map/ppermute | solution.py:190
  165.1 15.2 %collective-permute-start.37 = (bf16[72,1536]{1,0:T(8,128)(2,1)S(1)}, bf16[72,1536]{1,0:T(8,128)(2,1)S(1)}, u32[]{:S(2)}, u32[]{:S(2)}) collective-permute-start(bf16[72,1536]{1,0:T(8,128)(2,1)S(1)} %fusion.66), channel_id=1, source_target_pairs={{0,16},{4,20},{8,24},{12,28},{16,0},{20,4},{24,8},{28,12},{1,17},{... | collective-permute-start | bytes 663560 | tf_op jit(solution)/shard_map/ppermute | solution.py:190
  169.9 11.4 %collective-permute-start.34 = (bf16[72,1536]{1,0:T(8,128)(2,1)S(1)}, bf16[72,1536]{1,0:T(8,128)(2,1)S(1)}, u32[]{:S(2)}, u32[]{:S(2)}) collective-permute-start(bf16[72,1536]{1,0:T(8,128)(2,1)S(1)} %fusion.67), channel_id=1, source_target_pairs={{0,8},{4,12},{8,0},{12,4},{16,24},{20,28},{24,16},{28,20},{1,9},{5... | collective-permute-start | bytes 663560 | tf_op jit(solution)/shard_map/ppermute | solution.py:190
  (44 other events, 376.3 us)

commit v3 on v2

v3 whole, which is shorter than its diff:
```python
import functools

import jax
import jax.numpy as jnp
from jax import lax
from jax.experimental import pallas as pl
from jax.experimental.pallas import tpu as pltpu
from jax.sharding import PartitionSpec as P

DH = 128
F32 = jnp.float32
BF16 = jnp.bfloat16
SCALE = 1.0 / DH

SMEM = pl.BlockSpec(memory_space=pltpu.SMEM)
VMEM = pl.BlockSpec(memory_space=pltpu.VMEM)


def dot(left, right, left_dim, right_dim):
    return lax.dot_general(
        left, right, (((left_dim,), (right_dim,)), ((), ())), preferred_element_type=F32
    )


def silu_slope(value):
    sigma = jax.nn.sigmoid(value)
    return sigma * (1.0 + value * (1.0 - sigma))


def lanes_of(place_ref, slot, heads):
    head = lax.rem(place_ref[0] * (heads // 2) + slot, heads)
    return head, pl.ds(pl.multiple_of(head * DH, DH), DH)


def column(block_len):
    return lax.broadcasted_iota(jnp.int32, (block_len, 1), 0).astype(F32)


def decay_within(rate, block_len):
    rows = lax.broadcasted_iota(jnp.int32, (block_len, block_len), 0)
    cols = lax.broadcasted_iota(jnp.int32, (block_len, block_len), 1)
    distance = (rows - cols).astype(F32)
    return jnp.where(distance >= 0.0, jnp.exp(-rate * jnp.maximum(distance, 0.0)), 0.0)


def key_state_kernel(place_ref, rates_ref, k_ref, v_ref, mine_ref, other_ref):
    block_len, half = k_ref.shape[0], mine_ref.shape[0]
    steps = column(block_len)
    for slot in [*range(half, 2 * half), *range(half)]:
        head, lanes = lanes_of(place_ref, slot, 2 * half)
        power = jnp.exp(-rates_ref[head] * (block_len - steps))
        scaled = (k_ref[:, lanes].astype(F32) * power).astype(BF16)
        state_ref = (mine_ref, other_ref)[slot // half]
        state_ref[slot % half] = dot(scaled, v_ref[:, lanes], 0, 0).astype(BF16)


def pick_rows(choose_ref, rows, send_refs):
    capacity = choose_ref.shape[1]
    if capacity % 8:
        for k, send_ref in enumerate(send_refs):
            send_ref[...] = dot(choose_ref[k], rows, 1, 0).astype(BF16)
        return
    table = choose_ref[...].reshape(len(send_refs) * capacity, rows.shape[0])
    picked = dot(table.astype(BF16), rows, 1, 0)
    for k, send_ref in enumerate(send_refs):
        send_ref[...] = picked[k * capacity : (k + 1) * capacity].astype(BF16)


def route_kernel(
    order, place_ref, routes_ref, turned_ref, gates_ref, grad_ref, choose_ref, weigh_ref, *send_refs
):
    experts, capacity, block_len = choose_ref.shape
    rows = lax.broadcasted_iota(jnp.int32, (block_len, block_len), 0)
    cols = lax.broadcasted_iota(jnp.int32, (block_len, block_len), 1)

    first, second = turned_ref[0:1, :], turned_ref[1:2, :]
    names = lax.broadcasted_iota(jnp.int32, (32, block_len), 0)
    hit_first = jnp.where(names == first, 1.0, 0.0)
    hit_second = jnp.where(names == second, 1.0, 0.0)
    earlier = jnp.where(rows < cols, 1.0, 0.0).astype(BF16)
    before = dot((hit_first + hit_second).astype(BF16), earlier, 1, 0)
    slot_first = jnp.sum(before * hit_first, axis=0, keepdims=True).astype(jnp.int32)
    slot_second = jnp.sum(before * hit_second, axis=0, keepdims=True).astype(jnp.int32)
    slots = lax.broadcasted_iota(jnp.int32, (capacity, block_len), 0)
    for k in range(experts):
        expert = place_ref[1] ^ k
        named = ((slots == slot_first) & (first == expert)) | (
            (slots == slot_second) & (second == expert)
        )
        choose_ref[k] = jnp.where(named, 1.0, 0.0)
    pick_rows(choose_ref, grad_ref[...], send_refs)

    first, second = routes_ref[:, 0:1], routes_ref[:, 1:2]
    names = lax.broadcasted_iota(jnp.int32, (block_len, 128), 1)
    hit_first = jnp.where(names == first, 1.0, 0.0)
    hit_second = jnp.where(names == second, 1.0, 0.0)
    earlier = jnp.where(rows > cols, 1.0, 0.0).astype(BF16)
    before = dot(earlier, (hit_first + hit_second).astype(BF16), 1, 0)
    slot_first = jnp.sum(before * hit_first, axis=1, keepdims=True).astype(jnp.int32)
    slot_second = jnp.sum(before * hit_second, axis=1, keepdims=True).astype(jnp.int32)
    slots = lax.broadcasted_iota(jnp.int32, (block_len, capacity), 1)
    for position, (even, odd) in enumerate(order):
        expert = place_ref[1] ^ jnp.where(place_ref[2] == 0, even, odd)
        one = jnp.where((slots == slot_first) & (first == expert), gates_ref[:, 0:1], 0.0)
        two = jnp.where((slots == slot_second) & (second == expert), gates_ref[:, 1:2], 0.0)
        weigh_ref[position] = (one + two).astype(BF16)


def intra_kernel(place_ref, rates_ref, q_ref, k_ref, v_ref, intra_ref, weights_ref):
    block_len, heads = q_ref.shape[0], weights_ref.shape[0]
    for slot in range(heads):
        head, lanes = lanes_of(place_ref, slot, heads)
        within = decay_within(rates_ref[head], block_len)
        scores = dot(q_ref[:, lanes], k_ref[:, lanes], 1, 1)
        weights = (SCALE * scores * within).astype(BF16)
        weights_ref[slot] = weights
        intra_ref[:, lanes] = dot(weights, v_ref[:, lanes], 1, 0)


def attend_kernel(
    place_ref, rates_ref, q_ref, intra_ref, choose_ref, mine_ref, other_ref, *refs
):
    send_refs, attn_ref = refs[:-1], refs[-1]
    block_len, half = q_ref.shape[0], mine_ref.shape[0]
    steps = column(block_len)
    for slot in range(2 * half):
        head, lanes = lanes_of(place_ref, slot, 2 * half)
        entering = (mine_ref, other_ref)[slot // half][slot % half]
        power = SCALE * jnp.exp(-rates_ref[head] * steps)
        inter = power * dot(q_ref[:, lanes], entering, 1, 0)
        attn_ref[:, lanes] = (intra_ref[:, lanes] + inter).astype(BF16)
    pick_rows(choose_ref, attn_ref[...], send_refs)


def grad_kernel(place_ref, rates_ref, q_ref, out_grad_ref, weigh_ref, *refs):
    experts = weigh_ref.shape[0]
    home_refs, (grad_ref, mine_ref, other_ref) = refs[:experts], refs[experts:]
    block_len, half = q_ref.shape[0], mine_ref.shape[0]
    steps = column(block_len)
    total = out_grad_ref[...].astype(F32)
    for k in range(experts):
        total = total + dot(weigh_ref[k], home_refs[k][...], 1, 0)
    grad_ref[...] = total.astype(BF16)
    for slot in [*range(half, 2 * half), *range(half)]:
        head, lanes = lanes_of(place_ref, slot, 2 * half)
        power = jnp.exp(-rates_ref[head] * (steps + 1.0))
        scaled = (q_ref[:, lanes].astype(F32) * power).astype(BF16)
        state_ref = (mine_ref, other_ref)[slot // half]
        state_ref[slot % half] = dot(scaled, grad_ref[:, lanes], 0, 0).astype(BF16)


def near_kernel(
    place_ref, rates_ref, q_ref, k_ref, v_ref, grad_ref, mine_ref, other_ref, weights_ref,
    query_ref, key_ref, value_ref,
):
    block_len, half = q_ref.shape[0], mine_ref.shape[0]
    steps = column(block_len)
    for slot in range(2 * half):
        head, lanes = lanes_of(place_ref, slot, 2 * half)
        rate = rates_ref[head]
        grad = grad_ref[:, lanes]
        entering = (mine_ref, other_ref)[slot // half][slot % half]
        within = decay_within(rate, block_len)
        dweights = (SCALE * dot(grad, v_ref[:, lanes], 1, 1) * within).astype(BF16)
        query = dot(dweights, k_ref[:, lanes], 1, 0)
        query = query + SCALE * jnp.exp(-rate * steps) * dot(grad, entering, 1, 1)
        query_ref[:, lanes] = query.astype(BF16)
        key_ref[:, lanes] = dot(dweights, q_ref[:, lanes], 0, 0)
        value_ref[:, lanes] = dot(weights_ref[slot], grad, 0, 0)


def far_kernel(
    place_ref, rates_ref, k_ref, v_ref, key_near, value_near, mine_ref, other_ref, key_ref, value_ref
):
    block_len, half = k_ref.shape[0], mine_ref.shape[0]
    steps = column(block_len)
    for slot in range(2 * half):
        head, lanes = lanes_of(place_ref, slot, 2 * half)
        leaving = (mine_ref, other_ref)[slot // half][slot % half]
        power = SCALE * jnp.exp(-rates_ref[head] * (block_len - 1.0 - steps))
        key_ref[:, lanes] = (
            key_near[:, lanes] + power * dot(v_ref[:, lanes], leaving, 1, 1)
        ).astype(BF16)
        value_ref[:, lanes] = (
            value_near[:, lanes] + power * dot(k_ref[:, lanes], leaving, 1, 0)
        ).astype(BF16)


def call(kernel, out_shapes, scalars, arrays, flops, scratch=()):
    size = sum(leaf.size * leaf.dtype.itemsize for leaf in list(arrays) + list(out_shapes))
    return pl.pallas_call(
        kernel,
        out_shape=list(out_shapes),
        in_specs=[SMEM] * len(scalars) + [VMEM] * len(arrays),
        out_specs=[VMEM] * len(out_shapes),
        scratch_shapes=list(scratch),
        compiler_params=pltpu.CompilerParams(vmem_limit_bytes=16 * 1024 * 1024),
        cost_estimate=pl.CostEstimate(flops=flops, bytes_accessed=size, transcendentals=0),
    )(*scalars, *arrays)


def swap(array, axis, distance):
    size = lax.axis_size(axis)
    return lax.ppermute(array, axis, [(i, i ^ distance) for i in range(size)])


def trade(array, pairs, partner):
    return lax.ppermute(
        array, "ctx", [(2 * partner(i) + s, 2 * i + s) for i in range(pairs) for s in (0, 1)]
    )


def after(array, *events):
    return lax.optimization_barrier((array,) + events)[0]


def head_power(rates, place, half, tokens):
    mine = lax.dynamic_slice(rates, (place[0] * half,), (half,))[:, None, None]
    return jnp.exp(-mine * tokens)


def scan_total(mine, other, rates, place, block_len, reverse, *events):
    side = 1 - place[0] if reverse else place[0]
    whole = head_power(rates, place, mine.shape[0], block_len)
    partner = after(swap(other, "ctx", 1), *events)
    first = jnp.where(side == 0, mine, partner).astype(F32)
    second = jnp.where(side == 0, partner, mine).astype(F32)
    return (whole * first + second).astype(BF16), partner


def scan_step(before, total, reach, rates, place, block_len, reverse, *events):
    half = total.shape[0]
    pairs = lax.axis_size("ctx") // 2
    pair = pairs - 1 - place[1] if reverse else place[1]
    if before is None:
        upto = total
    else:
        whole = head_power(rates, place, half, 2.0 * block_len)
        upto = (whole * before + total.astype(F32)).astype(BF16)
    upto = after(upto, *events)
    lower, offset = (pair & reach) == 0, pair & (reach - 1)
    got = None
    for j in range(reach):

        def partner(i, j=j):
            i = pairs - 1 - i if reverse else i
            start = i - i % (2 * reach)
            first, second = start + reach - 1, start + reach + j
            i = {first: second, second: first}.get(i, i)
            return pairs - 1 - i if reverse else i

        one = trade(upto, pairs, partner)
        got = one if got is None else jnp.where(offset == j, one, got)
    scale = head_power(rates, place, half, 2.0 * block_len * offset.astype(F32))
    grown = scale * got.astype(F32)
    kept = 0.0 if before is None else before
    return jnp.where(lower, kept, kept + grown), upto


def scan_ends(before, mine, partner, rates, place, block_len, reverse):
    side = 1 - place[0] if reverse else place[0]
    whole = head_power(rates, place, mine.shape[0], block_len)
    first = jnp.where(side == 0, mine, partner).astype(F32)
    second_meets = whole * before + first
    keep = jnp.where(side == 0, before, second_meets).astype(BF16)
    give = jnp.where(side == 0, second_meets, before).astype(BF16)
    return keep, give


def split_rows(own, other, part, flag):
    count = len(part) // 2
    blocks = [
        jnp.where(flag == 0, side[part[i]], side[part[count + i]])
        for side in (own, other)
        for i in range(count)
    ]
    return jnp.concatenate(blocks, axis=0)


def sum_over_cores(own, other, part, multiply, *events):
    mine = lax.axis_index("exp") & 1
    sent = multiply(after(split_rows(own, other, part, 1 - mine), *events)).astype(BF16)
    got = swap(sent, "exp", 1)
    kept = multiply(after(split_rows(own, other, part, mine), sent))
    return (kept + got.astype(F32)).astype(BF16)


def sum_over_rest(part, bits):
    for bit in range(1, bits):
        part = (part.astype(F32) + swap(part, "exp", 1 << bit).astype(F32)).astype(BF16)
    return part


def on_device(
    queries, keys, values, out_grad, up_weight, down_weight, decay_rates, routes, gate_weights
):
    block_len, group = queries.shape
    heads = group // DH
    half = heads // 2
    experts = lax.axis_size("ctx") // 2
    bits = (lax.axis_size("exp") - 1).bit_length()
    capacity = block_len * 9 // (4 * experts)
    position = lax.axis_index("ctx").astype(jnp.int32)
    core = lax.axis_index("exp").astype(jnp.int32) & 1
    place = jnp.stack([position & 1, position >> 1, core])
    scalars = (place, decay_rates)
    up_local, down_local = up_weight[0], down_weight[0]
    near_part, far_part = range(experts // 2), range(experts // 2, experts)
    quarter = experts // 4
    order = [(k, k) for k in near_part]
    order += [(far_part[i], far_part[quarter + i]) for i in range(quarter)]
    order += [(far_part[quarter + i], far_part[i]) for i in range(quarter)]

    states = jax.ShapeDtypeStruct((half, DH, DH), BF16)
    weight_sq = jax.ShapeDtypeStruct((heads, block_len, block_len), BF16)
    wide = jax.ShapeDtypeStruct((block_len, group), F32)
    slim = jax.ShapeDtypeStruct((block_len, group), BF16)
    choose_table = jax.ShapeDtypeStruct((experts, capacity, block_len), F32)
    weigh_table = jax.ShapeDtypeStruct((experts, block_len, capacity), BF16)
    slots = jax.ShapeDtypeStruct((capacity, group), BF16)
    unit = 2 * block_len * DH * group

    reaches = [1 << i for i in range((experts - 1).bit_length())]
    pairs_of = lambda rows, k: swap(rows, "ctx", 2 * k) if k else rows

    key_mine, key_other = call(key_state_kernel, [states] * 2, scalars, (keys, values), unit)
    choose, weigh, *send_grad = call(
        functools.partial(route_kernel, order), [choose_table, weigh_table] + [slots] * experts,
        (place,), (routes, routes.T, gate_weights, out_grad), 3 * unit,
    )
    intra, weights = call(intra_kernel, [wide, weight_sq], scalars, (queries, keys, values), 2 * unit)

    grad_own, grad_other = {0: send_grad[0]}, {}
    for k in near_part[1:]:
        grad_own[k] = pairs_of(send_grad[k], k)
    total, partner = scan_total(
        key_mine, key_other, decay_rates, place, block_len, False,
        *[grad_own[k] for k in near_part],
    )
    for k in near_part:
        grad_other[k] = swap(after(grad_own[k], total), "ctx", 1)
    before = None
    for index, reach in enumerate(reaches):
        events = list(grad_other.values()) + [intra] if index == 1 else []
        before, upto = scan_step(
            before, total, reach, decay_rates, place, block_len, False, *events
        )
    keep, give = scan_ends(before, key_mine, partner, decay_rates, place, block_len, False)
    hidden_near = sum_over_cores(
        grad_own, grad_other, near_part, lambda rows: dot(rows, down_local, 1, 1), upto
    )
    give, hidden_near = lax.optimization_barrier((give, hidden_near))
    entering = (keep, swap(give, "ctx", 1))
    for k in far_part:
        grad_own[k] = pairs_of(after(send_grad[k], give), k)
    send_in = call(
        attend_kernel, [slots] * experts, scalars, (queries, intra, choose) + entering, 4 * unit,
        [pltpu.VMEM((block_len, group), BF16)],
    )
    for k in far_part:
        grad_other[k] = swap(after(grad_own[k], send_in[0]), "ctx", 1)

    in_own, in_other = {0: send_in[0]}, {}
    for k in [experts - 1, *near_part[1:]]:
        in_own[k] = pairs_of(send_in[k], k)
    for k in far_part[:-1]:
        in_own[k] = pairs_of(after(send_in[k], in_own[experts - 1]), k)
    for k in range(experts):
        in_other[k] = swap(in_own[k], "ctx", 1)

    by_down = lambda rows: dot(rows, down_local, 1, 1)
    by_up = lambda rows: dot(rows, up_local, 1, 0)
    hidden_near = sum_over_rest(hidden_near, bits)
    hidden_far = sum_over_cores(grad_own, grad_other, far_part, by_down, in_other[0])
    pre_near = sum_over_cores(in_own, in_other, near_part, by_up, hidden_near, hidden_far)
    hidden_far = sum_over_rest(hidden_far, bits)
    pre_far = sum_over_cores(in_own, in_other, far_part, by_up, pre_near)
    pre_near, pre_far = sum_over_rest(pre_near, bits), sum_over_rest(pre_far, bits)

    def returned(pre, hidden, *events):
        slope = (hidden.astype(F32) * silu_slope(pre.astype(F32))).astype(BF16)
        slope = after(slope, *events)
        slopes = (slope, swap(slope, "exp", 1))
        summed = []
        for slope in slopes:
            back = dot(after(slope, *events), up_local, 1, 1).astype(BF16)
            back = back.reshape(2, quarter * capacity, group)
            got = swap(back[1], "ctx", 1)
            events = events + (back,)
            summed.append((back[0], got))
        return summed

    def joined(item, *events):
        kept, got = item
        rows = (kept.astype(F32) + after(got, *events).astype(F32)).astype(BF16)
        return rows, [rows[i * capacity : (i + 1) * capacity] for i in range(quarter)]

    def far_home(rows, kept, i):
        moves = []
        size = lax.axis_size("exp")
        for c in range(2 * experts):
            for e in range(size):
                k = far_part[((e & 1) ^ (0 if kept else 1)) * quarter + i]
                moves.append((c * size + e, (c ^ (2 * k)) * size + e))
        return lax.ppermute(rows, ("ctx", "exp"), moves)

    near_items = returned(pre_near, hidden_near)
    far_items = returned(pre_far, hidden_far, near_items[0][0], near_items[1][0])
    first, near_first = joined(near_items[0])
    second, near_second = joined(near_items[1], first)
    homes = [jnp.where(core == 0, a, b) for a, b in zip(near_first, near_second)]
    homes += [jnp.where(core == 0, b, a) for a, b in zip(near_first, near_second)]
    homes = [pairs_of(rows, k) for k, rows in enumerate(homes)]
    first, far_first = joined(far_items[0])
    second, far_second = joined(far_items[1], first)
    homes += [far_home(rows, True, i) for i, rows in enumerate(far_first)]
    homes += [far_home(rows, False, i) for i, rows in enumerate(far_second)]

    grad_out, query_mine, query_other = call(
        grad_kernel, [slim, states, states], scalars, (queries, out_grad, weigh, *homes), 4 * unit
    )
    total, partner = scan_total(
        query_mine, query_other, decay_rates, place, block_len, True
    )
    before = None
    for reach in reaches:
        before, _ = scan_step(before, total, reach, decay_rates, place, block_len, True)
    keep, give = scan_ends(before, query_mine, partner, decay_rates, place, block_len, True)
    leaving = (keep, swap(give, "ctx", 1))
    query_g, key_near, value_near = call(
        near_kernel, [slim, wide, wide], scalars,
        (queries, keys, values, grad_out) + entering + (weights,), 5 * unit,
    )
    key_g, value_g = call(
        far_kernel, [slim, slim], scalars,
        (keys, values, key_near, value_near) + leaving, 2 * unit,
    )
    return query_g, key_g, value_g


def solution(mesh):
    placed = (
        P("ctx", "exp"),
        P("ctx", "exp"),
        P("ctx", "exp"),
        P("ctx", "exp"),
        P("ctx", "exp", None),
        P("ctx", None, "exp"),
        P("exp"),
        P("ctx", None),
        P("ctx", None),
    )
    return jax.shard_map(
        on_device,
        mesh=mesh,
        in_specs=placed,
        out_specs=(P("ctx", "exp"), P("ctx", "exp"), P("ctx", "exp")),
        check_vma=False,
    )
```

time: 215 us -> 232 us (1.079)
  starting transfers between devices: 57.1 us -> 68.5 us
  matrix products: 24 us -> 31.6 us
  Pallas kernels: 18.5 us -> 14.4 us
  waiting for transfers between devices: 94.6 us -> 98.2 us
    ppermute x0 -> x2, waiting for transfers between devices: none -> 10.1 us  [far_home(): return lax.ppermute(rows, ('ctx', 'exp'), moves)]
    ppermute x39 -> x33, starting transfers between devices: 48.9 us -> 56.6 us  [swap(): return lax.ppermute(array, axis, [(i, i ^ distance) for i in range(size)])]
    dot_general x6 -> x12, matrix products: 24 us -> 31.6 us  [dot(): lax.dot_general(left, right, (((left_dim,), (right_dim,)), ((), ())), pre...]
    pallas_call x7, Pallas kernels: 18.5 us -> 14.4 us  [call(): pl.pallas_call(kernel, out_shape=list(out_shapes), in_specs=[SMEM] * len(...]
    ppermute x6, waiting for transfers between devices: 14.4 us -> 10.7 us  [trade(): lax.ppermute(array, 'ctx', [(2 * partner(i) + s, 2 * i + s) for i in rang...]
    ppermute x39 -> x33, waiting for transfers between devices: 80.3 us -> 77.4 us  [swap(): return lax.ppermute(array, axis, [(i, i ^ distance) for i in range(size)])]
    ppermute x0 -> x2, starting transfers between devices: none -> 2.5 us  [far_home(): return lax.ppermute(rows, ('ctx', 'exp'), moves)]
    unnamed x48 -> x40, local copies, waits for them, and re-layouts: 6.08 us -> 6.93 us
  transfers between devices with their start and end apart: 45 -> 41, of which waited for: 20 -> 20; matrix products, arithmetic and copies ran while one was open for 16% -> 12% of each run, Pallas kernels for 6% -> 4%
where the time goes in v3:
time: 232 us; the launch traced here: 231 us
  waiting for transfers between devices  98.2 us (42%)
  starting transfers between devices  68.5 us (30%)
  matrix products  31.6 us (14%)
  Pallas kernels  14.4 us (6%)
  other arithmetic  9.63 us (4%)
  local copies, waits for them, and re-layouts  6.99 us (3%)
    ppermute x33, waiting for transfers between devices, swap(): return lax.ppermute(array, axis, [(i, i ^ distance) for i in range(size)])  77.4 us
    ppermute x33, starting transfers between devices, swap(): return lax.ppermute(array, axis, [(i, i ^ distance) for i in range(size)])  56.6 us
    dot_general x12, matrix products, dot(): lax.dot_general(left, right, (((left_dim,), (right_dim,)), ((), ())), pre...  31.6 us
    pallas_call x7, Pallas kernels, call(): pl.pallas_call(kernel, out_shape=list(out_shapes), in_specs=[SMEM] * len(...  14.4 us
    ppermute x6, waiting for transfers between devices, trade(): lax.ppermute(array, 'ctx', [(2 * partner(i) + s, 2 * i + s) for i in rang...  10.7 us
    ppermute x2, waiting for transfers between devices, far_home(): return lax.ppermute(rows, ('ctx', 'exp'), moves)  10.1 us
    ppermute x6, starting transfers between devices, trade(): lax.ppermute(array, 'ctx', [(2 * partner(i) + s, 2 * i + s) for i in rang...  9.41 us
    unnamed x40, local copies, waits for them, and re-layouts  6.93 us
  transfers between devices with their start and end apart: 41, of which 20 were waited for; matrix products, arithmetic and copies ran while one was open for 12% of the time, Pallas kernels for 4%

profile of v3, /device:TPU:0, one launch (start us, length us, event | category | flops | bytes accessed | tf_op | source)
XLA Modules:
  0.0 230.6 jit_solution(17293496356868174892)
XLA Ops:
  4.9 2.9 %collective-permute-start = (bf16[6,128,128]{2,1,0:T(8,128)(2,1)}, bf16[6,128,128]{2,1,0:T(8,128)(2,1)}, u32[]{:S(2)}, u32[]{:S(2)}) collective-permute-start(bf16[6,128,128]{2,1,0:T(8,128)(2,1)} %get-tuple-element.51), channel_id=1, source_target_pairs={{0,4},{4,0},{8,12},{12,8},{16,20},{20,16},{24,28},{28,24},{1,5},{5... | collective-permute-start | bytes 589832 | tf_op jit(solution)/shard_map/ppermute | solution.py:204
  15.1 2.5 %shard_map.114 = (f32[128,1536]{1,0:T(8,128)S(1)}, bf16[12,128,128]{2,1,0:T(8,128)(2,1)S(1)}) custom-call(s32[3]{0:T(128)S(1)} %pad_add_fusion.place_ref, f32[12]{0:T(128)S(1)} %copy-done.8, bf16[128,1536]{1,0:T(8,128)(2,1)S(1)} %copy-done.4, bf16[128,1536]{1,0:T(8,128)(2,1)S(1)} %copy-done.1, bf16[128,1536]{1,0:T(8,128)(2,1)S(1)} %copy-done.3), custom_call_target="tpu_custom_call" | custom-call | flops 100663296 | bytes 2359296 | tf_op jit(solution)/shard_map/pallas_call | solution.py:191
  17.8 3.0 %collective-permute-done.1 = bf16[72,1536]{1,0:T(8,128)(2,1)} collective-permute-done((bf16[72,1536]{1,0:T(8,128)(2,1)}, bf16[72,1536]{1,0:T(8,128)(2,1)}, u32[]{:S(2)}, u32[]{:S(2)}) %collective-permute-start.1) | collective-permute-done | bytes 221216 | tf_op jit(solution)/shard_map/ppermute | solution.py:204
  28.4 3.1 %collective-permute-done.3 = bf16[72,1536]{1,0:T(8,128)(2,1)S(1)} collective-permute-done((bf16[72,1536]{1,0:T(8,128)(2,1)S(1)}, bf16[72,1536]{1,0:T(8,128)(2,1)S(1)}, u32[]{:S(2)}, u32[]{:S(2)}) %collective-permute-start.3) | collective-permute-done | bytes 221216 | tf_op jit(solution)/shard_map/ppermute | solution.py:204
  34.7 6.4 %fusion.24 = bf16[144,2304]{1,0:T(8,128)(2,1)} fusion(bf16[144,1536]{1,0:T(8,128)(2,1)S(1)} %pad_maximum_fusion.1, bf16[1,2304,1536]{2,1,0:T(8,128)(2,1)} %param.14), kind=kOutput, calls=%fused_computation.24 | convolution fusion | flops 1019547648 | bytes 8183808 | tf_op jit(solution)/shard_map/dot_general | solution.py:20
  45.0 5.7 %add_convert_fusion.7 = bf16[144,2304]{1,0:T(8,128)(2,1)S(1)} fusion(bf16[144,2304]{1,0:T(8,128)(2,1)} %collective-permute-done.7, bf16[144,1536]{1,0:T(8,128)(2,1)S(1)} %pad_maximum_fusion, bf16[1,2304,1536]{2,1,0:T(8,128)(2,1)} %param.14), kind=kOutput, calls=%fused_computation.57 | convolution fusion | flops 1020211200 | bytes 8847360 | tf_op jit(solution)/shard_map/dot_general | solution.py:20
  51.3 13.3 %collective-permute-start.13 = (bf16[72,1536]{1,0:T(8,128)(2,1)S(1)}, bf16[72,1536]{1,0:T(8,128)(2,1)S(1)}, u32[]{:S(2)}, u32[]{:S(2)}) collective-permute-start(bf16[72,1536]{1,0:T(8,128)(2,1)S(1)} %copy-done.11), channel_id=1, source_target_pairs={{0,16},{4,20},{8,24},{12,28},{16,0},{20,4},{24,8},{28,12},{1,17},{... | collective-permute-start | bytes 663560 | tf_op jit(solution)/shard_map/ppermute | solution.py:204
  67.3 2.5 %collective-permute-start.25 = (bf16[72,1536]{1,0:T(8,128)(2,1)S(1)}, bf16[72,1536]{1,0:T(8,128)(2,1)S(1)}, u32[]{:S(2)}, u32[]{:S(2)}) collective-permute-start(bf16[72,1536]{1,0:T(8,128)(2,1)S(1)} %get-tuple-element.78), channel_id=1, source_target_pairs={{0,24},{4,28},{8,16},{12,20},{16,8},{20,12},{24,0},{28,4},{1,25},{... | collective-permute-start | bytes 663560 | tf_op jit(solution)/shard_map/ppermute | solution.py:204
  69.8 2.7 %collective-permute-start.10 = (bf16[72,1536]{1,0:T(8,128)(2,1)S(1)}, bf16[72,1536]{1,0:T(8,128)(2,1)S(1)}, u32[]{:S(2)}, u32[]{:S(2)}) collective-permute-start(bf16[72,1536]{1,0:T(8,128)(2,1)S(1)} %get-tuple-element.65), channel_id=1, source_target_pairs={{0,8},{4,12},{8,0},{12,4},{16,24},{20,28},{24,16},{28,20},{1,9},{5... | collective-permute-start | bytes 663560 | tf_op jit(solution)/shard_map/ppermute | solution.py:204
  74.0 11.2 %collective-permute-done.13 = bf16[72,1536]{1,0:T(8,128)(2,1)S(1)} collective-permute-done((bf16[72,1536]{1,0:T(8,128)(2,1)S(1)}, bf16[72,1536]{1,0:T(8,128)(2,1)S(1)}, u32[]{:S(2)}, u32[]{:S(2)}) %collective-permute-start.13) | collective-permute-done | bytes 221216 | tf_op jit(solution)/shard_map/ppermute | solution.py:204
  88.7 6.8 %collective-permute-start.26 = (bf16[72,1536]{1,0:T(8,128)(2,1)S(1)}, bf16[72,1536]{1,0:T(8,128)(2,1)S(1)}, u32[]{:S(2)}, u32[]{:S(2)}) collective-permute-start(bf16[72,1536]{1,0:T(8,128)(2,1)S(1)} %get-tuple-element.79), channel_id=1, source_target_pairs={{0,16},{4,20},{8,24},{12,28},{16,0},{20,4},{24,8},{28,12},{1,17},{... | collective-permute-start | bytes 663560 | tf_op jit(solution)/shard_map/ppermute | solution.py:204
  99.6 2.6 %collective-permute-done.16 = bf16[72,1536]{1,0:T(8,128)(2,1)S(1)} collective-permute-done((bf16[72,1536]{1,0:T(8,128)(2,1)S(1)}, bf16[72,1536]{1,0:T(8,128)(2,1)S(1)}, u32[]{:S(2)}, u32[]{:S(2)}) %collective-permute-start.16) | collective-permute-done | bytes 221216 | tf_op jit(solution)/shard_map/ppermute | solution.py:204
  122.2 14.3 %collective-permute-done.19 = bf16[144,2304]{1,0:T(8,128)(2,1)S(1)} collective-permute-done((bf16[144,2304]{1,0:T(8,128)(2,1)S(1)}, bf16[144,2304]{1,0:T(8,128)(2,1)S(1)}, u32[]{:S(2)}, u32[]{:S(2)}) %collective-permute-start.19) | collective-permute-done | bytes 663584 | tf_op jit(solution)/shard_map/ppermute | solution.py:204
  144.2 3.3 %collective-permute-done.20 = bf16[72,1536]{1,0:T(8,128)(2,1)S(1)} collective-permute-done((bf16[72,1536]{1,0:T(8,128)(2,1)S(1)}, bf16[72,1536]{1,0:T(8,128)(2,1)S(1)}, u32[]{:S(2)}, u32[]{:S(2)}) %collective-permute-start.20) | collective-permute-done | bytes 221216 | tf_op jit(solution)/shard_map/ppermute | solution.py:204
  151.5 12.7 %collective-permute-done.30 = bf16[144,2304]{1,0:T(8,128)(2,1)S(1)} collective-permute-done((bf16[144,2304]{1,0:T(8,128)(2,1)S(1)}, bf16[144,2304]{1,0:T(8,128)(2,1)S(1)}, u32[]{:S(2)}, u32[]{:S(2)}) %collective-permute-start.30) | collective-permute-done | bytes 663584 | tf_op jit(solution)/shard_map/ppermute | solution.py:204
  165.1 2.4 %fusion.42 = bf16[144,1536]{1,0:T(8,128)(2,1)S(1)} fusion(bf16[144,2304]{1,0:T(8,128)(2,1)S(1)} %fusion.61, bf16[1,1536,2304]{2,1,0:T(8,128)(2,1)S(1)} %bitcast.66), kind=kOutput, calls=%fused_computation.30 | convolution fusion | flops 1019437056 | bytes 8183808 | tf_op jit(solution)/shard_map/dot_general | solution.py:20
  168.9 6.6 %collective-permute-done.31 = bf16[72,1536]{1,0:T(8,128)(2,1)S(1)} collective-permute-done((bf16[72,1536]{1,0:T(8,128)(2,1)S(1)}, bf16[72,1536]{1,0:T(8,128)(2,1)S(1)}, u32[]{:S(2)}, u32[]{:S(2)}) %collective-permute-start.31) | collective-permute-done | bytes 221216 | tf_op jit(solution)/shard_map/ppermute | solution.py:204
  179.5 5.6 %collective-permute-done.34 = bf16[72,1536]{1,0:T(8,128)(2,1)S(1)} collective-permute-done((bf16[72,1536]{1,0:T(8,128)(2,1)S(1)}, bf16[72,1536]{1,0:T(8,128)(2,1)S(1)}, u32[]{:S(2)}, u32[]{:S(2)}) %collective-permute-start.34) | collective-permute-done | bytes 221216 | tf_op jit(solution)/shard_map/ppermute | solution.py:204
  187.1 10.1 %collective-permute-done.32.refs_2_ = bf16[72,1536]{1,0:T(8,128)(2,1)S(1)} collective-permute-done((bf16[72,1536]{1,0:T(8,128)(2,1)S(1)}, bf16[72,1536]{1,0:T(8,128)(2,1)S(1)}, u32[]{:S(2)}, u32[]{:S(2)}) %collective-permute-start.32) | collective-permute-done | bytes 221216 | tf_op jit(solution)/shard_map/ppermute | solution.py:405
  199.8 5.9 %collective-permute-done.36 = bf16[6,128,128]{2,1,0:T(8,128)(2,1)S(1)} collective-permute-done((bf16[6,128,128]{2,1,0:T(8,128)(2,1)S(1)}, bf16[6,128,128]{2,1,0:T(8,128)(2,1)S(1)}, u32[]{:S(2)}, u32[]{:S(2)}) %collective-permute-start.36) | collective-permute-done | bytes 196640 | tf_op jit(solution)/shard_map/ppermute | solution.py:204
  207.7 4.5 %collective-permute-done.37 = bf16[6,128,128]{2,1,0:T(8,128)(2,1)S(1)} collective-permute-done((bf16[6,128,128]{2,1,0:T(8,128)(2,1)S(1)}, bf16[6,128,128]{2,1,0:T(8,128)(2,1)S(1)}, u32[]{:S(2)}, u32[]{:S(2)}) %collective-permute-start.37) | collective-permute-done | bytes 196640 | tf_op jit(solution)/shard_map/ppermute | solution.py:208
  212.4 3.1 %collective-permute-start.38 = (bf16[6,128,128]{2,1,0:T(8,128)(2,1)S(1)}, bf16[6,128,128]{2,1,0:T(8,128)(2,1)S(1)}, u32[]{:S(2)}, u32[]{:S(2)}) collective-permute-start(bf16[6,128,128]{2,1,0:T(8,128)(2,1)S(1)} %add_convert_fusion.12), channel_id=1, source_target_pairs={{16,0},{20,4},{8,8},{12,12},{0,16},{4,20},{24,24},{28,28},{17,1},{... | collective-permute-start | bytes 589832 | tf_op jit(solution)/shard_map/ppermute | solution.py:208
  216.9 5.8 %collective-permute-done.38 = bf16[6,128,128]{2,1,0:T(8,128)(2,1)S(1)} collective-permute-done((bf16[6,128,128]{2,1,0:T(8,128)(2,1)S(1)}, bf16[6,128,128]{2,1,0:T(8,128)(2,1)S(1)}, u32[]{:S(2)}, u32[]{:S(2)}) %collective-permute-start.38) | collective-permute-done | bytes 196640 | tf_op jit(solution)/shard_map/ppermute | solution.py:208
  224.1 4.0 %shard_map.117 = (bf16[128,1536]{1,0:T(8,128)(2,1)}, f32[128,1536]{1,0:T(8,128)S(1)}, f32[128,1536]{1,0:T(8,128)S(1)}) custom-call(s32[3]{0:T(128)S(1)} %pad_add_fusion.place_ref, f32[12]{0:T(128)S(1)} %copy-done.8, bf16[128,1536]{1,0:T(8,128)(2,1)S(1)} %copy-done.4, bf16[128,1536]{1,0:T(8,128)(2,1)S(1)} %copy-done.1, bf16[128,1536]{1,0:T(8,128)(2,1)S(1)} %copy-done.3, ...), custom_call_target="tpu_custom_call" | custom-call | flops 251658240 | bytes 4325376 | tf_op jit(solution)/shard_map/pallas_call | solution.py:191
  (155 shorter events, 88.2 us)
Async XLA Ops:
  4.9 12.9 %collective-permute-start = (bf16[6,128,128]{2,1,0:T(8,128)(2,1)}, bf16[6,128,128]{2,1,0:T(8,128)(2,1)}, u32[]{:S(2)}, u32[]{:S(2)}) collective-permute-start(bf16[6,128,128]{2,1,0:T(8,128)(2,1)} %get-tuple-element.51), channel_id=1, source_target_pairs={{0,4},{4,0},{8,12},{12,8},{16,20},{20,16},{24,28},{28,24},{1,5},{5... | collective-permute-start | bytes 589832 | tf_op jit(solution)/shard_map/ppermute | solution.py:204
  24.0 9.9 %collective-permute-start.4 = (bf16[72,1536]{1,0:T(8,128)(2,1)}, bf16[72,1536]{1,0:T(8,128)(2,1)S(1)}, u32[]{:S(2)}, u32[]{:S(2)}) collective-permute-start(bf16[72,1536]{1,0:T(8,128)(2,1)} %collective-permute-done.1), channel_id=1, source_target_pairs={{0,4},{4,0},{8,12},{12,8},{16,20},{20,16},{24,28},{28,24},{1,5},{5... | collective-permute-start | bytes 663560 | tf_op jit(solution)/shard_map/ppermute | solution.py:204
  50.6 15.4 %collective-permute-start.9 = (bf16[6,128,128]{2,1,0:T(8,128)(2,1)S(1)}, bf16[6,128,128]{2,1,0:T(8,128)(2,1)S(1)}, u32[]{:S(2)}, u32[]{:S(2)}) collective-permute-start(bf16[6,128,128]{2,1,0:T(8,128)(2,1)S(1)} %get-tuple-element.63), channel_id=1, source_target_pairs={{0,4},{4,0},{8,12},{12,8},{16,20},{20,16},{24,28},{28,24},{1,5},{5... | collective-permute-start | bytes 589832 | tf_op jit(solution)/shard_map/ppermute | solution.py:204
  51.3 33.9 %collective-permute-start.13 = (bf16[72,1536]{1,0:T(8,128)(2,1)S(1)}, bf16[72,1536]{1,0:T(8,128)(2,1)S(1)}, u32[]{:S(2)}, u32[]{:S(2)}) collective-permute-start(bf16[72,1536]{1,0:T(8,128)(2,1)S(1)} %copy-done.11), channel_id=1, source_target_pairs={{0,16},{4,20},{8,24},{12,28},{16,0},{20,4},{24,8},{28,12},{1,17},{... | collective-permute-start | bytes 663560 | tf_op jit(solution)/shard_map/ppermute | solution.py:204
  64.7 22.0 %collective-permute-start.14 = (bf16[72,1536]{1,0:T(8,128)(2,1)S(1)}, bf16[72,1536]{1,0:T(8,128)(2,1)S(1)}, u32[]{:S(2)}, u32[]{:S(2)}) collective-permute-start(bf16[72,1536]{1,0:T(8,128)(2,1)S(1)} %get-tuple-element.69), channel_id=1, source_target_pairs={{0,24},{4,28},{8,16},{12,20},{16,8},{20,12},{24,0},{28,4},{1,25},{... | collective-permute-start | bytes 663560 | tf_op jit(solution)/shard_map/ppermute | solution.py:204
  67.3 19.9 %collective-permute-start.25 = (bf16[72,1536]{1,0:T(8,128)(2,1)S(1)}, bf16[72,1536]{1,0:T(8,128)(2,1)S(1)}, u32[]{:S(2)}, u32[]{:S(2)}) collective-permute-start(bf16[72,1536]{1,0:T(8,128)(2,1)S(1)} %get-tuple-element.78), channel_id=1, source_target_pairs={{0,24},{4,28},{8,16},{12,20},{16,8},{20,12},{24,0},{28,4},{1,25},{... | collective-permute-start | bytes 663560 | tf_op jit(solution)/shard_map/ppermute | solution.py:204
  69.8 18.9 %collective-permute-start.10 = (bf16[72,1536]{1,0:T(8,128)(2,1)S(1)}, bf16[72,1536]{1,0:T(8,128)(2,1)S(1)}, u32[]{:S(2)}, u32[]{:S(2)}) collective-permute-start(bf16[72,1536]{1,0:T(8,128)(2,1)S(1)} %get-tuple-element.65), channel_id=1, source_target_pairs={{0,8},{4,12},{8,0},{12,4},{16,24},{20,28},{24,16},{28,20},{1,9},{5... | collective-permute-start | bytes 663560 | tf_op jit(solution)/shard_map/ppermute | solution.py:204
  72.5 41.0 %collective-permute-start.8 = (bf16[144,2304]{1,0:T(8,128)(2,1)S(1)}, bf16[144,2304]{1,0:T(8,128)(2,1)S(1)}, u32[]{:S(2)}, u32[]{:S(2)}) collective-permute-start(bf16[144,2304]{1,0:T(8,128)(2,1)S(1)} %add_convert_fusion.7), channel_id=1, source_target_pairs={{0,2},{1,3},{2,0},{3,1},{4,6},{5,7},{6,4},{7,5},{8,10},{9,11},{10,... | collective-permute-start | bytes 1990664 | tf_op jit(solution)/shard_map/ppermute | solution.py:204
  85.2 19.2 %collective-permute-start.11 = (bf16[72,1536]{1,0:T(8,128)(2,1)S(1)}, bf16[72,1536]{1,0:T(8,128)(2,1)S(1)}, u32[]{:S(2)}, u32[]{:S(2)}) collective-permute-start(bf16[72,1536]{1,0:T(8,128)(2,1)S(1)} %get-tuple-element.64), channel_id=1, source_target_pairs={{0,4},{4,0},{8,12},{12,8},{16,20},{20,16},{24,28},{28,24},{1,5},{5... | collective-permute-start | bytes 663560 | tf_op jit(solution)/shard_map/ppermute | solution.py:204
  86.7 10.9 %collective-permute-start.15 = (bf16[72,1536]{1,0:T(8,128)(2,1)S(1)}, bf16[72,1536]{1,0:T(8,128)(2,1)S(1)}, u32[]{:S(2)}, u32[]{:S(2)}) collective-permute-start(bf16[72,1536]{1,0:T(8,128)(2,1)S(1)} %collective-permute-done.13), channel_id=1, source_target_pairs={{0,4},{4,0},{8,12},{12,8},{16,20},{20,16},{24,28},{28,24},{1,5},{5... | collective-permute-start | bytes 663560 | tf_op jit(solution)/shard_map/ppermute | solution.py:204
  87.3 15.0 %collective-permute-start.16 = (bf16[72,1536]{1,0:T(8,128)(2,1)S(1)}, bf16[72,1536]{1,0:T(8,128)(2,1)S(1)}, u32[]{:S(2)}, u32[]{:S(2)}) collective-permute-start(bf16[72,1536]{1,0:T(8,128)(2,1)S(1)} %collective-permute-done.14), channel_id=1, source_target_pairs={{0,4},{4,0},{8,12},{12,8},{16,20},{20,16},{24,28},{28,24},{1,5},{5... | collective-permute-start | bytes 663560 | tf_op jit(solution)/shard_map/ppermute | solution.py:204
  88.7 20.7 %collective-permute-start.26 = (bf16[72,1536]{1,0:T(8,128)(2,1)S(1)}, bf16[72,1536]{1,0:T(8,128)(2,1)S(1)}, u32[]{:S(2)}, u32[]{:S(2)}) collective-permute-start(bf16[72,1536]{1,0:T(8,128)(2,1)S(1)} %get-tuple-element.79), channel_id=1, source_target_pairs={{0,16},{4,20},{8,24},{12,28},{16,0},{20,4},{24,8},{28,12},{1,17},{... | collective-permute-start | bytes 663560 | tf_op jit(solution)/shard_map/ppermute | solution.py:204
  102.3 13.3 %collective-permute-start.28 = (bf16[72,1536]{1,0:T(8,128)(2,1)S(1)}, bf16[72,1536]{1,0:T(8,128)(2,1)S(1)}, u32[]{:S(2)}, u32[]{:S(2)}) collective-permute-start(bf16[72,1536]{1,0:T(8,128)(2,1)S(1)} %collective-permute-done.25), channel_id=1, source_target_pairs={{0,4},{4,0},{8,12},{12,8},{16,20},{20,16},{24,28},{28,24},{1,5},{5... | collective-permute-start | bytes 663560 | tf_op jit(solution)/shard_map/ppermute | solution.py:204
  118.7 17.8 %collective-permute-start.19 = (bf16[144,2304]{1,0:T(8,128)(2,1)S(1)}, bf16[144,2304]{1,0:T(8,128)(2,1)S(1)}, u32[]{:S(2)}, u32[]{:S(2)}) collective-permute-start(bf16[144,2304]{1,0:T(8,128)(2,1)S(1)} %add_convert_fusion.4), channel_id=1, source_target_pairs={{0,2},{1,3},{2,0},{3,1},{4,6},{5,7},{6,4},{7,5},{8,10},{9,11},{10,... | collective-permute-start | bytes 1990664 | tf_op jit(solution)/shard_map/ppermute | solution.py:204
  120.3 31.3 %collective-permute-start.24 = (bf16[144,2304]{1,0:T(8,128)(2,1)S(1)}, bf16[144,2304]{1,0:T(8,128)(2,1)S(1)}, u32[]{:S(2)}, u32[]{:S(2)}) collective-permute-start(bf16[144,2304]{1,0:T(8,128)(2,1)S(1)} %add_convert_fusion.5), channel_id=1, source_target_pairs={{0,2},{1,3},{2,0},{3,1},{4,6},{5,7},{6,4},{7,5},{8,10},{9,11},{10,... | collective-permute-start | bytes 1990664 | tf_op jit(solution)/shard_map/ppermute | solution.py:204
  122.1 19.1 %collective-permute-start.29 = (bf16[144,2304]{1,0:T(8,128)(2,1)S(1)}, bf16[144,2304]{1,0:T(8,128)(2,1)S(1)}, u32[]{:S(2)}, u32[]{:S(2)}) collective-permute-start(bf16[144,2304]{1,0:T(8,128)(2,1)S(1)} %fusion.33), channel_id=1, source_target_pairs={{0,1},{1,0},{2,3},{3,2},{4,5},{5,4},{6,7},{7,6},{8,9},{9,8},{10,11... | collective-permute-start | bytes 1990664 | tf_op jit(solution)/shard_map/ppermute | solution.py:204
  137.1 10.5 %collective-permute-start.21 = (bf16[144,2304]{1,0:T(8,128)(2,1)S(1)}, bf16[144,2304]{1,0:T(8,128)(2,1)S(1)}, u32[]{:S(2)}, u32[]{:S(2)}) collective-permute-start(bf16[144,2304]{1,0:T(8,128)(2,1)S(1)} %fusion.54), channel_id=1, source_target_pairs={{0,1},{1,0},{2,3},{3,2},{4,5},{5,4},{6,7},{7,6},{8,9},{9,8},{10,11... | collective-permute-start | bytes 1990664 | tf_op jit(solution)/shard_map/ppermute | solution.py:204
  142.6 21.6 %collective-permute-start.30 = (bf16[144,2304]{1,0:T(8,128)(2,1)S(1)}, bf16[144,2304]{1,0:T(8,128)(2,1)S(1)}, u32[]{:S(2)}, u32[]{:S(2)}) collective-permute-start(bf16[144,2304]{1,0:T(8,128)(2,1)S(1)} %add_convert_fusion.1), channel_id=1, source_target_pairs={{0,2},{1,3},{2,0},{3,1},{4,6},{5,7},{6,4},{7,5},{8,10},{9,11},{10,... | collective-permute-start | bytes 1990664 | tf_op jit(solution)/shard_map/ppermute | solution.py:204
  150.0 14.9 %collective-permute-start.22 = (bf16[72,1536]{1,0:T(8,128)(2,1)S(1)}, bf16[72,1536]{1,0:T(8,128)(2,1)S(1)}, u32[]{:S(2)}, u32[]{:S(2)}) collective-permute-start(bf16[72,1536]{1,0:T(8,128)(2,1)S(1)} %slice.43), channel_id=1, source_target_pairs={{0,4},{4,0},{8,12},{12,8},{16,20},{20,16},{24,28},{28,24},{1,5},{5... | collective-permute-start | bytes 663560 | tf_op jit(solution)/shard_map/ppermute | solution.py:204
  165.0 10.4 %collective-permute-start.33 = (bf16[144,2304]{1,0:T(8,128)(2,1)S(1)}, bf16[144,2304]{1,0:T(8,128)(2,1)S(1)}, u32[]{:S(2)}, u32[]{:S(2)}) collective-permute-start(bf16[144,2304]{1,0:T(8,128)(2,1)S(1)} %fusion.61), channel_id=1, source_target_pairs={{0,1},{1,0},{2,3},{3,2},{4,5},{5,4},{6,7},{7,6},{8,9},{9,8},{10,11... | collective-permute-start | bytes 1990664 | tf_op jit(solution)/shard_map/ppermute | solution.py:204
  168.5 18.6 %collective-permute-start.23 = (bf16[72,1536]{1,0:T(8,128)(2,1)S(1)}, bf16[72,1536]{1,0:T(8,128)(2,1)S(1)}, u32[]{:S(2)}, u32[]{:S(2)}) collective-permute-start(bf16[72,1536]{1,0:T(8,128)(2,1)S(1)} %get-tuple-element.101), channel_id=1, source_target_pairs={{0,8},{4,12},{8,0},{12,4},{16,24},{20,28},{24,16},{28,20},{1,9},{5... | collective-permute-start | bytes 663560 | tf_op jit(solution)/shard_map/ppermute | solution.py:204
  178.9 18.3 %collective-permute-start.32 = (bf16[72,1536]{1,0:T(8,128)(2,1)S(1)}, bf16[72,1536]{1,0:T(8,128)(2,1)S(1)}, u32[]{:S(2)}, u32[]{:S(2)}) collective-permute-start(bf16[72,1536]{1,0:T(8,128)(2,1)S(1)} %add_convert_fusion.9), channel_id=1, source_target_pairs={{0,16},{1,25},{2,18},{3,27},{4,20},{5,29},{6,22},{7,31},{8,24},{9,... | collective-permute-start | bytes 663560 | tf_op jit(solution)/shard_map/ppermute | solution.py:405
  185.1 12.1 %collective-permute-start.35 = (bf16[72,1536]{1,0:T(8,128)(2,1)S(1)}, bf16[72,1536]{1,0:T(8,128)(2,1)S(1)}, u32[]{:S(2)}, u32[]{:S(2)}) collective-permute-start(bf16[72,1536]{1,0:T(8,128)(2,1)S(1)} %add_convert_fusion.8), channel_id=1, source_target_pairs={{0,24},{1,17},{2,26},{3,19},{4,28},{5,21},{6,30},{7,23},{8,16},{9,... | collective-permute-start | bytes 663560 | tf_op jit(solution)/shard_map/ppermute | solution.py:405
  212.4 10.3 %collective-permute-start.38 = (bf16[6,128,128]{2,1,0:T(8,128)(2,1)S(1)}, bf16[6,128,128]{2,1,0:T(8,128)(2,1)S(1)}, u32[]{:S(2)}, u32[]{:S(2)}) collective-permute-start(bf16[6,128,128]{2,1,0:T(8,128)(2,1)S(1)} %add_convert_fusion.12), channel_id=1, source_target_pairs={{16,0},{20,4},{8,8},{12,12},{0,16},{4,20},{24,24},{28,28},{17,1},{... | collective-permute-start | bytes 589832 | tf_op jit(solution)/shard_map/ppermute | solution.py:208
  (36 other events, 334.3 us)

commit v4 on v3

--- a/solution.py
+++ b/solution.py
@@ -14,6 +14,7 @@
 
 SMEM = pl.BlockSpec(memory_space=pltpu.SMEM)
 VMEM = pl.BlockSpec(memory_space=pltpu.VMEM)
+SMALL = pl.CostEstimate(flops=1, bytes_accessed=1, transcendentals=0)
 
 
 def dot(left, right, left_dim, right_dim):
@@ -67,13 +68,13 @@
 
 
 def route_kernel(
-    order, place_ref, routes_ref, turned_ref, gates_ref, grad_ref, choose_ref, weigh_ref, *send_refs
+    order, place_ref, routes_ref, gates_ref, grad_ref, choose_ref, weigh_ref, *send_refs
 ):
     experts, capacity, block_len = choose_ref.shape
     rows = lax.broadcasted_iota(jnp.int32, (block_len, block_len), 0)
     cols = lax.broadcasted_iota(jnp.int32, (block_len, block_len), 1)
 
-    first, second = turned_ref[0:1, :], turned_ref[1:2, :]
+    first, second = routes_ref[0:1, :], routes_ref[1:2, :]
     names = lax.broadcasted_iota(jnp.int32, (32, block_len), 0)
     hit_first = jnp.where(names == first, 1.0, 0.0)
     hit_second = jnp.where(names == second, 1.0, 0.0)
@@ -90,19 +91,19 @@
         choose_ref[k] = jnp.where(named, 1.0, 0.0)
     pick_rows(choose_ref, grad_ref[...], send_refs)
 
-    first, second = routes_ref[:, 0:1], routes_ref[:, 1:2]
-    names = lax.broadcasted_iota(jnp.int32, (block_len, 128), 1)
-    hit_first = jnp.where(names == first, 1.0, 0.0)
-    hit_second = jnp.where(names == second, 1.0, 0.0)
-    earlier = jnp.where(rows > cols, 1.0, 0.0).astype(BF16)
-    before = dot(earlier, (hit_first + hit_second).astype(BF16), 1, 0)
-    slot_first = jnp.sum(before * hit_first, axis=1, keepdims=True).astype(jnp.int32)
-    slot_second = jnp.sum(before * hit_second, axis=1, keepdims=True).astype(jnp.int32)
+    columns = jnp.concatenate(
+        [first.astype(F32), second.astype(F32), slot_first.astype(F32), slot_second.astype(F32)]
+        + [gates_ref[0:1, :], gates_ref[1:2, :]] + [jnp.zeros((2, block_len), F32)],
+        axis=0,
+    ).T
+    first, second, slot_first, slot_second = [
+        columns[:, i : i + 1].astype(jnp.int32) for i in range(4)
+    ]
     slots = lax.broadcasted_iota(jnp.int32, (block_len, capacity), 1)
     for position, (even, odd) in enumerate(order):
         expert = place_ref[1] ^ jnp.where(place_ref[2] == 0, even, odd)
-        one = jnp.where((slots == slot_first) & (first == expert), gates_ref[:, 0:1], 0.0)
-        two = jnp.where((slots == slot_second) & (second == expert), gates_ref[:, 1:2], 0.0)
+        one = jnp.where((slots == slot_first) & (first == expert), columns[:, 4:5], 0.0)
+        two = jnp.where((slots == slot_second) & (second == expert), columns[:, 5:6], 0.0)
         weigh_ref[position] = (one + two).astype(BF16)
 
 
@@ -186,8 +187,7 @@
         ).astype(BF16)
 
 
-def call(kernel, out_shapes, scalars, arrays, flops, scratch=()):
-    size = sum(leaf.size * leaf.dtype.itemsize for leaf in list(arrays) + list(out_shapes))
+def call(kernel, out_shapes, scalars, arrays, scratch=()):
     return pl.pallas_call(
         kernel,
         out_shape=list(out_shapes),
@@ -195,8 +195,47 @@
         out_specs=[VMEM] * len(out_shapes),
         scratch_shapes=list(scratch),
         compiler_params=pltpu.CompilerParams(vmem_limit_bytes=16 * 1024 * 1024),
-        cost_estimate=pl.CostEstimate(flops=flops, bytes_accessed=size, transcendentals=0),
+        cost_estimate=SMALL,
     )(*scalars, *arrays)
+
+
+def halves_kernel(place_ref, own0, own1, other0, other1, weight_ref, sent_ref, kept_ref, rows_ref):
+    count = sent_ref.shape[0]
+
+    @pl.when(pl.program_id(0) == 0)
+    def _():
+        even = jnp.concatenate([own0[...].astype(F32), other0[...].astype(F32)], axis=0)
+        odd = jnp.concatenate([own1[...].astype(F32), other1[...].astype(F32)], axis=0)
+        first = place_ref[2] == 0
+        rows_ref[:count] = jnp.where(first, odd, even).astype(BF16)
+        rows_ref[count:] = jnp.where(first, even, odd).astype(BF16)
+
+    out = dot(rows_ref[...], weight_ref[...], 1, 1).astype(BF16)
+    sent_ref[...] = out[:count]
+    kept_ref[...] = out[count:]
+
+
+def halves_by_down(place, own, other, part, weight, tile=384):
+    count = len(part) // 2
+    join = lambda side, first: (
+        side[part[first]] if count == 1
+        else jnp.concatenate([side[part[first + i]] for i in range(count)], axis=0)
+    )
+    blocks = [join(own, 0), join(own, count), join(other, 0), join(other, count)]
+    rows, depth = blocks[0].shape
+    width = weight.shape[0]
+    whole = pl.BlockSpec((rows, depth), lambda j: (0, 0))
+    out = jax.ShapeDtypeStruct((2 * rows, width), BF16)
+    return pl.pallas_call(
+        halves_kernel,
+        grid=(width // tile,),
+        out_shape=[out, out],
+        in_specs=[SMEM] + [whole] * 4 + [pl.BlockSpec((tile, depth), lambda j: (j, 0))],
+        out_specs=[pl.BlockSpec((2 * rows, tile), lambda j: (0, j))] * 2,
+        scratch_shapes=[pltpu.VMEM((4 * rows, depth), BF16)],
+        compiler_params=pltpu.CompilerParams(vmem_limit_bytes=16 * 1024 * 1024),
+        cost_estimate=SMALL,
+    )(place, *blocks, weight)
 
 
 def swap(array, axis, distance):
@@ -318,48 +357,47 @@
     choose_table = jax.ShapeDtypeStruct((experts, capacity, block_len), F32)
     weigh_table = jax.ShapeDtypeStruct((experts, block_len, capacity), BF16)
     slots = jax.ShapeDtypeStruct((capacity, group), BF16)
-    unit = 2 * block_len * DH * group
 
     reaches = [1 << i for i in range((experts - 1).bit_length())]
     pairs_of = lambda rows, k: swap(rows, "ctx", 2 * k) if k else rows
 
-    key_mine, key_other = call(key_state_kernel, [states] * 2, scalars, (keys, values), unit)
+    key_mine, key_other = call(key_state_kernel, [states] * 2, scalars, (keys, values))
     choose, weigh, *send_grad = call(
         functools.partial(route_kernel, order), [choose_table, weigh_table] + [slots] * experts,
-        (place,), (routes, routes.T, gate_weights, out_grad), 3 * unit,
-    )
-    intra, weights = call(intra_kernel, [wide, weight_sq], scalars, (queries, keys, values), 2 * unit)
-
-    grad_own, grad_other = {0: send_grad[0]}, {}
-    for k in near_part[1:]:
-        grad_own[k] = pairs_of(send_grad[k], k)
+        (place,), (routes.T, gate_weights.T, out_grad)
+    )
+    intra, weights = call(intra_kernel, [wide, weight_sq], scalars, (queries, keys, values))
+
+    grad_own = {k: pairs_of(send_grad[k], k) for k in reversed(range(experts))}
     total, partner = scan_total(
-        key_mine, key_other, decay_rates, place, block_len, False,
-        *[grad_own[k] for k in near_part],
-    )
-    for k in near_part:
-        grad_other[k] = swap(after(grad_own[k], total), "ctx", 1)
+        key_mine, key_other, decay_rates, place, block_len, False, send_grad[0]
+    )
     before = None
     for index, reach in enumerate(reaches):
-        events = list(grad_other.values()) + [intra] if index == 1 else []
+        events = list(grad_own.values()) + [intra] if index == 1 else []
         before, upto = scan_step(
             before, total, reach, decay_rates, place, block_len, False, *events
         )
+    grad_other = {k: swap(after(grad_own[k], upto if k else total), "ctx", 1) for k in near_part}
     keep, give = scan_ends(before, key_mine, partner, decay_rates, place, block_len, False)
-    hidden_near = sum_over_cores(
-        grad_own, grad_other, near_part, lambda rows: dot(rows, down_local, 1, 1), upto
-    )
-    give, hidden_near = lax.optimization_barrier((give, hidden_near))
-    entering = (keep, swap(give, "ctx", 1))
+    entering = [keep, swap(give, "ctx", 1)]
+
+    def over_cores(sent, kept):
+        return (kept.astype(F32) + swap(sent, "exp", 1).astype(F32)).astype(BF16)
+
+    grad_own[0] = after(grad_own[0], give)
+    near_halves = halves_by_down(place, grad_own, grad_other, near_part, down_local)
+    entering[1], *near_halves = lax.optimization_barrier((entering[1], *near_halves))
     for k in far_part:
-        grad_own[k] = pairs_of(after(send_grad[k], give), k)
+        grad_other[k] = swap(after(grad_own[k], entering[1]), "ctx", 1)
+    entering = tuple(entering)
     send_in = call(
-        attend_kernel, [slots] * experts, scalars, (queries, intra, choose) + entering, 4 * unit,
+        attend_kernel, [slots] * experts, scalars, (queries, intra, choose) + entering,
         [pltpu.VMEM((block_len, group), BF16)],
     )
-    for k in far_part:
-        grad_other[k] = swap(after(grad_own[k], send_in[0]), "ctx", 1)
-
+    hidden_near = over_cores(*near_halves)
+    grad_own[far_part[0]] = after(grad_own[far_part[0]], send_in[0], hidden_near)
+    hidden_far = over_cores(*halves_by_down(place, grad_own, grad_other, far_part, down_local))
     in_own, in_other = {0: send_in[0]}, {}
     for k in [experts - 1, *near_part[1:]]:
         in_own[k] = pairs_of(send_in[k], k)
@@ -368,10 +406,8 @@
     for k in range(experts):
         in_other[k] = swap(in_own[k], "ctx", 1)
 
-    by_down = lambda rows: dot(rows, down_local, 1, 1)
     by_up = lambda rows: dot(rows, up_local, 1, 0)
     hidden_near = sum_over_rest(hidden_near, bits)
-    hidden_far = sum_over_cores(grad_own, grad_other, far_part, by_down, in_other[0])
     pre_near = sum_over_cores(in_own, in_other, near_part, by_up, hidden_near, hidden_far)
     hidden_far = sum_over_rest(hidden_far, bits)
     pre_far = sum_over_cores(in_own, in_other, far_part, by_up, pre_near)
@@ -417,7 +453,7 @@
     homes += [far_home(rows, False, i) for i, rows in enumerate(far_second)]
 
     grad_out, query_mine, query_other = call(
-        grad_kernel, [slim, states, states], scalars, (queries, out_grad, weigh, *homes), 4 * unit
+        grad_kernel, [slim, states, states], scalars, (queries, out_grad, weigh, *homes)
     )
     total, partner = scan_total(
         query_mine, query_other, decay_rates, place, block_len, True
@@ -429,11 +465,11 @@
     leaving = (keep, swap(give, "ctx", 1))
     query_g, key_near, value_near = call(
         near_kernel, [slim, wide, wide], scalars,
-        (queries, keys, values, grad_out) + entering + (weights,), 5 * unit,
+        (queries, keys, values, grad_out) + entering + (weights,)
     )
     key_g, value_g = call(
         far_kernel, [slim, slim], scalars,
-        (keys, values, key_near, value_near) + leaving, 2 * unit,
+        (keys, values, key_near, value_near) + leaving
     )
     return query_g, key_g, value_g
 

time: 232 us -> 225 us (0.970)
  matrix products: 31.6 us -> 14.5 us
  starting transfers between devices: 68.5 us -> 57.4 us
  Pallas kernels: 14.4 us -> 24.9 us
  local copies, waits for them, and re-layouts: 6.99 us -> 13.5 us
  waiting for transfers between devices: 98.2 us -> 103 us
    ppermute x33, starting transfers between devices: 56.6 us -> 38.2 us  [swap(): return lax.ppermute(array, axis, [(i, i ^ distance) for i in range(size)])]
    dot_general x12 -> x8, matrix products: 31.6 us -> 14.5 us  [dot(): lax.dot_general(left, right, (((left_dim,), (right_dim,)), ((), ())), pre...]
    pallas_call x0 -> x2, Pallas kernels: none -> 10.2 us  [halves_by_down(): pl.pallas_call(halves_kernel, grid=(width // tile,), out_shape=[out, out]...]
    ppermute x6, starting transfers between devices: 9.41 us -> 16.6 us  [trade(): lax.ppermute(array, 'ctx', [(2 * partner(i) + s, 2 * i + s) for i in rang...]
    unnamed x40 -> x64, local copies, waits for them, and re-layouts: 6.93 us -> 13.4 us
    ppermute x33, waiting for transfers between devices: 77.4 us -> 82.1 us  [swap(): return lax.ppermute(array, axis, [(i, i ^ distance) for i in range(size)])]
  transfers between devices with their start and end apart: 41 -> 41, of which waited for: 20 -> 21; matrix products, arithmetic and copies ran while one was open for 12% -> 9% of each run, Pallas kernels for 4% -> 8%
where the time goes in v4:
time: 225 us; the launch traced here: 223 us
  waiting for transfers between devices  103 us (46%)
  starting transfers between devices  57.4 us (26%)
  Pallas kernels  24.9 us (11%)
  matrix products  14.5 us (6%)
  local copies, waits for them, and re-layouts  13.5 us (6%)
  other arithmetic  9.02 us (4%)
    ppermute x33, waiting for transfers between devices, swap(): return lax.ppermute(array, axis, [(i, i ^ distance) for i in range(size)])  82.1 us
    ppermute x33, starting transfers between devices, swap(): return lax.ppermute(array, axis, [(i, i ^ distance) for i in range(size)])  38.2 us
    ppermute x6, starting transfers between devices, trade(): lax.ppermute(array, 'ctx', [(2 * partner(i) + s, 2 * i + s) for i in rang...  16.6 us
    pallas_call x7, Pallas kernels, call(): pl.pallas_call(kernel, out_shape=list(out_shapes), in_specs=[SMEM] * len(...  14.6 us
    dot_general x8, matrix products, dot(): lax.dot_general(left, right, (((left_dim,), (right_dim,)), ((), ())), pre...  14.5 us
    unnamed x64, local copies, waits for them, and re-layouts  13.4 us
    ppermute x2, waiting for transfers between devices, far_home(): return lax.ppermute(rows, ('ctx', 'exp'), moves)  11.1 us
    pallas_call x2, Pallas kernels, halves_by_down(): pl.pallas_call(halves_kernel, grid=(width // tile,), out_shape=[out, out]...  10.2 us
  transfers between devices with their start and end apart: 41, of which 21 were waited for; matrix products, arithmetic and copies ran while one was open for 9% of the time, Pallas kernels for 8%

profile of v4, /device:TPU:0, one launch (start us, length us, event | category | flops | bytes accessed | tf_op | source)
XLA Modules:
  0.0 223.4 jit_solution(1647239314807416665)
XLA Ops:
  4.3 3.0 %collective-permute-start = (bf16[6,128,128]{2,1,0:T(8,128)(2,1)S(1)}, bf16[6,128,128]{2,1,0:T(8,128)(2,1)S(1)}, u32[]{:S(2)}, u32[]{:S(2)}) collective-permute-start(bf16[6,128,128]{2,1,0:T(8,128)(2,1)S(1)} %get-tuple-element.52), channel_id=1, source_target_pairs={{0,4},{4,0},{8,12},{12,8},{16,20},{20,16},{24,28},{28,24},{1,5},{5... | collective-permute-start | bytes 589832 | tf_op jit(solution)/shard_map/ppermute | solution.py:243
  24.0 4.5 %collective-permute-done.2.own1 = bf16[72,1536]{1,0:T(8,128)(2,1)S(1)} collective-permute-done((bf16[72,1536]{1,0:T(8,128)(2,1)}, bf16[72,1536]{1,0:T(8,128)(2,1)S(1)}, u32[]{:S(2)}, u32[]{:S(2)}) %collective-permute-start.2) | collective-permute-done | bytes 221216 | tf_op jit(solution)/shard_map/ppermute | solution.py:243
  28.5 8.6 %collective-permute-done.3.own0 = bf16[72,1536]{1,0:T(8,128)(2,1)S(1)} collective-permute-done((bf16[72,1536]{1,0:T(8,128)(2,1)}, bf16[72,1536]{1,0:T(8,128)(2,1)S(1)}, u32[]{:S(2)}, u32[]{:S(2)}) %collective-permute-start.3) | collective-permute-done | bytes 221216 | tf_op jit(solution)/shard_map/ppermute | solution.py:243
  47.1 4.3 %collective-permute-done.8.other0 = bf16[72,1536]{1,0:T(8,128)(2,1)S(1)} collective-permute-done((bf16[72,1536]{1,0:T(8,128)(2,1)S(1)}, bf16[72,1536]{1,0:T(8,128)(2,1)S(1)}, u32[]{:S(2)}, u32[]{:S(2)}) %collective-permute-start.8) | collective-permute-done | bytes 221216 | tf_op jit(solution)/shard_map/ppermute | solution.py:243
  51.4 4.5 %collective-permute-done.9.other1 = bf16[72,1536]{1,0:T(8,128)(2,1)S(1)} collective-permute-done((bf16[72,1536]{1,0:T(8,128)(2,1)}, bf16[72,1536]{1,0:T(8,128)(2,1)S(1)}, u32[]{:S(2)}, u32[]{:S(2)}) %collective-permute-start.9) | collective-permute-done | bytes 221216 | tf_op jit(solution)/shard_map/ppermute | solution.py:243
  55.9 3.0 %copy-done = bf16[1,2304,1536]{2,1,0:T(8,128)(2,1)S(1)} copy-done((bf16[1,2304,1536]{2,1,0:T(8,128)(2,1)S(1)}, bf16[1,2304,1536]{2,1,0:T(8,128)(2,1)}, u32[]{:S(2)}) %copy-start) | copy-done | bytes 7077912
  59.8 5.2 %shard_map.115 = (bf16[144,2304]{1,0:T(8,128)(2,1)S(1)}, bf16[144,2304]{1,0:T(8,128)(2,1)S(1)}) custom-call(s32[3]{0:T(128)S(1)} %pad_add_fusion.place_ref, bf16[72,1536]{1,0:T(8,128)(2,1)S(1)} %copy-done.15, bf16[72,1536]{1,0:T(8,128)(2,1)} %collective-permute-done.4.own1, bf16[72,1536]{1,0:T(8,128)(2,1)S(1)} %collective-permute-done.8.other0, ...), custom_call_target="tpu_custom_call" | custom-call | flops 1 | bytes 1 | tf_op jit(solution)/shard_map/pallas_call | solution.py:229
  73.0 3.6 %collective-permute-done.25 = bf16[72,1536]{1,0:T(8,128)(2,1)S(1)} collective-permute-done((bf16[72,1536]{1,0:T(8,128)(2,1)}, bf16[72,1536]{1,0:T(8,128)(2,1)S(1)}, u32[]{:S(2)}, u32[]{:S(2)}) %collective-permute-start.25) | collective-permute-done | bytes 221216 | tf_op jit(solution)/shard_map/ppermute | solution.py:243
  76.6 6.4 %collective-permute-start.26 = (bf16[72,1536]{1,0:T(8,128)(2,1)}, bf16[72,1536]{1,0:T(8,128)(2,1)S(1)}, u32[]{:S(2)}, u32[]{:S(2)}) collective-permute-start(bf16[72,1536]{1,0:T(8,128)(2,1)} %copy-done.23), channel_id=1, source_target_pairs={{0,16},{4,20},{8,24},{12,28},{16,0},{20,4},{24,8},{28,12},{1,17},{... | collective-permute-start | bytes 663560 | tf_op jit(solution)/shard_map/ppermute | solution.py:243
  86.0 5.3 %collective-permute-done.14 = bf16[72,1536]{1,0:T(8,128)(2,1)S(1)} collective-permute-done((bf16[72,1536]{1,0:T(8,128)(2,1)S(1)}, bf16[72,1536]{1,0:T(8,128)(2,1)S(1)}, u32[]{:S(2)}, u32[]{:S(2)}) %collective-permute-start.14) | collective-permute-done | bytes 221216 | tf_op jit(solution)/shard_map/ppermute | solution.py:243
  96.1 3.0 %copy-done.1 = bf16[1,2304,1536]{2,1,0:T(8,128)(2,1)S(1)} copy-done((bf16[1,2304,1536]{2,1,0:T(8,128)(2,1)S(1)}, bf16[1,2304,1536]{2,1,0:T(8,128)(2,1)}, u32[]{:S(2)}) %copy-start.1) | copy-done | bytes 7077912
  99.1 5.0 %shard_map.117 = (bf16[144,2304]{1,0:T(8,128)(2,1)S(1)}, bf16[144,2304]{1,0:T(8,128)(2,1)S(1)}) custom-call(s32[3]{0:T(128)S(1)} %pad_add_fusion.place_ref, bf16[72,1536]{1,0:T(8,128)(2,1)S(1)} %copy-done.13, bf16[72,1536]{1,0:T(8,128)(2,1)S(1)} %copy-done.11, bf16[72,1536]{1,0:T(8,128)(2,1)S(1)} %collective-permute-done.15.other0, ...), custom_call_target="tpu_custom_call" | custom-call | flops 1 | bytes 1 | tf_op jit(solution)/shard_map/pallas_call | solution.py:229
  114.5 14.3 %collective-permute-done.19 = bf16[144,2304]{1,0:T(8,128)(2,1)S(1)} collective-permute-done((bf16[144,2304]{1,0:T(8,128)(2,1)S(1)}, bf16[144,2304]{1,0:T(8,128)(2,1)S(1)}, u32[]{:S(2)}, u32[]{:S(2)}) %collective-permute-start.19) | collective-permute-done | bytes 663584 | tf_op jit(solution)/shard_map/ppermute | solution.py:243
  135.4 4.5 %collective-permute-done.20 = bf16[72,1536]{1,0:T(8,128)(2,1)S(1)} collective-permute-done((bf16[72,1536]{1,0:T(8,128)(2,1)S(1)}, bf16[72,1536]{1,0:T(8,128)(2,1)S(1)}, u32[]{:S(2)}, u32[]{:S(2)}) %collective-permute-start.20) | collective-permute-done | bytes 221216 | tf_op jit(solution)/shard_map/ppermute | solution.py:243
  143.1 13.4 %collective-permute-done.30 = bf16[144,2304]{1,0:T(8,128)(2,1)S(1)} collective-permute-done((bf16[144,2304]{1,0:T(8,128)(2,1)S(1)}, bf16[144,2304]{1,0:T(8,128)(2,1)S(1)}, u32[]{:S(2)}, u32[]{:S(2)}) %collective-permute-start.30) | collective-permute-done | bytes 663584 | tf_op jit(solution)/shard_map/ppermute | solution.py:243
  162.2 5.5 %collective-permute-done.31 = bf16[72,1536]{1,0:T(8,128)(2,1)S(1)} collective-permute-done((bf16[72,1536]{1,0:T(8,128)(2,1)S(1)}, bf16[72,1536]{1,0:T(8,128)(2,1)S(1)}, u32[]{:S(2)}, u32[]{:S(2)}) %collective-permute-start.31) | collective-permute-done | bytes 221216 | tf_op jit(solution)/shard_map/ppermute | solution.py:243
  172.8 4.5 %collective-permute-done.34 = bf16[72,1536]{1,0:T(8,128)(2,1)S(1)} collective-permute-done((bf16[72,1536]{1,0:T(8,128)(2,1)S(1)}, bf16[72,1536]{1,0:T(8,128)(2,1)S(1)}, u32[]{:S(2)}, u32[]{:S(2)}) %collective-permute-start.34) | collective-permute-done | bytes 221216 | tf_op jit(solution)/shard_map/ppermute | solution.py:243
  178.0 11.1 %collective-permute-done.32.refs_2_ = bf16[72,1536]{1,0:T(8,128)(2,1)S(1)} collective-permute-done((bf16[72,1536]{1,0:T(8,128)(2,1)S(1)}, bf16[72,1536]{1,0:T(8,128)(2,1)S(1)}, u32[]{:S(2)}, u32[]{:S(2)}) %collective-permute-start.32) | collective-permute-done | bytes 221216 | tf_op jit(solution)/shard_map/ppermute | solution.py:441
  192.0 4.2 %collective-permute-done.36 = bf16[6,128,128]{2,1,0:T(8,128)(2,1)S(1)} collective-permute-done((bf16[6,128,128]{2,1,0:T(8,128)(2,1)S(1)}, bf16[6,128,128]{2,1,0:T(8,128)(2,1)S(1)}, u32[]{:S(2)}, u32[]{:S(2)}) %collective-permute-start.36) | collective-permute-done | bytes 196640 | tf_op jit(solution)/shard_map/ppermute | solution.py:243
  196.4 4.6 %collective-permute-start.37 = (bf16[6,128,128]{2,1,0:T(8,128)(2,1)S(1)}, bf16[6,128,128]{2,1,0:T(8,128)(2,1)S(1)}, u32[]{:S(2)}, u32[]{:S(2)}) collective-permute-start(bf16[6,128,128]{2,1,0:T(8,128)(2,1)S(1)} %fusion.51), channel_id=1, source_target_pairs={{8,0},{12,4},{0,8},{4,12},{24,16},{28,20},{16,24},{20,28},{9,1},{1... | collective-permute-start | bytes 589832 | tf_op jit(solution)/shard_map/ppermute | solution.py:247
  201.0 4.2 %collective-permute-done.37 = bf16[6,128,128]{2,1,0:T(8,128)(2,1)S(1)} collective-permute-done((bf16[6,128,128]{2,1,0:T(8,128)(2,1)S(1)}, bf16[6,128,128]{2,1,0:T(8,128)(2,1)S(1)}, u32[]{:S(2)}, u32[]{:S(2)}) %collective-permute-start.37) | collective-permute-done | bytes 196640 | tf_op jit(solution)/shard_map/ppermute | solution.py:247
  205.3 3.1 %collective-permute-start.38 = (bf16[6,128,128]{2,1,0:T(8,128)(2,1)S(1)}, bf16[6,128,128]{2,1,0:T(8,128)(2,1)S(1)}, u32[]{:S(2)}, u32[]{:S(2)}) collective-permute-start(bf16[6,128,128]{2,1,0:T(8,128)(2,1)S(1)} %add_convert_fusion.12), channel_id=1, source_target_pairs={{16,0},{20,4},{8,8},{12,12},{0,16},{4,20},{24,24},{28,28},{17,1},{... | collective-permute-start | bytes 589832 | tf_op jit(solution)/shard_map/ppermute | solution.py:247
  209.8 5.7 %collective-permute-done.38 = bf16[6,128,128]{2,1,0:T(8,128)(2,1)S(1)} collective-permute-done((bf16[6,128,128]{2,1,0:T(8,128)(2,1)S(1)}, bf16[6,128,128]{2,1,0:T(8,128)(2,1)S(1)}, u32[]{:S(2)}, u32[]{:S(2)}) %collective-permute-start.38) | collective-permute-done | bytes 196640 | tf_op jit(solution)/shard_map/ppermute | solution.py:247
  217.3 4.0 %shard_map.119 = (bf16[128,1536]{1,0:T(8,128)(2,1)}, f32[128,1536]{1,0:T(8,128)S(1)}, f32[128,1536]{1,0:T(8,128)S(1)}) custom-call(s32[3]{0:T(128)S(1)} %pad_add_fusion.place_ref, f32[12]{0:T(128)S(1)} %copy-done.19, bf16[128,1536]{1,0:T(8,128)(2,1)S(1)} %copy-done.6, bf16[128,1536]{1,0:T(8,128)(2,1)S(1)} %copy-done.3, bf16[128,1536]{1,0:T(8,128)(2,1)S(1)} %copy-done.5, ...), custom_call_target="tpu_custom_call" | custom-call | flops 1 | bytes 1 | tf_op jit(solution)/shard_map/pallas_call | solution.py:191
  (169 shorter events, 86.7 us)
Async XLA Ops:
  15.2 13.3 %collective-permute-start.2 = (bf16[72,1536]{1,0:T(8,128)(2,1)}, bf16[72,1536]{1,0:T(8,128)(2,1)S(1)}, u32[]{:S(2)}, u32[]{:S(2)}) collective-permute-start(bf16[72,1536]{1,0:T(8,128)(2,1)} %get-tuple-element.55), channel_id=1, source_target_pairs={{0,24},{4,28},{8,16},{12,20},{16,8},{20,12},{24,0},{28,4},{1,25},{... | collective-permute-start | bytes 663560 | tf_op jit(solution)/shard_map/ppermute | solution.py:243
  17.6 19.4 %collective-permute-start.3 = (bf16[72,1536]{1,0:T(8,128)(2,1)}, bf16[72,1536]{1,0:T(8,128)(2,1)S(1)}, u32[]{:S(2)}, u32[]{:S(2)}) collective-permute-start(bf16[72,1536]{1,0:T(8,128)(2,1)} %get-tuple-element.56), channel_id=1, source_target_pairs={{0,16},{4,20},{8,24},{12,28},{16,0},{20,4},{24,8},{28,12},{1,17},{... | collective-permute-start | bytes 663560 | tf_op jit(solution)/shard_map/ppermute | solution.py:243
  17.8 19.3 %collective-permute-start.4 = (bf16[72,1536]{1,0:T(8,128)(2,1)}, bf16[72,1536]{1,0:T(8,128)(2,1)}, u32[]{:S(2)}, u32[]{:S(2)}) collective-permute-start(bf16[72,1536]{1,0:T(8,128)(2,1)} %get-tuple-element.57), channel_id=1, source_target_pairs={{0,8},{4,12},{8,0},{12,4},{16,24},{20,28},{24,16},{28,20},{1,9},{5... | collective-permute-start | bytes 663560 | tf_op jit(solution)/shard_map/ppermute | solution.py:243
  43.6 12.3 %collective-permute-start.9 = (bf16[72,1536]{1,0:T(8,128)(2,1)}, bf16[72,1536]{1,0:T(8,128)(2,1)S(1)}, u32[]{:S(2)}, u32[]{:S(2)}) collective-permute-start(bf16[72,1536]{1,0:T(8,128)(2,1)} %collective-permute-done.4.own1), channel_id=1, source_target_pairs={{0,4},{4,0},{8,12},{12,8},{16,20},{20,16},{24,28},{28,24},{1,5},{5... | collective-permute-start | bytes 663560 | tf_op jit(solution)/shard_map/ppermute | solution.py:243
  46.4 18.7 %collective-permute-start.7 = (bf16[6,128,128]{2,1,0:T(8,128)(2,1)S(1)}, bf16[6,128,128]{2,1,0:T(8,128)(2,1)S(1)}, u32[]{:S(2)}, u32[]{:S(2)}) collective-permute-start(bf16[6,128,128]{2,1,0:T(8,128)(2,1)S(1)} %get-tuple-element.102), channel_id=1, source_target_pairs={{0,4},{4,0},{8,12},{12,8},{16,20},{20,16},{24,28},{28,24},{1,5},{5... | collective-permute-start | bytes 589832 | tf_op jit(solution)/shard_map/ppermute | solution.py:243
  69.9 13.0 %collective-permute-start.12 = (bf16[72,1536]{1,0:T(8,128)(2,1)}, bf16[72,1536]{1,0:T(8,128)(2,1)S(1)}, u32[]{:S(2)}, u32[]{:S(2)}) collective-permute-start(bf16[72,1536]{1,0:T(8,128)(2,1)} %get-tuple-element.70), channel_id=1, source_target_pairs={{0,8},{4,12},{8,0},{12,4},{16,24},{20,28},{24,16},{28,20},{1,9},{5... | collective-permute-start | bytes 663560 | tf_op jit(solution)/shard_map/ppermute | solution.py:243
  70.9 22.5 %collective-permute-start.10 = (bf16[144,2304]{1,0:T(8,128)(2,1)}, bf16[144,2304]{1,0:T(8,128)(2,1)S(1)}, u32[]{:S(2)}, u32[]{:S(2)}) collective-permute-start(bf16[144,2304]{1,0:T(8,128)(2,1)} %copy-done.22), channel_id=1, source_target_pairs={{0,1},{1,0},{2,3},{3,2},{4,5},{5,4},{6,7},{7,6},{8,9},{9,8},{10,11... | collective-permute-start | bytes 1990664 | tf_op jit(solution)/shard_map/ppermute | solution.py:243
  70.9 13.5 %collective-permute-start.13 = (bf16[72,1536]{1,0:T(8,128)(2,1)}, bf16[72,1536]{1,0:T(8,128)(2,1)S(1)}, u32[]{:S(2)}, u32[]{:S(2)}) collective-permute-start(bf16[72,1536]{1,0:T(8,128)(2,1)} %copy-done.9), channel_id=1, source_target_pairs={{0,4},{4,0},{8,12},{12,8},{16,20},{20,16},{24,28},{28,24},{1,5},{5... | collective-permute-start | bytes 663560 | tf_op jit(solution)/shard_map/ppermute | solution.py:243
  71.5 23.8 %collective-permute-start.15 = (bf16[72,1536]{1,0:T(8,128)(2,1)}, bf16[72,1536]{1,0:T(8,128)(2,1)S(1)}, u32[]{:S(2)}, u32[]{:S(2)}) collective-permute-start(bf16[72,1536]{1,0:T(8,128)(2,1)} %copy-done.12), channel_id=1, source_target_pairs={{0,4},{4,0},{8,12},{12,8},{16,20},{20,16},{24,28},{28,24},{1,5},{5... | collective-permute-start | bytes 663560 | tf_op jit(solution)/shard_map/ppermute | solution.py:243
  76.6 15.3 %collective-permute-start.26 = (bf16[72,1536]{1,0:T(8,128)(2,1)}, bf16[72,1536]{1,0:T(8,128)(2,1)S(1)}, u32[]{:S(2)}, u32[]{:S(2)}) collective-permute-start(bf16[72,1536]{1,0:T(8,128)(2,1)} %copy-done.23), channel_id=1, source_target_pairs={{0,16},{4,20},{8,24},{12,28},{16,0},{20,4},{24,8},{28,12},{1,17},{... | collective-permute-start | bytes 663560 | tf_op jit(solution)/shard_map/ppermute | solution.py:243
  84.5 11.6 %collective-permute-start.16 = (bf16[72,1536]{1,0:T(8,128)(2,1)}, bf16[72,1536]{1,0:T(8,128)(2,1)S(1)}, u32[]{:S(2)}, u32[]{:S(2)}) collective-permute-start(bf16[72,1536]{1,0:T(8,128)(2,1)} %copy-done.10), channel_id=1, source_target_pairs={{0,4},{4,0},{8,12},{12,8},{16,20},{20,16},{24,28},{28,24},{1,5},{5... | collective-permute-start | bytes 663560 | tf_op jit(solution)/shard_map/ppermute | solution.py:243
  91.3 16.5 %collective-permute-start.28 = (bf16[72,1536]{1,0:T(8,128)(2,1)S(1)}, bf16[72,1536]{1,0:T(8,128)(2,1)S(1)}, u32[]{:S(2)}, u32[]{:S(2)}) collective-permute-start(bf16[72,1536]{1,0:T(8,128)(2,1)S(1)} %collective-permute-done.25), channel_id=1, source_target_pairs={{0,4},{4,0},{8,12},{12,8},{16,20},{20,16},{24,28},{28,24},{1,5},{5... | collective-permute-start | bytes 663560 | tf_op jit(solution)/shard_map/ppermute | solution.py:243
  91.9 16.0 %collective-permute-start.27 = (bf16[72,1536]{1,0:T(8,128)(2,1)S(1)}, bf16[72,1536]{1,0:T(8,128)(2,1)S(1)}, u32[]{:S(2)}, u32[]{:S(2)}) collective-permute-start(bf16[72,1536]{1,0:T(8,128)(2,1)S(1)} %collective-permute-done.26), channel_id=1, source_target_pairs={{0,4},{4,0},{8,12},{12,8},{16,20},{20,16},{24,28},{28,24},{1,5},{5... | collective-permute-start | bytes 663560 | tf_op jit(solution)/shard_map/ppermute | solution.py:243
  93.6 11.2 %collective-permute-start.11 = (bf16[144,2304]{1,0:T(8,128)(2,1)S(1)}, bf16[144,2304]{1,0:T(8,128)(2,1)S(1)}, u32[]{:S(2)}, u32[]{:S(2)}) collective-permute-start(bf16[144,2304]{1,0:T(8,128)(2,1)S(1)} %add_convert_fusion.7), channel_id=1, source_target_pairs={{0,2},{1,3},{2,0},{3,1},{4,6},{5,7},{6,4},{7,5},{8,10},{9,11},{10,... | collective-permute-start | bytes 1990664 | tf_op jit(solution)/shard_map/ppermute | solution.py:243
  111.0 17.8 %collective-permute-start.19 = (bf16[144,2304]{1,0:T(8,128)(2,1)S(1)}, bf16[144,2304]{1,0:T(8,128)(2,1)S(1)}, u32[]{:S(2)}, u32[]{:S(2)}) collective-permute-start(bf16[144,2304]{1,0:T(8,128)(2,1)S(1)} %add_convert_fusion.4), channel_id=1, source_target_pairs={{0,2},{1,3},{2,0},{3,1},{4,6},{5,7},{6,4},{7,5},{8,10},{9,11},{10,... | collective-permute-start | bytes 1990664 | tf_op jit(solution)/shard_map/ppermute | solution.py:243
  112.6 30.4 %collective-permute-start.24 = (bf16[144,2304]{1,0:T(8,128)(2,1)S(1)}, bf16[144,2304]{1,0:T(8,128)(2,1)S(1)}, u32[]{:S(2)}, u32[]{:S(2)}) collective-permute-start(bf16[144,2304]{1,0:T(8,128)(2,1)S(1)} %add_convert_fusion.5), channel_id=1, source_target_pairs={{0,2},{1,3},{2,0},{3,1},{4,6},{5,7},{6,4},{7,5},{8,10},{9,11},{10,... | collective-permute-start | bytes 1990664 | tf_op jit(solution)/shard_map/ppermute | solution.py:243
  114.4 18.1 %collective-permute-start.29 = (bf16[144,2304]{1,0:T(8,128)(2,1)S(1)}, bf16[144,2304]{1,0:T(8,128)(2,1)S(1)}, u32[]{:S(2)}, u32[]{:S(2)}) collective-permute-start(bf16[144,2304]{1,0:T(8,128)(2,1)S(1)} %fusion.19), channel_id=1, source_target_pairs={{0,1},{1,0},{2,3},{3,2},{4,5},{5,4},{6,7},{7,6},{8,9},{9,8},{10,11... | collective-permute-start | bytes 1990664 | tf_op jit(solution)/shard_map/ppermute | solution.py:243
  129.4 10.5 %collective-permute-start.21 = (bf16[144,2304]{1,0:T(8,128)(2,1)S(1)}, bf16[144,2304]{1,0:T(8,128)(2,1)S(1)}, u32[]{:S(2)}, u32[]{:S(2)}) collective-permute-start(bf16[144,2304]{1,0:T(8,128)(2,1)S(1)} %fusion.40), channel_id=1, source_target_pairs={{0,1},{1,0},{2,3},{3,2},{4,5},{5,4},{6,7},{7,6},{8,9},{9,8},{10,11... | collective-permute-start | bytes 1990664 | tf_op jit(solution)/shard_map/ppermute | solution.py:243
  133.8 22.7 %collective-permute-start.30 = (bf16[144,2304]{1,0:T(8,128)(2,1)S(1)}, bf16[144,2304]{1,0:T(8,128)(2,1)S(1)}, u32[]{:S(2)}, u32[]{:S(2)}) collective-permute-start(bf16[144,2304]{1,0:T(8,128)(2,1)S(1)} %add_convert_fusion.1), channel_id=1, source_target_pairs={{0,2},{1,3},{2,0},{3,1},{4,6},{5,7},{6,4},{7,5},{8,10},{9,11},{10,... | collective-permute-start | bytes 1990664 | tf_op jit(solution)/shard_map/ppermute | solution.py:243
  142.4 14.8 %collective-permute-start.22 = (bf16[72,1536]{1,0:T(8,128)(2,1)S(1)}, bf16[72,1536]{1,0:T(8,128)(2,1)S(1)}, u32[]{:S(2)}, u32[]{:S(2)}) collective-permute-start(bf16[72,1536]{1,0:T(8,128)(2,1)S(1)} %slice.43), channel_id=1, source_target_pairs={{0,4},{4,0},{8,12},{12,8},{16,20},{20,16},{24,28},{28,24},{1,5},{5... | collective-permute-start | bytes 663560 | tf_op jit(solution)/shard_map/ppermute | solution.py:243
  157.3 10.4 %collective-permute-start.33 = (bf16[144,2304]{1,0:T(8,128)(2,1)S(1)}, bf16[144,2304]{1,0:T(8,128)(2,1)S(1)}, u32[]{:S(2)}, u32[]{:S(2)}) collective-permute-start(bf16[144,2304]{1,0:T(8,128)(2,1)S(1)} %fusion.47), channel_id=1, source_target_pairs={{0,1},{1,0},{2,3},{3,2},{4,5},{5,4},{6,7},{7,6},{8,9},{9,8},{10,11... | collective-permute-start | bytes 1990664 | tf_op jit(solution)/shard_map/ppermute | solution.py:243
  160.4 17.6 %collective-permute-start.23 = (bf16[72,1536]{1,0:T(8,128)(2,1)S(1)}, bf16[72,1536]{1,0:T(8,128)(2,1)S(1)}, u32[]{:S(2)}, u32[]{:S(2)}) collective-permute-start(bf16[72,1536]{1,0:T(8,128)(2,1)S(1)} %get-tuple-element.103), channel_id=1, source_target_pairs={{0,8},{4,12},{8,0},{12,4},{16,24},{20,28},{24,16},{28,20},{1,9},{5... | collective-permute-start | bytes 663560 | tf_op jit(solution)/shard_map/ppermute | solution.py:243
  170.8 18.2 %collective-permute-start.32 = (bf16[72,1536]{1,0:T(8,128)(2,1)S(1)}, bf16[72,1536]{1,0:T(8,128)(2,1)S(1)}, u32[]{:S(2)}, u32[]{:S(2)}) collective-permute-start(bf16[72,1536]{1,0:T(8,128)(2,1)S(1)} %add_convert_fusion.9), channel_id=1, source_target_pairs={{0,16},{1,25},{2,18},{3,27},{4,20},{5,29},{6,22},{7,31},{8,24},{9,... | collective-permute-start | bytes 663560 | tf_op jit(solution)/shard_map/ppermute | solution.py:441
  177.4 11.7 %collective-permute-start.35 = (bf16[72,1536]{1,0:T(8,128)(2,1)S(1)}, bf16[72,1536]{1,0:T(8,128)(2,1)S(1)}, u32[]{:S(2)}, u32[]{:S(2)}) collective-permute-start(bf16[72,1536]{1,0:T(8,128)(2,1)S(1)} %add_convert_fusion.8), channel_id=1, source_target_pairs={{0,24},{1,17},{2,26},{3,19},{4,28},{5,21},{6,30},{7,23},{8,16},{9,... | collective-permute-start | bytes 663560 | tf_op jit(solution)/shard_map/ppermute | solution.py:441
  (49 other events, 462.7 us)

commit v5 on v4

--- a/solution.py
+++ b/solution.py
@@ -14,6 +14,7 @@
 
 SMEM = pl.BlockSpec(memory_space=pltpu.SMEM)
 VMEM = pl.BlockSpec(memory_space=pltpu.VMEM)
+LARGE = pl.CostEstimate(flops=1, bytes_accessed=40_000_000, transcendentals=0)
 SMALL = pl.CostEstimate(flops=1, bytes_accessed=1, transcendentals=0)
 
 
@@ -68,7 +69,7 @@
 
 
 def route_kernel(
-    order, place_ref, routes_ref, gates_ref, grad_ref, choose_ref, weigh_ref, *send_refs
+    place_ref, routes_ref, gates_ref, grad_ref, choose_ref, weigh_ref, *send_refs
 ):
     experts, capacity, block_len = choose_ref.shape
     rows = lax.broadcasted_iota(jnp.int32, (block_len, block_len), 0)
@@ -100,11 +101,11 @@
         columns[:, i : i + 1].astype(jnp.int32) for i in range(4)
     ]
     slots = lax.broadcasted_iota(jnp.int32, (block_len, capacity), 1)
-    for position, (even, odd) in enumerate(order):
-        expert = place_ref[1] ^ jnp.where(place_ref[2] == 0, even, odd)
+    for k in range(experts):
+        expert = place_ref[1] ^ k
         one = jnp.where((slots == slot_first) & (first == expert), columns[:, 4:5], 0.0)
         two = jnp.where((slots == slot_second) & (second == expert), columns[:, 5:6], 0.0)
-        weigh_ref[position] = (one + two).astype(BF16)
+        weigh_ref[k] = (one + two).astype(BF16)
 
 
 def intra_kernel(place_ref, rates_ref, q_ref, k_ref, v_ref, intra_ref, weights_ref):
@@ -187,7 +188,7 @@
         ).astype(BF16)
 
 
-def call(kernel, out_shapes, scalars, arrays, scratch=()):
+def call(kernel, out_shapes, scalars, arrays, scratch=(), cost=SMALL):
     return pl.pallas_call(
         kernel,
         out_shape=list(out_shapes),
@@ -195,47 +196,8 @@
         out_specs=[VMEM] * len(out_shapes),
         scratch_shapes=list(scratch),
         compiler_params=pltpu.CompilerParams(vmem_limit_bytes=16 * 1024 * 1024),
-        cost_estimate=SMALL,
+        cost_estimate=cost,
     )(*scalars, *arrays)
-
-
-def halves_kernel(place_ref, own0, own1, other0, other1, weight_ref, sent_ref, kept_ref, rows_ref):
-    count = sent_ref.shape[0]
-
-    @pl.when(pl.program_id(0) == 0)
-    def _():
-        even = jnp.concatenate([own0[...].astype(F32), other0[...].astype(F32)], axis=0)
-        odd = jnp.concatenate([own1[...].astype(F32), other1[...].astype(F32)], axis=0)
-        first = place_ref[2] == 0
-        rows_ref[:count] = jnp.where(first, odd, even).astype(BF16)
-        rows_ref[count:] = jnp.where(first, even, odd).astype(BF16)
-
-    out = dot(rows_ref[...], weight_ref[...], 1, 1).astype(BF16)
-    sent_ref[...] = out[:count]
-    kept_ref[...] = out[count:]
-
-
-def halves_by_down(place, own, other, part, weight, tile=384):
-    count = len(part) // 2
-    join = lambda side, first: (
-        side[part[first]] if count == 1
-        else jnp.concatenate([side[part[first + i]] for i in range(count)], axis=0)
-    )
-    blocks = [join(own, 0), join(own, count), join(other, 0), join(other, count)]
-    rows, depth = blocks[0].shape
-    width = weight.shape[0]
-    whole = pl.BlockSpec((rows, depth), lambda j: (0, 0))
-    out = jax.ShapeDtypeStruct((2 * rows, width), BF16)
-    return pl.pallas_call(
-        halves_kernel,
-        grid=(width // tile,),
-        out_shape=[out, out],
-        in_specs=[SMEM] + [whole] * 4 + [pl.BlockSpec((tile, depth), lambda j: (j, 0))],
-        out_specs=[pl.BlockSpec((2 * rows, tile), lambda j: (0, j))] * 2,
-        scratch_shapes=[pltpu.VMEM((4 * rows, depth), BF16)],
-        compiler_params=pltpu.CompilerParams(vmem_limit_bytes=16 * 1024 * 1024),
-        cost_estimate=SMALL,
-    )(place, *blocks, weight)
 
 
 def swap(array, axis, distance):
@@ -306,22 +268,18 @@
     return keep, give
 
 
-def split_rows(own, other, part, flag):
-    count = len(part) // 2
-    blocks = [
-        jnp.where(flag == 0, side[part[i]], side[part[count + i]])
-        for side in (own, other)
-        for i in range(count)
-    ]
-    return jnp.concatenate(blocks, axis=0)
-
-
 def sum_over_cores(own, other, part, multiply, *events):
     mine = lax.axis_index("exp") & 1
-    sent = multiply(after(split_rows(own, other, part, 1 - mine), *events)).astype(BF16)
-    got = swap(sent, "exp", 1)
-    kept = multiply(after(split_rows(own, other, part, mine), sent))
-    return (kept + got.astype(F32)).astype(BF16)
+    rows = lambda flag: jnp.concatenate(
+        [jnp.where(flag == 0, own[k], other[k]) for k in part], axis=0
+    )
+    sent = multiply(after(rows(1 - mine), *events)).astype(BF16)
+    kept = multiply(after(rows(mine), sent)).astype(BF16)
+    return sent, kept
+
+
+def over_cores(sent, kept):
+    return (kept.astype(F32) + swap(sent, "exp", 1).astype(F32)).astype(BF16)
 
 
 def sum_over_rest(part, bits):
@@ -344,12 +302,10 @@
     place = jnp.stack([position & 1, position >> 1, core])
     scalars = (place, decay_rates)
     up_local, down_local = up_weight[0], down_weight[0]
-    near_part, far_part = range(experts // 2), range(experts // 2, experts)
-    quarter = experts // 4
-    order = [(k, k) for k in near_part]
-    order += [(far_part[i], far_part[quarter + i]) for i in range(quarter)]
-    order += [(far_part[quarter + i], far_part[i]) for i in range(quarter)]
-
+    quarter = max(experts // 4, 1)
+    near_part = range(experts // 2)
+    first_far = range(experts - quarter, experts)
+    second_far = range(experts // 2, experts - quarter)
     states = jax.ShapeDtypeStruct((half, DH, DH), BF16)
     weight_sq = jax.ShapeDtypeStruct((heads, block_len, block_len), BF16)
     wide = jax.ShapeDtypeStruct((block_len, group), F32)
@@ -363,94 +319,84 @@
 
     key_mine, key_other = call(key_state_kernel, [states] * 2, scalars, (keys, values))
     choose, weigh, *send_grad = call(
-        functools.partial(route_kernel, order), [choose_table, weigh_table] + [slots] * experts,
+        route_kernel, [choose_table, weigh_table] + [slots] * experts,
         (place,), (routes.T, gate_weights.T, out_grad)
     )
-    intra, weights = call(intra_kernel, [wide, weight_sq], scalars, (queries, keys, values))
-
-    grad_own = {k: pairs_of(send_grad[k], k) for k in reversed(range(experts))}
+    intra, weights = call(
+        intra_kernel, [wide, weight_sq], scalars, (queries, keys, values), cost=LARGE
+    )
+
     total, partner = scan_total(
         key_mine, key_other, decay_rates, place, block_len, False, send_grad[0]
     )
+    grad_own = {0: send_grad[0]}
+    for k in [*near_part[1:], *first_far]:
+        grad_own[k] = pairs_of(after(send_grad[k], total), k)
     before = None
     for index, reach in enumerate(reaches):
-        events = list(grad_own.values()) + [intra] if index == 1 else []
+        events = [intra] if index == 1 else []
         before, upto = scan_step(
             before, total, reach, decay_rates, place, block_len, False, *events
         )
-    grad_other = {k: swap(after(grad_own[k], upto if k else total), "ctx", 1) for k in near_part}
     keep, give = scan_ends(before, key_mine, partner, decay_rates, place, block_len, False)
-    entering = [keep, swap(give, "ctx", 1)]
-
-    def over_cores(sent, kept):
-        return (kept.astype(F32) + swap(sent, "exp", 1).astype(F32)).astype(BF16)
-
-    grad_own[0] = after(grad_own[0], give)
-    near_halves = halves_by_down(place, grad_own, grad_other, near_part, down_local)
-    entering[1], *near_halves = lax.optimization_barrier((entering[1], *near_halves))
-    for k in far_part:
-        grad_other[k] = swap(after(grad_own[k], entering[1]), "ctx", 1)
-    entering = tuple(entering)
+    grad_other = {0: swap(after(grad_own[0], total), "ctx", 1)}
+    for k in [*near_part[1:], *first_far]:
+        grad_other[k] = swap(after(grad_own[k], upto), "ctx", 1)
+    for k in second_far:
+        grad_own[k] = pairs_of(after(send_grad[k], give), k)
+
+    by_down = lambda rows: dot(rows, down_local, 1, 1)
+    by_up = lambda rows: dot(rows, up_local, 1, 0)
+    given = swap(give, "ctx", 1)
+    hidden_near = over_cores(*sum_over_cores(grad_own, grad_other, near_part, by_down, give))
+    given, hidden_near = lax.optimization_barrier((given, hidden_near))
     send_in = call(
-        attend_kernel, [slots] * experts, scalars, (queries, intra, choose) + entering,
+        attend_kernel, [slots] * experts, scalars, (queries, intra, choose, keep, given),
         [pltpu.VMEM((block_len, group), BF16)],
     )
-    hidden_near = over_cores(*near_halves)
-    grad_own[far_part[0]] = after(grad_own[far_part[0]], send_in[0], hidden_near)
-    hidden_far = over_cores(*halves_by_down(place, grad_own, grad_other, far_part, down_local))
+    for k in second_far:
+        grad_other[k] = swap(after(grad_own[k], send_in[0]), "ctx", 1)
+    hidden_first = over_cores(
+        *sum_over_cores(grad_own, grad_other, first_far, by_down, send_in[0])
+    )
+
     in_own, in_other = {0: send_in[0]}, {}
-    for k in [experts - 1, *near_part[1:]]:
+    for k in [*near_part[1:], *first_far]:
         in_own[k] = pairs_of(send_in[k], k)
-    for k in far_part[:-1]:
-        in_own[k] = pairs_of(after(send_in[k], in_own[experts - 1]), k)
+    for k in second_far:
+        in_own[k] = pairs_of(after(send_in[k], in_own[first_far[0]], hidden_first), k)
     for k in range(experts):
         in_other[k] = swap(in_own[k], "ctx", 1)
 
-    by_up = lambda rows: dot(rows, up_local, 1, 0)
-    hidden_near = sum_over_rest(hidden_near, bits)
-    pre_near = sum_over_cores(in_own, in_other, near_part, by_up, hidden_near, hidden_far)
-    hidden_far = sum_over_rest(hidden_far, bits)
-    pre_far = sum_over_cores(in_own, in_other, far_part, by_up, pre_near)
-    pre_near, pre_far = sum_over_rest(pre_near, bits), sum_over_rest(pre_far, bits)
-
-    def returned(pre, hidden, *events):
+    pre_near = over_cores(*sum_over_cores(in_own, in_other, near_part, by_up, hidden_first))
+    pre_first = over_cores(*sum_over_cores(in_own, in_other, first_far, by_up, pre_near))
+    hidden_second = over_cores(
+        *sum_over_cores(grad_own, grad_other, second_far, by_down, pre_first)
+    )
+    pre_second = over_cores(*sum_over_cores(in_own, in_other, second_far, by_up, hidden_second))
+
+    homes = {}
+    back = None
+    for part, pre, hidden in (
+        (near_part, pre_near, hidden_near),
+        (first_far, pre_first, hidden_first),
+        (second_far, pre_second, hidden_second),
+    ):
+        pre, hidden = sum_over_rest(pre, bits), sum_over_rest(hidden, bits)
         slope = (hidden.astype(F32) * silu_slope(pre.astype(F32))).astype(BF16)
-        slope = after(slope, *events)
-        slopes = (slope, swap(slope, "exp", 1))
-        summed = []
-        for slope in slopes:
-            back = dot(after(slope, *events), up_local, 1, 1).astype(BF16)
-            back = back.reshape(2, quarter * capacity, group)
-            got = swap(back[1], "ctx", 1)
-            events = events + (back,)
-            summed.append((back[0], got))
-        return summed
-
-    def joined(item, *events):
-        kept, got = item
-        rows = (kept.astype(F32) + after(got, *events).astype(F32)).astype(BF16)
-        return rows, [rows[i * capacity : (i + 1) * capacity] for i in range(quarter)]
-
-    def far_home(rows, kept, i):
-        moves = []
-        size = lax.axis_size("exp")
-        for c in range(2 * experts):
-            for e in range(size):
-                k = far_part[((e & 1) ^ (0 if kept else 1)) * quarter + i]
-                moves.append((c * size + e, (c ^ (2 * k)) * size + e))
-        return lax.ppermute(rows, ("ctx", "exp"), moves)
-
-    near_items = returned(pre_near, hidden_near)
-    far_items = returned(pre_far, hidden_far, near_items[0][0], near_items[1][0])
-    first, near_first = joined(near_items[0])
-    second, near_second = joined(near_items[1], first)
-    homes = [jnp.where(core == 0, a, b) for a, b in zip(near_first, near_second)]
-    homes += [jnp.where(core == 0, b, a) for a, b in zip(near_first, near_second)]
-    homes = [pairs_of(rows, k) for k, rows in enumerate(homes)]
-    first, far_first = joined(far_items[0])
-    second, far_second = joined(far_items[1], first)
-    homes += [far_home(rows, True, i) for i, rows in enumerate(far_first)]
-    homes += [far_home(rows, False, i) for i, rows in enumerate(far_second)]
+        got = swap(slope, "exp", 1)
+        if back is not None:
+            got = after(got, back)
+        slope = jnp.concatenate(
+            [jnp.where(core == 0, slope, got), jnp.where(core == 0, got, slope)], axis=0
+        )
+        back = dot(slope, up_local, 1, 1).astype(BF16)
+        blocks = back.reshape(2, len(part) * capacity, group)
+        got = swap(blocks[1], "ctx", 1)
+        rows = (blocks[0].astype(F32) + got.astype(F32)).astype(BF16)
+        for i, k in enumerate(part):
+            homes[k] = pairs_of(rows[i * capacity : (i + 1) * capacity], k)
+    homes = [homes[k] for k in range(experts)]
 
     grad_out, query_mine, query_other = call(
         grad_kernel, [slim, states, states], scalars, (queries, out_grad, weigh, *homes)
@@ -461,11 +407,12 @@
     before = None
     for reach in reaches:
         before, _ = scan_step(before, total, reach, decay_rates, place, block_len, True)
+    keep_in = keep
     keep, give = scan_ends(before, query_mine, partner, decay_rates, place, block_len, True)
     leaving = (keep, swap(give, "ctx", 1))
     query_g, key_near, value_near = call(
         near_kernel, [slim, wide, wide], scalars,
-        (queries, keys, values, grad_out) + entering + (weights,)
+        (queries, keys, values, grad_out, keep_in, given, weights)
     )
     key_g, value_g = call(
         far_kernel, [slim, slim], scalars,

time: 225 us -> 196 us (0.87)
  waiting for transfers between devices: 103 us -> 82.1 us
  matrix products: 14.5 us -> 32.3 us
  Pallas kernels: 24.9 us -> 13.2 us
  local copies, waits for them, and re-layouts: 13.5 us -> 8.14 us
  other arithmetic: 9.02 us -> 4.42 us
  starting transfers between devices: 57.4 us -> 54.4 us
    dot_general x8 -> x15, matrix products: 14.5 us -> 32.3 us  [dot(): lax.dot_general(left, right, (((left_dim,), (right_dim,)), ((), ())), pre...]
    ppermute x2 -> x0, waiting for transfers between devices: 11.1 us -> none  [far_home(): return lax.ppermute(rows, ('ctx', 'exp'), moves)]
    ppermute x33 -> x39, waiting for transfers between devices: 82.1 us -> 71 us  [swap(): return lax.ppermute(array, axis, [(i, i ^ distance) for i in range(size)])]
    pallas_call x2 -> x0, Pallas kernels: 10.2 us -> none  [halves_by_down(): pl.pallas_call(halves_kernel, grid=(width // tile,), out_shape=[out, out]...]
    ppermute x6, starting transfers between devices: 16.6 us -> 9.3 us  [trade(): lax.ppermute(array, 'ctx', [(2 * partner(i) + s, 2 * i + s) for i in rang...]
    ppermute x33 -> x39, starting transfers between devices: 38.2 us -> 45.1 us  [swap(): return lax.ppermute(array, axis, [(i, i ^ distance) for i in range(size)])]
    unnamed x64 -> x36, local copies, waits for them, and re-layouts: 13.4 us -> 8.05 us
    ppermute x2 -> x0, starting transfers between devices: 2.55 us -> none  [far_home(): return lax.ppermute(rows, ('ctx', 'exp'), moves)]
  transfers between devices with their start and end apart: 41 -> 45, of which waited for: 21 -> 22; matrix products, arithmetic and copies ran while one was open for 9% -> 18% of each run, Pallas kernels for 8% -> 5%
where the time goes in v5:
time: 196 us
  waiting for transfers between devices  82.1 us (42%)
  starting transfers between devices  54.4 us (28%)
  matrix products  32.3 us (16%)
  Pallas kernels  13.2 us (7%)
  local copies, waits for them, and re-layouts  8.14 us (4%)
  other arithmetic  4.42 us (2%)
    ppermute x39, waiting for transfers between devices, swap(): return lax.ppermute(array, axis, [(i, i ^ distance) for i in range(size)])  71 us
    ppermute x39, starting transfers between devices, swap(): return lax.ppermute(array, axis, [(i, i ^ distance) for i in range(size)])  45.1 us
    dot_general x15, matrix products, dot(): lax.dot_general(left, right, (((left_dim,), (right_dim,)), ((), ())), pre...  32.3 us
    pallas_call x7, Pallas kernels, call(): pl.pallas_call(kernel, out_shape=list(out_shapes), in_specs=[SMEM] * len(...  13.2 us
    ppermute x6, waiting for transfers between devices, trade(): lax.ppermute(array, 'ctx', [(2 * partner(i) + s, 2 * i + s) for i in rang...  11.1 us
    ppermute x6, starting transfers between devices, trade(): lax.ppermute(array, 'ctx', [(2 * partner(i) + s, 2 * i + s) for i in rang...  9.3 us
    unnamed x36, local copies, waits for them, and re-layouts  8.05 us
  transfers between devices with their start and end apart: 45, of which 22 were waited for; matrix products, arithmetic and copies ran while one was open for 18% of the time, Pallas kernels for 5%

profile of v5, /device:TPU:0, one launch (start us, length us, event | category | flops | bytes accessed | tf_op | source)
XLA Modules:
  0.0 195.9 jit_solution(8912604919247712741)
XLA Ops:
  4.3 3.0 %collective-permute-start = (bf16[6,128,128]{2,1,0:T(8,128)(2,1)S(1)}, bf16[6,128,128]{2,1,0:T(8,128)(2,1)S(1)}, u32[]{:S(2)}, u32[]{:S(2)}) collective-permute-start(bf16[6,128,128]{2,1,0:T(8,128)(2,1)S(1)} %get-tuple-element.53), channel_id=1, source_target_pairs={{0,4},{4,0},{8,12},{12,8},{16,20},{20,16},{24,28},{28,24},{1,5},{5... | collective-permute-start | bytes 589832 | tf_op jit(solution)/shard_map/ppermute | solution.py:205
  17.2 2.5 %shard_map.114 = (f32[128,1536]{1,0:T(8,128)S(1)}, bf16[12,128,128]{2,1,0:T(8,128)(2,1)S(1)}) custom-call(s32[3]{0:T(128)S(1)} %pad_add_fusion.place_ref, f32[12]{0:T(128)S(1)} %copy-done.10, bf16[128,1536]{1,0:T(8,128)(2,1)S(1)} %copy-done.6, bf16[128,1536]{1,0:T(8,128)(2,1)S(1)} %copy-done.1, bf16[128,1536]{1,0:T(8,128)(2,1)S(1)} %copy-done.4), custom_call_target="tpu_custom_call" | custom-call | flops 1 | bytes 40000000 | tf_op jit(solution)/shard_map/pallas_call | solution.py:192
  21.8 3.6 %collective-permute-start.13 = (bf16[72,1536]{1,0:T(8,128)(2,1)S(1)}, bf16[72,1536]{1,0:T(8,128)(2,1)S(1)}, u32[]{:S(2)}, u32[]{:S(2)}) collective-permute-start(bf16[72,1536]{1,0:T(8,128)(2,1)S(1)} %get-tuple-element.70), channel_id=1, source_target_pairs={{0,24},{4,28},{8,16},{12,20},{16,8},{20,12},{24,0},{28,4},{1,25},{... | collective-permute-start | bytes 663560 | tf_op jit(solution)/shard_map/ppermute | solution.py:205
  27.3 8.6 %collective-permute-done.13 = bf16[72,1536]{1,0:T(8,128)(2,1)S(1)} collective-permute-done((bf16[72,1536]{1,0:T(8,128)(2,1)S(1)}, bf16[72,1536]{1,0:T(8,128)(2,1)S(1)}, u32[]{:S(2)}, u32[]{:S(2)}) %collective-permute-start.13) | collective-permute-done | bytes 221216 | tf_op jit(solution)/shard_map/ppermute | solution.py:205
  38.9 3.7 %collective-permute-start.21 = (bf16[72,1536]{1,0:T(8,128)(2,1)S(1)}, bf16[72,1536]{1,0:T(8,128)(2,1)S(1)}, u32[]{:S(2)}, u32[]{:S(2)}) collective-permute-start(bf16[72,1536]{1,0:T(8,128)(2,1)S(1)} %get-tuple-element.77), channel_id=1, source_target_pairs={{0,16},{4,20},{8,24},{12,28},{16,0},{20,4},{24,8},{28,12},{1,17},{... | collective-permute-start | bytes 663560 | tf_op jit(solution)/shard_map/ppermute | solution.py:205
  42.9 5.6 %fusion.30 = bf16[144,2304]{1,0:T(8,128)(2,1)S(1)} fusion(bf16[144,1536]{1,0:T(8,128)(2,1)S(1)} %pad_maximum_fusion.1, bf16[1,2304,1536]{2,1,0:T(8,128)(2,1)} %param.14), kind=kOutput, calls=%fused_computation.30 | convolution fusion | flops 1019547648 | bytes 8183808 | tf_op jit(solution)/shard_map/dot_general | solution.py:22
  50.7 2.4 %add_convert_fusion.3 = bf16[144,2304]{1,0:T(8,128)(2,1)S(1)} fusion(bf16[144,2304]{1,0:T(8,128)(2,1)S(1)} %collective-permute-done.8, bf16[144,1536]{1,0:T(8,128)(2,1)S(1)} %pad_maximum_fusion, bf16[1,2304,1536]{2,1,0:T(8,128)(2,1)S(1)} %bitcast.116), kind=kOutput, calls=%fused_computation.74 | convolution fusion | flops 1020874752 | bytes 8847360 | tf_op jit(solution)/shard_map/dot_general | solution.py:22
  56.3 4.0 %collective-permute-start.11 = (bf16[72,1536]{1,0:T(8,128)(2,1)S(1)}, bf16[72,1536]{1,0:T(8,128)(2,1)S(1)}, u32[]{:S(2)}, u32[]{:S(2)}) collective-permute-start(bf16[72,1536]{1,0:T(8,128)(2,1)S(1)} %get-tuple-element.68), channel_id=1, source_target_pairs={{0,8},{4,12},{8,0},{12,4},{16,24},{20,28},{24,16},{28,20},{1,9},{5... | collective-permute-start | bytes 663560 | tf_op jit(solution)/shard_map/ppermute | solution.py:205
  68.2 2.5 %collective-permute-done.23 = bf16[72,1536]{1,0:T(8,128)(2,1)S(1)} collective-permute-done((bf16[72,1536]{1,0:T(8,128)(2,1)S(1)}, bf16[72,1536]{1,0:T(8,128)(2,1)S(1)}, u32[]{:S(2)}, u32[]{:S(2)}) %collective-permute-start.23) | collective-permute-done | bytes 221216 | tf_op jit(solution)/shard_map/ppermute | solution.py:205
  75.6 3.5 %collective-permute-done.12 = bf16[72,1536]{1,0:T(8,128)(2,1)S(1)} collective-permute-done((bf16[72,1536]{1,0:T(8,128)(2,1)S(1)}, bf16[72,1536]{1,0:T(8,128)(2,1)S(1)}, u32[]{:S(2)}, u32[]{:S(2)}) %collective-permute-start.12) | collective-permute-done | bytes 221216 | tf_op jit(solution)/shard_map/ppermute | solution.py:205
  96.6 2.5 %fusion.75 = bf16[72,2304]{1,0:T(8,128)(2,1)S(1)} fusion(bf16[72,1536]{1,0:T(8,128)(2,1)S(1)} %get-tuple-element.83, bf16[1,2304,1536]{2,1,0:T(8,128)(2,1)S(1)} %bitcast.116, bf16[72,2304]{1,0:T(8,128)(2,1)S(1)} %collective-permute-done.26), kind=kOutput, calls=%fused_computation.45 | convolution fusion | flops 510437376 | bytes 7962624 | tf_op jit(solution)/shard_map/dot_general | solution.py:22
  101.1 11.3 %collective-permute-done.17 = bf16[144,2304]{1,0:T(8,128)(2,1)S(1)} collective-permute-done((bf16[144,2304]{1,0:T(8,128)(2,1)S(1)}, bf16[144,2304]{1,0:T(8,128)(2,1)S(1)}, u32[]{:S(2)}, u32[]{:S(2)}) %collective-permute-start.17) | collective-permute-done | bytes 663584 | tf_op jit(solution)/shard_map/ppermute | solution.py:205
  113.2 6.3 %collective-permute-done.34 = bf16[72,2304]{1,0:T(8,128)(2,1)S(1)} collective-permute-done((bf16[72,2304]{1,0:T(8,128)(2,1)S(1)}, bf16[72,2304]{1,0:T(8,128)(2,1)S(1)}, u32[]{:S(2)}, u32[]{:S(2)}) %collective-permute-start.34) | collective-permute-done | bytes 331808 | tf_op jit(solution)/shard_map/ppermute | solution.py:205
  124.3 2.4 %fusion.111 = bf16[144,1536]{1,0:T(8,128)(2,1)S(1)} fusion(bf16[1,1536,2304]{2,1,0:T(8,128)(2,1)S(1)} %bitcast.114, bf16[72,2304]{1,0:T(8,128)(2,1)S(1)} %get-tuple-element.110, bf16[72,2304]{1,0:T(8,128)(2,1)S(1)} %get-tuple-element.109), kind=kOutput, calls=%fused_computation.57 | convolution fusion | flops 1020764160 | bytes 8183808 | tf_op jit(solution)/shard_map/dot_general | solution.py:22
  128.3 3.6 %collective-permute-done.31 = bf16[72,2304]{1,0:T(8,128)(2,1)S(1)} collective-permute-done((bf16[72,2304]{1,0:T(8,128)(2,1)S(1)}, bf16[72,2304]{1,0:T(8,128)(2,1)S(1)}, u32[]{:S(2)}, u32[]{:S(2)}) %collective-permute-start.31) | collective-permute-done | bytes 331808 | tf_op jit(solution)/shard_map/ppermute | solution.py:205
  134.4 3.4 %collective-permute-start.39 = (bf16[72,1536]{1,0:T(8,128)(2,1)S(1)}, bf16[72,1536]{1,0:T(8,128)(2,1)S(1)}, u32[]{:S(2)}, u32[]{:S(2)}) collective-permute-start(bf16[72,1536]{1,0:T(8,128)(2,1)S(1)} %add_convert_fusion.9), channel_id=1, source_target_pairs={{0,24},{4,28},{8,16},{12,20},{16,8},{20,12},{24,0},{28,4},{1,25},{... | collective-permute-start | bytes 663560 | tf_op jit(solution)/shard_map/ppermute | solution.py:205
  141.9 3.5 %collective-permute-done.19 = bf16[144,1536]{1,0:T(8,128)(2,1)S(1)} collective-permute-done((bf16[144,1536]{1,0:T(8,128)(2,1)S(1)}, bf16[144,1536]{1,0:T(8,128)(2,1)S(1)}, u32[]{:S(2)}, u32[]{:S(2)}) %collective-permute-start.19) | collective-permute-done | bytes 442400 | tf_op jit(solution)/shard_map/ppermute | solution.py:205
  145.7 4.1 %collective-permute-done.36 = bf16[72,1536]{1,0:T(8,128)(2,1)S(1)} collective-permute-done((bf16[72,1536]{1,0:T(8,128)(2,1)S(1)}, bf16[72,1536]{1,0:T(8,128)(2,1)S(1)}, u32[]{:S(2)}, u32[]{:S(2)}) %collective-permute-start.36) | collective-permute-done | bytes 221216 | tf_op jit(solution)/shard_map/ppermute | solution.py:205
  152.2 10.3 %collective-permute-done.37.refs_2_ = bf16[72,1536]{1,0:T(8,128)(2,1)S(1)} collective-permute-done((bf16[72,1536]{1,0:T(8,128)(2,1)S(1)}, bf16[72,1536]{1,0:T(8,128)(2,1)S(1)}, u32[]{:S(2)}, u32[]{:S(2)}) %collective-permute-start.37) | collective-permute-done | bytes 221216 | tf_op jit(solution)/shard_map/ppermute | solution.py:205
  165.4 4.6 %collective-permute-done.40 = bf16[6,128,128]{2,1,0:T(8,128)(2,1)S(1)} collective-permute-done((bf16[6,128,128]{2,1,0:T(8,128)(2,1)S(1)}, bf16[6,128,128]{2,1,0:T(8,128)(2,1)S(1)}, u32[]{:S(2)}, u32[]{:S(2)}) %collective-permute-start.40) | collective-permute-done | bytes 196640 | tf_op jit(solution)/shard_map/ppermute | solution.py:205
  170.2 5.7 %collective-permute-done.41 = bf16[6,128,128]{2,1,0:T(8,128)(2,1)S(1)} collective-permute-done((bf16[6,128,128]{2,1,0:T(8,128)(2,1)S(1)}, bf16[6,128,128]{2,1,0:T(8,128)(2,1)S(1)}, u32[]{:S(2)}, u32[]{:S(2)}) %collective-permute-start.41) | collective-permute-done | bytes 196640 | tf_op jit(solution)/shard_map/ppermute | solution.py:209
  176.7 4.9 %collective-permute-start.42 = (bf16[6,128,128]{2,1,0:T(8,128)(2,1)S(1)}, bf16[6,128,128]{2,1,0:T(8,128)(2,1)}, u32[]{:S(2)}, u32[]{:S(2)}) collective-permute-start(bf16[6,128,128]{2,1,0:T(8,128)(2,1)S(1)} %add_convert_fusion.11), channel_id=1, source_target_pairs={{16,0},{20,4},{8,8},{12,12},{0,16},{4,20},{24,24},{28,28},{17,1},{... | collective-permute-start | bytes 589832 | tf_op jit(solution)/shard_map/ppermute | solution.py:209
  181.6 5.4 %collective-permute-done.42 = bf16[6,128,128]{2,1,0:T(8,128)(2,1)} collective-permute-done((bf16[6,128,128]{2,1,0:T(8,128)(2,1)S(1)}, bf16[6,128,128]{2,1,0:T(8,128)(2,1)}, u32[]{:S(2)}, u32[]{:S(2)}) %collective-permute-start.42) | collective-permute-done | bytes 196640 | tf_op jit(solution)/shard_map/ppermute | solution.py:209
  189.8 4.0 %shard_map.117 = (bf16[128,1536]{1,0:T(8,128)(2,1)}, f32[128,1536]{1,0:T(8,128)S(1)}, f32[128,1536]{1,0:T(8,128)S(1)}) custom-call(s32[3]{0:T(128)S(1)} %pad_add_fusion.place_ref, f32[12]{0:T(128)S(1)} %copy-done.11, bf16[128,1536]{1,0:T(8,128)(2,1)S(1)} %copy-done.7, bf16[128,1536]{1,0:T(8,128)(2,1)S(1)} %copy-done.2, bf16[128,1536]{1,0:T(8,128)(2,1)S(1)} %copy-done.5, ...), custom_call_target="tpu_custom_call" | custom-call | flops 1 | bytes 1 | tf_op jit(solution)/shard_map/pallas_call | solution.py:192
  (160 shorter events, 83.2 us)
Async XLA Ops:
  12.3 13.1 %collective-permute-start.1 = (bf16[6,128,128]{2,1,0:T(8,128)(2,1)S(1)}, bf16[6,128,128]{2,1,0:T(8,128)(2,1)S(1)}, u32[]{:S(2)}, u32[]{:S(2)}) collective-permute-start(bf16[6,128,128]{2,1,0:T(8,128)(2,1)S(1)} %fusion.148), channel_id=1, source_target_pairs={{8,0},{12,4},{0,8},{4,12},{24,16},{28,20},{16,24},{20,28},{9,1},{1... | collective-permute-start | bytes 589832 | tf_op jit(solution)/shard_map/ppermute | solution.py:209
  19.8 18.2 %collective-permute-start.5 = (bf16[72,1536]{1,0:T(8,128)(2,1)S(1)}, bf16[72,1536]{1,0:T(8,128)(2,1)S(1)}, u32[]{:S(2)}, u32[]{:S(2)}) collective-permute-start(bf16[72,1536]{1,0:T(8,128)(2,1)S(1)} %get-tuple-element.58), channel_id=1, source_target_pairs={{0,4},{4,0},{8,12},{12,8},{16,20},{20,16},{24,28},{28,24},{1,5},{5... | collective-permute-start | bytes 663560 | tf_op jit(solution)/shard_map/ppermute | solution.py:205
  21.3 14.7 %collective-permute-start.6 = (bf16[72,1536]{1,0:T(8,128)(2,1)S(1)}, bf16[72,1536]{1,0:T(8,128)(2,1)S(1)}, u32[]{:S(2)}, u32[]{:S(2)}) collective-permute-start(bf16[72,1536]{1,0:T(8,128)(2,1)S(1)} %get-tuple-element.60), channel_id=1, source_target_pairs={{0,8},{4,12},{8,0},{12,4},{16,24},{20,28},{24,16},{28,20},{1,9},{5... | collective-permute-start | bytes 663560 | tf_op jit(solution)/shard_map/ppermute | solution.py:205
  21.8 14.2 %collective-permute-start.13 = (bf16[72,1536]{1,0:T(8,128)(2,1)S(1)}, bf16[72,1536]{1,0:T(8,128)(2,1)S(1)}, u32[]{:S(2)}, u32[]{:S(2)}) collective-permute-start(bf16[72,1536]{1,0:T(8,128)(2,1)S(1)} %get-tuple-element.70), channel_id=1, source_target_pairs={{0,24},{4,28},{8,16},{12,20},{16,8},{20,12},{24,0},{28,4},{1,25},{... | collective-permute-start | bytes 663560 | tf_op jit(solution)/shard_map/ppermute | solution.py:205
  25.5 12.5 %collective-permute-start.3 = (bf16[6,128,128]{2,1,0:T(8,128)(2,1)S(1)}, bf16[6,128,128]{2,1,0:T(8,128)(2,1)S(1)}, u32[]{:S(2)}, u32[]{:S(2)}) collective-permute-start(bf16[6,128,128]{2,1,0:T(8,128)(2,1)S(1)} %add_convert_fusion.12), channel_id=1, source_target_pairs={{0,0},{4,4},{16,8},{20,12},{8,16},{12,20},{24,24},{28,28},{1,1},{5... | collective-permute-start | bytes 589832 | tf_op jit(solution)/shard_map/ppermute | solution.py:209
  26.4 11.7 %collective-permute-start.2 = (bf16[6,128,128]{2,1,0:T(8,128)(2,1)S(1)}, bf16[6,128,128]{2,1,0:T(8,128)(2,1)S(1)}, u32[]{:S(2)}, u32[]{:S(2)}) collective-permute-start(bf16[6,128,128]{2,1,0:T(8,128)(2,1)S(1)} %add_convert_fusion.12), channel_id=1, source_target_pairs={{0,0},{4,4},{24,8},{28,12},{16,16},{20,20},{8,24},{12,28},{1,1},{5... | collective-permute-start | bytes 589832 | tf_op jit(solution)/shard_map/ppermute | solution.py:209
  36.5 12.1 %collective-permute-start.14 = (bf16[72,1536]{1,0:T(8,128)(2,1)S(1)}, bf16[72,1536]{1,0:T(8,128)(2,1)S(1)}, u32[]{:S(2)}, u32[]{:S(2)}) collective-permute-start(bf16[72,1536]{1,0:T(8,128)(2,1)S(1)} %collective-permute-done.13), channel_id=1, source_target_pairs={{0,4},{4,0},{8,12},{12,8},{16,20},{20,16},{24,28},{28,24},{1,5},{5... | collective-permute-start | bytes 663560 | tf_op jit(solution)/shard_map/ppermute | solution.py:205
  38.3 14.8 %collective-permute-start.4 = (bf16[6,128,128]{2,1,0:T(8,128)(2,1)S(1)}, bf16[6,128,128]{2,1,0:T(8,128)(2,1)S(1)}, u32[]{:S(2)}, u32[]{:S(2)}) collective-permute-start(bf16[6,128,128]{2,1,0:T(8,128)(2,1)S(1)} %get-tuple-element.106), channel_id=1, source_target_pairs={{0,4},{4,0},{8,12},{12,8},{16,20},{20,16},{24,28},{28,24},{1,5},{5... | collective-permute-start | bytes 589832 | tf_op jit(solution)/shard_map/ppermute | solution.py:205
  38.9 24.0 %collective-permute-start.21 = (bf16[72,1536]{1,0:T(8,128)(2,1)S(1)}, bf16[72,1536]{1,0:T(8,128)(2,1)S(1)}, u32[]{:S(2)}, u32[]{:S(2)}) collective-permute-start(bf16[72,1536]{1,0:T(8,128)(2,1)S(1)} %get-tuple-element.77), channel_id=1, source_target_pairs={{0,16},{4,20},{8,24},{12,28},{16,0},{20,4},{24,8},{28,12},{1,17},{... | collective-permute-start | bytes 663560 | tf_op jit(solution)/shard_map/ppermute | solution.py:205
  54.4 17.8 %collective-permute-start.10 = (bf16[72,1536]{1,0:T(8,128)(2,1)S(1)}, bf16[72,1536]{1,0:T(8,128)(2,1)S(1)}, u32[]{:S(2)}, u32[]{:S(2)}) collective-permute-start(bf16[72,1536]{1,0:T(8,128)(2,1)S(1)} %get-tuple-element.67), channel_id=1, source_target_pairs={{0,4},{4,0},{8,12},{12,8},{16,20},{20,16},{24,28},{28,24},{1,5},{5... | collective-permute-start | bytes 663560 | tf_op jit(solution)/shard_map/ppermute | solution.py:205
  56.3 10.4 %collective-permute-start.11 = (bf16[72,1536]{1,0:T(8,128)(2,1)S(1)}, bf16[72,1536]{1,0:T(8,128)(2,1)S(1)}, u32[]{:S(2)}, u32[]{:S(2)}) collective-permute-start(bf16[72,1536]{1,0:T(8,128)(2,1)S(1)} %get-tuple-element.68), channel_id=1, source_target_pairs={{0,8},{4,12},{8,0},{12,4},{16,24},{20,28},{24,16},{28,20},{1,9},{5... | collective-permute-start | bytes 663560 | tf_op jit(solution)/shard_map/ppermute | solution.py:205
  60.3 10.4 %collective-permute-start.23 = (bf16[72,1536]{1,0:T(8,128)(2,1)S(1)}, bf16[72,1536]{1,0:T(8,128)(2,1)S(1)}, u32[]{:S(2)}, u32[]{:S(2)}) collective-permute-start(bf16[72,1536]{1,0:T(8,128)(2,1)S(1)} %get-tuple-element.79), channel_id=1, source_target_pairs={{0,24},{4,28},{8,16},{12,20},{16,8},{20,12},{24,0},{28,4},{1,25},{... | collective-permute-start | bytes 663560 | tf_op jit(solution)/shard_map/ppermute | solution.py:205
  63.1 22.3 %collective-permute-start.22 = (bf16[72,1536]{1,0:T(8,128)(2,1)S(1)}, bf16[72,1536]{1,0:T(8,128)(2,1)S(1)}, u32[]{:S(2)}, u32[]{:S(2)}) collective-permute-start(bf16[72,1536]{1,0:T(8,128)(2,1)S(1)} %collective-permute-done.21), channel_id=1, source_target_pairs={{0,4},{4,0},{8,12},{12,8},{16,20},{20,16},{24,28},{28,24},{1,5},{5... | collective-permute-start | bytes 663560 | tf_op jit(solution)/shard_map/ppermute | solution.py:205
  66.7 34.3 %collective-permute-start.9 = (bf16[144,2304]{1,0:T(8,128)(2,1)S(1)}, bf16[144,2304]{1,0:T(8,128)(2,1)S(1)}, u32[]{:S(2)}, u32[]{:S(2)}) collective-permute-start(bf16[144,2304]{1,0:T(8,128)(2,1)S(1)} %add_convert_fusion.3), channel_id=1, source_target_pairs={{0,2},{1,3},{2,0},{3,1},{4,6},{5,7},{6,4},{7,5},{8,10},{9,11},{10,... | collective-permute-start | bytes 1990664 | tf_op jit(solution)/shard_map/ppermute | solution.py:205
  75.1 11.9 %collective-permute-start.28 = (bf16[72,1536]{1,0:T(8,128)(2,1)S(1)}, bf16[72,1536]{1,0:T(8,128)(2,1)S(1)}, u32[]{:S(2)}, u32[]{:S(2)}) collective-permute-start(bf16[72,1536]{1,0:T(8,128)(2,1)S(1)} %get-tuple-element.85), channel_id=1, source_target_pairs={{0,16},{4,20},{8,24},{12,28},{16,0},{20,4},{24,8},{28,12},{1,17},{... | collective-permute-start | bytes 663560 | tf_op jit(solution)/shard_map/ppermute | solution.py:205
  85.4 27.7 %collective-permute-start.33 = (bf16[72,2304]{1,0:T(8,128)(2,1)S(1)}, bf16[72,2304]{1,0:T(8,128)(2,1)S(1)}, u32[]{:S(2)}, u32[]{:S(2)}) collective-permute-start(bf16[72,2304]{1,0:T(8,128)(2,1)S(1)} %fusion.60), channel_id=1, source_target_pairs={{0,2},{1,3},{2,0},{3,1},{4,6},{5,7},{6,4},{7,5},{8,10},{9,11},{10,... | collective-permute-start | bytes 995336 | tf_op jit(solution)/shard_map/ppermute | solution.py:205
  94.5 17.9 %collective-permute-start.17 = (bf16[144,2304]{1,0:T(8,128)(2,1)S(1)}, bf16[144,2304]{1,0:T(8,128)(2,1)S(1)}, u32[]{:S(2)}, u32[]{:S(2)}) collective-permute-start(bf16[144,2304]{1,0:T(8,128)(2,1)S(1)} %add_convert_fusion.1), channel_id=1, source_target_pairs={{0,2},{1,3},{2,0},{3,1},{4,6},{5,7},{6,4},{7,5},{8,10},{9,11},{10,... | collective-permute-start | bytes 1990664 | tf_op jit(solution)/shard_map/ppermute | solution.py:205
  95.0 24.5 %collective-permute-start.34 = (bf16[72,2304]{1,0:T(8,128)(2,1)S(1)}, bf16[72,2304]{1,0:T(8,128)(2,1)S(1)}, u32[]{:S(2)}, u32[]{:S(2)}) collective-permute-start(bf16[72,2304]{1,0:T(8,128)(2,1)S(1)} %fusion.90), channel_id=1, source_target_pairs={{0,2},{1,3},{2,0},{3,1},{4,6},{5,7},{6,4},{7,5},{8,10},{9,11},{10,... | collective-permute-start | bytes 995336 | tf_op jit(solution)/shard_map/ppermute | solution.py:205
  99.0 29.3 %collective-permute-start.27 = (bf16[72,2304]{1,0:T(8,128)(2,1)S(1)}, bf16[72,2304]{1,0:T(8,128)(2,1)S(1)}, u32[]{:S(2)}, u32[]{:S(2)}) collective-permute-start(bf16[72,2304]{1,0:T(8,128)(2,1)S(1)} %fusion.75), channel_id=1, source_target_pairs={{0,2},{1,3},{2,0},{3,1},{4,6},{5,7},{6,4},{7,5},{8,10},{9,11},{10,... | collective-permute-start | bytes 995336 | tf_op jit(solution)/shard_map/ppermute | solution.py:205
  101.0 18.9 %collective-permute-start.30 = (bf16[72,2304]{1,0:T(8,128)(2,1)S(1)}, bf16[72,2304]{1,0:T(8,128)(2,1)S(1)}, u32[]{:S(2)}, u32[]{:S(2)}) collective-permute-start(bf16[72,2304]{1,0:T(8,128)(2,1)S(1)} %fusion.93), channel_id=1, source_target_pairs={{0,1},{1,0},{2,3},{3,2},{4,5},{5,4},{6,7},{7,6},{8,9},{9,8},{10,11... | collective-permute-start | bytes 995336 | tf_op jit(solution)/shard_map/ppermute | solution.py:205
  121.3 10.6 %collective-permute-start.31 = (bf16[72,2304]{1,0:T(8,128)(2,1)S(1)}, bf16[72,2304]{1,0:T(8,128)(2,1)S(1)}, u32[]{:S(2)}, u32[]{:S(2)}) collective-permute-start(bf16[72,2304]{1,0:T(8,128)(2,1)S(1)} %fusion.105), channel_id=1, source_target_pairs={{0,2},{1,3},{2,0},{3,1},{4,6},{5,7},{6,4},{7,5},{8,10},{9,11},{10,... | collective-permute-start | bytes 995336 | tf_op jit(solution)/shard_map/ppermute | solution.py:205
  132.4 13.0 %collective-permute-start.19 = (bf16[144,1536]{1,0:T(8,128)(2,1)S(1)}, bf16[144,1536]{1,0:T(8,128)(2,1)S(1)}, u32[]{:S(2)}, u32[]{:S(2)}) collective-permute-start(bf16[144,1536]{1,0:T(8,128)(2,1)S(1)} %slice.39), channel_id=1, source_target_pairs={{0,4},{4,0},{8,12},{12,8},{16,20},{20,16},{24,28},{28,24},{1,5},{5... | collective-permute-start | bytes 1327112 | tf_op jit(solution)/shard_map/ppermute | solution.py:205
  134.4 15.4 %collective-permute-start.39 = (bf16[72,1536]{1,0:T(8,128)(2,1)S(1)}, bf16[72,1536]{1,0:T(8,128)(2,1)S(1)}, u32[]{:S(2)}, u32[]{:S(2)}) collective-permute-start(bf16[72,1536]{1,0:T(8,128)(2,1)S(1)} %add_convert_fusion.9), channel_id=1, source_target_pairs={{0,24},{4,28},{8,16},{12,20},{16,8},{20,12},{24,0},{28,4},{1,25},{... | collective-permute-start | bytes 663560 | tf_op jit(solution)/shard_map/ppermute | solution.py:205
  149.8 12.7 %collective-permute-start.37 = (bf16[72,1536]{1,0:T(8,128)(2,1)S(1)}, bf16[72,1536]{1,0:T(8,128)(2,1)S(1)}, u32[]{:S(2)}, u32[]{:S(2)}) collective-permute-start(bf16[72,1536]{1,0:T(8,128)(2,1)S(1)} %add_convert_fusion.10), channel_id=1, source_target_pairs={{0,16},{4,20},{8,24},{12,28},{16,0},{20,4},{24,8},{28,12},{1,17},{... | collective-permute-start | bytes 663560 | tf_op jit(solution)/shard_map/ppermute | solution.py:205
  (39 other events, 346.8 us)

commit v6 on v5

--- a/solution.py
+++ b/solution.py
@@ -14,6 +14,7 @@
 
 SMEM = pl.BlockSpec(memory_space=pltpu.SMEM)
 VMEM = pl.BlockSpec(memory_space=pltpu.VMEM)
+HBM = pl.BlockSpec(memory_space=pl.ANY)
 LARGE = pl.CostEstimate(flops=1, bytes_accessed=40_000_000, transcendentals=0)
 SMALL = pl.CostEstimate(flops=1, bytes_accessed=1, transcendentals=0)
 
@@ -69,7 +70,7 @@
 
 
 def route_kernel(
-    place_ref, routes_ref, gates_ref, grad_ref, choose_ref, weigh_ref, *send_refs
+    place_ref, grad_ref, routes_ref, gates_ref, choose_ref, weigh_ref, *send_refs
 ):
     experts, capacity, block_len = choose_ref.shape
     rows = lax.broadcasted_iota(jnp.int32, (block_len, block_len), 0)
@@ -188,13 +189,32 @@
         ).astype(BF16)
 
 
-def call(kernel, out_shapes, scalars, arrays, scratch=(), cost=SMALL):
+def fetched(kernel, scalars, count, *refs):
+    sources, rest = refs[scalars : scalars + count], refs[scalars + count : -1 - count]
+    buffers, sems = refs[-1 - count : -1], refs[-1]
+    copies = [
+        pltpu.make_async_copy(source, buffer, sems.at[i])
+        for i, (source, buffer) in enumerate(zip(sources, buffers))
+    ]
+    for copy in copies:
+        copy.start()
+    for copy in copies:
+        copy.wait()
+    kernel(*refs[:scalars], *buffers, *rest)
+
+
+def call(kernel, out_shapes, scalars, arrays, scratch=(), cost=SMALL, fetch=0):
+    scratch = list(scratch)
+    if fetch:
+        kernel = functools.partial(fetched, kernel, len(scalars), fetch)
+        scratch += [pltpu.VMEM(array.shape, array.dtype) for array in arrays[:fetch]]
+        scratch += [pltpu.SemaphoreType.DMA((fetch,))]
     return pl.pallas_call(
         kernel,
         out_shape=list(out_shapes),
-        in_specs=[SMEM] * len(scalars) + [VMEM] * len(arrays),
+        in_specs=[SMEM] * len(scalars) + [HBM] * fetch + [VMEM] * (len(arrays) - fetch),
         out_specs=[VMEM] * len(out_shapes),
-        scratch_shapes=list(scratch),
+        scratch_shapes=scratch,
         compiler_params=pltpu.CompilerParams(vmem_limit_bytes=16 * 1024 * 1024),
         cost_estimate=cost,
     )(*scalars, *arrays)
@@ -317,76 +337,90 @@
     reaches = [1 << i for i in range((experts - 1).bit_length())]
     pairs_of = lambda rows, k: swap(rows, "ctx", 2 * k) if k else rows
 
-    key_mine, key_other = call(key_state_kernel, [states] * 2, scalars, (keys, values))
+    key_mine, key_other = call(
+        key_state_kernel, [states] * 2, scalars, (keys, values), cost=LARGE, fetch=2
+    )
     choose, weigh, *send_grad = call(
         route_kernel, [choose_table, weigh_table] + [slots] * experts,
-        (place,), (routes.T, gate_weights.T, out_grad)
+        (place,), (out_grad, routes.T, gate_weights.T), cost=LARGE, fetch=1,
     )
     intra, weights = call(
-        intra_kernel, [wide, weight_sq], scalars, (queries, keys, values), cost=LARGE
-    )
+        intra_kernel, [wide, weight_sq], scalars, (queries, keys, values), cost=LARGE, fetch=3
+    )
+    by_down = lambda rows: dot(rows, down_local, 1, 1)
+    by_up = lambda rows: dot(rows, up_local, 1, 0)
+
+    def hidden_of(part, *events):
+        return over_cores(*sum_over_cores(grad_own, grad_other, part, by_down, *events))
 
     total, partner = scan_total(
         key_mine, key_other, decay_rates, place, block_len, False, send_grad[0]
     )
-    grad_own = {0: send_grad[0]}
-    for k in [*near_part[1:], *first_far]:
-        grad_own[k] = pairs_of(after(send_grad[k], total), k)
+    grad_own, grad_other = {0: send_grad[0]}, {0: swap(send_grad[0], "ctx", 1)}
     before = None
     for index, reach in enumerate(reaches):
-        events = [intra] if index == 1 else []
+        events = [intra, grad_other[0]] if index == 1 else []
         before, upto = scan_step(
             before, total, reach, decay_rates, place, block_len, False, *events
         )
+    for k in near_part[1:]:
+        grad_own[k] = pairs_of(after(send_grad[k], upto), k)
+        grad_other[k] = swap(grad_own[k], "ctx", 1)
+    hidden = {0: hidden_of([0], upto)}
+    before = after(before, hidden[0], *[grad_own[k] for k in near_part[1:]])
     keep, give = scan_ends(before, key_mine, partner, decay_rates, place, block_len, False)
-    grad_other = {0: swap(after(grad_own[0], total), "ctx", 1)}
-    for k in [*near_part[1:], *first_far]:
-        grad_other[k] = swap(after(grad_own[k], upto), "ctx", 1)
-    for k in second_far:
+    for k in first_far:
         grad_own[k] = pairs_of(after(send_grad[k], give), k)
-
-    by_down = lambda rows: dot(rows, down_local, 1, 1)
-    by_up = lambda rows: dot(rows, up_local, 1, 0)
     given = swap(give, "ctx", 1)
-    hidden_near = over_cores(*sum_over_cores(grad_own, grad_other, near_part, by_down, give))
-    given, hidden_near = lax.optimization_barrier((given, hidden_near))
+    for k in near_part[1:]:
+        hidden[k] = hidden_of([k], give)
+    given, *ready = lax.optimization_barrier((given, *[hidden[k] for k in near_part[1:]]))
+    for k, rows in zip(near_part[1:], ready):
+        hidden[k] = rows
     send_in = call(
         attend_kernel, [slots] * experts, scalars, (queries, intra, choose, keep, given),
         [pltpu.VMEM((block_len, group), BF16)],
     )
-    for k in second_far:
-        grad_other[k] = swap(after(grad_own[k], send_in[0]), "ctx", 1)
-    hidden_first = over_cores(
-        *sum_over_cores(grad_own, grad_other, first_far, by_down, send_in[0])
-    )
-
     in_own, in_other = {0: send_in[0]}, {}
     for k in [*near_part[1:], *first_far]:
         in_own[k] = pairs_of(send_in[k], k)
+    for k in first_far:
+        grad_other[k] = swap(after(grad_own[k], send_in[0]), "ctx", 1)
+        hidden[k] = hidden_of([k])
+    ready = [hidden[k] for k in first_far]
     for k in second_far:
-        in_own[k] = pairs_of(after(send_in[k], in_own[first_far[0]], hidden_first), k)
-    for k in range(experts):
+        in_own[k] = pairs_of(after(send_in[k], in_own[first_far[0]]), k)
+        grad_own[k] = pairs_of(after(send_grad[k], in_own[first_far[0]]), k)
+    for k in near_part:
         in_other[k] = swap(in_own[k], "ctx", 1)
-
-    pre_near = over_cores(*sum_over_cores(in_own, in_other, near_part, by_up, hidden_first))
+    for k in first_far:
+        in_other[k] = swap(after(in_own[k], in_other[near_part[-1]]), "ctx", 1)
+    pre_near = over_cores(*sum_over_cores(in_own, in_other, near_part, by_up, *ready))
+    for k in second_far:
+        in_other[k] = swap(after(in_own[k], pre_near), "ctx", 1)
+        grad_other[k] = swap(after(grad_own[k], in_other[k]), "ctx", 1)
     pre_first = over_cores(*sum_over_cores(in_own, in_other, first_far, by_up, pre_near))
-    hidden_second = over_cores(
-        *sum_over_cores(grad_own, grad_other, second_far, by_down, pre_first)
-    )
-    pre_second = over_cores(*sum_over_cores(in_own, in_other, second_far, by_up, hidden_second))
+    for k in second_far:
+        hidden[k] = hidden_of([k], pre_first)
+    pre_near = sum_over_rest(pre_near, bits)
+    ready = [hidden[k] for k in second_far]
+    pre_second = over_cores(
+        *sum_over_cores(in_own, in_other, second_far, by_up, pre_near, *ready)
+    )
 
     homes = {}
     back = None
-    for part, pre, hidden in (
-        (near_part, pre_near, hidden_near),
-        (first_far, pre_first, hidden_first),
-        (second_far, pre_second, hidden_second),
+    for part, pre in (
+        (near_part, pre_near),
+        (first_far, pre_first),
+        (second_far, pre_second),
     ):
-        pre, hidden = sum_over_rest(pre, bits), sum_over_rest(hidden, bits)
-        slope = (hidden.astype(F32) * silu_slope(pre.astype(F32))).astype(BF16)
+        if back is not None:
+            pre = after(sum_over_rest(pre, bits), back)
+        rows = [sum_over_rest(hidden[k], bits) for k in part]
+        grad = rows[0] if len(rows) == 1 else jnp.concatenate(rows, axis=0)
+        slope = (grad.astype(F32) * silu_slope(pre.astype(F32))).astype(BF16)
         got = swap(slope, "exp", 1)
-        if back is not None:
-            got = after(got, back)
         slope = jnp.concatenate(
             [jnp.where(core == 0, slope, got), jnp.where(core == 0, got, slope)], axis=0
         )

time: 196 us -> 216 us (1.10)
  matrix products: 32.3 us -> 43.4 us
  waiting for transfers between devices: 82.1 us -> 84.9 us
  starting transfers between devices: 54.4 us -> 56.6 us
    dot_general x15 -> x17, matrix products: 32.3 us -> 43.4 us  [dot(): lax.dot_general(left, right, (((left_dim,), (right_dim,)), ((), ())), pre...]
    ppermute x6, waiting for transfers between devices: 11.1 us -> 14.4 us  [trade(): lax.ppermute(array, 'ctx', [(2 * partner(i) + s, 2 * i + s) for i in rang...]
    ppermute x6, starting transfers between devices: 9.3 us -> 12.1 us  [trade(): lax.ppermute(array, 'ctx', [(2 * partner(i) + s, 2 * i + s) for i in rang...]
    ppermute x39 -> x41, starting transfers between devices: 45.1 us -> 44.5 us  [swap(): return lax.ppermute(array, axis, [(i, i ^ distance) for i in range(size)])]
    ppermute x39 -> x41, waiting for transfers between devices: 71 us -> 70.6 us  [swap(): return lax.ppermute(array, axis, [(i, i ^ distance) for i in range(size)])]
    unnamed x36 -> x50, local copies, waits for them, and re-layouts: 8.05 us -> 8.07 us
  transfers between devices with their start and end apart: 45 -> 47, of which waited for: 22 -> 22; matrix products, arithmetic and copies ran while one was open for 18% -> 19% of each run, Pallas kernels for 5% -> 5%
where the time goes in v6:
time: 216 us; the launch traced here: 215 us
  waiting for transfers between devices  84.9 us (39%)
  starting transfers between devices  56.6 us (26%)
  matrix products  43.4 us (20%)
  Pallas kernels  14.4 us (7%)
  local copies, waits for them, and re-layouts  8.17 us (4%)
  other arithmetic  6.11 us (3%)
    ppermute x41, waiting for transfers between devices, swap(): return lax.ppermute(array, axis, [(i, i ^ distance) for i in range(size)])  70.6 us
    ppermute x41, starting transfers between devices, swap(): return lax.ppermute(array, axis, [(i, i ^ distance) for i in range(size)])  44.5 us
    dot_general x17, matrix products, dot(): lax.dot_general(left, right, (((left_dim,), (right_dim,)), ((), ())), pre...  43.4 us
    pallas_call x7, Pallas kernels, call(): pl.pallas_call(kernel, out_shape=list(out_shapes), in_specs=[SMEM] * len(...  14.4 us
    ppermute x6, waiting for transfers between devices, trade(): lax.ppermute(array, 'ctx', [(2 * partner(i) + s, 2 * i + s) for i in rang...  14.4 us
    ppermute x6, starting transfers between devices, trade(): lax.ppermute(array, 'ctx', [(2 * partner(i) + s, 2 * i + s) for i in rang...  12.1 us
    unnamed x50, local copies, waits for them, and re-layouts  8.07 us
  transfers between devices with their start and end apart: 47, of which 22 were waited for; matrix products, arithmetic and copies ran while one was open for 19% of the time, Pallas kernels for 5%

profile of v6, /device:TPU:0, one launch (start us, length us, event | category | flops | bytes accessed | tf_op | source)
XLA Modules:
  0.0 214.9 jit_solution(15690041050871871184)
XLA Ops:
  4.7 3.0 %collective-permute-start.1 = (bf16[6,128,128]{2,1,0:T(8,128)(2,1)S(1)}, bf16[6,128,128]{2,1,0:T(8,128)(2,1)S(1)}, u32[]{:S(2)}, u32[]{:S(2)}) collective-permute-start(bf16[6,128,128]{2,1,0:T(8,128)(2,1)S(1)} %get-tuple-element.56), channel_id=1, source_target_pairs={{0,4},{4,0},{8,12},{12,8},{16,20},{20,16},{24,28},{28,24},{1,5},{5... | collective-permute-start | bytes 589832 | tf_op jit(solution)/shard_map/ppermute | solution.py:225
  14.5 3.1 %shard_map.114 = (f32[128,1536]{1,0:T(8,128)S(1)}, bf16[12,128,128]{2,1,0:T(8,128)(2,1)S(1)}) custom-call(s32[3]{0:T(128)S(1)} %pad_add_fusion.refs_0_.place_ref, f32[12]{0:T(128)S(1)} %copy-done.10, bf16[128,1536]{1,0:T(8,128)(2,1)S(1)} %copy-done.6, bf16[128,1536]{1,0:T(8,128)(2,1)S(1)} %copy-done.1, bf16[128,1536]{1,0:T(8,128)(2,1)S(1)} %copy-done.4), custom_call_target="tpu_custom_call" | custom-call | flops 1 | bytes 40000000 | tf_op jit(solution)/shard_map/pallas_call | solution.py:212
  20.7 4.3 %collective-permute-done.2 = bf16[6,128,128]{2,1,0:T(8,128)(2,1)S(1)} collective-permute-done((bf16[6,128,128]{2,1,0:T(8,128)(2,1)S(1)}, bf16[6,128,128]{2,1,0:T(8,128)(2,1)S(1)}, u32[]{:S(2)}, u32[]{:S(2)}) %collective-permute-start.2) | collective-permute-done | bytes 196640 | tf_op jit(solution)/shard_map/ppermute | solution.py:229
  27.4 3.0 %collective-permute-start.5 = (bf16[6,128,128]{2,1,0:T(8,128)(2,1)}, bf16[6,128,128]{2,1,0:T(8,128)(2,1)}, u32[]{:S(2)}, u32[]{:S(2)}) collective-permute-start(bf16[6,128,128]{2,1,0:T(8,128)(2,1)} %add_convert_fusion.12), channel_id=1, source_target_pairs={{0,0},{4,4},{24,8},{28,12},{16,16},{20,20},{8,24},{12,28},{1,1},{5... | collective-permute-start | bytes 589832 | tf_op jit(solution)/shard_map/ppermute | solution.py:229
  30.4 6.0 %fusion.43 = bf16[72,2304]{1,0:T(8,128)(2,1)} fusion(bf16[72,1536]{1,0:T(8,128)(2,1)S(1)} %get-tuple-element.60, bf16[1,2304,1536]{2,1,0:T(8,128)(2,1)} %param.14), kind=kOutput, calls=%fused_computation.37 | convolution fusion | flops 509773824 | bytes 7630848 | tf_op jit(solution)/shard_map/dot_general | solution.py:23
  36.4 3.4 %collective-permute-start.7 = (bf16[72,1536]{1,0:T(8,128)(2,1)S(1)}, bf16[72,1536]{1,0:T(8,128)(2,1)S(1)}, u32[]{:S(2)}, u32[]{:S(2)}) collective-permute-start(bf16[72,1536]{1,0:T(8,128)(2,1)S(1)} %get-tuple-element.63), channel_id=1, source_target_pairs={{0,8},{4,12},{8,0},{12,4},{16,24},{20,28},{24,16},{28,20},{1,9},{5... | collective-permute-start | bytes 663560 | tf_op jit(solution)/shard_map/ppermute | solution.py:225
  40.0 5.9 %collective-permute-done.7 = bf16[72,1536]{1,0:T(8,128)(2,1)S(1)} collective-permute-done((bf16[72,1536]{1,0:T(8,128)(2,1)S(1)}, bf16[72,1536]{1,0:T(8,128)(2,1)S(1)}, u32[]{:S(2)}, u32[]{:S(2)}) %collective-permute-start.7) | collective-permute-done | bytes 221216 | tf_op jit(solution)/shard_map/ppermute | solution.py:225
  47.4 5.3 %fusion.55 = bf16[72,2304]{1,0:T(8,128)(2,1)S(1)} fusion(bf16[72,1536]{1,0:T(8,128)(2,1)S(1)} %get-tuple-element.61, bf16[1,2304,1536]{2,1,0:T(8,128)(2,1)} %param.14, bf16[72,2304]{1,0:T(8,128)(2,1)} %collective-permute-done.3), kind=kOutput, calls=%fused_computation.41 | convolution fusion | flops 510437376 | bytes 7962624 | tf_op jit(solution)/shard_map/dot_general | solution.py:23
  53.2 5.5 %fusion.58 = bf16[72,2304]{1,0:T(8,128)(2,1)S(1)} fusion(bf16[72,1536]{1,0:T(8,128)(2,1)S(1)} %get-tuple-element.65, bf16[1,2304,1536]{2,1,0:T(8,128)(2,1)} %param.14), kind=kOutput, calls=%fused_computation.42 | convolution fusion | flops 509773824 | bytes 7630848 | tf_op jit(solution)/shard_map/dot_general | solution.py:23
  61.7 3.2 %collective-permute-start.15 = (bf16[72,1536]{1,0:T(8,128)(2,1)S(1)}, bf16[72,1536]{1,0:T(8,128)(2,1)S(1)}, u32[]{:S(2)}, u32[]{:S(2)}) collective-permute-start(bf16[72,1536]{1,0:T(8,128)(2,1)S(1)} %get-tuple-element.73), channel_id=1, source_target_pairs={{0,24},{4,28},{8,16},{12,20},{16,8},{20,12},{24,0},{28,4},{1,25},{... | collective-permute-start | bytes 663560 | tf_op jit(solution)/shard_map/ppermute | solution.py:225
  73.0 4.4 %collective-permute-start.13 = (bf16[72,1536]{1,0:T(8,128)(2,1)S(1)}, bf16[72,1536]{1,0:T(8,128)(2,1)S(1)}, u32[]{:S(2)}, u32[]{:S(2)}) collective-permute-start(bf16[72,1536]{1,0:T(8,128)(2,1)S(1)} %get-tuple-element.71), channel_id=1, source_target_pairs={{0,8},{4,12},{8,0},{12,4},{16,24},{20,28},{24,16},{28,20},{1,9},{5... | collective-permute-start | bytes 663560 | tf_op jit(solution)/shard_map/ppermute | solution.py:225
  82.4 5.6 %collective-permute-done.23 = bf16[72,1536]{1,0:T(8,128)(2,1)S(1)} collective-permute-done((bf16[72,1536]{1,0:T(8,128)(2,1)S(1)}, bf16[72,1536]{1,0:T(8,128)(2,1)S(1)}, u32[]{:S(2)}, u32[]{:S(2)}) %collective-permute-start.23) | collective-permute-done | bytes 221216 | tf_op jit(solution)/shard_map/ppermute | solution.py:225
  88.0 2.9 %collective-permute-start.25 = (bf16[72,1536]{1,0:T(8,128)(2,1)S(1)}, bf16[72,1536]{1,0:T(8,128)(2,1)S(1)}, u32[]{:S(2)}, u32[]{:S(2)}) collective-permute-start(bf16[72,1536]{1,0:T(8,128)(2,1)S(1)} %get-tuple-element.82), channel_id=1, source_target_pairs={{0,16},{4,20},{8,24},{12,28},{16,0},{20,4},{24,8},{28,12},{1,17},{... | collective-permute-start | bytes 663560 | tf_op jit(solution)/shard_map/ppermute | solution.py:225
  91.8 7.0 %collective-permute-done.14 = bf16[72,1536]{1,0:T(8,128)(2,1)S(1)} collective-permute-done((bf16[72,1536]{1,0:T(8,128)(2,1)S(1)}, bf16[72,1536]{1,0:T(8,128)(2,1)S(1)}, u32[]{:S(2)}, u32[]{:S(2)}) %collective-permute-start.14) | collective-permute-done | bytes 221216 | tf_op jit(solution)/shard_map/ppermute | solution.py:225
  109.9 4.5 %collective-permute-done.26 = bf16[72,1536]{1,0:T(8,128)(2,1)S(1)} collective-permute-done((bf16[72,1536]{1,0:T(8,128)(2,1)S(1)}, bf16[72,1536]{1,0:T(8,128)(2,1)S(1)}, u32[]{:S(2)}, u32[]{:S(2)}) %collective-permute-start.26) | collective-permute-done | bytes 221216 | tf_op jit(solution)/shard_map/ppermute | solution.py:225
  122.7 5.5 %collective-permute-done.19 = bf16[144,2304]{1,0:T(8,128)(2,1)S(1)} collective-permute-done((bf16[144,2304]{1,0:T(8,128)(2,1)S(1)}, bf16[144,2304]{1,0:T(8,128)(2,1)S(1)}, u32[]{:S(2)}, u32[]{:S(2)}) %collective-permute-start.19) | collective-permute-done | bytes 663584 | tf_op jit(solution)/shard_map/ppermute | solution.py:225
  142.7 8.9 %collective-permute-done.33 = bf16[72,2304]{1,0:T(8,128)(2,1)S(1)} collective-permute-done((bf16[72,2304]{1,0:T(8,128)(2,1)S(1)}, bf16[72,2304]{1,0:T(8,128)(2,1)S(1)}, u32[]{:S(2)}, u32[]{:S(2)}) %collective-permute-start.33) | collective-permute-done | bytes 331808 | tf_op jit(solution)/shard_map/ppermute | solution.py:225
  162.6 5.1 %collective-permute-done.38 = bf16[72,1536]{1,0:T(8,128)(2,1)S(1)} collective-permute-done((bf16[72,1536]{1,0:T(8,128)(2,1)S(1)}, bf16[72,1536]{1,0:T(8,128)(2,1)S(1)}, u32[]{:S(2)}, u32[]{:S(2)}) %collective-permute-start.38) | collective-permute-done | bytes 221216 | tf_op jit(solution)/shard_map/ppermute | solution.py:225
  170.2 12.5 %collective-permute-done.39.refs_2_ = bf16[72,1536]{1,0:T(8,128)(2,1)S(1)} collective-permute-done((bf16[72,1536]{1,0:T(8,128)(2,1)S(1)}, bf16[72,1536]{1,0:T(8,128)(2,1)S(1)}, u32[]{:S(2)}, u32[]{:S(2)}) %collective-permute-start.39) | collective-permute-done | bytes 221216 | tf_op jit(solution)/shard_map/ppermute | solution.py:225
  185.4 4.6 %collective-permute-done.42 = bf16[6,128,128]{2,1,0:T(8,128)(2,1)S(1)} collective-permute-done((bf16[6,128,128]{2,1,0:T(8,128)(2,1)S(1)}, bf16[6,128,128]{2,1,0:T(8,128)(2,1)S(1)}, u32[]{:S(2)}, u32[]{:S(2)}) %collective-permute-start.42) | collective-permute-done | bytes 196640 | tf_op jit(solution)/shard_map/ppermute | solution.py:225
  190.5 5.7 %collective-permute-done.43 = bf16[6,128,128]{2,1,0:T(8,128)(2,1)S(1)} collective-permute-done((bf16[6,128,128]{2,1,0:T(8,128)(2,1)S(1)}, bf16[6,128,128]{2,1,0:T(8,128)(2,1)S(1)}, u32[]{:S(2)}, u32[]{:S(2)}) %collective-permute-start.43) | collective-permute-done | bytes 196640 | tf_op jit(solution)/shard_map/ppermute | solution.py:229
  197.0 4.6 %collective-permute-start.44 = (bf16[6,128,128]{2,1,0:T(8,128)(2,1)S(1)}, bf16[6,128,128]{2,1,0:T(8,128)(2,1)}, u32[]{:S(2)}, u32[]{:S(2)}) collective-permute-start(bf16[6,128,128]{2,1,0:T(8,128)(2,1)S(1)} %add_convert_fusion.11), channel_id=1, source_target_pairs={{16,0},{20,4},{8,8},{12,12},{0,16},{4,20},{24,24},{28,28},{17,1},{... | collective-permute-start | bytes 589832 | tf_op jit(solution)/shard_map/ppermute | solution.py:229
  201.6 4.4 %collective-permute-done.44 = bf16[6,128,128]{2,1,0:T(8,128)(2,1)} collective-permute-done((bf16[6,128,128]{2,1,0:T(8,128)(2,1)S(1)}, bf16[6,128,128]{2,1,0:T(8,128)(2,1)}, u32[]{:S(2)}, u32[]{:S(2)}) %collective-permute-start.44) | collective-permute-done | bytes 196640 | tf_op jit(solution)/shard_map/ppermute | solution.py:229
  208.6 4.0 %shard_map.117 = (bf16[128,1536]{1,0:T(8,128)(2,1)}, f32[128,1536]{1,0:T(8,128)S(1)}, f32[128,1536]{1,0:T(8,128)S(1)}) custom-call(s32[3]{0:T(128)S(1)} %pad_add_fusion.refs_0_.place_ref, f32[12]{0:T(128)S(1)} %copy-done.11, bf16[128,1536]{1,0:T(8,128)(2,1)S(1)} %copy-done.7, bf16[128,1536]{1,0:T(8,128)(2,1)S(1)} %copy-done.2, ...), custom_call_target="tpu_custom_call" | custom-call | flops 1 | bytes 1 | tf_op jit(solution)/shard_map/pallas_call | solution.py:212
  (183 shorter events, 91.2 us)
Async XLA Ops:
  4.7 13.7 %collective-permute-start.1 = (bf16[6,128,128]{2,1,0:T(8,128)(2,1)S(1)}, bf16[6,128,128]{2,1,0:T(8,128)(2,1)S(1)}, u32[]{:S(2)}, u32[]{:S(2)}) collective-permute-start(bf16[6,128,128]{2,1,0:T(8,128)(2,1)S(1)} %get-tuple-element.56), channel_id=1, source_target_pairs={{0,4},{4,0},{8,12},{12,8},{16,20},{20,16},{24,28},{28,24},{1,5},{5... | collective-permute-start | bytes 589832 | tf_op jit(solution)/shard_map/ppermute | solution.py:225
  25.8 14.0 %collective-permute-start.6 = (bf16[6,128,128]{2,1,0:T(8,128)(2,1)}, bf16[6,128,128]{2,1,0:T(8,128)(2,1)S(1)}, u32[]{:S(2)}, u32[]{:S(2)}) collective-permute-start(bf16[6,128,128]{2,1,0:T(8,128)(2,1)} %add_convert_fusion.12), channel_id=1, source_target_pairs={{0,0},{4,4},{16,8},{20,12},{8,16},{12,20},{24,24},{28,28},{1,1},{5... | collective-permute-start | bytes 589832 | tf_op jit(solution)/shard_map/ppermute | solution.py:229
  27.4 12.4 %collective-permute-start.5 = (bf16[6,128,128]{2,1,0:T(8,128)(2,1)}, bf16[6,128,128]{2,1,0:T(8,128)(2,1)}, u32[]{:S(2)}, u32[]{:S(2)}) collective-permute-start(bf16[6,128,128]{2,1,0:T(8,128)(2,1)} %add_convert_fusion.12), channel_id=1, source_target_pairs={{0,0},{4,4},{24,8},{28,12},{16,16},{20,20},{8,24},{12,28},{1,1},{5... | collective-permute-start | bytes 589832 | tf_op jit(solution)/shard_map/ppermute | solution.py:229
  36.3 11.0 %collective-permute-start.3 = (bf16[72,2304]{1,0:T(8,128)(2,1)}, bf16[72,2304]{1,0:T(8,128)(2,1)}, u32[]{:S(2)}, u32[]{:S(2)}) collective-permute-start(bf16[72,2304]{1,0:T(8,128)(2,1)} %fusion.43), channel_id=1, source_target_pairs={{0,1},{1,0},{2,3},{3,2},{4,5},{5,4},{6,7},{7,6},{8,9},{9,8},{10,11... | collective-permute-start | bytes 995336 | tf_op jit(solution)/shard_map/ppermute | solution.py:225
  36.4 9.5 %collective-permute-start.7 = (bf16[72,1536]{1,0:T(8,128)(2,1)S(1)}, bf16[72,1536]{1,0:T(8,128)(2,1)S(1)}, u32[]{:S(2)}, u32[]{:S(2)}) collective-permute-start(bf16[72,1536]{1,0:T(8,128)(2,1)S(1)} %get-tuple-element.63), channel_id=1, source_target_pairs={{0,8},{4,12},{8,0},{12,4},{16,24},{20,28},{24,16},{28,20},{1,9},{5... | collective-permute-start | bytes 663560 | tf_op jit(solution)/shard_map/ppermute | solution.py:225
  60.1 11.4 %collective-permute-start.4 = (bf16[72,2304]{1,0:T(8,128)(2,1)S(1)}, bf16[72,2304]{1,0:T(8,128)(2,1)S(1)}, u32[]{:S(2)}, u32[]{:S(2)}) collective-permute-start(bf16[72,2304]{1,0:T(8,128)(2,1)S(1)} %fusion.55), channel_id=1, source_target_pairs={{0,2},{1,3},{2,0},{3,1},{4,6},{5,7},{6,4},{7,5},{8,10},{9,11},{10,... | collective-permute-start | bytes 995336 | tf_op jit(solution)/shard_map/ppermute | solution.py:225
  70.8 9.2 %collective-permute-start.16 = (bf16[72,1536]{1,0:T(8,128)(2,1)S(1)}, bf16[72,1536]{1,0:T(8,128)(2,1)S(1)}, u32[]{:S(2)}, u32[]{:S(2)}) collective-permute-start(bf16[72,1536]{1,0:T(8,128)(2,1)S(1)} %collective-permute-done.15), channel_id=1, source_target_pairs={{0,4},{4,0},{8,12},{12,8},{16,20},{20,16},{24,28},{28,24},{1,5},{5... | collective-permute-start | bytes 663560 | tf_op jit(solution)/shard_map/ppermute | solution.py:225
  71.6 19.3 %collective-permute-start.12 = (bf16[72,1536]{1,0:T(8,128)(2,1)S(1)}, bf16[72,1536]{1,0:T(8,128)(2,1)S(1)}, u32[]{:S(2)}, u32[]{:S(2)}) collective-permute-start(bf16[72,1536]{1,0:T(8,128)(2,1)S(1)} %get-tuple-element.70), channel_id=1, source_target_pairs={{0,4},{4,0},{8,12},{12,8},{16,20},{20,16},{24,28},{28,24},{1,5},{5... | collective-permute-start | bytes 663560 | tf_op jit(solution)/shard_map/ppermute | solution.py:225
  73.0 15.1 %collective-permute-start.13 = (bf16[72,1536]{1,0:T(8,128)(2,1)S(1)}, bf16[72,1536]{1,0:T(8,128)(2,1)S(1)}, u32[]{:S(2)}, u32[]{:S(2)}) collective-permute-start(bf16[72,1536]{1,0:T(8,128)(2,1)S(1)} %get-tuple-element.71), channel_id=1, source_target_pairs={{0,8},{4,12},{8,0},{12,4},{16,24},{20,28},{24,16},{28,20},{1,9},{5... | collective-permute-start | bytes 663560 | tf_op jit(solution)/shard_map/ppermute | solution.py:225
  77.4 10.7 %collective-permute-start.23 = (bf16[72,1536]{1,0:T(8,128)(2,1)S(1)}, bf16[72,1536]{1,0:T(8,128)(2,1)S(1)}, u32[]{:S(2)}, u32[]{:S(2)}) collective-permute-start(bf16[72,1536]{1,0:T(8,128)(2,1)S(1)} %get-tuple-element.79), channel_id=1, source_target_pairs={{0,24},{4,28},{8,16},{12,20},{16,8},{20,12},{24,0},{28,4},{1,25},{... | collective-permute-start | bytes 663560 | tf_op jit(solution)/shard_map/ppermute | solution.py:225
  79.5 12.2 %collective-permute-start.11 = (bf16[72,2304]{1,0:T(8,128)(2,1)S(1)}, bf16[72,2304]{1,0:T(8,128)(2,1)S(1)}, u32[]{:S(2)}, u32[]{:S(2)}) collective-permute-start(bf16[72,2304]{1,0:T(8,128)(2,1)S(1)} %fusion.70), channel_id=1, source_target_pairs={{0,2},{1,3},{2,0},{3,1},{4,6},{5,7},{6,4},{7,5},{8,10},{9,11},{10,... | collective-permute-start | bytes 995336 | tf_op jit(solution)/shard_map/ppermute | solution.py:225
  82.4 17.3 %collective-permute-start.17 = (bf16[72,2304]{1,0:T(8,128)(2,1)S(1)}, bf16[72,2304]{1,0:T(8,128)(2,1)S(1)}, u32[]{:S(2)}, u32[]{:S(2)}) collective-permute-start(bf16[72,2304]{1,0:T(8,128)(2,1)S(1)} %fusion.73), channel_id=1, source_target_pairs={{0,1},{1,0},{2,3},{3,2},{4,5},{5,4},{6,7},{7,6},{8,9},{9,8},{10,11... | collective-permute-start | bytes 995336 | tf_op jit(solution)/shard_map/ppermute | solution.py:225
  88.0 21.9 %collective-permute-start.24 = (bf16[72,1536]{1,0:T(8,128)(2,1)S(1)}, bf16[72,1536]{1,0:T(8,128)(2,1)S(1)}, u32[]{:S(2)}, u32[]{:S(2)}) collective-permute-start(bf16[72,1536]{1,0:T(8,128)(2,1)S(1)} %get-tuple-element.80), channel_id=1, source_target_pairs={{0,16},{4,20},{8,24},{12,28},{16,0},{20,4},{24,8},{28,12},{1,17},{... | collective-permute-start | bytes 663560 | tf_op jit(solution)/shard_map/ppermute | solution.py:225
  88.0 19.7 %collective-permute-start.25 = (bf16[72,1536]{1,0:T(8,128)(2,1)S(1)}, bf16[72,1536]{1,0:T(8,128)(2,1)S(1)}, u32[]{:S(2)}, u32[]{:S(2)}) collective-permute-start(bf16[72,1536]{1,0:T(8,128)(2,1)S(1)} %get-tuple-element.82), channel_id=1, source_target_pairs={{0,16},{4,20},{8,24},{12,28},{16,0},{20,4},{24,8},{28,12},{1,17},{... | collective-permute-start | bytes 663560 | tf_op jit(solution)/shard_map/ppermute | solution.py:225
  103.3 37.6 %collective-permute-start.34 = (bf16[72,2304]{1,0:T(8,128)(2,1)S(1)}, bf16[72,2304]{1,0:T(8,128)(2,1)S(1)}, u32[]{:S(2)}, u32[]{:S(2)}) collective-permute-start(bf16[72,2304]{1,0:T(8,128)(2,1)S(1)} %fusion.85), channel_id=1, source_target_pairs={{0,2},{1,3},{2,0},{3,1},{4,6},{5,7},{6,4},{7,5},{8,10},{9,11},{10,... | collective-permute-start | bytes 995336 | tf_op jit(solution)/shard_map/ppermute | solution.py:225
  106.6 21.6 %collective-permute-start.19 = (bf16[144,2304]{1,0:T(8,128)(2,1)S(1)}, bf16[144,2304]{1,0:T(8,128)(2,1)S(1)}, u32[]{:S(2)}, u32[]{:S(2)}) collective-permute-start(bf16[144,2304]{1,0:T(8,128)(2,1)S(1)} %add_convert_fusion.1), channel_id=1, source_target_pairs={{0,2},{1,3},{2,0},{3,1},{4,6},{5,7},{6,4},{7,5},{8,10},{9,11},{10,... | collective-permute-start | bytes 1990664 | tf_op jit(solution)/shard_map/ppermute | solution.py:225
  117.3 17.6 %collective-permute-start.35 = (bf16[72,2304]{1,0:T(8,128)(2,1)S(1)}, bf16[72,2304]{1,0:T(8,128)(2,1)S(1)}, u32[]{:S(2)}, u32[]{:S(2)}) collective-permute-start(bf16[72,2304]{1,0:T(8,128)(2,1)S(1)} %fusion.115), channel_id=1, source_target_pairs={{0,2},{1,3},{2,0},{3,1},{4,6},{5,7},{6,4},{7,5},{8,10},{9,11},{10,... | collective-permute-start | bytes 995336 | tf_op jit(solution)/shard_map/ppermute | solution.py:225
  128.8 9.8 %collective-permute-start.20 = (bf16[144,2304]{1,0:T(8,128)(2,1)S(1)}, bf16[144,2304]{1,0:T(8,128)(2,1)S(1)}, u32[]{:S(2)}, u32[]{:S(2)}) collective-permute-start(bf16[144,2304]{1,0:T(8,128)(2,1)S(1)} %fusion.148), channel_id=1, source_target_pairs={{0,1},{1,0},{2,3},{3,2},{4,5},{5,4},{6,7},{7,6},{8,9},{9,8},{10,11... | collective-permute-start | bytes 1990664 | tf_op jit(solution)/shard_map/ppermute | solution.py:225
  135.0 20.6 %collective-permute-start.31 = (bf16[72,2304]{1,0:T(8,128)(2,1)S(1)}, bf16[72,2304]{1,0:T(8,128)(2,1)S(1)}, u32[]{:S(2)}, u32[]{:S(2)}) collective-permute-start(bf16[72,2304]{1,0:T(8,128)(2,1)S(1)} %fusion.100), channel_id=1, source_target_pairs={{0,2},{1,3},{2,0},{3,1},{4,6},{5,7},{6,4},{7,5},{8,10},{9,11},{10,... | collective-permute-start | bytes 995336 | tf_op jit(solution)/shard_map/ppermute | solution.py:225
  136.9 14.6 %collective-permute-start.33 = (bf16[72,2304]{1,0:T(8,128)(2,1)S(1)}, bf16[72,2304]{1,0:T(8,128)(2,1)S(1)}, u32[]{:S(2)}, u32[]{:S(2)}) collective-permute-start(bf16[72,2304]{1,0:T(8,128)(2,1)S(1)} %fusion.130), channel_id=1, source_target_pairs={{0,2},{1,3},{2,0},{3,1},{4,6},{5,7},{6,4},{7,5},{8,10},{9,11},{10,... | collective-permute-start | bytes 995336 | tf_op jit(solution)/shard_map/ppermute | solution.py:225
  141.3 10.4 %collective-permute-start.36 = (bf16[72,2304]{1,0:T(8,128)(2,1)S(1)}, bf16[72,2304]{1,0:T(8,128)(2,1)S(1)}, u32[]{:S(2)}, u32[]{:S(2)}) collective-permute-start(bf16[72,2304]{1,0:T(8,128)(2,1)S(1)} %fusion.158), channel_id=1, source_target_pairs={{0,1},{1,0},{2,3},{3,2},{4,5},{5,4},{6,7},{7,6},{8,9},{9,8},{10,11... | collective-permute-start | bytes 995336 | tf_op jit(solution)/shard_map/ppermute | solution.py:225
  141.3 14.6 %collective-permute-start.21 = (bf16[144,1536]{1,0:T(8,128)(2,1)S(1)}, bf16[144,1536]{1,0:T(8,128)(2,1)S(1)}, u32[]{:S(2)}, u32[]{:S(2)}) collective-permute-start(bf16[144,1536]{1,0:T(8,128)(2,1)S(1)} %slice.39), channel_id=1, source_target_pairs={{0,4},{4,0},{8,12},{12,8},{16,20},{20,16},{24,28},{28,24},{1,5},{5... | collective-permute-start | bytes 1327112 | tf_op jit(solution)/shard_map/ppermute | solution.py:225
  156.2 12.6 %collective-permute-start.22 = (bf16[72,1536]{1,0:T(8,128)(2,1)S(1)}, bf16[72,1536]{1,0:T(8,128)(2,1)S(1)}, u32[]{:S(2)}, u32[]{:S(2)}) collective-permute-start(bf16[72,1536]{1,0:T(8,128)(2,1)S(1)} %get-tuple-element.123), channel_id=1, source_target_pairs={{0,8},{4,12},{8,0},{12,4},{16,24},{20,28},{24,16},{28,20},{1,9},{5... | collective-permute-start | bytes 663560 | tf_op jit(solution)/shard_map/ppermute | solution.py:225
  167.7 14.9 %collective-permute-start.39 = (bf16[72,1536]{1,0:T(8,128)(2,1)S(1)}, bf16[72,1536]{1,0:T(8,128)(2,1)S(1)}, u32[]{:S(2)}, u32[]{:S(2)}) collective-permute-start(bf16[72,1536]{1,0:T(8,128)(2,1)S(1)} %add_convert_fusion.10), channel_id=1, source_target_pairs={{0,16},{4,20},{8,24},{12,28},{16,0},{20,4},{24,8},{28,12},{1,17},{... | collective-permute-start | bytes 663560 | tf_op jit(solution)/shard_map/ppermute | solution.py:225
  (48 other events, 647.9 us)

commit v7 on v6

--- a/solution.py
+++ b/solution.py
@@ -8,13 +8,14 @@
 from jax.sharding import PartitionSpec as P
 
 DH = 128
+TILE = 256
 F32 = jnp.float32
 BF16 = jnp.bfloat16
 SCALE = 1.0 / DH
 
 SMEM = pl.BlockSpec(memory_space=pltpu.SMEM)
 VMEM = pl.BlockSpec(memory_space=pltpu.VMEM)
-HBM = pl.BlockSpec(memory_space=pl.ANY)
+HBM = pl.BlockSpec(memory_space=pltpu.HBM)
 LARGE = pl.CostEstimate(flops=1, bytes_accessed=40_000_000, transcendentals=0)
 SMALL = pl.CostEstimate(flops=1, bytes_accessed=1, transcendentals=0)
 
@@ -203,7 +204,7 @@
     kernel(*refs[:scalars], *buffers, *rest)
 
 
-def call(kernel, out_shapes, scalars, arrays, scratch=(), cost=SMALL, fetch=0):
+def call(kernel, out_shapes, scalars, arrays, scratch=(), cost=SMALL, fetch=0, limit=16):
     scratch = list(scratch)
     if fetch:
         kernel = functools.partial(fetched, kernel, len(scalars), fetch)
@@ -215,9 +216,68 @@
         in_specs=[SMEM] * len(scalars) + [HBM] * fetch + [VMEM] * (len(arrays) - fetch),
         out_specs=[VMEM] * len(out_shapes),
         scratch_shapes=scratch,
-        compiler_params=pltpu.CompilerParams(vmem_limit_bytes=16 * 1024 * 1024),
+        compiler_params=pltpu.CompilerParams(vmem_limit_bytes=limit * 1024 * 1024),
         cost_estimate=cost,
     )(*scalars, *arrays)
+
+
+def joined(refs):
+    rows = [ref[...].astype(F32) for ref in refs]
+    return rows[0] if len(rows) == 1 else jnp.concatenate(rows, axis=0)
+
+
+def halves_kernel(turned, place_ref, weight_ref, *refs):
+    sent_ref, kept_ref, rows_ref = refs[-3:]
+    count = (len(refs) - 3) // 2
+    own, other = joined(refs[:count]), joined(refs[count:-3])
+    first = place_ref[2] == 0
+    rows = [jnp.where(first, other, own), jnp.where(first, own, other)]
+    rows_ref[...] = jnp.concatenate(rows, axis=0).astype(BF16)
+    half, width = sent_ref.shape
+    for start in range(0, width, TILE):
+        lanes = slice(start, start + TILE)
+        weight = weight_ref[lanes, :] if turned else weight_ref[:, lanes]
+        out = dot(rows_ref[...], weight, 1, 1 if turned else 0)
+        sent_ref[:, lanes] = out[:half].astype(BF16)
+        kept_ref[:, lanes] = out[half:].astype(BF16)
+
+
+def back_kernel(place_ref, weight_ref, mine_ref, got_ref, own_ref, other_ref, rows_ref):
+    mine, got = mine_ref[...].astype(F32), got_ref[...].astype(F32)
+    first = place_ref[2] == 0
+    rows = [jnp.where(first, mine, got), jnp.where(first, got, mine)]
+    rows_ref[...] = jnp.concatenate(rows, axis=0).astype(BF16)
+    half, width = own_ref.shape
+    for start in range(0, width, TILE):
+        lanes = slice(start, start + TILE)
+        out = dot(rows_ref[...], weight_ref[lanes, :], 1, 1)
+        own_ref[:, lanes] = out[:half].astype(BF16)
+        other_ref[:, lanes] = out[half:].astype(BF16)
+
+
+def matmul_call(kernel, place, weight, arrays, rows, depth, width):
+    out = jax.ShapeDtypeStruct((rows, width), BF16)
+    return call(
+        kernel, [out, out], (place,), (weight, *arrays),
+        [pltpu.VMEM((2 * rows, depth), BF16)], limit=24,
+    )
+
+
+def sides_times(place, own, other, part, weight, turned, *events):
+    blocks = 2 if len(part) * own[part[0]].shape[0] > 72 else 1
+    each = len(part) // blocks
+    join = lambda rows: rows[0] if len(rows) == 1 else jnp.concatenate(rows, axis=0)
+    arrays = [
+        join([side[k] for k in part[i * each : (i + 1) * each]])
+        for side in (own, other)
+        for i in range(blocks)
+    ]
+    arrays[0] = after(arrays[0], *events)
+    rows, depth = blocks * arrays[0].shape[0], arrays[0].shape[1]
+    width = weight.shape[0] if turned else weight.shape[1]
+    return matmul_call(
+        functools.partial(halves_kernel, turned), place, weight, arrays, rows, depth, width
+    )
 
 
 def swap(array, axis, distance):
@@ -288,23 +348,27 @@
     return keep, give
 
 
-def sum_over_cores(own, other, part, multiply, *events):
-    mine = lax.axis_index("exp") & 1
-    rows = lambda flag: jnp.concatenate(
-        [jnp.where(flag == 0, own[k], other[k]) for k in part], axis=0
-    )
-    sent = multiply(after(rows(1 - mine), *events)).astype(BF16)
-    kept = multiply(after(rows(mine), sent)).astype(BF16)
-    return sent, kept
-
-
 def over_cores(sent, kept):
     return (kept.astype(F32) + swap(sent, "exp", 1).astype(F32)).astype(BF16)
 
 
-def sum_over_rest(part, bits):
+def scatter_rest(part, bits):
     for bit in range(1, bits):
-        part = (part.astype(F32) + swap(part, "exp", 1 << bit).astype(F32)).astype(BF16)
+        mine = (lax.axis_index("exp") >> bit) & 1
+        width = part.shape[1] // 2
+        sent = lax.dynamic_slice_in_dim(part, (1 - mine) * width, width, 1)
+        kept = lax.dynamic_slice_in_dim(part, mine * width, width, 1)
+        part = (kept.astype(F32) + swap(sent, "exp", 1 << bit).astype(F32)).astype(BF16)
+    return part
+
+
+def gather_rest(part, bits):
+    for bit in reversed(range(1, bits)):
+        mine = (lax.axis_index("exp") >> bit) & 1
+        got = swap(part, "exp", 1 << bit)
+        part = jnp.concatenate(
+            [jnp.where(mine == 0, part, got), jnp.where(mine == 0, got, part)], axis=1
+        )
     return part
 
 
@@ -347,11 +411,14 @@
     intra, weights = call(
         intra_kernel, [wide, weight_sq], scalars, (queries, keys, values), cost=LARGE, fetch=3
     )
-    by_down = lambda rows: dot(rows, down_local, 1, 1)
-    by_up = lambda rows: dot(rows, up_local, 1, 0)
-
     def hidden_of(part, *events):
-        return over_cores(*sum_over_cores(grad_own, grad_other, part, by_down, *events))
+        return sides_times(place, grad_own, grad_other, part, down_local, True, *events)
+
+    def pre_of(part, *events):
+        return sides_times(place, in_own, in_other, part, up_local, False, *events)
+
+    def over_exp(sent, kept):
+        return scatter_rest(over_cores(sent, kept), bits)
 
     total, partner = scan_total(
         key_mine, key_other, decay_rates, place, block_len, False, send_grad[0]
@@ -366,68 +433,67 @@
     for k in near_part[1:]:
         grad_own[k] = pairs_of(after(send_grad[k], upto), k)
         grad_other[k] = swap(grad_own[k], "ctx", 1)
-    hidden = {0: hidden_of([0], upto)}
-    before = after(before, hidden[0], *[grad_own[k] for k in near_part[1:]])
     keep, give = scan_ends(before, key_mine, partner, decay_rates, place, block_len, False)
     for k in first_far:
         grad_own[k] = pairs_of(after(send_grad[k], give), k)
     given = swap(give, "ctx", 1)
-    for k in near_part[1:]:
-        hidden[k] = hidden_of([k], give)
-    given, *ready = lax.optimization_barrier((given, *[hidden[k] for k in near_part[1:]]))
-    for k, rows in zip(near_part[1:], ready):
-        hidden[k] = rows
     send_in = call(
         attend_kernel, [slots] * experts, scalars, (queries, intra, choose, keep, given),
         [pltpu.VMEM((block_len, group), BF16)],
     )
-    in_own, in_other = {0: send_in[0]}, {}
+    in_own, in_other = {0: send_in[0]}, {0: swap(send_in[0], "ctx", 1)}
     for k in [*near_part[1:], *first_far]:
         in_own[k] = pairs_of(send_in[k], k)
     for k in first_far:
         grad_other[k] = swap(after(grad_own[k], send_in[0]), "ctx", 1)
-        hidden[k] = hidden_of([k])
-    ready = [hidden[k] for k in first_far]
-    for k in second_far:
-        in_own[k] = pairs_of(after(send_in[k], in_own[first_far[0]]), k)
-        grad_own[k] = pairs_of(after(send_grad[k], in_own[first_far[0]]), k)
-    for k in near_part:
+    near_ready = [in_other[0], *[in_own[k] for k in near_part[1:]]]
+    first_ready = [in_own[k] for k in first_far]
+    hidden_near = hidden_of(near_part, *near_ready)
+    hidden_first = hidden_of(first_far, hidden_near[0], *first_ready)
+    for k in near_part[1:]:
         in_other[k] = swap(in_own[k], "ctx", 1)
     for k in first_far:
-        in_other[k] = swap(after(in_own[k], in_other[near_part[-1]]), "ctx", 1)
-    pre_near = over_cores(*sum_over_cores(in_own, in_other, near_part, by_up, *ready))
+        in_other[k] = swap(in_own[k], "ctx", 1)
     for k in second_far:
-        in_other[k] = swap(after(in_own[k], pre_near), "ctx", 1)
-        grad_other[k] = swap(after(grad_own[k], in_other[k]), "ctx", 1)
-    pre_first = over_cores(*sum_over_cores(in_own, in_other, first_far, by_up, pre_near))
+        in_own[k] = pairs_of(after(send_in[k], *first_ready), k)
+        grad_own[k] = pairs_of(after(send_grad[k], *first_ready), k)
+    hidden_near = over_exp(*hidden_near)
+    pre_near = pre_of(near_part, hidden_first[0], hidden_near)
     for k in second_far:
-        hidden[k] = hidden_of([k], pre_first)
-    pre_near = sum_over_rest(pre_near, bits)
-    ready = [hidden[k] for k in second_far]
-    pre_second = over_cores(
-        *sum_over_cores(in_own, in_other, second_far, by_up, pre_near, *ready)
-    )
-
+        in_other[k] = swap(after(in_own[k], pre_near[0]), "ctx", 1)
+        grad_other[k] = swap(after(grad_own[k], pre_near[0]), "ctx", 1)
+    hidden_first = over_exp(*hidden_first)
+    pre_first = pre_of(first_far, pre_near[0], hidden_first)
+    pre_near = over_exp(*pre_near)
+    hidden_second = hidden_of(second_far, pre_first[0], pre_near)
+    pre_second = pre_of(second_far, hidden_second[0])
+
+    def slope_of(pre, grad):
+        return (grad.astype(F32) * silu_slope(pre.astype(F32))).astype(BF16)
+
+    returned = []
+
+    def give_back(slope, *events):
+        slope = gather_rest(slope, bits)
+        got = swap(slope, "exp", 1)
+        got = after(got, *events)
+        back, other = matmul_call(
+            back_kernel, place, up_local, (slope, got), *slope.shape, group
+        )
+        returned.append((back, swap(other, "ctx", 1)))
+        return back
+
+    event = give_back(slope_of(pre_near, hidden_near), pre_second[0])
+    pre_first = over_exp(*pre_first)
+    event = give_back(slope_of(pre_first, hidden_first), event)
+    hidden_second, pre_second = over_exp(*hidden_second), over_exp(*pre_second)
+    give_back(slope_of(pre_second, hidden_second), event)
     homes = {}
-    back = None
-    for part, pre in (
-        (near_part, pre_near),
-        (first_far, pre_first),
-        (second_far, pre_second),
-    ):
-        if back is not None:
-            pre = after(sum_over_rest(pre, bits), back)
-        rows = [sum_over_rest(hidden[k], bits) for k in part]
-        grad = rows[0] if len(rows) == 1 else jnp.concatenate(rows, axis=0)
-        slope = (grad.astype(F32) * silu_slope(pre.astype(F32))).astype(BF16)
-        got = swap(slope, "exp", 1)
-        slope = jnp.concatenate(
-            [jnp.where(core == 0, slope, got), jnp.where(core == 0, got, slope)], axis=0
-        )
-        back = dot(slope, up_local, 1, 1).astype(BF16)
-        blocks = back.reshape(2, len(part) * capacity, group)
-        got = swap(blocks[1], "ctx", 1)
-        rows = (blocks[0].astype(F32) + got.astype(F32)).astype(BF16)
+    for index, part in enumerate((near_part, first_far, second_far)):
+        back, got = returned[index]
+        if index < 2:
+            got = after(got, returned[index + 1][0])
+        rows = (back.astype(F32) + got.astype(F32)).astype(BF16)
         for i, k in enumerate(part):
             homes[k] = pairs_of(rows[i * capacity : (i + 1) * capacity], k)
     homes = [homes[k] for k in range(experts)]

time: 216 us -> 251 us (1.16)
  matrix products: 43.4 us -> 0 us
  Pallas kernels: 14.4 us -> 40.6 us
  waiting for transfers between devices: 84.9 us -> 108 us
  local copies, waits for them, and re-layouts: 8.17 us -> 28 us
  other arithmetic: 6.11 us -> 13 us
    dot_general x17 -> x0, matrix products: 43.4 us -> none  [dot(): lax.dot_general(left, right, (((left_dim,), (right_dim,)), ((), ())), pre...]
    pallas_call x7 -> x16, Pallas kernels: 14.4 us -> 40.6 us  [call(): pl.pallas_call(kernel, out_shape=list(out_shapes), in_specs=[SMEM] * len(...]
    ppermute x41 -> x42, waiting for transfers between devices: 70.6 us -> 96.2 us  [swap(): return lax.ppermute(array, axis, [(i, i ^ distance) for i in range(size)])]
    unnamed x50 -> x104, local copies, waits for them, and re-layouts: 8.07 us -> 27.8 us
    convert_element_type x11 -> x14, other arithmetic: 1.94 us -> 6.3 us  [the longest x6 2.91 us: over_cores(): return (kept.astype(F32) + swap(sent, 'exp', 1).astype(F32)).astype(BF16)]
    ppermute x6, waiting for transfers between devices: 14.4 us -> 11.7 us  [trade(): lax.ppermute(array, 'ctx', [(2 * partner(i) + s, 2 * i + s) for i in rang...]
    ppermute x41 -> x42, starting transfers between devices: 44.5 us -> 46.4 us  [swap(): return lax.ppermute(array, axis, [(i, i ^ distance) for i in range(size)])]
  transfers between devices with their start and end apart: 47 -> 48, of which waited for: 22 -> 21; matrix products, arithmetic and copies ran while one was open for 19% -> 4% of each run, Pallas kernels for 5% -> 11%
where the time goes in v7:
time: 251 us; the launch traced here: 249 us
  waiting for transfers between devices  108 us (43%)
  starting transfers between devices  58.1 us (23%)
  Pallas kernels  40.6 us (16%)
  local copies, waits for them, and re-layouts  28 us (11%)
  other arithmetic  13 us (5%)
    ppermute x42, waiting for transfers between devices, swap(): return lax.ppermute(array, axis, [(i, i ^ distance) for i in range(size)])  96.2 us
    ppermute x42, starting transfers between devices, swap(): return lax.ppermute(array, axis, [(i, i ^ distance) for i in range(size)])  46.4 us
    pallas_call x16, Pallas kernels, call(): pl.pallas_call(kernel, out_shape=list(out_shapes), in_specs=[SMEM] * len(...  40.6 us
    unnamed x104, local copies, waits for them, and re-layouts  27.8 us
    ppermute x6, starting transfers between devices, trade(): lax.ppermute(array, 'ctx', [(2 * partner(i) + s, 2 * i + s) for i in rang...  11.7 us
    ppermute x6, waiting for transfers between devices, trade(): lax.ppermute(array, 'ctx', [(2 * partner(i) + s, 2 * i + s) for i in rang...  11.7 us
  transfers between devices with their start and end apart: 48, of which 21 were waited for; matrix products, arithmetic and copies ran while one was open for 4% of the time, Pallas kernels for 11%

profile of v7, /device:TPU:0, one launch (start us, length us, event | category | flops | bytes accessed | tf_op | source)
XLA Modules:
  0.0 249.0 jit_solution(17782908196618780626)
XLA Ops:
  4.7 3.0 %collective-permute-start = (bf16[6,128,128]{2,1,0:T(8,128)(2,1)S(1)}, bf16[6,128,128]{2,1,0:T(8,128)(2,1)S(1)}, u32[]{:S(2)}, u32[]{:S(2)}) collective-permute-start(bf16[6,128,128]{2,1,0:T(8,128)(2,1)S(1)} %get-tuple-element.68), channel_id=1, source_target_pairs={{0,4},{4,0},{8,12},{12,8},{16,20},{20,16},{24,28},{28,24},{1,5},{5... | collective-permute-start | bytes 589832 | tf_op jit(solution)/shard_map/ppermute | solution.py:285
  20.9 3.1 %shard_map.113 = (f32[128,1536]{1,0:T(8,128)S(1)}, bf16[12,128,128]{2,1,0:T(8,128)(2,1)S(1)}) custom-call(s32[3]{0:T(128)S(1)} %pad_add_fusion.refs_0_.place_ref, f32[12]{0:T(128)S(1)} %copy-done.35, bf16[128,1536]{1,0:T(8,128)(2,1)S(1)} %copy-done.9, bf16[128,1536]{1,0:T(8,128)(2,1)S(1)} %copy-done.5, bf16[128,1536]{1,0:T(8,128)(2,1)S(1)} %copy-done.7), custom_call_target="tpu_custom_call" | custom-call | flops 1 | bytes 40000000 | tf_op jit(solution)/shard_map/pallas_call | solution.py:213
  37.3 4.2 %collective-permute-start.12 = (bf16[72,1536]{1,0:T(8,128)(2,1)S(1)}, bf16[72,1536]{1,0:T(8,128)(2,1)S(1)}, u32[]{:S(2)}, u32[]{:S(2)}) collective-permute-start(bf16[72,1536]{1,0:T(8,128)(2,1)S(1)} %copy-done.44), channel_id=1, source_target_pairs={{0,24},{4,28},{8,16},{12,20},{16,8},{20,12},{24,0},{28,4},{1,25},{... | collective-permute-start | bytes 663560 | tf_op jit(solution)/shard_map/ppermute | solution.py:285
  43.0 4.2 %collective-permute-done.5.other_ref = bf16[6,128,128]{2,1,0:T(8,128)(2,1)S(1)} collective-permute-done((bf16[6,128,128]{2,1,0:T(8,128)(2,1)S(1)}, bf16[6,128,128]{2,1,0:T(8,128)(2,1)S(1)}, u32[]{:S(2)}, u32[]{:S(2)}) %collective-permute-start.5) | collective-permute-done | bytes 196640 | tf_op jit(solution)/shard_map/ppermute | solution.py:285
  63.4 3.0 %copy-done.2 = bf16[1,2304,1536]{2,1,0:T(8,128)(2,1)S(1)} copy-done((bf16[1,2304,1536]{2,1,0:T(8,128)(2,1)S(1)}, bf16[1,2304,1536]{2,1,0:T(8,128)(2,1)}, u32[]{:S(2)}) %copy-start.2) | copy-done | bytes 7077912
  66.4 3.5 %shard_map.116 = (bf16[144,2304]{1,0:T(8,128)(2,1)S(1)}, bf16[144,2304]{1,0:T(8,128)(2,1)S(1)}) custom-call(s32[3]{0:T(128)S(1)} %pad_add_fusion.refs_0_.place_ref, bf16[2304,1536]{1,0:T(8,128)(2,1)S(1)} %bitcast.15, bf16[72,1536]{1,0:T(8,128)(2,1)} %get-tuple-element.73.refs_0_, bf16[72,1536]{1,0:T(8,128)(2,1)S(1)} %collective-permute-done.8.refs_1_, ...), custom_call_target="tpu_custom_call" | custom-call | flops 1 | bytes 1 | tf_op jit(solution)/shard_map/pallas_call | solution.py:213
  70.8 3.7 %shard_map.117 = (bf16[72,2304]{1,0:T(8,128)(2,1)}, bf16[72,2304]{1,0:T(8,128)(2,1)S(1)}) custom-call(s32[3]{0:T(128)S(1)} %pad_add_fusion.refs_0_.place_ref, bf16[2304,1536]{1,0:T(8,128)(2,1)S(1)} %bitcast.18, bf16[72,1536]{1,0:T(8,128)(2,1)S(1)} %collective-permute-done.12.refs_0_, bf16[72,1536]{1,0:T(8,128)(2,1)S(1)} %collective-permute-done.14.refs_1_), custom_call_target="tpu_custom_call" | custom-call | flops 1 | bytes 1 | tf_op jit(solution)/shard_map/pallas_call | solution.py:213
  81.3 4.8 %collective-permute-done.23 = bf16[72,1152]{1,0:T(8,128)(2,1)S(1)} collective-permute-done((bf16[72,1152]{1,0:T(8,128)(2,1)S(1)}, bf16[72,1152]{1,0:T(8,128)(2,1)S(1)}, u32[]{:S(2)}, u32[]{:S(2)}) %collective-permute-start.23) | collective-permute-done | bytes 165920 | tf_op jit(solution)/shard_map/ppermute | solution.py:285
  86.8 4.9 %collective-permute-done.11 = bf16[144,1152]{1,0:T(8,128)(2,1)S(1)} collective-permute-done((bf16[144,1152]{1,0:T(8,128)(2,1)S(1)}, bf16[144,1152]{1,0:T(8,128)(2,1)S(1)}, u32[]{:S(2)}, u32[]{:S(2)}) %collective-permute-start.11) | collective-permute-done | bytes 331808 | tf_op jit(solution)/shard_map/ppermute | solution.py:285
  95.5 3.3 %shard_map.118 = (bf16[144,2304]{1,0:T(8,128)(2,1)S(1)}, bf16[144,2304]{1,0:T(8,128)(2,1)S(1)}) custom-call(s32[3]{0:T(128)S(1)} %pad_add_fusion.refs_0_.place_ref, bf16[1536,2304]{1,0:T(8,128)(2,1)S(1)} %bitcast.7, bf16[72,1536]{1,0:T(8,128)(2,1)S(1)} %copy-done.25, bf16[72,1536]{1,0:T(8,128)(2,1)} %collective-permute-done.7.refs_1_, ...), custom_call_target="tpu_custom_call" | custom-call | flops 1 | bytes 1 | tf_op jit(solution)/shard_map/pallas_call | solution.py:213
  108.4 18.2 %collective-permute-done.21.refs_0_ = bf16[72,1536]{1,0:T(8,128)(2,1)S(1)} collective-permute-done((bf16[72,1536]{1,0:T(8,128)(2,1)S(1)}, bf16[72,1536]{1,0:T(8,128)(2,1)S(1)}, u32[]{:S(2)}, u32[]{:S(2)}) %collective-permute-start.21) | collective-permute-done | bytes 221216 | tf_op jit(solution)/shard_map/ppermute | solution.py:285
  136.2 6.2 %collective-permute-done.17 = bf16[144,1152]{1,0:T(8,128)(2,1)S(1)} collective-permute-done((bf16[144,1152]{1,0:T(8,128)(2,1)S(1)}, bf16[144,1152]{1,0:T(8,128)(2,1)S(1)}, u32[]{:S(2)}, u32[]{:S(2)}) %collective-permute-start.17) | collective-permute-done | bytes 331808 | tf_op jit(solution)/shard_map/ppermute | solution.py:285
  142.7 3.1 %copy-done.3 = bf16[1,2304,1536]{2,1,0:T(8,128)(2,1)S(1)} copy-done((bf16[1,2304,1536]{2,1,0:T(8,128)(2,1)S(1)}, bf16[1,2304,1536]{2,1,0:T(8,128)(2,1)}, u32[]{:S(2)}) %copy-start.3) | copy-done | bytes 7077912
  155.4 4.7 %collective-permute-done.18 = bf16[144,1152]{1,0:T(8,128)(2,1)S(1)} collective-permute-done((bf16[144,1152]{1,0:T(8,128)(2,1)S(1)}, bf16[144,1152]{1,0:T(8,128)(2,1)S(1)}, u32[]{:S(2)}, u32[]{:S(2)}) %collective-permute-start.18) | collective-permute-done | bytes 331808 | tf_op jit(solution)/shard_map/ppermute | solution.py:285
  160.2 3.5 %collective-permute-done.34 = bf16[72,1152]{1,0:T(8,128)(2,1)S(1)} collective-permute-done((bf16[72,1152]{1,0:T(8,128)(2,1)S(1)}, bf16[72,1152]{1,0:T(8,128)(2,1)S(1)}, u32[]{:S(2)}, u32[]{:S(2)}) %collective-permute-start.34) | collective-permute-done | bytes 165920 | tf_op jit(solution)/shard_map/ppermute | solution.py:285
  168.2 3.8 %collective-permute-done.37 = bf16[72,1152]{1,0:T(8,128)(2,1)S(1)} collective-permute-done((bf16[72,1152]{1,0:T(8,128)(2,1)S(1)}, bf16[72,1152]{1,0:T(8,128)(2,1)S(1)}, u32[]{:S(2)}, u32[]{:S(2)}) %collective-permute-start.37) | collective-permute-done | bytes 165920 | tf_op jit(solution)/shard_map/ppermute | solution.py:285
  184.2 5.0 %collective-permute-done.39 = bf16[72,1536]{1,0:T(8,128)(2,1)S(1)} collective-permute-done((bf16[72,1536]{1,0:T(8,128)(2,1)S(1)}, bf16[72,1536]{1,0:T(8,128)(2,1)S(1)}, u32[]{:S(2)}, u32[]{:S(2)}) %collective-permute-start.39) | collective-permute-done | bytes 221216 | tf_op jit(solution)/shard_map/ppermute | solution.py:285
  189.4 13.6 %collective-permute-done.41 = bf16[72,1536]{1,0:T(8,128)(2,1)S(1)} collective-permute-done((bf16[72,1536]{1,0:T(8,128)(2,1)S(1)}, bf16[72,1536]{1,0:T(8,128)(2,1)S(1)}, u32[]{:S(2)}, u32[]{:S(2)}) %collective-permute-start.41) | collective-permute-done | bytes 221216 | tf_op jit(solution)/shard_map/ppermute | solution.py:285
  205.3 8.1 %collective-permute-done.42.refs_3_ = bf16[72,1536]{1,0:T(8,128)(2,1)S(1)} collective-permute-done((bf16[72,1536]{1,0:T(8,128)(2,1)S(1)}, bf16[72,1536]{1,0:T(8,128)(2,1)S(1)}, u32[]{:S(2)}, u32[]{:S(2)}) %collective-permute-start.42) | collective-permute-done | bytes 221216 | tf_op jit(solution)/shard_map/ppermute | solution.py:285
  213.4 3.4 %collective-permute-done.32.refs_1_ = bf16[72,1536]{1,0:T(8,128)(2,1)S(1)} collective-permute-done((bf16[72,1536]{1,0:T(8,128)(2,1)S(1)}, bf16[72,1536]{1,0:T(8,128)(2,1)S(1)}, u32[]{:S(2)}, u32[]{:S(2)}) %collective-permute-start.32) | collective-permute-done | bytes 221216 | tf_op jit(solution)/shard_map/ppermute | solution.py:285
  219.5 5.5 %collective-permute-done.43 = bf16[6,128,128]{2,1,0:T(8,128)(2,1)S(1)} collective-permute-done((bf16[6,128,128]{2,1,0:T(8,128)(2,1)S(1)}, bf16[6,128,128]{2,1,0:T(8,128)(2,1)S(1)}, u32[]{:S(2)}, u32[]{:S(2)}) %collective-permute-start.43) | collective-permute-done | bytes 196640 | tf_op jit(solution)/shard_map/ppermute | solution.py:285
  225.3 5.9 %collective-permute-done.44 = bf16[6,128,128]{2,1,0:T(8,128)(2,1)S(1)} collective-permute-done((bf16[6,128,128]{2,1,0:T(8,128)(2,1)S(1)}, bf16[6,128,128]{2,1,0:T(8,128)(2,1)S(1)}, u32[]{:S(2)}, u32[]{:S(2)}) %collective-permute-start.44) | collective-permute-done | bytes 196640 | tf_op jit(solution)/shard_map/ppermute | solution.py:289
  235.4 5.8 %collective-permute-done.45 = bf16[6,128,128]{2,1,0:T(8,128)(2,1)S(1)} collective-permute-done((bf16[6,128,128]{2,1,0:T(8,128)(2,1)S(1)}, bf16[6,128,128]{2,1,0:T(8,128)(2,1)S(1)}, u32[]{:S(2)}, u32[]{:S(2)}) %collective-permute-start.45) | collective-permute-done | bytes 196640 | tf_op jit(solution)/shard_map/ppermute | solution.py:289
  243.0 4.0 %shard_map.126 = (bf16[128,1536]{1,0:T(8,128)(2,1)}, f32[128,1536]{1,0:T(8,128)S(1)}, f32[128,1536]{1,0:T(8,128)S(1)}) custom-call(s32[3]{0:T(128)S(1)} %pad_add_fusion.refs_0_.place_ref, f32[12]{0:T(128)S(1)} %copy-done.35, bf16[128,1536]{1,0:T(8,128)(2,1)S(1)} %copy-done.11, bf16[128,1536]{1,0:T(8,128)(2,1)S(1)} %copy-done.5, ...), custom_call_target="tpu_custom_call" | custom-call | flops 1 | bytes 1 | tf_op jit(solution)/shard_map/pallas_call | solution.py:213
  (230 shorter events, 119.2 us)
Async XLA Ops:
  33.6 21.9 %collective-permute-start.8 = (bf16[72,1536]{1,0:T(8,128)(2,1)}, bf16[72,1536]{1,0:T(8,128)(2,1)S(1)}, u32[]{:S(2)}, u32[]{:S(2)}) collective-permute-start(bf16[72,1536]{1,0:T(8,128)(2,1)} %copy-done.45), channel_id=1, source_target_pairs={{0,8},{4,12},{8,0},{12,4},{16,24},{20,28},{24,16},{28,20},{1,9},{5... | collective-permute-start | bytes 663560 | tf_op jit(solution)/shard_map/ppermute | solution.py:285
  37.3 19.9 %collective-permute-start.12 = (bf16[72,1536]{1,0:T(8,128)(2,1)S(1)}, bf16[72,1536]{1,0:T(8,128)(2,1)S(1)}, u32[]{:S(2)}, u32[]{:S(2)}) collective-permute-start(bf16[72,1536]{1,0:T(8,128)(2,1)S(1)} %copy-done.44), channel_id=1, source_target_pairs={{0,24},{4,28},{8,16},{12,20},{16,8},{20,12},{24,0},{28,4},{1,25},{... | collective-permute-start | bytes 663560 | tf_op jit(solution)/shard_map/ppermute | solution.py:285
  56.0 14.8 %collective-permute-start.13 = (bf16[72,1536]{1,0:T(8,128)(2,1)S(1)}, bf16[72,1536]{1,0:T(8,128)(2,1)S(1)}, u32[]{:S(2)}, u32[]{:S(2)}) collective-permute-start(bf16[72,1536]{1,0:T(8,128)(2,1)S(1)} %get-tuple-element.80), channel_id=1, source_target_pairs={{0,24},{4,28},{8,16},{12,20},{16,8},{20,12},{24,0},{28,4},{1,25},{... | collective-permute-start | bytes 663560 | tf_op jit(solution)/shard_map/ppermute | solution.py:285
  57.3 13.5 %collective-permute-start.14 = (bf16[72,1536]{1,0:T(8,128)(2,1)S(1)}, bf16[72,1536]{1,0:T(8,128)(2,1)S(1)}, u32[]{:S(2)}, u32[]{:S(2)}) collective-permute-start(bf16[72,1536]{1,0:T(8,128)(2,1)S(1)} %collective-permute-done.12.refs_0_), channel_id=1, source_target_pairs={{0,4},{4,0},{8,12},{12,8},{16,20},{20,16},{24,28},{28,24},{1,5},{5... | collective-permute-start | bytes 663560 | tf_op jit(solution)/shard_map/ppermute | solution.py:285
  75.7 16.8 %collective-permute-start.15 = (bf16[72,1536]{1,0:T(8,128)(2,1)}, bf16[72,1536]{1,0:T(8,128)(2,1)S(1)}, u32[]{:S(2)}, u32[]{:S(2)}) collective-permute-start(bf16[72,1536]{1,0:T(8,128)(2,1)} %collective-permute-done.7.refs_1_), channel_id=1, source_target_pairs={{0,4},{4,0},{8,12},{12,8},{16,20},{20,16},{24,28},{28,24},{1,5},{5... | collective-permute-start | bytes 663560 | tf_op jit(solution)/shard_map/ppermute | solution.py:285
  76.9 21.9 %collective-permute-start.24 = (bf16[72,1536]{1,0:T(8,128)(2,1)}, bf16[72,1536]{1,0:T(8,128)(2,1)S(1)}, u32[]{:S(2)}, u32[]{:S(2)}) collective-permute-start(bf16[72,1536]{1,0:T(8,128)(2,1)} %copy-done.28), channel_id=1, source_target_pairs={{0,4},{4,0},{8,12},{12,8},{16,20},{20,16},{24,28},{28,24},{1,5},{5... | collective-permute-start | bytes 663560 | tf_op jit(solution)/shard_map/ppermute | solution.py:285
  80.7 11.0 %collective-permute-start.11 = (bf16[144,1152]{1,0:T(8,128)(2,1)S(1)}, bf16[144,1152]{1,0:T(8,128)(2,1)S(1)}, u32[]{:S(2)}, u32[]{:S(2)}) collective-permute-start(bf16[144,1152]{1,0:T(8,128)(2,1)S(1)} %constant_dynamic-slice_fusion.5), channel_id=1, source_target_pairs={{0,2},{1,3},{2,0},{3,1},{4,6},{5,7},{6,4},{7,5},{8,10},{9,11},{10,... | collective-permute-start | bytes 995336 | tf_op jit(solution)/shard_map/ppermute | solution.py:285
  103.7 24.1 %collective-permute-start.20 = (bf16[72,1536]{1,0:T(8,128)(2,1)S(1)}, bf16[72,1536]{1,0:T(8,128)(2,1)S(1)}, u32[]{:S(2)}, u32[]{:S(2)}) collective-permute-start(bf16[72,1536]{1,0:T(8,128)(2,1)S(1)} %copy-done.42), channel_id=1, source_target_pairs={{0,16},{4,20},{8,24},{12,28},{16,0},{20,4},{24,8},{28,12},{1,17},{... | collective-permute-start | bytes 663560 | tf_op jit(solution)/shard_map/ppermute | solution.py:285
  105.3 21.3 %collective-permute-start.21 = (bf16[72,1536]{1,0:T(8,128)(2,1)S(1)}, bf16[72,1536]{1,0:T(8,128)(2,1)S(1)}, u32[]{:S(2)}, u32[]{:S(2)}) collective-permute-start(bf16[72,1536]{1,0:T(8,128)(2,1)S(1)} %copy-done.40), channel_id=1, source_target_pairs={{0,16},{4,20},{8,24},{12,28},{16,0},{20,4},{24,8},{28,12},{1,17},{... | collective-permute-start | bytes 663560 | tf_op jit(solution)/shard_map/ppermute | solution.py:285
  106.7 24.8 %collective-permute-start.16 = (bf16[144,2304]{1,0:T(8,128)(2,1)S(1)}, bf16[144,2304]{1,0:T(8,128)(2,1)}, u32[]{:S(2)}, u32[]{:S(2)}) collective-permute-start(bf16[144,2304]{1,0:T(8,128)(2,1)S(1)} %get-tuple-element.86), channel_id=1, source_target_pairs={{0,1},{1,0},{2,3},{3,2},{4,5},{5,4},{6,7},{7,6},{8,9},{9,8},{10,11... | collective-permute-start | bytes 1990664 | tf_op jit(solution)/shard_map/ppermute | solution.py:285
  106.8 21.9 %collective-permute-start.29 = (bf16[72,1152]{1,0:T(8,128)(2,1)S(1)}, bf16[72,1152]{1,0:T(8,128)(2,1)}, u32[]{:S(2)}, u32[]{:S(2)}) collective-permute-start(bf16[72,1152]{1,0:T(8,128)(2,1)S(1)} %constant_dynamic-slice_fusion.2), channel_id=1, source_target_pairs={{0,2},{1,3},{2,0},{3,1},{4,6},{5,7},{6,4},{7,5},{8,10},{9,11},{10,... | collective-permute-start | bytes 497672 | tf_op jit(solution)/shard_map/ppermute | solution.py:285
  126.6 16.0 %collective-permute-start.25 = (bf16[72,1536]{1,0:T(8,128)(2,1)S(1)}, bf16[72,1536]{1,0:T(8,128)(2,1)S(1)}, u32[]{:S(2)}, u32[]{:S(2)}) collective-permute-start(bf16[72,1536]{1,0:T(8,128)(2,1)S(1)} %collective-permute-done.21.refs_0_), channel_id=1, source_target_pairs={{0,4},{4,0},{8,12},{12,8},{16,20},{20,16},{24,28},{28,24},{1,5},{5... | collective-permute-start | bytes 663560 | tf_op jit(solution)/shard_map/ppermute | solution.py:285
  127.8 23.1 %collective-permute-start.26 = (bf16[72,1536]{1,0:T(8,128)(2,1)S(1)}, bf16[72,1536]{1,0:T(8,128)(2,1)S(1)}, u32[]{:S(2)}, u32[]{:S(2)}) collective-permute-start(bf16[72,1536]{1,0:T(8,128)(2,1)S(1)} %collective-permute-done.20.refs_0_), channel_id=1, source_target_pairs={{0,4},{4,0},{8,12},{12,8},{16,20},{20,16},{24,28},{28,24},{1,5},{5... | collective-permute-start | bytes 663560 | tf_op jit(solution)/shard_map/ppermute | solution.py:285
  132.9 9.5 %collective-permute-start.17 = (bf16[144,1152]{1,0:T(8,128)(2,1)S(1)}, bf16[144,1152]{1,0:T(8,128)(2,1)S(1)}, u32[]{:S(2)}, u32[]{:S(2)}) collective-permute-start(bf16[144,1152]{1,0:T(8,128)(2,1)S(1)} %constant_dynamic-slice_fusion.4), channel_id=1, source_target_pairs={{0,2},{1,3},{2,0},{3,1},{4,6},{5,7},{6,4},{7,5},{8,10},{9,11},{10,... | collective-permute-start | bytes 995336 | tf_op jit(solution)/shard_map/ppermute | solution.py:285
  148.9 26.1 %collective-permute-start.31 = (bf16[72,2304]{1,0:T(8,128)(2,1)S(1)}, bf16[72,2304]{1,0:T(8,128)(2,1)S(1)}, u32[]{:S(2)}, u32[]{:S(2)}) collective-permute-start(bf16[72,2304]{1,0:T(8,128)(2,1)S(1)} %pad_maximum_fusion.1.mine_ref), channel_id=1, source_target_pairs={{0,1},{1,0},{2,3},{3,2},{4,5},{5,4},{6,7},{7,6},{8,9},{9,8},{10,11... | collective-permute-start | bytes 995336 | tf_op jit(solution)/shard_map/ppermute | solution.py:285
  149.5 10.7 %collective-permute-start.18 = (bf16[144,1152]{1,0:T(8,128)(2,1)S(1)}, bf16[144,1152]{1,0:T(8,128)(2,1)S(1)}, u32[]{:S(2)}, u32[]{:S(2)}) collective-permute-start(bf16[144,1152]{1,0:T(8,128)(2,1)S(1)} %fusion.6), channel_id=1, source_target_pairs={{0,2},{1,3},{2,0},{3,1},{4,6},{5,7},{6,4},{7,5},{8,10},{9,11},{10,... | collective-permute-start | bytes 995336 | tf_op jit(solution)/shard_map/ppermute | solution.py:285
  153.1 10.6 %collective-permute-start.34 = (bf16[72,1152]{1,0:T(8,128)(2,1)S(1)}, bf16[72,1152]{1,0:T(8,128)(2,1)S(1)}, u32[]{:S(2)}, u32[]{:S(2)}) collective-permute-start(bf16[72,1152]{1,0:T(8,128)(2,1)S(1)} %constant_dynamic-slice_fusion.1), channel_id=1, source_target_pairs={{0,2},{1,3},{2,0},{3,1},{4,6},{5,7},{6,4},{7,5},{8,10},{9,11},{10,... | collective-permute-start | bytes 497672 | tf_op jit(solution)/shard_map/ppermute | solution.py:285
  154.8 11.6 %collective-permute-start.36 = (bf16[72,1152]{1,0:T(8,128)(2,1)S(1)}, bf16[72,1152]{1,0:T(8,128)(2,1)S(1)}, u32[]{:S(2)}, u32[]{:S(2)}) collective-permute-start(bf16[72,1152]{1,0:T(8,128)(2,1)S(1)} %constant_dynamic-slice_fusion), channel_id=1, source_target_pairs={{0,2},{1,3},{2,0},{3,1},{4,6},{5,7},{6,4},{7,5},{8,10},{9,11},{10,... | collective-permute-start | bytes 497672 | tf_op jit(solution)/shard_map/ppermute | solution.py:285
  182.2 22.9 %collective-permute-start.27 = (bf16[144,1536]{1,0:T(8,128)(2,1)S(1)}, bf16[144,1536]{1,0:T(8,128)(2,1)S(1)}, u32[]{:S(2)}, u32[]{:S(2)}) collective-permute-start(bf16[144,1536]{1,0:T(8,128)(2,1)S(1)} %get-tuple-element.102), channel_id=1, source_target_pairs={{0,4},{4,0},{8,12},{12,8},{16,20},{20,16},{24,28},{28,24},{1,5},{5... | collective-permute-start | bytes 1327112 | tf_op jit(solution)/shard_map/ppermute | solution.py:285
  183.1 20.0 %collective-permute-start.41 = (bf16[72,1536]{1,0:T(8,128)(2,1)S(1)}, bf16[72,1536]{1,0:T(8,128)(2,1)S(1)}, u32[]{:S(2)}, u32[]{:S(2)}) collective-permute-start(bf16[72,1536]{1,0:T(8,128)(2,1)S(1)} %get-tuple-element.112), channel_id=1, source_target_pairs={{0,4},{4,0},{8,12},{12,8},{16,20},{20,16},{24,28},{28,24},{1,5},{5... | collective-permute-start | bytes 663560 | tf_op jit(solution)/shard_map/ppermute | solution.py:285
  189.4 16.0 %collective-permute-start.40 = (bf16[72,1536]{1,0:T(8,128)(2,1)S(1)}, bf16[72,1536]{1,0:T(8,128)(2,1)S(1)}, u32[]{:S(2)}, u32[]{:S(2)}) collective-permute-start(bf16[72,1536]{1,0:T(8,128)(2,1)S(1)} %add_convert_fusion.10), channel_id=1, source_target_pairs={{0,16},{4,20},{8,24},{12,28},{16,0},{20,4},{24,8},{28,12},{1,17},{... | collective-permute-start | bytes 663560 | tf_op jit(solution)/shard_map/ppermute | solution.py:285
  203.1 10.3 %collective-permute-start.42 = (bf16[72,1536]{1,0:T(8,128)(2,1)S(1)}, bf16[72,1536]{1,0:T(8,128)(2,1)S(1)}, u32[]{:S(2)}, u32[]{:S(2)}) collective-permute-start(bf16[72,1536]{1,0:T(8,128)(2,1)S(1)} %add_convert_fusion.9), channel_id=1, source_target_pairs={{0,24},{4,28},{8,16},{12,20},{16,8},{20,12},{24,0},{28,4},{1,25},{... | collective-permute-start | bytes 663560 | tf_op jit(solution)/shard_map/ppermute | solution.py:285
  205.2 11.5 %collective-permute-start.32 = (bf16[72,1536]{1,0:T(8,128)(2,1)S(1)}, bf16[72,1536]{1,0:T(8,128)(2,1)S(1)}, u32[]{:S(2)}, u32[]{:S(2)}) collective-permute-start(bf16[72,1536]{1,0:T(8,128)(2,1)S(1)} %get-tuple-element.133), channel_id=1, source_target_pairs={{0,8},{4,12},{8,0},{12,4},{16,24},{20,28},{24,16},{28,20},{1,9},{5... | collective-permute-start | bytes 663560 | tf_op jit(solution)/shard_map/ppermute | solution.py:285
  231.3 9.9 %collective-permute-start.45 = (bf16[6,128,128]{2,1,0:T(8,128)(2,1)S(1)}, bf16[6,128,128]{2,1,0:T(8,128)(2,1)S(1)}, u32[]{:S(2)}, u32[]{:S(2)}) collective-permute-start(bf16[6,128,128]{2,1,0:T(8,128)(2,1)S(1)} %add_convert_fusion.11), channel_id=1, source_target_pairs={{16,0},{20,4},{8,8},{12,12},{0,16},{4,20},{24,24},{28,28},{17,1},{... | collective-permute-start | bytes 589832 | tf_op jit(solution)/shard_map/ppermute | solution.py:289
  (76 other events, 606.5 us)

commit v8 on v5

--- a/solution.py
+++ b/solution.py
@@ -14,8 +14,6 @@
 
 SMEM = pl.BlockSpec(memory_space=pltpu.SMEM)
 VMEM = pl.BlockSpec(memory_space=pltpu.VMEM)
-LARGE = pl.CostEstimate(flops=1, bytes_accessed=40_000_000, transcendentals=0)
-SMALL = pl.CostEstimate(flops=1, bytes_accessed=1, transcendentals=0)
 
 
 def dot(left, right, left_dim, right_dim):
@@ -188,7 +186,7 @@
         ).astype(BF16)
 
 
-def call(kernel, out_shapes, scalars, arrays, scratch=(), cost=SMALL):
+def call(kernel, out_shapes, scalars, arrays, scratch=(), micros=1.0):
     return pl.pallas_call(
         kernel,
         out_shape=list(out_shapes),
@@ -196,7 +194,9 @@
         out_specs=[VMEM] * len(out_shapes),
         scratch_shapes=list(scratch),
         compiler_params=pltpu.CompilerParams(vmem_limit_bytes=16 * 1024 * 1024),
-        cost_estimate=cost,
+        cost_estimate=pl.CostEstimate(
+            flops=1, bytes_accessed=int(micros * 3.69e6), transcendentals=0
+        ),
     )(*scalars, *arrays)
 
 
@@ -266,6 +266,18 @@
     keep = jnp.where(side == 0, before, second_meets).astype(BF16)
     give = jnp.where(side == 0, second_meets, before).astype(BF16)
     return keep, give
+
+
+def sides_product(own, other, part, multiply, *events):
+    rows = [side[k] for side in (own, other) for k in part]
+    whole = multiply(after(jnp.concatenate(rows, axis=0), *events)).astype(BF16)
+    return whole.reshape(2, whole.shape[0] // 2, whole.shape[1])
+
+
+def sum_sides(whole):
+    mine = lax.axis_index("exp") & 1
+    sent = lax.dynamic_index_in_dim(whole, 1 - mine, 0, False)
+    return over_cores(sent, lax.dynamic_index_in_dim(whole, mine, 0, False))
 
 
 def sum_over_cores(own, other, part, multiply, *events):
@@ -320,58 +332,66 @@
     key_mine, key_other = call(key_state_kernel, [states] * 2, scalars, (keys, values))
     choose, weigh, *send_grad = call(
         route_kernel, [choose_table, weigh_table] + [slots] * experts,
-        (place,), (routes.T, gate_weights.T, out_grad)
+        (place,), (routes.T, gate_weights.T, out_grad), micros=1.2
     )
     intra, weights = call(
-        intra_kernel, [wide, weight_sq], scalars, (queries, keys, values), cost=LARGE
+        intra_kernel, [wide, weight_sq], scalars, (queries, keys, values), micros=2.5
     )
 
     total, partner = scan_total(
         key_mine, key_other, decay_rates, place, block_len, False, send_grad[0]
     )
-    grad_own = {0: send_grad[0]}
-    for k in [*near_part[1:], *first_far]:
+    by_down = lambda rows: dot(rows, down_local, 1, 1)
+    by_up = lambda rows: dot(rows, up_local, 1, 0)
+    grad_own, grad_other = {0: send_grad[0]}, {0: swap(send_grad[0], "ctx", 1)}
+    for k in near_part[1:]:
         grad_own[k] = pairs_of(after(send_grad[k], total), k)
+        grad_other[k] = swap(grad_own[k], "ctx", 1)
     before = None
     for index, reach in enumerate(reaches):
-        events = [intra] if index == 1 else []
+        events = [intra, grad_other[0], *grad_own.values()] if index == 1 else []
         before, upto = scan_step(
             before, total, reach, decay_rates, place, block_len, False, *events
         )
+    hidden_near = sides_product(grad_own, grad_other, near_part, by_down, upto)
+    before, hidden_near = lax.optimization_barrier((before, hidden_near))
+    hidden_near = sum_sides(hidden_near)
     keep, give = scan_ends(before, key_mine, partner, decay_rates, place, block_len, False)
-    grad_other = {0: swap(after(grad_own[0], total), "ctx", 1)}
-    for k in [*near_part[1:], *first_far]:
-        grad_other[k] = swap(after(grad_own[k], upto), "ctx", 1)
-    for k in second_far:
+    for k in first_far:
         grad_own[k] = pairs_of(after(send_grad[k], give), k)
 
-    by_down = lambda rows: dot(rows, down_local, 1, 1)
-    by_up = lambda rows: dot(rows, up_local, 1, 0)
     given = swap(give, "ctx", 1)
-    hidden_near = over_cores(*sum_over_cores(grad_own, grad_other, near_part, by_down, give))
     given, hidden_near = lax.optimization_barrier((given, hidden_near))
     send_in = call(
         attend_kernel, [slots] * experts, scalars, (queries, intra, choose, keep, given),
         [pltpu.VMEM((block_len, group), BF16)],
     )
-    for k in second_far:
+    hidden_near = sum_over_rest(hidden_near, bits)
+    for k in first_far:
         grad_other[k] = swap(after(grad_own[k], send_in[0]), "ctx", 1)
-    hidden_first = over_cores(
-        *sum_over_cores(grad_own, grad_other, first_far, by_down, send_in[0])
+    hidden_first = sum_sides(
+        sides_product(grad_own, grad_other, first_far, by_down, send_in[0])
     )
 
     in_own, in_other = {0: send_in[0]}, {}
     for k in [*near_part[1:], *first_far]:
         in_own[k] = pairs_of(send_in[k], k)
     for k in second_far:
-        in_own[k] = pairs_of(after(send_in[k], in_own[first_far[0]], hidden_first), k)
-    for k in range(experts):
+        in_own[k] = pairs_of(after(send_in[k], in_own[first_far[0]]), k)
+        grad_own[k] = pairs_of(after(send_grad[k], in_own[first_far[0]]), k)
+    for k in [*near_part, *first_far]:
         in_other[k] = swap(in_own[k], "ctx", 1)
 
-    pre_near = over_cores(*sum_over_cores(in_own, in_other, near_part, by_up, hidden_first))
-    pre_first = over_cores(*sum_over_cores(in_own, in_other, first_far, by_up, pre_near))
-    hidden_second = over_cores(
-        *sum_over_cores(grad_own, grad_other, second_far, by_down, pre_first)
+    pre_near = over_cores(
+        *sum_over_cores(in_own, in_other, near_part, by_up, hidden_first, hidden_near)
+    )
+    pre_first = sum_over_cores(in_own, in_other, first_far, by_up, pre_near)
+    for k in second_far:
+        grad_other[k] = swap(after(grad_own[k], pre_first[0]), "ctx", 1)
+        in_other[k] = swap(after(in_own[k], pre_first[0]), "ctx", 1)
+    pre_first = over_cores(*pre_first)
+    hidden_second = sum_sides(
+        sides_product(grad_own, grad_other, second_far, by_down, pre_first)
     )
     pre_second = over_cores(*sum_over_cores(in_own, in_other, second_far, by_up, hidden_second))
 
@@ -382,7 +402,9 @@
         (first_far, pre_first, hidden_first),
         (second_far, pre_second, hidden_second),
     ):
-        pre, hidden = sum_over_rest(pre, bits), sum_over_rest(hidden, bits)
+        pre = sum_over_rest(pre, bits)
+        if part is not near_part:
+            hidden = sum_over_rest(hidden, bits)
         slope = (hidden.astype(F32) * silu_slope(pre.astype(F32))).astype(BF16)
         got = swap(slope, "exp", 1)
         if back is not None:
@@ -412,11 +434,11 @@
     leaving = (keep, swap(give, "ctx", 1))
     query_g, key_near, value_near = call(
         near_kernel, [slim, wide, wide], scalars,
-        (queries, keys, values, grad_out, keep_in, given, weights)
+        (queries, keys, values, grad_out, keep_in, given, weights), micros=4.0
     )
     key_g, value_g = call(
         far_kernel, [slim, slim], scalars,
-        (keys, values, key_near, value_near) + leaving
+        (keys, values, key_near, value_near) + leaving, micros=2.0
     )
     return query_g, key_g, value_g
 

time: 196 us -> 212 us (1.082); the launches traced: 196 us -> 209 us
  other arithmetic: 4.42 us -> 14 us
  matrix products: 32.3 us -> 28.7 us
  waiting for transfers between devices: 82.1 us -> 85.1 us
  starting transfers between devices: 54.4 us -> 57.1 us
    ppermute x6, starting transfers between devices: 9.3 us -> 14 us  [trade(): lax.ppermute(array, 'ctx', [(2 * partner(i) + s, 2 * i + s) for i in rang...]
    ppermute x39, waiting for transfers between devices: 71 us -> 75.5 us  [swap(): return lax.ppermute(array, axis, [(i, i ^ distance) for i in range(size)])]
    dot_general x15 -> x12, matrix products: 32.3 us -> 28.7 us  [dot(): lax.dot_general(left, right, (((left_dim,), (right_dim,)), ((), ())), pre...]
    convert_element_type x0 -> x4, other arithmetic: none -> 2.61 us  [the longest x3 2.45 us: over_cores(): return (kept.astype(F32) + swap(sent, 'exp', 1).astype(F32)).astype(BF16)]
    concatenate x0 -> x3, other arithmetic: none -> 2.25 us  [sides_product(): whole = multiply(after(jnp.concatenate(rows, axis=0), *events)).astype(BF16)]
    unnamed x36 -> x44, local copies, waits for them, and re-layouts: 8.05 us -> 8.26 us
  transfers between devices with their start and end apart: 45 -> 45, of which waited for: 22 -> 21; matrix products, arithmetic and copies ran while one was open for 18% -> 16% of each run, Pallas kernels for 5% -> 5%
where the time goes in v8:
time: 212 us; the launch traced here: 209 us
  waiting for transfers between devices  85.1 us (40%)
  starting transfers between devices  57.1 us (27%)
  matrix products  28.7 us (14%)
  other arithmetic  14 us (7%)
  Pallas kernels  13.8 us (7%)
  local copies, waits for them, and re-layouts  9.3 us (4%)
    ppermute x39, waiting for transfers between devices, swap(): return lax.ppermute(array, axis, [(i, i ^ distance) for i in range(size)])  75.5 us
    ppermute x39, starting transfers between devices, swap(): return lax.ppermute(array, axis, [(i, i ^ distance) for i in range(size)])  43.1 us
    dot_general x12, matrix products, dot(): lax.dot_general(left, right, (((left_dim,), (right_dim,)), ((), ())), pre...  28.7 us
    ppermute x6, starting transfers between devices, trade(): lax.ppermute(array, 'ctx', [(2 * partner(i) + s, 2 * i + s) for i in rang...  14 us
    pallas_call x7, Pallas kernels, call(): pl.pallas_call(kernel, out_shape=list(out_shapes), in_specs=[SMEM] * len(...  13.8 us
    ppermute x6, waiting for transfers between devices, trade(): lax.ppermute(array, 'ctx', [(2 * partner(i) + s, 2 * i + s) for i in rang...  9.55 us
    unnamed x44, local copies, waits for them, and re-layouts  8.26 us
  transfers between devices with their start and end apart: 45, of which 21 were waited for; matrix products, arithmetic and copies ran while one was open for 16% of the time, Pallas kernels for 5%

profile of v8, /device:TPU:0, one launch (start us, length us, event | category | flops | bytes accessed | tf_op | source)
XLA Modules:
  0.0 209.2 jit_solution(2803555117568947569)
XLA Ops:
  4.3 3.0 %collective-permute-start = (bf16[6,128,128]{2,1,0:T(8,128)(2,1)S(1)}, bf16[6,128,128]{2,1,0:T(8,128)(2,1)}, u32[]{:S(2)}, u32[]{:S(2)}) collective-permute-start(bf16[6,128,128]{2,1,0:T(8,128)(2,1)S(1)} %get-tuple-element.51), channel_id=1, source_target_pairs={{0,4},{4,0},{8,12},{12,8},{16,20},{20,16},{24,28},{28,24},{1,5},{5... | collective-permute-start | bytes 589832 | tf_op jit(solution)/shard_map/ppermute | solution.py:205
  22.2 4.0 %collective-permute-done.3 = bf16[72,1536]{1,0:T(8,128)(2,1)} collective-permute-done((bf16[72,1536]{1,0:T(8,128)(2,1)}, bf16[72,1536]{1,0:T(8,128)(2,1)}, u32[]{:S(2)}, u32[]{:S(2)}) %collective-permute-start.3) | collective-permute-done | bytes 221216 | tf_op jit(solution)/shard_map/ppermute | solution.py:205
  29.2 3.0 %collective-permute-start.5 = (bf16[6,128,128]{2,1,0:T(8,128)(2,1)}, bf16[6,128,128]{2,1,0:T(8,128)(2,1)}, u32[]{:S(2)}, u32[]{:S(2)}) collective-permute-start(bf16[6,128,128]{2,1,0:T(8,128)(2,1)} %add_convert_fusion.11), channel_id=1, source_target_pairs={{0,0},{4,4},{16,8},{20,12},{8,16},{12,20},{24,24},{28,28},{1,1},{5... | collective-permute-start | bytes 589832 | tf_op jit(solution)/shard_map/ppermute | solution.py:209
  34.6 3.8 %collective-permute-done.6 = bf16[72,1536]{1,0:T(8,128)(2,1)S(1)} collective-permute-done((bf16[72,1536]{1,0:T(8,128)(2,1)}, bf16[72,1536]{1,0:T(8,128)(2,1)S(1)}, u32[]{:S(2)}, u32[]{:S(2)}) %collective-permute-start.6) | collective-permute-done | bytes 221216 | tf_op jit(solution)/shard_map/ppermute | solution.py:205
  39.4 5.3 %fusion.24 = bf16[288,2304]{1,0:T(8,128)(2,1)S(1)} fusion(bf16[288,1536]{1,0:T(8,128)(2,1)S(1)} %pad_maximum_fusion, bf16[1,2304,1536]{2,1,0:T(8,128)(2,1)} %param.14), kind=kOutput, calls=%fused_computation.24 | convolution fusion | flops 2039095296 | bytes 9289728 | tf_op jit(solution)/shard_map/dot_general | solution.py:20
  48.5 3.8 %collective-permute-start.13 = (bf16[72,1536]{1,0:T(8,128)(2,1)}, bf16[72,1536]{1,0:T(8,128)(2,1)}, u32[]{:S(2)}, u32[]{:S(2)}) collective-permute-start(bf16[72,1536]{1,0:T(8,128)(2,1)} %get-tuple-element.67), channel_id=1, source_target_pairs={{0,24},{4,28},{8,16},{12,20},{16,8},{20,12},{24,0},{28,4},{1,25},{... | collective-permute-start | bytes 663560 | tf_op jit(solution)/shard_map/ppermute | solution.py:205
  62.1 5.3 %collective-permute-start.11 = (bf16[72,1536]{1,0:T(8,128)(2,1)}, bf16[72,1536]{1,0:T(8,128)(2,1)S(1)}, u32[]{:S(2)}, u32[]{:S(2)}) collective-permute-start(bf16[72,1536]{1,0:T(8,128)(2,1)} %copy-done.13), channel_id=1, source_target_pairs={{0,8},{4,12},{8,0},{12,4},{16,24},{20,28},{24,16},{28,20},{1,9},{5... | collective-permute-start | bytes 663560 | tf_op jit(solution)/shard_map/ppermute | solution.py:205
  67.5 3.4 %collective-permute-start.21 = (bf16[72,1536]{1,0:T(8,128)(2,1)}, bf16[72,1536]{1,0:T(8,128)(2,1)S(1)}, u32[]{:S(2)}, u32[]{:S(2)}) collective-permute-start(bf16[72,1536]{1,0:T(8,128)(2,1)} %copy-done.14), channel_id=1, source_target_pairs={{0,24},{4,28},{8,16},{12,20},{16,8},{20,12},{24,0},{28,4},{1,25},{... | collective-permute-start | bytes 663560 | tf_op jit(solution)/shard_map/ppermute | solution.py:205
  72.0 5.7 %fusion.27 = bf16[144,2304]{1,0:T(8,128)(2,1)S(1)} fusion(bf16[144,1536]{1,0:T(8,128)(2,1)S(1)} %pad_maximum_fusion.3, bf16[1,2304,1536]{2,1,0:T(8,128)(2,1)} %param.14), kind=kOutput, calls=%fused_computation.25 | convolution fusion | flops 1019547648 | bytes 8183808 | tf_op jit(solution)/shard_map/dot_general | solution.py:20
  83.8 5.5 %collective-permute-done.12 = bf16[72,1536]{1,0:T(8,128)(2,1)S(1)} collective-permute-done((bf16[72,1536]{1,0:T(8,128)(2,1)S(1)}, bf16[72,1536]{1,0:T(8,128)(2,1)S(1)}, u32[]{:S(2)}, u32[]{:S(2)}) %collective-permute-start.12) | collective-permute-done | bytes 221216 | tf_op jit(solution)/shard_map/ppermute | solution.py:205
  91.4 3.8 %collective-permute-done.23 = bf16[72,1536]{1,0:T(8,128)(2,1)S(1)} collective-permute-done((bf16[72,1536]{1,0:T(8,128)(2,1)S(1)}, bf16[72,1536]{1,0:T(8,128)(2,1)S(1)}, u32[]{:S(2)}, u32[]{:S(2)}) %collective-permute-start.23) | collective-permute-done | bytes 221216 | tf_op jit(solution)/shard_map/ppermute | solution.py:205
  97.9 3.8 %collective-permute-done.28 = bf16[72,1536]{1,0:T(8,128)(2,1)S(1)} collective-permute-done((bf16[72,1536]{1,0:T(8,128)(2,1)S(1)}, bf16[72,1536]{1,0:T(8,128)(2,1)S(1)}, u32[]{:S(2)}, u32[]{:S(2)}) %collective-permute-start.28) | collective-permute-done | bytes 221216 | tf_op jit(solution)/shard_map/ppermute | solution.py:205
  105.8 4.3 %collective-permute-done.29 = bf16[72,1536]{1,0:T(8,128)(2,1)S(1)} collective-permute-done((bf16[72,1536]{1,0:T(8,128)(2,1)S(1)}, bf16[72,1536]{1,0:T(8,128)(2,1)S(1)}, u32[]{:S(2)}, u32[]{:S(2)}) %collective-permute-start.29) | collective-permute-done | bytes 221216 | tf_op jit(solution)/shard_map/ppermute | solution.py:205
  110.0 3.6 %collective-permute-done.24 = bf16[72,1536]{1,0:T(8,128)(2,1)S(1)} collective-permute-done((bf16[72,1536]{1,0:T(8,128)(2,1)S(1)}, bf16[72,1536]{1,0:T(8,128)(2,1)S(1)}, u32[]{:S(2)}, u32[]{:S(2)}) %collective-permute-start.24) | collective-permute-done | bytes 221216 | tf_op jit(solution)/shard_map/ppermute | solution.py:205
  119.3 7.7 %collective-permute-done.17 = bf16[144,2304]{1,0:T(8,128)(2,1)S(1)} collective-permute-done((bf16[144,2304]{1,0:T(8,128)(2,1)S(1)}, bf16[144,2304]{1,0:T(8,128)(2,1)S(1)}, u32[]{:S(2)}, u32[]{:S(2)}) %collective-permute-start.17) | collective-permute-done | bytes 663584 | tf_op jit(solution)/shard_map/ppermute | solution.py:205
  147.2 9.8 %collective-permute-done.38 = bf16[72,1536]{1,0:T(8,128)(2,1)S(1)} collective-permute-done((bf16[72,1536]{1,0:T(8,128)(2,1)S(1)}, bf16[72,1536]{1,0:T(8,128)(2,1)S(1)}, u32[]{:S(2)}, u32[]{:S(2)}) %collective-permute-start.38) | collective-permute-done | bytes 221216 | tf_op jit(solution)/shard_map/ppermute | solution.py:205
  161.7 4.8 %collective-permute-done.36 = bf16[72,1536]{1,0:T(8,128)(2,1)S(1)} collective-permute-done((bf16[72,1536]{1,0:T(8,128)(2,1)S(1)}, bf16[72,1536]{1,0:T(8,128)(2,1)S(1)}, u32[]{:S(2)}, u32[]{:S(2)}) %collective-permute-start.36) | collective-permute-done | bytes 221216 | tf_op jit(solution)/shard_map/ppermute | solution.py:205
  166.6 5.8 %collective-permute-done.20.refs_1_ = bf16[72,1536]{1,0:T(8,128)(2,1)S(1)} collective-permute-done((bf16[72,1536]{1,0:T(8,128)(2,1)S(1)}, bf16[72,1536]{1,0:T(8,128)(2,1)S(1)}, u32[]{:S(2)}, u32[]{:S(2)}) %collective-permute-start.20) | collective-permute-done | bytes 221216 | tf_op jit(solution)/shard_map/ppermute | solution.py:205
  172.5 5.6 %collective-permute-done.37.refs_2_ = bf16[72,1536]{1,0:T(8,128)(2,1)S(1)} collective-permute-done((bf16[72,1536]{1,0:T(8,128)(2,1)S(1)}, bf16[72,1536]{1,0:T(8,128)(2,1)S(1)}, u32[]{:S(2)}, u32[]{:S(2)}) %collective-permute-start.37) | collective-permute-done | bytes 221216 | tf_op jit(solution)/shard_map/ppermute | solution.py:205
  181.2 4.0 %collective-permute-done.40 = bf16[6,128,128]{2,1,0:T(8,128)(2,1)S(1)} collective-permute-done((bf16[6,128,128]{2,1,0:T(8,128)(2,1)S(1)}, bf16[6,128,128]{2,1,0:T(8,128)(2,1)S(1)}, u32[]{:S(2)}, u32[]{:S(2)}) %collective-permute-start.40) | collective-permute-done | bytes 196640 | tf_op jit(solution)/shard_map/ppermute | solution.py:205
  185.9 5.2 %collective-permute-done.41 = bf16[6,128,128]{2,1,0:T(8,128)(2,1)S(1)} collective-permute-done((bf16[6,128,128]{2,1,0:T(8,128)(2,1)S(1)}, bf16[6,128,128]{2,1,0:T(8,128)(2,1)S(1)}, u32[]{:S(2)}, u32[]{:S(2)}) %collective-permute-start.41) | collective-permute-done | bytes 196640 | tf_op jit(solution)/shard_map/ppermute | solution.py:209
  191.2 4.3 %collective-permute-start.42 = (bf16[6,128,128]{2,1,0:T(8,128)(2,1)S(1)}, bf16[6,128,128]{2,1,0:T(8,128)(2,1)S(1)}, u32[]{:S(2)}, u32[]{:S(2)}) collective-permute-start(bf16[6,128,128]{2,1,0:T(8,128)(2,1)S(1)} %add_convert_fusion.10), channel_id=1, source_target_pairs={{16,0},{20,4},{8,8},{12,12},{0,16},{4,20},{24,24},{28,28},{17,1},{... | collective-permute-start | bytes 589832 | tf_op jit(solution)/shard_map/ppermute | solution.py:209
  196.9 4.4 %collective-permute-done.42 = bf16[6,128,128]{2,1,0:T(8,128)(2,1)S(1)} collective-permute-done((bf16[6,128,128]{2,1,0:T(8,128)(2,1)S(1)}, bf16[6,128,128]{2,1,0:T(8,128)(2,1)S(1)}, u32[]{:S(2)}, u32[]{:S(2)}) %collective-permute-start.42) | collective-permute-done | bytes 196640 | tf_op jit(solution)/shard_map/ppermute | solution.py:209
  203.2 4.0 %shard_map.117 = (bf16[128,1536]{1,0:T(8,128)(2,1)}, f32[128,1536]{1,0:T(8,128)S(1)}, f32[128,1536]{1,0:T(8,128)S(1)}) custom-call(s32[3]{0:T(128)S(1)} %pad_add_fusion.place_ref, f32[12]{0:T(128)S(1)} %copy-done.8, bf16[128,1536]{1,0:T(8,128)(2,1)S(1)} %copy-done.4, bf16[128,1536]{1,0:T(8,128)(2,1)S(1)} %copy-done.1, bf16[128,1536]{1,0:T(8,128)(2,1)S(1)} %copy-done.3, ...), custom_call_target="tpu_custom_call" | custom-call | flops 1 | bytes 14760000 | tf_op jit(solution)/shard_map/pallas_call | solution.py:190
  (170 shorter events, 94.0 us)
Async XLA Ops:
  48.5 10.1 %collective-permute-start.13 = (bf16[72,1536]{1,0:T(8,128)(2,1)}, bf16[72,1536]{1,0:T(8,128)(2,1)}, u32[]{:S(2)}, u32[]{:S(2)}) collective-permute-start(bf16[72,1536]{1,0:T(8,128)(2,1)} %get-tuple-element.67), channel_id=1, source_target_pairs={{0,24},{4,28},{8,16},{12,20},{16,8},{20,12},{24,0},{28,4},{1,25},{... | collective-permute-start | bytes 663560 | tf_op jit(solution)/shard_map/ppermute | solution.py:205
  58.6 12.3 %collective-permute-start.14 = (bf16[72,1536]{1,0:T(8,128)(2,1)}, bf16[72,1536]{1,0:T(8,128)(2,1)S(1)}, u32[]{:S(2)}, u32[]{:S(2)}) collective-permute-start(bf16[72,1536]{1,0:T(8,128)(2,1)} %collective-permute-done.13), channel_id=1, source_target_pairs={{0,4},{4,0},{8,12},{12,8},{16,20},{20,16},{24,28},{28,24},{1,5},{5... | collective-permute-start | bytes 663560 | tf_op jit(solution)/shard_map/ppermute | solution.py:205
  59.8 23.6 %collective-permute-start.10 = (bf16[72,1536]{1,0:T(8,128)(2,1)S(1)}, bf16[72,1536]{1,0:T(8,128)(2,1)S(1)}, u32[]{:S(2)}, u32[]{:S(2)}) collective-permute-start(bf16[72,1536]{1,0:T(8,128)(2,1)S(1)} %get-tuple-element.64), channel_id=1, source_target_pairs={{0,4},{4,0},{8,12},{12,8},{16,20},{20,16},{24,28},{28,24},{1,5},{5... | collective-permute-start | bytes 663560 | tf_op jit(solution)/shard_map/ppermute | solution.py:205
  60.6 29.3 %collective-permute-start.9 = (bf16[144,2304]{1,0:T(8,128)(2,1)}, bf16[144,2304]{1,0:T(8,128)(2,1)S(1)}, u32[]{:S(2)}, u32[]{:S(2)}) collective-permute-start(bf16[144,2304]{1,0:T(8,128)(2,1)} %fusion.91), channel_id=1, source_target_pairs={{0,2},{1,3},{2,0},{3,1},{4,6},{5,7},{6,4},{7,5},{8,10},{9,11},{10,... | collective-permute-start | bytes 1990664 | tf_op jit(solution)/shard_map/ppermute | solution.py:205
  62.1 19.3 %collective-permute-start.11 = (bf16[72,1536]{1,0:T(8,128)(2,1)}, bf16[72,1536]{1,0:T(8,128)(2,1)S(1)}, u32[]{:S(2)}, u32[]{:S(2)}) collective-permute-start(bf16[72,1536]{1,0:T(8,128)(2,1)} %copy-done.13), channel_id=1, source_target_pairs={{0,8},{4,12},{8,0},{12,4},{16,24},{20,28},{24,16},{28,20},{1,9},{5... | collective-permute-start | bytes 663560 | tf_op jit(solution)/shard_map/ppermute | solution.py:205
  67.5 12.8 %collective-permute-start.21 = (bf16[72,1536]{1,0:T(8,128)(2,1)}, bf16[72,1536]{1,0:T(8,128)(2,1)S(1)}, u32[]{:S(2)}, u32[]{:S(2)}) collective-permute-start(bf16[72,1536]{1,0:T(8,128)(2,1)} %copy-done.14), channel_id=1, source_target_pairs={{0,24},{4,28},{8,16},{12,20},{16,8},{20,12},{24,0},{28,4},{1,25},{... | collective-permute-start | bytes 663560 | tf_op jit(solution)/shard_map/ppermute | solution.py:205
  77.8 12.0 %collective-permute-start.15 = (bf16[72,2304]{1,0:T(8,128)(2,1)S(1)}, bf16[72,2304]{1,0:T(8,128)(2,1)S(1)}, u32[]{:S(2)}, u32[]{:S(2)}) collective-permute-start(bf16[72,2304]{1,0:T(8,128)(2,1)S(1)} %dynamic-slice_bitcast_fusion.2), channel_id=1, source_target_pairs={{0,1},{1,0},{2,3},{3,2},{4,5},{5,4},{6,7},{7,6},{8,9},{9,8},{10,11... | collective-permute-start | bytes 995336 | tf_op jit(solution)/shard_map/ppermute | solution.py:205
  80.3 23.8 %collective-permute-start.22 = (bf16[72,1536]{1,0:T(8,128)(2,1)S(1)}, bf16[72,1536]{1,0:T(8,128)(2,1)S(1)}, u32[]{:S(2)}, u32[]{:S(2)}) collective-permute-start(bf16[72,1536]{1,0:T(8,128)(2,1)S(1)} %get-tuple-element.74), channel_id=1, source_target_pairs={{0,16},{4,20},{8,24},{12,28},{16,0},{20,4},{24,8},{28,12},{1,17},{... | collective-permute-start | bytes 663560 | tf_op jit(solution)/shard_map/ppermute | solution.py:205
  81.5 20.2 %collective-permute-start.28 = (bf16[72,1536]{1,0:T(8,128)(2,1)S(1)}, bf16[72,1536]{1,0:T(8,128)(2,1)S(1)}, u32[]{:S(2)}, u32[]{:S(2)}) collective-permute-start(bf16[72,1536]{1,0:T(8,128)(2,1)S(1)} %copy-done.12), channel_id=1, source_target_pairs={{0,16},{4,20},{8,24},{12,28},{16,0},{20,4},{24,8},{28,12},{1,17},{... | collective-permute-start | bytes 663560 | tf_op jit(solution)/shard_map/ppermute | solution.py:205
  102.0 29.2 %collective-permute-start.33 = (bf16[72,2304]{1,0:T(8,128)(2,1)S(1)}, bf16[72,2304]{1,0:T(8,128)(2,1)S(1)}, u32[]{:S(2)}, u32[]{:S(2)}) collective-permute-start(bf16[72,2304]{1,0:T(8,128)(2,1)S(1)} %fusion.113), channel_id=1, source_target_pairs={{0,2},{1,3},{2,0},{3,1},{4,6},{5,7},{6,4},{7,5},{8,10},{9,11},{10,... | collective-permute-start | bytes 995336 | tf_op jit(solution)/shard_map/ppermute | solution.py:205
  103.6 23.4 %collective-permute-start.17 = (bf16[144,2304]{1,0:T(8,128)(2,1)S(1)}, bf16[144,2304]{1,0:T(8,128)(2,1)S(1)}, u32[]{:S(2)}, u32[]{:S(2)}) collective-permute-start(bf16[144,2304]{1,0:T(8,128)(2,1)S(1)} %add_convert_fusion.1), channel_id=1, source_target_pairs={{0,2},{1,3},{2,0},{3,1},{4,6},{5,7},{6,4},{7,5},{8,10},{9,11},{10,... | collective-permute-start | bytes 1990664 | tf_op jit(solution)/shard_map/ppermute | solution.py:205
  104.1 9.6 %collective-permute-start.25 = (bf16[72,2304]{1,0:T(8,128)(2,1)S(1)}, bf16[72,2304]{1,0:T(8,128)(2,1)S(1)}, u32[]{:S(2)}, u32[]{:S(2)}) collective-permute-start(bf16[72,2304]{1,0:T(8,128)(2,1)S(1)} %fusion.42), channel_id=1, source_target_pairs={{0,1},{1,0},{2,3},{3,2},{4,5},{5,4},{6,7},{7,6},{8,9},{9,8},{10,11... | collective-permute-start | bytes 995336 | tf_op jit(solution)/shard_map/ppermute | solution.py:205
  104.1 9.5 %collective-permute-start.24 = (bf16[72,1536]{1,0:T(8,128)(2,1)S(1)}, bf16[72,1536]{1,0:T(8,128)(2,1)S(1)}, u32[]{:S(2)}, u32[]{:S(2)}) collective-permute-start(bf16[72,1536]{1,0:T(8,128)(2,1)S(1)} %collective-permute-done.22), channel_id=1, source_target_pairs={{0,4},{4,0},{8,12},{12,8},{16,20},{20,16},{24,28},{28,24},{1,5},{5... | collective-permute-start | bytes 663560 | tf_op jit(solution)/shard_map/ppermute | solution.py:205
  115.1 19.0 %collective-permute-start.34 = (bf16[72,2304]{1,0:T(8,128)(2,1)S(1)}, bf16[72,2304]{1,0:T(8,128)(2,1)S(1)}, u32[]{:S(2)}, u32[]{:S(2)}) collective-permute-start(bf16[72,2304]{1,0:T(8,128)(2,1)S(1)} %fusion.54), channel_id=1, source_target_pairs={{0,2},{1,3},{2,0},{3,1},{4,6},{5,7},{6,4},{7,5},{8,10},{9,11},{10,... | collective-permute-start | bytes 995336 | tf_op jit(solution)/shard_map/ppermute | solution.py:205
  127.6 9.9 %collective-permute-start.18 = (bf16[144,2304]{1,0:T(8,128)(2,1)S(1)}, bf16[144,2304]{1,0:T(8,128)(2,1)S(1)}, u32[]{:S(2)}, u32[]{:S(2)}) collective-permute-start(bf16[144,2304]{1,0:T(8,128)(2,1)S(1)} %fusion.87), channel_id=1, source_target_pairs={{0,1},{1,0},{2,3},{3,2},{4,5},{5,4},{6,7},{7,6},{8,9},{9,8},{10,11... | collective-permute-start | bytes 1990664 | tf_op jit(solution)/shard_map/ppermute | solution.py:205
  127.8 16.8 %collective-permute-start.27 = (bf16[72,2304]{1,0:T(8,128)(2,1)S(1)}, bf16[72,2304]{1,0:T(8,128)(2,1)S(1)}, u32[]{:S(2)}, u32[]{:S(2)}) collective-permute-start(bf16[72,2304]{1,0:T(8,128)(2,1)S(1)} %fusion.112), channel_id=1, source_target_pairs={{0,2},{1,3},{2,0},{3,1},{4,6},{5,7},{6,4},{7,5},{8,10},{9,11},{10,... | collective-permute-start | bytes 995336 | tf_op jit(solution)/shard_map/ppermute | solution.py:205
  136.0 10.8 %collective-permute-start.31 = (bf16[72,2304]{1,0:T(8,128)(2,1)S(1)}, bf16[72,2304]{1,0:T(8,128)(2,1)S(1)}, u32[]{:S(2)}, u32[]{:S(2)}) collective-permute-start(bf16[72,2304]{1,0:T(8,128)(2,1)S(1)} %fusion.69), channel_id=1, source_target_pairs={{0,2},{1,3},{2,0},{3,1},{4,6},{5,7},{6,4},{7,5},{8,10},{9,11},{10,... | collective-permute-start | bytes 995336 | tf_op jit(solution)/shard_map/ppermute | solution.py:205
  139.9 21.5 %collective-permute-start.19 = (bf16[144,1536]{1,0:T(8,128)(2,1)S(1)}, bf16[144,1536]{1,0:T(8,128)(2,1)S(1)}, u32[]{:S(2)}, u32[]{:S(2)}) collective-permute-start(bf16[144,1536]{1,0:T(8,128)(2,1)S(1)} %slice.39), channel_id=1, source_target_pairs={{0,4},{4,0},{8,12},{12,8},{16,20},{20,16},{24,28},{28,24},{1,5},{5... | collective-permute-start | bytes 1327112 | tf_op jit(solution)/shard_map/ppermute | solution.py:205
  144.2 12.9 %collective-permute-start.38 = (bf16[72,1536]{1,0:T(8,128)(2,1)S(1)}, bf16[72,1536]{1,0:T(8,128)(2,1)S(1)}, u32[]{:S(2)}, u32[]{:S(2)}) collective-permute-start(bf16[72,1536]{1,0:T(8,128)(2,1)S(1)} %slice.45), channel_id=1, source_target_pairs={{0,4},{4,0},{8,12},{12,8},{16,20},{20,16},{24,28},{28,24},{1,5},{5... | collective-permute-start | bytes 663560 | tf_op jit(solution)/shard_map/ppermute | solution.py:205
  147.1 10.0 %collective-permute-start.32 = (bf16[72,2304]{1,0:T(8,128)(2,1)S(1)}, bf16[72,2304]{1,0:T(8,128)(2,1)S(1)}, u32[]{:S(2)}, u32[]{:S(2)}) collective-permute-start(bf16[72,2304]{1,0:T(8,128)(2,1)S(1)} %fusion.98), channel_id=1, source_target_pairs={{0,1},{1,0},{2,3},{3,2},{4,5},{5,4},{6,7},{7,6},{8,9},{9,8},{10,11... | collective-permute-start | bytes 995336 | tf_op jit(solution)/shard_map/ppermute | solution.py:205
  157.1 9.6 %collective-permute-start.39 = (bf16[72,1536]{1,0:T(8,128)(2,1)S(1)}, bf16[72,1536]{1,0:T(8,128)(2,1)S(1)}, u32[]{:S(2)}, u32[]{:S(2)}) collective-permute-start(bf16[72,1536]{1,0:T(8,128)(2,1)S(1)} %add_convert_fusion.8), channel_id=1, source_target_pairs={{0,24},{4,28},{8,16},{12,20},{16,8},{20,12},{24,0},{28,4},{1,25},{... | collective-permute-start | bytes 663560 | tf_op jit(solution)/shard_map/ppermute | solution.py:205
  161.6 10.9 %collective-permute-start.20 = (bf16[72,1536]{1,0:T(8,128)(2,1)S(1)}, bf16[72,1536]{1,0:T(8,128)(2,1)S(1)}, u32[]{:S(2)}, u32[]{:S(2)}) collective-permute-start(bf16[72,1536]{1,0:T(8,128)(2,1)S(1)} %get-tuple-element.111), channel_id=1, source_target_pairs={{0,8},{4,12},{8,0},{12,4},{16,24},{20,28},{24,16},{28,20},{1,9},{5... | collective-permute-start | bytes 663560 | tf_op jit(solution)/shard_map/ppermute | solution.py:205
  166.6 11.5 %collective-permute-start.37 = (bf16[72,1536]{1,0:T(8,128)(2,1)S(1)}, bf16[72,1536]{1,0:T(8,128)(2,1)S(1)}, u32[]{:S(2)}, u32[]{:S(2)}) collective-permute-start(bf16[72,1536]{1,0:T(8,128)(2,1)S(1)} %add_convert_fusion.9), channel_id=1, source_target_pairs={{0,16},{4,20},{8,24},{12,28},{16,0},{20,4},{24,8},{28,12},{1,17},{... | collective-permute-start | bytes 663560 | tf_op jit(solution)/shard_map/ppermute | solution.py:205
  191.2 10.0 %collective-permute-start.42 = (bf16[6,128,128]{2,1,0:T(8,128)(2,1)S(1)}, bf16[6,128,128]{2,1,0:T(8,128)(2,1)S(1)}, u32[]{:S(2)}, u32[]{:S(2)}) collective-permute-start(bf16[6,128,128]{2,1,0:T(8,128)(2,1)S(1)} %add_convert_fusion.10), channel_id=1, source_target_pairs={{16,0},{20,4},{8,8},{12,12},{0,16},{4,20},{24,24},{28,28},{17,1},{... | collective-permute-start | bytes 589832 | tf_op jit(solution)/shard_map/ppermute | solution.py:209
  (43 other events, 272.0 us)

commit v9 on v5

--- a/solution.py
+++ b/solution.py
@@ -42,18 +42,18 @@
     rows = lax.broadcasted_iota(jnp.int32, (block_len, block_len), 0)
     cols = lax.broadcasted_iota(jnp.int32, (block_len, block_len), 1)
     distance = (rows - cols).astype(F32)
-    return jnp.where(distance >= 0.0, jnp.exp(-rate * jnp.maximum(distance, 0.0)), 0.0)
-
-
-def key_state_kernel(place_ref, rates_ref, k_ref, v_ref, mine_ref, other_ref):
-    block_len, half = k_ref.shape[0], mine_ref.shape[0]
+    return jnp.where(distance >= 0.0, jnp.exp(rate * jnp.maximum(distance, 0.0)), 0.0)
+
+
+def key_state_kernel(place_ref, rates_ref, pair_ref, mine_ref, other_ref):
+    block_len, half = pair_ref.shape[0] // 2, mine_ref.shape[0]
     steps = column(block_len)
     for slot in [*range(half, 2 * half), *range(half)]:
         head, lanes = lanes_of(place_ref, slot, 2 * half)
-        power = jnp.exp(-rates_ref[head] * (block_len - steps))
-        scaled = (k_ref[:, lanes].astype(F32) * power).astype(BF16)
+        power = jnp.exp(rates_ref[head] * (block_len - steps))
+        scaled = (pair_ref[:block_len, lanes].astype(F32) * power).astype(BF16)
         state_ref = (mine_ref, other_ref)[slot // half]
-        state_ref[slot % half] = dot(scaled, v_ref[:, lanes], 0, 0).astype(BF16)
+        state_ref[slot % half] = dot(scaled, pair_ref[block_len:, lanes], 0, 0).astype(BF16)
 
 
 def pick_rows(choose_ref, rows, send_refs):
@@ -69,13 +69,13 @@
 
 
 def route_kernel(
-    place_ref, routes_ref, gates_ref, grad_ref, choose_ref, weigh_ref, *send_refs
+    place_ref, slots_ref, grad_ref, choose_ref, weigh_ref, *send_refs
 ):
     experts, capacity, block_len = choose_ref.shape
     rows = lax.broadcasted_iota(jnp.int32, (block_len, block_len), 0)
     cols = lax.broadcasted_iota(jnp.int32, (block_len, block_len), 1)
 
-    first, second = routes_ref[0:1, :], routes_ref[1:2, :]
+    first, second = [slots_ref[i : i + 1, :].astype(jnp.int32) for i in range(2)]
     names = lax.broadcasted_iota(jnp.int32, (32, block_len), 0)
     hit_first = jnp.where(names == first, 1.0, 0.0)
     hit_second = jnp.where(names == second, 1.0, 0.0)
@@ -94,7 +94,7 @@
 
     columns = jnp.concatenate(
         [first.astype(F32), second.astype(F32), slot_first.astype(F32), slot_second.astype(F32)]
-        + [gates_ref[0:1, :], gates_ref[1:2, :]] + [jnp.zeros((2, block_len), F32)],
+        + [slots_ref[2:3, :], slots_ref[3:4, :]] + [jnp.zeros((2, block_len), F32)],
         axis=0,
     ).T
     first, second, slot_first, slot_second = [
@@ -108,15 +108,15 @@
         weigh_ref[k] = (one + two).astype(BF16)
 
 
-def intra_kernel(place_ref, rates_ref, q_ref, k_ref, v_ref, intra_ref, weights_ref):
+def intra_kernel(place_ref, rates_ref, q_ref, pair_ref, intra_ref, weights_ref):
     block_len, heads = q_ref.shape[0], weights_ref.shape[0]
     for slot in range(heads):
         head, lanes = lanes_of(place_ref, slot, heads)
         within = decay_within(rates_ref[head], block_len)
-        scores = dot(q_ref[:, lanes], k_ref[:, lanes], 1, 1)
+        scores = dot(q_ref[:, lanes], pair_ref[:block_len, lanes], 1, 1)
         weights = (SCALE * scores * within).astype(BF16)
         weights_ref[slot] = weights
-        intra_ref[:, lanes] = dot(weights, v_ref[:, lanes], 1, 0)
+        intra_ref[:, lanes] = dot(weights, pair_ref[block_len:, lanes], 1, 0)
 
 
 def attend_kernel(
@@ -128,7 +128,7 @@
     for slot in range(2 * half):
         head, lanes = lanes_of(place_ref, slot, 2 * half)
         entering = (mine_ref, other_ref)[slot // half][slot % half]
-        power = SCALE * jnp.exp(-rates_ref[head] * steps)
+        power = SCALE * jnp.exp(rates_ref[head] * steps)
         inter = power * dot(q_ref[:, lanes], entering, 1, 0)
         attn_ref[:, lanes] = (intra_ref[:, lanes] + inter).astype(BF16)
     pick_rows(choose_ref, attn_ref[...], send_refs)
@@ -145,14 +145,14 @@
     grad_ref[...] = total.astype(BF16)
     for slot in [*range(half, 2 * half), *range(half)]:
         head, lanes = lanes_of(place_ref, slot, 2 * half)
-        power = jnp.exp(-rates_ref[head] * (steps + 1.0))
+        power = jnp.exp(rates_ref[head] * (steps + 1.0))
         scaled = (q_ref[:, lanes].astype(F32) * power).astype(BF16)
         state_ref = (mine_ref, other_ref)[slot // half]
         state_ref[slot % half] = dot(scaled, grad_ref[:, lanes], 0, 0).astype(BF16)
 
 
 def near_kernel(
-    place_ref, rates_ref, q_ref, k_ref, v_ref, grad_ref, mine_ref, other_ref, weights_ref,
+    place_ref, rates_ref, q_ref, pair_ref, grad_ref, mine_ref, other_ref, weights_ref,
     query_ref, key_ref, value_ref,
 ):
     block_len, half = q_ref.shape[0], mine_ref.shape[0]
@@ -163,28 +163,28 @@
         grad = grad_ref[:, lanes]
         entering = (mine_ref, other_ref)[slot // half][slot % half]
         within = decay_within(rate, block_len)
-        dweights = (SCALE * dot(grad, v_ref[:, lanes], 1, 1) * within).astype(BF16)
-        query = dot(dweights, k_ref[:, lanes], 1, 0)
-        query = query + SCALE * jnp.exp(-rate * steps) * dot(grad, entering, 1, 1)
+        dweights = (SCALE * dot(grad, pair_ref[block_len:, lanes], 1, 1) * within).astype(BF16)
+        query = dot(dweights, pair_ref[:block_len, lanes], 1, 0)
+        query = query + SCALE * jnp.exp(rate * steps) * dot(grad, entering, 1, 1)
         query_ref[:, lanes] = query.astype(BF16)
         key_ref[:, lanes] = dot(dweights, q_ref[:, lanes], 0, 0)
         value_ref[:, lanes] = dot(weights_ref[slot], grad, 0, 0)
 
 
 def far_kernel(
-    place_ref, rates_ref, k_ref, v_ref, key_near, value_near, mine_ref, other_ref, key_ref, value_ref
+    place_ref, rates_ref, pair_ref, key_near, value_near, mine_ref, other_ref, key_ref, value_ref
 ):
-    block_len, half = k_ref.shape[0], mine_ref.shape[0]
+    block_len, half = pair_ref.shape[0] // 2, mine_ref.shape[0]
     steps = column(block_len)
     for slot in range(2 * half):
         head, lanes = lanes_of(place_ref, slot, 2 * half)
         leaving = (mine_ref, other_ref)[slot // half][slot % half]
-        power = SCALE * jnp.exp(-rates_ref[head] * (block_len - 1.0 - steps))
+        power = SCALE * jnp.exp(rates_ref[head] * (block_len - 1.0 - steps))
         key_ref[:, lanes] = (
-            key_near[:, lanes] + power * dot(v_ref[:, lanes], leaving, 1, 1)
+            key_near[:, lanes] + power * dot(pair_ref[block_len:, lanes], leaving, 1, 1)
         ).astype(BF16)
         value_ref[:, lanes] = (
-            value_near[:, lanes] + power * dot(k_ref[:, lanes], leaving, 1, 0)
+            value_near[:, lanes] + power * dot(pair_ref[:block_len, lanes], leaving, 1, 0)
         ).astype(BF16)
 
 
@@ -268,14 +268,22 @@
     return keep, give
 
 
-def sum_over_cores(own, other, part, multiply, *events):
+def two_products(own, other, part, multiply, *events):
     mine = lax.axis_index("exp") & 1
     rows = lambda flag: jnp.concatenate(
         [jnp.where(flag == 0, own[k], other[k]) for k in part], axis=0
     )
     sent = multiply(after(rows(1 - mine), *events)).astype(BF16)
-    kept = multiply(after(rows(mine), sent)).astype(BF16)
-    return sent, kept
+    return sent, multiply(after(rows(mine), sent)).astype(BF16)
+
+
+def one_product(own, other, part, multiply, *events):
+    mine = lax.axis_index("exp") & 1
+    rows = [side[k] for side in (own, other) for k in part]
+    whole = multiply(after(jnp.concatenate(rows, axis=0), *events)).astype(BF16)
+    whole = whole.reshape(2, whole.shape[0] // 2, whole.shape[1])
+    sent = lax.dynamic_index_in_dim(whole, 1 - mine, 0, False)
+    return sent, lax.dynamic_index_in_dim(whole, mine, 0, False)
 
 
 def over_cores(sent, kept):
@@ -300,7 +308,8 @@
     position = lax.axis_index("ctx").astype(jnp.int32)
     core = lax.axis_index("exp").astype(jnp.int32) & 1
     place = jnp.stack([position & 1, position >> 1, core])
-    scalars = (place, decay_rates)
+    scalars = (place, -decay_rates)
+    pair = jnp.concatenate([keys, values], axis=0)
     up_local, down_local = up_weight[0], down_weight[0]
     quarter = max(experts // 4, 1)
     near_part = range(experts // 2)
@@ -314,23 +323,27 @@
     weigh_table = jax.ShapeDtypeStruct((experts, block_len, capacity), BF16)
     slots = jax.ShapeDtypeStruct((capacity, group), BF16)
 
+    slots_of = jnp.concatenate([routes.astype(F32), gate_weights], axis=1).T
     reaches = [1 << i for i in range((experts - 1).bit_length())]
     pairs_of = lambda rows, k: swap(rows, "ctx", 2 * k) if k else rows
 
-    key_mine, key_other = call(key_state_kernel, [states] * 2, scalars, (keys, values))
+    key_mine, key_other = call(key_state_kernel, [states] * 2, scalars, (pair,))
     choose, weigh, *send_grad = call(
         route_kernel, [choose_table, weigh_table] + [slots] * experts,
-        (place,), (routes.T, gate_weights.T, out_grad)
+        (place,), (slots_of, out_grad)
     )
     intra, weights = call(
-        intra_kernel, [wide, weight_sq], scalars, (queries, keys, values), cost=LARGE
+        intra_kernel, [wide, weight_sq], scalars, (queries, pair), cost=LARGE
     )
 
     total, partner = scan_total(
         key_mine, key_other, decay_rates, place, block_len, False, send_grad[0]
     )
+    by_down = lambda rows: dot(rows, down_local, 1, 1)
+    by_up = lambda rows: dot(rows, up_local, 1, 0)
     grad_own = {0: send_grad[0]}
-    for k in [*near_part[1:], *first_far]:
+    grad_other = {0: swap(after(send_grad[0], total), "ctx", 1)}
+    for k in near_part[1:]:
         grad_own[k] = pairs_of(after(send_grad[k], total), k)
     before = None
     for index, reach in enumerate(reaches):
@@ -338,62 +351,74 @@
         before, upto = scan_step(
             before, total, reach, decay_rates, place, block_len, False, *events
         )
+    for k in near_part[1:]:
+        grad_other[k] = swap(after(grad_own[k], upto), "ctx", 1)
+    for k in first_far:
+        grad_own[k] = pairs_of(after(send_grad[k], upto), k)
     keep, give = scan_ends(before, key_mine, partner, decay_rates, place, block_len, False)
-    grad_other = {0: swap(after(grad_own[0], total), "ctx", 1)}
-    for k in [*near_part[1:], *first_far]:
-        grad_other[k] = swap(after(grad_own[k], upto), "ctx", 1)
     for k in second_far:
         grad_own[k] = pairs_of(after(send_grad[k], give), k)
-
-    by_down = lambda rows: dot(rows, down_local, 1, 1)
-    by_up = lambda rows: dot(rows, up_local, 1, 0)
+    for k in first_far:
+        grad_other[k] = swap(grad_own[k], "ctx", 1)
     given = swap(give, "ctx", 1)
-    hidden_near = over_cores(*sum_over_cores(grad_own, grad_other, near_part, by_down, give))
-    given, hidden_near = lax.optimization_barrier((given, hidden_near))
+    hidden_near = one_product(grad_own, grad_other, near_part, by_down, give)
+    hidden_near_sum = over_cores(*hidden_near)
+    hidden_near_all = sum_over_rest(hidden_near_sum, bits)
     send_in = call(
         attend_kernel, [slots] * experts, scalars, (queries, intra, choose, keep, given),
         [pltpu.VMEM((block_len, group), BF16)],
     )
-    for k in second_far:
-        grad_other[k] = swap(after(grad_own[k], send_in[0]), "ctx", 1)
-    hidden_first = over_cores(
-        *sum_over_cores(grad_own, grad_other, first_far, by_down, send_in[0])
-    )
-
-    in_own, in_other = {0: send_in[0]}, {}
+    in_own, in_other = {0: send_in[0]}, {0: swap(send_in[0], "ctx", 1)}
     for k in [*near_part[1:], *first_far]:
         in_own[k] = pairs_of(send_in[k], k)
     for k in second_far:
-        in_own[k] = pairs_of(after(send_in[k], in_own[first_far[0]], hidden_first), k)
-    for k in range(experts):
+        grad_other[k] = swap(after(grad_own[k], send_in[0]), "ctx", 1)
+    for k in near_part[1:]:
         in_other[k] = swap(in_own[k], "ctx", 1)
-
-    pre_near = over_cores(*sum_over_cores(in_own, in_other, near_part, by_up, hidden_first))
-    pre_first = over_cores(*sum_over_cores(in_own, in_other, first_far, by_up, pre_near))
-    hidden_second = over_cores(
-        *sum_over_cores(grad_own, grad_other, second_far, by_down, pre_first)
-    )
-    pre_second = over_cores(*sum_over_cores(in_own, in_other, second_far, by_up, hidden_second))
-
-    homes = {}
-    back = None
-    for part, pre, hidden in (
-        (near_part, pre_near, hidden_near),
-        (first_far, pre_first, hidden_first),
-        (second_far, pre_second, hidden_second),
+    hidden_first = one_product(grad_own, grad_other, first_far, by_down, send_in[0])
+    hidden_first_sum = over_cores(*hidden_first)
+    hidden_first_all = sum_over_rest(hidden_first_sum, bits)
+    for k in second_far:
+        in_own[k] = pairs_of(after(send_in[k], *[in_own[k] for k in first_far], hidden_near_sum), k)
+    for k in first_far:
+        in_other[k] = swap(in_own[k], "ctx", 1)
+    for k in second_far:
+        in_other[k] = swap(in_own[k], "ctx", 1)
+    pre_near = two_products(in_own, in_other, near_part, by_up, hidden_first_sum)
+    pre_near_sum = over_cores(*pre_near)
+    pre_near_all = sum_over_rest(pre_near_sum, bits)
+    pre_first = two_products(in_own, in_other, first_far, by_up, pre_near[0])
+    pre_first_sum = over_cores(*pre_first)
+    pre_first_all = sum_over_rest(pre_first_sum, bits)
+    hidden_second = one_product(grad_own, grad_other, second_far, by_down, pre_first_sum)
+    hidden_second_sum = over_cores(*hidden_second)
+    hidden_second_all = sum_over_rest(hidden_second_sum, bits)
+    pre_second = two_products(in_own, in_other, second_far, by_up, pre_first_sum)
+    pre_second_sum = over_cores(*pre_second)
+    pre_second_all = sum_over_rest(pre_second_sum, bits)
+
+    returned = []
+    for pre, hidden in (
+        (pre_near_all, hidden_near_all),
+        (pre_first_all, hidden_first_all),
+        (pre_second_all, hidden_second_all),
     ):
-        pre, hidden = sum_over_rest(pre, bits), sum_over_rest(hidden, bits)
         slope = (hidden.astype(F32) * silu_slope(pre.astype(F32))).astype(BF16)
         got = swap(slope, "exp", 1)
-        if back is not None:
-            got = after(got, back)
+        if returned:
+            got = after(got, returned[-1][0])
         slope = jnp.concatenate(
             [jnp.where(core == 0, slope, got), jnp.where(core == 0, got, slope)], axis=0
         )
         back = dot(slope, up_local, 1, 1).astype(BF16)
-        blocks = back.reshape(2, len(part) * capacity, group)
-        got = swap(blocks[1], "ctx", 1)
-        rows = (blocks[0].astype(F32) + got.astype(F32)).astype(BF16)
+        back = back.reshape(2, back.shape[0] // 2, group)
+        returned.append((back, swap(back[1], "ctx", 1)))
+    homes = {}
+    for index, part in enumerate((near_part, first_far, second_far)):
+        back, got = returned[index]
+        if index == 1:
+            got = after(got, returned[2][0])
+        rows = (back[0].astype(F32) + got.astype(F32)).astype(BF16)
         for i, k in enumerate(part):
             homes[k] = pairs_of(rows[i * capacity : (i + 1) * capacity], k)
     homes = [homes[k] for k in range(experts)]
@@ -412,11 +437,11 @@
     leaving = (keep, swap(give, "ctx", 1))
     query_g, key_near, value_near = call(
         near_kernel, [slim, wide, wide], scalars,
-        (queries, keys, values, grad_out, keep_in, given, weights)
+        (queries, pair, grad_out, keep_in, given, weights)
     )
     key_g, value_g = call(
         far_kernel, [slim, slim], scalars,
-        (keys, values, key_near, value_near) + leaving
+        (pair, key_near, value_near) + leaving
     )
     return query_g, key_g, value_g
 

time: 196 us -> 202 us (1.031)
  starting transfers between devices: 54.4 us -> 61.7 us
  matrix products: 32.3 us -> 25.4 us
  other arithmetic: 4.42 us -> 10.4 us
  local copies, waits for them, and re-layouts: 8.14 us -> 5.11 us
  waiting for transfers between devices: 82.1 us -> 84.3 us
    dot_general x15 -> x12, matrix products: 32.3 us -> 25.4 us  [dot(): lax.dot_general(left, right, (((left_dim,), (right_dim,)), ((), ())), pre...]
    ppermute x39, starting transfers between devices: 45.1 us -> 49.4 us  [swap(): return lax.ppermute(array, axis, [(i, i ^ distance) for i in range(size)])]
    unnamed x36 -> x33, local copies, waits for them, and re-layouts: 8.05 us -> 3.88 us
    ppermute x6, starting transfers between devices: 9.3 us -> 12.2 us  [trade(): lax.ppermute(array, 'ctx', [(2 * partner(i) + s, 2 * i + s) for i in rang...]
  transfers between devices with their start and end apart: 45 -> 45, of which waited for: 22 -> 21; matrix products, arithmetic and copies ran while one was open for 18% -> 16% of each run, Pallas kernels for 5% -> 4%
where the time goes in v9:
time: 202 us; the launch traced here: 201 us
  waiting for transfers between devices  84.3 us (42%)
  starting transfers between devices  61.7 us (31%)
  matrix products  25.4 us (13%)
  Pallas kernels  13.2 us (7%)
  other arithmetic  10.4 us (5%)
  local copies, waits for them, and re-layouts  5.11 us (3%)
    ppermute x39, waiting for transfers between devices, swap(): return lax.ppermute(array, axis, [(i, i ^ distance) for i in range(size)])  72 us
    ppermute x39, starting transfers between devices, swap(): return lax.ppermute(array, axis, [(i, i ^ distance) for i in range(size)])  49.4 us
    dot_general x12, matrix products, dot(): lax.dot_general(left, right, (((left_dim,), (right_dim,)), ((), ())), pre...  25.4 us
    pallas_call x7, Pallas kernels, call(): pl.pallas_call(kernel, out_shape=list(out_shapes), in_specs=[SMEM] * len(...  13.2 us
    ppermute x6, waiting for transfers between devices, trade(): lax.ppermute(array, 'ctx', [(2 * partner(i) + s, 2 * i + s) for i in rang...  12.3 us
    ppermute x6, starting transfers between devices, trade(): lax.ppermute(array, 'ctx', [(2 * partner(i) + s, 2 * i + s) for i in rang...  12.2 us
  transfers between devices with their start and end apart: 45, of which 21 were waited for; matrix products, arithmetic and copies ran while one was open for 16% of the time, Pallas kernels for 4%

profile of v9, /device:TPU:0, one launch (start us, length us, event | category | flops | bytes accessed | tf_op | source)
XLA Modules:
  0.0 201.3 jit_solution(8538192583411804833)
XLA Ops:
  4.5 3.0 %collective-permute-start = (bf16[6,128,128]{2,1,0:T(8,128)(2,1)S(1)}, bf16[6,128,128]{2,1,0:T(8,128)(2,1)S(1)}, u32[]{:S(2)}, u32[]{:S(2)}) collective-permute-start(bf16[6,128,128]{2,1,0:T(8,128)(2,1)S(1)} %get-tuple-element.47), channel_id=1, source_target_pairs={{0,4},{4,0},{8,12},{12,8},{16,20},{20,16},{24,28},{28,24},{1,5},{5... | collective-permute-start | bytes 589832 | tf_op jit(solution)/shard_map/ppermute | solution.py:205
  15.0 2.5 %shard_map.114 = (f32[128,1536]{1,0:T(8,128)S(1)}, bf16[12,128,128]{2,1,0:T(8,128)(2,1)S(1)}) custom-call(s32[3]{0:T(128)S(1)} %pad_add_fusion.place_ref, f32[12]{0:T(128)S(1)} %neg.11.rates_ref, bf16[128,1536]{1,0:T(8,128)(2,1)S(1)} %copy-done, bf16[256,1536]{1,0:T(8,128)(2,1)S(1)} %constant_dynamic-update-slice_fusion.pair_ref), custom_call_target="tpu_custom_call" | custom-call | flops 1 | bytes 40000000 | tf_op jit(solution)/shard_map/pallas_call | solution.py:192
  21.8 3.0 %collective-permute-start.5 = (bf16[6,128,128]{2,1,0:T(8,128)(2,1)}, bf16[6,128,128]{2,1,0:T(8,128)(2,1)}, u32[]{:S(2)}, u32[]{:S(2)}) collective-permute-start(bf16[6,128,128]{2,1,0:T(8,128)(2,1)} %add_convert_fusion.11), channel_id=1, source_target_pairs={{0,0},{4,4},{24,8},{28,12},{16,16},{20,20},{8,24},{12,28},{1,1},{5... | collective-permute-start | bytes 589832 | tf_op jit(solution)/shard_map/ppermute | solution.py:209
  24.8 3.0 %collective-permute-start.6 = (bf16[6,128,128]{2,1,0:T(8,128)(2,1)}, bf16[6,128,128]{2,1,0:T(8,128)(2,1)}, u32[]{:S(2)}, u32[]{:S(2)}) collective-permute-start(bf16[6,128,128]{2,1,0:T(8,128)(2,1)} %add_convert_fusion.11), channel_id=1, source_target_pairs={{0,0},{4,4},{16,8},{20,12},{8,16},{12,20},{24,24},{28,28},{1,1},{5... | collective-permute-start | bytes 589832 | tf_op jit(solution)/shard_map/ppermute | solution.py:209
  29.4 3.8 %collective-permute-start.13 = (bf16[72,1536]{1,0:T(8,128)(2,1)}, bf16[72,1536]{1,0:T(8,128)(2,1)S(1)}, u32[]{:S(2)}, u32[]{:S(2)}) collective-permute-start(bf16[72,1536]{1,0:T(8,128)(2,1)} %copy-done.5), channel_id=1, source_target_pairs={{0,24},{4,28},{8,16},{12,20},{16,8},{20,12},{24,0},{28,4},{1,25},{... | collective-permute-start | bytes 663560 | tf_op jit(solution)/shard_map/ppermute | solution.py:205
  36.7 9.6 %collective-permute-start.21 = (bf16[72,1536]{1,0:T(8,128)(2,1)}, bf16[72,1536]{1,0:T(8,128)(2,1)S(1)}, u32[]{:S(2)}, u32[]{:S(2)}) collective-permute-start(bf16[72,1536]{1,0:T(8,128)(2,1)} %copy-done.4), channel_id=1, source_target_pairs={{0,16},{4,20},{8,24},{12,28},{16,0},{20,4},{24,8},{28,12},{1,17},{... | collective-permute-start | bytes 663560 | tf_op jit(solution)/shard_map/ppermute | solution.py:205
  48.1 5.5 %fusion.24 = bf16[288,2304]{1,0:T(8,128)(2,1)S(1)} fusion(bf16[288,1536]{1,0:T(8,128)(2,1)S(1)} %pad_maximum_fusion, bf16[1,2304,1536]{2,1,0:T(8,128)(2,1)} %param.14), kind=kOutput, calls=%fused_computation.24 | convolution fusion | flops 2039095296 | bytes 9289728 | tf_op jit(solution)/shard_map/dot_general | solution.py:22
  55.0 6.3 %collective-permute-start.11 = (bf16[72,1536]{1,0:T(8,128)(2,1)S(1)}, bf16[72,1536]{1,0:T(8,128)(2,1)S(1)}, u32[]{:S(2)}, u32[]{:S(2)}) collective-permute-start(bf16[72,1536]{1,0:T(8,128)(2,1)S(1)} %get-tuple-element.57), channel_id=1, source_target_pairs={{0,8},{4,12},{8,0},{12,4},{16,24},{20,28},{24,16},{28,20},{1,9},{5... | collective-permute-start | bytes 663560 | tf_op jit(solution)/shard_map/ppermute | solution.py:205
  69.6 2.8 %collective-permute-done.23 = bf16[72,1536]{1,0:T(8,128)(2,1)S(1)} collective-permute-done((bf16[72,1536]{1,0:T(8,128)(2,1)S(1)}, bf16[72,1536]{1,0:T(8,128)(2,1)S(1)}, u32[]{:S(2)}, u32[]{:S(2)}) %collective-permute-start.23) | collective-permute-done | bytes 221216 | tf_op jit(solution)/shard_map/ppermute | solution.py:205
  75.8 3.2 %collective-permute-done.12 = bf16[72,1536]{1,0:T(8,128)(2,1)S(1)} collective-permute-done((bf16[72,1536]{1,0:T(8,128)(2,1)S(1)}, bf16[72,1536]{1,0:T(8,128)(2,1)S(1)}, u32[]{:S(2)}, u32[]{:S(2)}) %collective-permute-start.12) | collective-permute-done | bytes 221216 | tf_op jit(solution)/shard_map/ppermute | solution.py:205
  80.5 2.6 %collective-permute-done.24 = bf16[72,1536]{1,0:T(8,128)(2,1)S(1)} collective-permute-done((bf16[72,1536]{1,0:T(8,128)(2,1)S(1)}, bf16[72,1536]{1,0:T(8,128)(2,1)S(1)}, u32[]{:S(2)}, u32[]{:S(2)}) %collective-permute-start.24) | collective-permute-done | bytes 221216 | tf_op jit(solution)/shard_map/ppermute | solution.py:205
  84.9 3.1 %collective-permute-start.8 = (bf16[144,2304]{1,0:T(8,128)(2,1)S(1)}, bf16[144,2304]{1,0:T(8,128)(2,1)S(1)}, u32[]{:S(2)}, u32[]{:S(2)}) collective-permute-start(bf16[144,2304]{1,0:T(8,128)(2,1)S(1)} %fusion.91), channel_id=1, source_target_pairs={{0,2},{1,3},{2,0},{3,1},{4,6},{5,7},{6,4},{7,5},{8,10},{9,11},{10,... | collective-permute-start | bytes 1990664 | tf_op jit(solution)/shard_map/ppermute | solution.py:205
  88.0 10.1 %collective-permute-done.28 = bf16[72,1536]{1,0:T(8,128)(2,1)S(1)} collective-permute-done((bf16[72,1536]{1,0:T(8,128)(2,1)S(1)}, bf16[72,1536]{1,0:T(8,128)(2,1)S(1)}, u32[]{:S(2)}, u32[]{:S(2)}) %collective-permute-start.28) | collective-permute-done | bytes 221216 | tf_op jit(solution)/shard_map/ppermute | solution.py:205
  102.0 2.4 %fusion.30 = bf16[144,2304]{1,0:T(8,128)(2,1)S(1)} fusion(bf16[144,1536]{1,0:T(8,128)(2,1)S(1)} %pad_maximum_fusion.4, bf16[1,2304,1536]{2,1,0:T(8,128)(2,1)S(1)} %bitcast.101), kind=kOutput, calls=%fused_computation.26 | convolution fusion | flops 1019547648 | bytes 8183808 | tf_op jit(solution)/shard_map/dot_general | solution.py:22
  118.1 15.7 %collective-permute-done.27 = bf16[72,2304]{1,0:T(8,128)(2,1)S(1)} collective-permute-done((bf16[72,2304]{1,0:T(8,128)(2,1)S(1)}, bf16[72,2304]{1,0:T(8,128)(2,1)S(1)}, u32[]{:S(2)}, u32[]{:S(2)}) %collective-permute-start.27) | collective-permute-done | bytes 331808 | tf_op jit(solution)/shard_map/ppermute | solution.py:205
  133.8 6.5 %collective-permute-done.31 = bf16[72,2304]{1,0:T(8,128)(2,1)S(1)} collective-permute-done((bf16[72,2304]{1,0:T(8,128)(2,1)S(1)}, bf16[72,2304]{1,0:T(8,128)(2,1)S(1)}, u32[]{:S(2)}, u32[]{:S(2)}) %collective-permute-start.31) | collective-permute-done | bytes 331808 | tf_op jit(solution)/shard_map/ppermute | solution.py:205
  149.4 3.8 %collective-permute-done.33 = bf16[72,1536]{1,0:T(8,128)(2,1)S(1)} collective-permute-done((bf16[72,1536]{1,0:T(8,128)(2,1)S(1)}, bf16[72,1536]{1,0:T(8,128)(2,1)S(1)}, u32[]{:S(2)}, u32[]{:S(2)}) %collective-permute-start.33) | collective-permute-done | bytes 221216 | tf_op jit(solution)/shard_map/ppermute | solution.py:205
  154.7 7.2 %collective-permute-done.19 = bf16[144,1536]{1,0:T(8,128)(2,1)S(1)} collective-permute-done((bf16[144,1536]{1,0:T(8,128)(2,1)S(1)}, bf16[144,1536]{1,0:T(8,128)(2,1)S(1)}, u32[]{:S(2)}, u32[]{:S(2)}) %collective-permute-start.19) | collective-permute-done | bytes 442400 | tf_op jit(solution)/shard_map/ppermute | solution.py:205
  165.0 4.7 %collective-permute-done.20.refs_1_ = bf16[72,1536]{1,0:T(8,128)(2,1)S(1)} collective-permute-done((bf16[72,1536]{1,0:T(8,128)(2,1)S(1)}, bf16[72,1536]{1,0:T(8,128)(2,1)S(1)}, u32[]{:S(2)}, u32[]{:S(2)}) %collective-permute-start.20) | collective-permute-done | bytes 221216 | tf_op jit(solution)/shard_map/ppermute | solution.py:205
  171.4 5.8 %collective-permute-done.40 = bf16[6,128,128]{2,1,0:T(8,128)(2,1)S(1)} collective-permute-done((bf16[6,128,128]{2,1,0:T(8,128)(2,1)S(1)}, bf16[6,128,128]{2,1,0:T(8,128)(2,1)S(1)}, u32[]{:S(2)}, u32[]{:S(2)}) %collective-permute-start.40) | collective-permute-done | bytes 196640 | tf_op jit(solution)/shard_map/ppermute | solution.py:205
  177.9 5.1 %collective-permute-done.41 = bf16[6,128,128]{2,1,0:T(8,128)(2,1)S(1)} collective-permute-done((bf16[6,128,128]{2,1,0:T(8,128)(2,1)S(1)}, bf16[6,128,128]{2,1,0:T(8,128)(2,1)S(1)}, u32[]{:S(2)}, u32[]{:S(2)}) %collective-permute-start.41) | collective-permute-done | bytes 196640 | tf_op jit(solution)/shard_map/ppermute | solution.py:209
  183.1 3.1 %collective-permute-start.42 = (bf16[6,128,128]{2,1,0:T(8,128)(2,1)S(1)}, bf16[6,128,128]{2,1,0:T(8,128)(2,1)S(1)}, u32[]{:S(2)}, u32[]{:S(2)}) collective-permute-start(bf16[6,128,128]{2,1,0:T(8,128)(2,1)S(1)} %add_convert_fusion.10), channel_id=1, source_target_pairs={{16,0},{20,4},{8,8},{12,12},{0,16},{4,20},{24,24},{28,28},{17,1},{... | collective-permute-start | bytes 589832 | tf_op jit(solution)/shard_map/ppermute | solution.py:209
  187.0 5.1 %collective-permute-done.42 = bf16[6,128,128]{2,1,0:T(8,128)(2,1)S(1)} collective-permute-done((bf16[6,128,128]{2,1,0:T(8,128)(2,1)S(1)}, bf16[6,128,128]{2,1,0:T(8,128)(2,1)S(1)}, u32[]{:S(2)}, u32[]{:S(2)}) %collective-permute-start.42) | collective-permute-done | bytes 196640 | tf_op jit(solution)/shard_map/ppermute | solution.py:209
  194.0 4.0 %shard_map.117 = (bf16[128,1536]{1,0:T(8,128)(2,1)}, f32[128,1536]{1,0:T(8,128)S(1)}, f32[128,1536]{1,0:T(8,128)S(1)}) custom-call(s32[3]{0:T(128)S(1)} %pad_add_fusion.place_ref, f32[12]{0:T(128)S(1)} %neg.11.rates_ref, bf16[128,1536]{1,0:T(8,128)(2,1)S(1)} %copy-done, bf16[256,1536]{1,0:T(8,128)(2,1)S(1)} %constant_dynamic-update-slice_fusion.pair_ref, ...), custom_call_target="tpu_custom_call" | custom-call | flops 1 | bytes 1 | tf_op jit(solution)/shard_map/pallas_call | solution.py:192
  (161 shorter events, 78.3 us)
Async XLA Ops:
  17.6 15.6 %collective-permute-start.1 = (bf16[72,1536]{1,0:T(8,128)(2,1)}, bf16[72,1536]{1,0:T(8,128)(2,1)}, u32[]{:S(2)}, u32[]{:S(2)}) collective-permute-start(bf16[72,1536]{1,0:T(8,128)(2,1)} %copy-done.6), channel_id=1, source_target_pairs={{0,8},{4,12},{8,0},{12,4},{16,24},{20,28},{24,16},{28,20},{1,9},{5... | collective-permute-start | bytes 663560 | tf_op jit(solution)/shard_map/ppermute | solution.py:205
  21.8 11.8 %collective-permute-start.5 = (bf16[6,128,128]{2,1,0:T(8,128)(2,1)}, bf16[6,128,128]{2,1,0:T(8,128)(2,1)}, u32[]{:S(2)}, u32[]{:S(2)}) collective-permute-start(bf16[6,128,128]{2,1,0:T(8,128)(2,1)} %add_convert_fusion.11), channel_id=1, source_target_pairs={{0,0},{4,4},{24,8},{28,12},{16,16},{20,20},{8,24},{12,28},{1,1},{5... | collective-permute-start | bytes 589832 | tf_op jit(solution)/shard_map/ppermute | solution.py:209
  27.8 19.1 %collective-permute-start.2 = (bf16[72,1536]{1,0:T(8,128)(2,1)S(1)}, bf16[72,1536]{1,0:T(8,128)(2,1)S(1)}, u32[]{:S(2)}, u32[]{:S(2)}) collective-permute-start(bf16[72,1536]{1,0:T(8,128)(2,1)S(1)} %get-tuple-element.50), channel_id=1, source_target_pairs={{0,4},{4,0},{8,12},{12,8},{16,20},{20,16},{24,28},{28,24},{1,5},{5... | collective-permute-start | bytes 663560 | tf_op jit(solution)/shard_map/ppermute | solution.py:205
  29.4 16.9 %collective-permute-start.13 = (bf16[72,1536]{1,0:T(8,128)(2,1)}, bf16[72,1536]{1,0:T(8,128)(2,1)S(1)}, u32[]{:S(2)}, u32[]{:S(2)}) collective-permute-start(bf16[72,1536]{1,0:T(8,128)(2,1)} %copy-done.5), channel_id=1, source_target_pairs={{0,24},{4,28},{8,16},{12,20},{16,8},{20,12},{24,0},{28,4},{1,25},{... | collective-permute-start | bytes 663560 | tf_op jit(solution)/shard_map/ppermute | solution.py:205
  33.2 13.7 %collective-permute-start.4 = (bf16[72,1536]{1,0:T(8,128)(2,1)}, bf16[72,1536]{1,0:T(8,128)(2,1)S(1)}, u32[]{:S(2)}, u32[]{:S(2)}) collective-permute-start(bf16[72,1536]{1,0:T(8,128)(2,1)} %collective-permute-done.1), channel_id=1, source_target_pairs={{0,4},{4,0},{8,12},{12,8},{16,20},{20,16},{24,28},{28,24},{1,5},{5... | collective-permute-start | bytes 663560 | tf_op jit(solution)/shard_map/ppermute | solution.py:205
  35.0 18.8 %collective-permute-start.9 = (bf16[6,128,128]{2,1,0:T(8,128)(2,1)S(1)}, bf16[6,128,128]{2,1,0:T(8,128)(2,1)S(1)}, u32[]{:S(2)}, u32[]{:S(2)}) collective-permute-start(bf16[6,128,128]{2,1,0:T(8,128)(2,1)S(1)} %get-tuple-element.90), channel_id=1, source_target_pairs={{0,4},{4,0},{8,12},{12,8},{16,20},{20,16},{24,28},{28,24},{1,5},{5... | collective-permute-start | bytes 589832 | tf_op jit(solution)/shard_map/ppermute | solution.py:205
  36.7 24.7 %collective-permute-start.21 = (bf16[72,1536]{1,0:T(8,128)(2,1)}, bf16[72,1536]{1,0:T(8,128)(2,1)S(1)}, u32[]{:S(2)}, u32[]{:S(2)}) collective-permute-start(bf16[72,1536]{1,0:T(8,128)(2,1)} %copy-done.4), channel_id=1, source_target_pairs={{0,16},{4,20},{8,24},{12,28},{16,0},{20,4},{24,8},{28,12},{1,17},{... | collective-permute-start | bytes 663560 | tf_op jit(solution)/shard_map/ppermute | solution.py:205
  46.3 15.4 %collective-permute-start.14 = (bf16[72,1536]{1,0:T(8,128)(2,1)S(1)}, bf16[72,1536]{1,0:T(8,128)(2,1)S(1)}, u32[]{:S(2)}, u32[]{:S(2)}) collective-permute-start(bf16[72,1536]{1,0:T(8,128)(2,1)S(1)} %collective-permute-done.13), channel_id=1, source_target_pairs={{0,4},{4,0},{8,12},{12,8},{16,20},{20,16},{24,28},{28,24},{1,5},{5... | collective-permute-start | bytes 663560 | tf_op jit(solution)/shard_map/ppermute | solution.py:205
  53.7 30.9 %collective-permute-start.7 = (bf16[144,2304]{1,0:T(8,128)(2,1)S(1)}, bf16[144,2304]{1,0:T(8,128)(2,1)S(1)}, u32[]{:S(2)}, u32[]{:S(2)}) collective-permute-start(bf16[144,2304]{1,0:T(8,128)(2,1)S(1)} %dynamic-slice_bitcast_fusion), channel_id=1, source_target_pairs={{0,1},{1,0},{2,3},{3,2},{4,5},{5,4},{6,7},{7,6},{8,9},{9,8},{10,11... | collective-permute-start | bytes 1990664 | tf_op jit(solution)/shard_map/ppermute | solution.py:205
  55.0 12.7 %collective-permute-start.11 = (bf16[72,1536]{1,0:T(8,128)(2,1)S(1)}, bf16[72,1536]{1,0:T(8,128)(2,1)S(1)}, u32[]{:S(2)}, u32[]{:S(2)}) collective-permute-start(bf16[72,1536]{1,0:T(8,128)(2,1)S(1)} %get-tuple-element.57), channel_id=1, source_target_pairs={{0,8},{4,12},{8,0},{12,4},{16,24},{20,28},{24,16},{28,20},{1,9},{5... | collective-permute-start | bytes 663560 | tf_op jit(solution)/shard_map/ppermute | solution.py:205
  61.7 12.6 %collective-permute-start.22 = (bf16[72,1536]{1,0:T(8,128)(2,1)S(1)}, bf16[72,1536]{1,0:T(8,128)(2,1)S(1)}, u32[]{:S(2)}, u32[]{:S(2)}) collective-permute-start(bf16[72,1536]{1,0:T(8,128)(2,1)S(1)} %collective-permute-done.21), channel_id=1, source_target_pairs={{0,4},{4,0},{8,12},{12,8},{16,20},{20,16},{24,28},{28,24},{1,5},{5... | collective-permute-start | bytes 663560 | tf_op jit(solution)/shard_map/ppermute | solution.py:205
  74.5 36.8 %collective-permute-start.35 = (bf16[72,2304]{1,0:T(8,128)(2,1)S(1)}, bf16[72,2304]{1,0:T(8,128)(2,1)S(1)}, u32[]{:S(2)}, u32[]{:S(2)}) collective-permute-start(bf16[72,2304]{1,0:T(8,128)(2,1)S(1)} %fusion.113), channel_id=1, source_target_pairs={{0,2},{1,3},{2,0},{3,1},{4,6},{5,7},{6,4},{7,5},{8,10},{9,11},{10,... | collective-permute-start | bytes 995336 | tf_op jit(solution)/shard_map/ppermute | solution.py:205
  80.4 26.5 %collective-permute-start.16 = (bf16[144,2304]{1,0:T(8,128)(2,1)S(1)}, bf16[144,2304]{1,0:T(8,128)(2,1)S(1)}, u32[]{:S(2)}, u32[]{:S(2)}) collective-permute-start(bf16[144,2304]{1,0:T(8,128)(2,1)S(1)} %fusion.33), channel_id=1, source_target_pairs={{0,1},{1,0},{2,3},{3,2},{4,5},{5,4},{6,7},{7,6},{8,9},{9,8},{10,11... | collective-permute-start | bytes 1990664 | tf_op jit(solution)/shard_map/ppermute | solution.py:205
  84.5 13.9 %collective-permute-start.25 = (bf16[72,2304]{1,0:T(8,128)(2,1)S(1)}, bf16[72,2304]{1,0:T(8,128)(2,1)S(1)}, u32[]{:S(2)}, u32[]{:S(2)}) collective-permute-start(bf16[72,2304]{1,0:T(8,128)(2,1)S(1)} %fusion.42), channel_id=1, source_target_pairs={{0,1},{1,0},{2,3},{3,2},{4,5},{5,4},{6,7},{7,6},{8,9},{9,8},{10,11... | collective-permute-start | bytes 995336 | tf_op jit(solution)/shard_map/ppermute | solution.py:205
  84.8 13.3 %collective-permute-start.28 = (bf16[72,1536]{1,0:T(8,128)(2,1)S(1)}, bf16[72,1536]{1,0:T(8,128)(2,1)S(1)}, u32[]{:S(2)}, u32[]{:S(2)}) collective-permute-start(bf16[72,1536]{1,0:T(8,128)(2,1)S(1)} %get-tuple-element.71), channel_id=1, source_target_pairs={{0,16},{4,20},{8,24},{12,28},{16,0},{20,4},{24,8},{28,12},{1,17},{... | collective-permute-start | bytes 663560 | tf_op jit(solution)/shard_map/ppermute | solution.py:205
  84.9 56.4 %collective-permute-start.8 = (bf16[144,2304]{1,0:T(8,128)(2,1)S(1)}, bf16[144,2304]{1,0:T(8,128)(2,1)S(1)}, u32[]{:S(2)}, u32[]{:S(2)}) collective-permute-start(bf16[144,2304]{1,0:T(8,128)(2,1)S(1)} %fusion.91), channel_id=1, source_target_pairs={{0,2},{1,3},{2,0},{3,1},{4,6},{5,7},{6,4},{7,5},{8,10},{9,11},{10,... | collective-permute-start | bytes 1990664 | tf_op jit(solution)/shard_map/ppermute | solution.py:205
  99.7 11.6 %collective-permute-start.36 = (bf16[72,2304]{1,0:T(8,128)(2,1)S(1)}, bf16[72,2304]{1,0:T(8,128)(2,1)S(1)}, u32[]{:S(2)}, u32[]{:S(2)}) collective-permute-start(bf16[72,2304]{1,0:T(8,128)(2,1)S(1)} %fusion.54), channel_id=1, source_target_pairs={{0,2},{1,3},{2,0},{3,1},{4,6},{5,7},{6,4},{7,5},{8,10},{9,11},{10,... | collective-permute-start | bytes 995336 | tf_op jit(solution)/shard_map/ppermute | solution.py:205
  108.7 32.6 %collective-permute-start.17 = (bf16[144,2304]{1,0:T(8,128)(2,1)S(1)}, bf16[144,2304]{1,0:T(8,128)(2,1)S(1)}, u32[]{:S(2)}, u32[]{:S(2)}) collective-permute-start(bf16[144,2304]{1,0:T(8,128)(2,1)S(1)} %add_convert_fusion.1), channel_id=1, source_target_pairs={{0,2},{1,3},{2,0},{3,1},{4,6},{5,7},{6,4},{7,5},{8,10},{9,11},{10,... | collective-permute-start | bytes 1990664 | tf_op jit(solution)/shard_map/ppermute | solution.py:205
  111.3 22.5 %collective-permute-start.27 = (bf16[72,2304]{1,0:T(8,128)(2,1)S(1)}, bf16[72,2304]{1,0:T(8,128)(2,1)S(1)}, u32[]{:S(2)}, u32[]{:S(2)}) collective-permute-start(bf16[72,2304]{1,0:T(8,128)(2,1)S(1)} %fusion.112), channel_id=1, source_target_pairs={{0,2},{1,3},{2,0},{3,1},{4,6},{5,7},{6,4},{7,5},{8,10},{9,11},{10,... | collective-permute-start | bytes 995336 | tf_op jit(solution)/shard_map/ppermute | solution.py:205
  113.2 27.1 %collective-permute-start.31 = (bf16[72,2304]{1,0:T(8,128)(2,1)S(1)}, bf16[72,2304]{1,0:T(8,128)(2,1)S(1)}, u32[]{:S(2)}, u32[]{:S(2)}) collective-permute-start(bf16[72,2304]{1,0:T(8,128)(2,1)S(1)} %fusion.69), channel_id=1, source_target_pairs={{0,2},{1,3},{2,0},{3,1},{4,6},{5,7},{6,4},{7,5},{8,10},{9,11},{10,... | collective-permute-start | bytes 995336 | tf_op jit(solution)/shard_map/ppermute | solution.py:205
  117.8 22.9 %collective-permute-start.38 = (bf16[72,1536]{1,0:T(8,128)(2,1)S(1)}, bf16[72,1536]{1,0:T(8,128)(2,1)S(1)}, u32[]{:S(2)}, u32[]{:S(2)}) collective-permute-start(bf16[72,1536]{1,0:T(8,128)(2,1)S(1)} %slice.45), channel_id=1, source_target_pairs={{0,4},{4,0},{8,12},{12,8},{16,20},{20,16},{24,28},{28,24},{1,5},{5... | collective-permute-start | bytes 663560 | tf_op jit(solution)/shard_map/ppermute | solution.py:205
  140.8 22.9 %collective-permute-start.39 = (bf16[72,1536]{1,0:T(8,128)(2,1)S(1)}, bf16[72,1536]{1,0:T(8,128)(2,1)S(1)}, u32[]{:S(2)}, u32[]{:S(2)}) collective-permute-start(bf16[72,1536]{1,0:T(8,128)(2,1)S(1)} %add_convert_fusion.8), channel_id=1, source_target_pairs={{0,24},{4,28},{8,16},{12,20},{16,8},{20,12},{24,0},{28,4},{1,25},{... | collective-permute-start | bytes 663560 | tf_op jit(solution)/shard_map/ppermute | solution.py:205
  147.7 14.2 %collective-permute-start.19 = (bf16[144,1536]{1,0:T(8,128)(2,1)S(1)}, bf16[144,1536]{1,0:T(8,128)(2,1)S(1)}, u32[]{:S(2)}, u32[]{:S(2)}) collective-permute-start(bf16[144,1536]{1,0:T(8,128)(2,1)S(1)} %slice.39), channel_id=1, source_target_pairs={{0,4},{4,0},{8,12},{12,8},{16,20},{20,16},{24,28},{28,24},{1,5},{5... | collective-permute-start | bytes 1327112 | tf_op jit(solution)/shard_map/ppermute | solution.py:205
  153.2 11.7 %collective-permute-start.34 = (bf16[72,1536]{1,0:T(8,128)(2,1)S(1)}, bf16[72,1536]{1,0:T(8,128)(2,1)S(1)}, u32[]{:S(2)}, u32[]{:S(2)}) collective-permute-start(bf16[72,1536]{1,0:T(8,128)(2,1)S(1)} %add_convert_fusion.9), channel_id=1, source_target_pairs={{0,16},{4,20},{8,24},{12,28},{16,0},{20,4},{24,8},{28,12},{1,17},{... | collective-permute-start | bytes 663560 | tf_op jit(solution)/shard_map/ppermute | solution.py:205
  (37 other events, 298.6 us)

commit v10 on v9

--- a/solution.py
+++ b/solution.py
@@ -345,18 +345,16 @@
     grad_other = {0: swap(after(send_grad[0], total), "ctx", 1)}
     for k in near_part[1:]:
         grad_own[k] = pairs_of(after(send_grad[k], total), k)
+    for k in near_part[1:]:
+        grad_other[k] = swap(grad_own[k], "ctx", 1)
     before = None
     for index, reach in enumerate(reaches):
         events = [intra] if index == 1 else []
         before, upto = scan_step(
             before, total, reach, decay_rates, place, block_len, False, *events
         )
-    for k in near_part[1:]:
-        grad_other[k] = swap(after(grad_own[k], upto), "ctx", 1)
+    keep, give = scan_ends(before, key_mine, partner, decay_rates, place, block_len, False)
     for k in first_far:
-        grad_own[k] = pairs_of(after(send_grad[k], upto), k)
-    keep, give = scan_ends(before, key_mine, partner, decay_rates, place, block_len, False)
-    for k in second_far:
         grad_own[k] = pairs_of(after(send_grad[k], give), k)
     for k in first_far:
         grad_other[k] = swap(grad_own[k], "ctx", 1)
@@ -364,6 +362,8 @@
     hidden_near = one_product(grad_own, grad_other, near_part, by_down, give)
     hidden_near_sum = over_cores(*hidden_near)
     hidden_near_all = sum_over_rest(hidden_near_sum, bits)
+    given, hidden_near_sum = lax.optimization_barrier((given, hidden_near_sum))
+    hidden_near_all = sum_over_rest(hidden_near_sum, bits)
     send_in = call(
         attend_kernel, [slots] * experts, scalars, (queries, intra, choose, keep, given),
         [pltpu.VMEM((block_len, group), BF16)],
@@ -371,29 +371,31 @@
     in_own, in_other = {0: send_in[0]}, {0: swap(send_in[0], "ctx", 1)}
     for k in [*near_part[1:], *first_far]:
         in_own[k] = pairs_of(send_in[k], k)
-    for k in second_far:
-        grad_other[k] = swap(after(grad_own[k], send_in[0]), "ctx", 1)
     for k in near_part[1:]:
         in_other[k] = swap(in_own[k], "ctx", 1)
-    hidden_first = one_product(grad_own, grad_other, first_far, by_down, send_in[0])
+    hidden_first = one_product(grad_own, grad_other, first_far, by_down, hidden_near_sum, *[in_own[k] for k in first_far])
     hidden_first_sum = over_cores(*hidden_first)
     hidden_first_all = sum_over_rest(hidden_first_sum, bits)
     for k in second_far:
-        in_own[k] = pairs_of(after(send_in[k], *[in_own[k] for k in first_far], hidden_near_sum), k)
+        in_own[k] = pairs_of(after(send_in[k], *[in_own[k] for k in first_far]), k)
+    for k in second_far:
+        grad_own[k] = pairs_of(after(send_grad[k], *[in_own[k] for k in first_far]), k)
     for k in first_far:
-        in_other[k] = swap(in_own[k], "ctx", 1)
-    for k in second_far:
-        in_other[k] = swap(in_own[k], "ctx", 1)
-    pre_near = two_products(in_own, in_other, near_part, by_up, hidden_first_sum)
+        in_other[k] = swap(after(in_own[k], *[in_other[k] for k in near_part[1:]]), "ctx", 1)
+    pre_near = two_products(in_own, in_other, near_part, by_up, hidden_first_sum, hidden_near_all)
     pre_near_sum = over_cores(*pre_near)
     pre_near_all = sum_over_rest(pre_near_sum, bits)
-    pre_first = two_products(in_own, in_other, first_far, by_up, pre_near[0])
+    for k in second_far:
+        in_other[k] = swap(after(in_own[k], pre_near_sum), "ctx", 1)
+    for k in second_far:
+        grad_other[k] = swap(after(grad_own[k], pre_near_sum), "ctx", 1)
+    pre_first = two_products(in_own, in_other, first_far, by_up, pre_near_sum, hidden_near_all)
     pre_first_sum = over_cores(*pre_first)
     pre_first_all = sum_over_rest(pre_first_sum, bits)
     hidden_second = one_product(grad_own, grad_other, second_far, by_down, pre_first_sum)
     hidden_second_sum = over_cores(*hidden_second)
     hidden_second_all = sum_over_rest(hidden_second_sum, bits)
-    pre_second = two_products(in_own, in_other, second_far, by_up, pre_first_sum)
+    pre_second = two_products(in_own, in_other, second_far, by_up, hidden_second[0], pre_first_all)
     pre_second_sum = over_cores(*pre_second)
     pre_second_all = sum_over_rest(pre_second_sum, bits)
 
@@ -406,19 +408,17 @@
         slope = (hidden.astype(F32) * silu_slope(pre.astype(F32))).astype(BF16)
         got = swap(slope, "exp", 1)
         if returned:
-            got = after(got, returned[-1][0])
+            got = after(got, returned[-1][2])
         slope = jnp.concatenate(
             [jnp.where(core == 0, slope, got), jnp.where(core == 0, got, slope)], axis=0
         )
         back = dot(slope, up_local, 1, 1).astype(BF16)
-        back = back.reshape(2, back.shape[0] // 2, group)
-        returned.append((back, swap(back[1], "ctx", 1)))
+        sides = back.reshape(2, back.shape[0] // 2, group)
+        returned.append((sides[0], swap(sides[1], "ctx", 1), back))
     homes = {}
     for index, part in enumerate((near_part, first_far, second_far)):
-        back, got = returned[index]
-        if index == 1:
-            got = after(got, returned[2][0])
-        rows = (back[0].astype(F32) + got.astype(F32)).astype(BF16)
+        kept, got, _ = returned[index]
+        rows = (kept.astype(F32) + got.astype(F32)).astype(BF16)
         for i, k in enumerate(part):
             homes[k] = pairs_of(rows[i * capacity : (i + 1) * capacity], k)
     homes = [homes[k] for k in range(experts)]

time: 202 us -> 206 us (1.020)
  matrix products: 25.4 us -> 28.6 us
  other arithmetic: 10.4 us -> 13.4 us
    dot_general x12, matrix products: 25.4 us -> 28.6 us  [dot(): lax.dot_general(left, right, (((left_dim,), (right_dim,)), ((), ())), pre...]
  transfers between devices with their start and end apart: 45 -> 45, of which waited for: 21 -> 19; matrix products, arithmetic and copies ran while one was open for 16% -> 16% of each run, Pallas kernels for 4% -> 4%
where the time goes in v10:
time: 206 us
  waiting for transfers between devices  83.1 us (40%)
  starting transfers between devices  61.1 us (30%)
  matrix products  28.6 us (14%)
  other arithmetic  13.4 us (7%)
  Pallas kernels  13.2 us (6%)
  local copies, waits for them, and re-layouts  5 us (2%)
    ppermute x39, waiting for transfers between devices, swap(): return lax.ppermute(array, axis, [(i, i ^ distance) for i in range(size)])  71 us
    ppermute x39, starting transfers between devices, swap(): return lax.ppermute(array, axis, [(i, i ^ distance) for i in range(size)])  47.9 us
    dot_general x12, matrix products, dot(): lax.dot_general(left, right, (((left_dim,), (right_dim,)), ((), ())), pre...  28.6 us
    pallas_call x7, Pallas kernels, call(): pl.pallas_call(kernel, out_shape=list(out_shapes), in_specs=[SMEM] * len(...  13.2 us
    ppermute x6, starting transfers between devices, trade(): lax.ppermute(array, 'ctx', [(2 * partner(i) + s, 2 * i + s) for i in rang...  13.2 us
    ppermute x6, waiting for transfers between devices, trade(): lax.ppermute(array, 'ctx', [(2 * partner(i) + s, 2 * i + s) for i in rang...  12.2 us
  transfers between devices with their start and end apart: 45, of which 19 were waited for; matrix products, arithmetic and copies ran while one was open for 16% of the time, Pallas kernels for 4%

profile of v10, /device:TPU:0, one launch (start us, length us, event | category | flops | bytes accessed | tf_op | source)
XLA Modules:
  0.0 205.6 jit_solution(16663701309947126346)
XLA Ops:
  4.5 3.0 %collective-permute-start = (bf16[6,128,128]{2,1,0:T(8,128)(2,1)S(1)}, bf16[6,128,128]{2,1,0:T(8,128)(2,1)S(1)}, u32[]{:S(2)}, u32[]{:S(2)}) collective-permute-start(bf16[6,128,128]{2,1,0:T(8,128)(2,1)S(1)} %get-tuple-element.50), channel_id=1, source_target_pairs={{0,4},{4,0},{8,12},{12,8},{16,20},{20,16},{24,28},{28,24},{1,5},{5... | collective-permute-start | bytes 589832 | tf_op jit(solution)/shard_map/ppermute | solution.py:205
  21.9 3.0 %collective-permute-start.3 = (bf16[6,128,128]{2,1,0:T(8,128)(2,1)}, bf16[6,128,128]{2,1,0:T(8,128)(2,1)}, u32[]{:S(2)}, u32[]{:S(2)}) collective-permute-start(bf16[6,128,128]{2,1,0:T(8,128)(2,1)} %add_convert_fusion.11), channel_id=1, source_target_pairs={{0,0},{4,4},{16,8},{20,12},{8,16},{12,20},{24,24},{28,28},{1,1},{5... | collective-permute-start | bytes 589832 | tf_op jit(solution)/shard_map/ppermute | solution.py:209
  24.8 3.0 %collective-permute-start.2 = (bf16[6,128,128]{2,1,0:T(8,128)(2,1)}, bf16[6,128,128]{2,1,0:T(8,128)(2,1)}, u32[]{:S(2)}, u32[]{:S(2)}) collective-permute-start(bf16[6,128,128]{2,1,0:T(8,128)(2,1)} %add_convert_fusion.11), channel_id=1, source_target_pairs={{0,0},{4,4},{24,8},{28,12},{16,16},{20,20},{8,24},{12,28},{1,1},{5... | collective-permute-start | bytes 589832 | tf_op jit(solution)/shard_map/ppermute | solution.py:209
  31.9 3.6 %collective-permute-done.6 = bf16[72,1536]{1,0:T(8,128)(2,1)S(1)} collective-permute-done((bf16[72,1536]{1,0:T(8,128)(2,1)S(1)}, bf16[72,1536]{1,0:T(8,128)(2,1)S(1)}, u32[]{:S(2)}, u32[]{:S(2)}) %collective-permute-start.6) | collective-permute-done | bytes 221216 | tf_op jit(solution)/shard_map/ppermute | solution.py:205
  38.9 5.3 %fusion.24 = bf16[288,2304]{1,0:T(8,128)(2,1)S(1)} fusion(bf16[288,1536]{1,0:T(8,128)(2,1)S(1)} %pad_maximum_fusion, bf16[1,2304,1536]{2,1,0:T(8,128)(2,1)} %param.14), kind=kOutput, calls=%fused_computation.24 | convolution fusion | flops 2039095296 | bytes 9289728 | tf_op jit(solution)/shard_map/dot_general | solution.py:22
  45.5 2.7 %collective-permute-start.13 = (bf16[72,1536]{1,0:T(8,128)(2,1)S(1)}, bf16[72,1536]{1,0:T(8,128)(2,1)}, u32[]{:S(2)}, u32[]{:S(2)}) collective-permute-start(bf16[72,1536]{1,0:T(8,128)(2,1)S(1)} %copy-done.7), channel_id=1, source_target_pairs={{0,24},{4,28},{8,16},{12,20},{16,8},{20,12},{24,0},{28,4},{1,25},{... | collective-permute-start | bytes 663560 | tf_op jit(solution)/shard_map/ppermute | solution.py:205
  49.7 5.4 %collective-permute-done.13 = bf16[72,1536]{1,0:T(8,128)(2,1)} collective-permute-done((bf16[72,1536]{1,0:T(8,128)(2,1)S(1)}, bf16[72,1536]{1,0:T(8,128)(2,1)}, u32[]{:S(2)}, u32[]{:S(2)}) %collective-permute-start.13) | collective-permute-done | bytes 221216 | tf_op jit(solution)/shard_map/ppermute | solution.py:205
  58.9 3.1 %collective-permute-start.15 = (bf16[72,1536]{1,0:T(8,128)(2,1)S(1)}, bf16[72,1536]{1,0:T(8,128)(2,1)S(1)}, u32[]{:S(2)}, u32[]{:S(2)}) collective-permute-start(bf16[72,1536]{1,0:T(8,128)(2,1)S(1)} %get-tuple-element.66), channel_id=1, source_target_pairs={{0,24},{4,28},{8,16},{12,20},{16,8},{20,12},{24,0},{28,4},{1,25},{... | collective-permute-start | bytes 663560 | tf_op jit(solution)/shard_map/ppermute | solution.py:205
  63.2 5.9 %collective-permute-start.11 = (bf16[72,1536]{1,0:T(8,128)(2,1)S(1)}, bf16[72,1536]{1,0:T(8,128)(2,1)S(1)}, u32[]{:S(2)}, u32[]{:S(2)}) collective-permute-start(bf16[72,1536]{1,0:T(8,128)(2,1)S(1)} %get-tuple-element.63), channel_id=1, source_target_pairs={{0,8},{4,12},{8,0},{12,4},{16,24},{20,28},{24,16},{28,20},{1,9},{5... | collective-permute-start | bytes 663560 | tf_op jit(solution)/shard_map/ppermute | solution.py:205
  71.7 5.6 %fusion.27 = bf16[144,2304]{1,0:T(8,128)(2,1)S(1)} fusion(bf16[144,1536]{1,0:T(8,128)(2,1)S(1)} %pad_maximum_fusion.3, bf16[1,2304,1536]{2,1,0:T(8,128)(2,1)} %param.14), kind=kOutput, calls=%fused_computation.25 | convolution fusion | flops 1019547648 | bytes 8183808 | tf_op jit(solution)/shard_map/dot_general | solution.py:22
  81.1 7.2 %collective-permute-done.12 = bf16[72,1536]{1,0:T(8,128)(2,1)S(1)} collective-permute-done((bf16[72,1536]{1,0:T(8,128)(2,1)S(1)}, bf16[72,1536]{1,0:T(8,128)(2,1)S(1)}, u32[]{:S(2)}, u32[]{:S(2)}) %collective-permute-start.12) | collective-permute-done | bytes 221216 | tf_op jit(solution)/shard_map/ppermute | solution.py:205
  91.6 3.6 %collective-permute-done.24 = bf16[72,1536]{1,0:T(8,128)(2,1)S(1)} collective-permute-done((bf16[72,1536]{1,0:T(8,128)(2,1)S(1)}, bf16[72,1536]{1,0:T(8,128)(2,1)S(1)}, u32[]{:S(2)}, u32[]{:S(2)}) %collective-permute-start.24) | collective-permute-done | bytes 221216 | tf_op jit(solution)/shard_map/ppermute | solution.py:205
  103.2 4.8 %collective-permute-done.29 = bf16[72,1536]{1,0:T(8,128)(2,1)S(1)} collective-permute-done((bf16[72,1536]{1,0:T(8,128)(2,1)S(1)}, bf16[72,1536]{1,0:T(8,128)(2,1)S(1)}, u32[]{:S(2)}, u32[]{:S(2)}) %collective-permute-start.29) | collective-permute-done | bytes 221216 | tf_op jit(solution)/shard_map/ppermute | solution.py:205
  108.0 3.2 %collective-permute-done.23 = bf16[72,1536]{1,0:T(8,128)(2,1)S(1)} collective-permute-done((bf16[72,1536]{1,0:T(8,128)(2,1)S(1)}, bf16[72,1536]{1,0:T(8,128)(2,1)S(1)}, u32[]{:S(2)}, u32[]{:S(2)}) %collective-permute-start.23) | collective-permute-done | bytes 221216 | tf_op jit(solution)/shard_map/ppermute | solution.py:205
  116.9 5.3 %collective-permute-done.30 = bf16[72,2304]{1,0:T(8,128)(2,1)S(1)} collective-permute-done((bf16[72,2304]{1,0:T(8,128)(2,1)S(1)}, bf16[72,2304]{1,0:T(8,128)(2,1)S(1)}, u32[]{:S(2)}, u32[]{:S(2)}) %collective-permute-start.30) | collective-permute-done | bytes 331808 | tf_op jit(solution)/shard_map/ppermute | solution.py:205
  136.1 6.2 %collective-permute-done.32 = bf16[72,2304]{1,0:T(8,128)(2,1)S(1)} collective-permute-done((bf16[72,2304]{1,0:T(8,128)(2,1)S(1)}, bf16[72,2304]{1,0:T(8,128)(2,1)S(1)}, u32[]{:S(2)}, u32[]{:S(2)}) %collective-permute-start.32) | collective-permute-done | bytes 331808 | tf_op jit(solution)/shard_map/ppermute | solution.py:205
  149.1 6.7 %collective-permute-done.20 = bf16[144,1536]{1,0:T(8,128)(2,1)S(1)} collective-permute-done((bf16[144,1536]{1,0:T(8,128)(2,1)S(1)}, bf16[144,1536]{1,0:T(8,128)(2,1)S(1)}, u32[]{:S(2)}, u32[]{:S(2)}) %collective-permute-start.20) | collective-permute-done | bytes 442400 | tf_op jit(solution)/shard_map/ppermute | solution.py:205
  157.2 2.9 %collective-permute-done.36 = bf16[72,1536]{1,0:T(8,128)(2,1)S(1)} collective-permute-done((bf16[72,1536]{1,0:T(8,128)(2,1)S(1)}, bf16[72,1536]{1,0:T(8,128)(2,1)S(1)}, u32[]{:S(2)}, u32[]{:S(2)}) %collective-permute-start.36) | collective-permute-done | bytes 221216 | tf_op jit(solution)/shard_map/ppermute | solution.py:205
  162.6 10.3 %collective-permute-done.37.refs_2_ = bf16[72,1536]{1,0:T(8,128)(2,1)S(1)} collective-permute-done((bf16[72,1536]{1,0:T(8,128)(2,1)S(1)}, bf16[72,1536]{1,0:T(8,128)(2,1)S(1)}, u32[]{:S(2)}, u32[]{:S(2)}) %collective-permute-start.37) | collective-permute-done | bytes 221216 | tf_op jit(solution)/shard_map/ppermute | solution.py:205
  175.8 4.4 %collective-permute-done.40 = bf16[6,128,128]{2,1,0:T(8,128)(2,1)S(1)} collective-permute-done((bf16[6,128,128]{2,1,0:T(8,128)(2,1)S(1)}, bf16[6,128,128]{2,1,0:T(8,128)(2,1)S(1)}, u32[]{:S(2)}, u32[]{:S(2)}) %collective-permute-start.40) | collective-permute-done | bytes 196640 | tf_op jit(solution)/shard_map/ppermute | solution.py:205
  180.4 5.7 %collective-permute-done.41 = bf16[6,128,128]{2,1,0:T(8,128)(2,1)S(1)} collective-permute-done((bf16[6,128,128]{2,1,0:T(8,128)(2,1)S(1)}, bf16[6,128,128]{2,1,0:T(8,128)(2,1)S(1)}, u32[]{:S(2)}, u32[]{:S(2)}) %collective-permute-start.41) | collective-permute-done | bytes 196640 | tf_op jit(solution)/shard_map/ppermute | solution.py:209
  186.9 4.6 %collective-permute-start.42 = (bf16[6,128,128]{2,1,0:T(8,128)(2,1)S(1)}, bf16[6,128,128]{2,1,0:T(8,128)(2,1)S(1)}, u32[]{:S(2)}, u32[]{:S(2)}) collective-permute-start(bf16[6,128,128]{2,1,0:T(8,128)(2,1)S(1)} %add_convert_fusion.10), channel_id=1, source_target_pairs={{16,0},{20,4},{8,8},{12,12},{0,16},{4,20},{24,24},{28,28},{17,1},{... | collective-permute-start | bytes 589832 | tf_op jit(solution)/shard_map/ppermute | solution.py:209
  191.5 4.3 %collective-permute-done.42 = bf16[6,128,128]{2,1,0:T(8,128)(2,1)S(1)} collective-permute-done((bf16[6,128,128]{2,1,0:T(8,128)(2,1)S(1)}, bf16[6,128,128]{2,1,0:T(8,128)(2,1)S(1)}, u32[]{:S(2)}, u32[]{:S(2)}) %collective-permute-start.42) | collective-permute-done | bytes 196640 | tf_op jit(solution)/shard_map/ppermute | solution.py:209
  199.7 4.0 %shard_map.117 = (bf16[128,1536]{1,0:T(8,128)(2,1)}, f32[128,1536]{1,0:T(8,128)S(1)}, f32[128,1536]{1,0:T(8,128)S(1)}) custom-call(s32[3]{0:T(128)S(1)} %pad_add_fusion.place_ref, f32[12]{0:T(128)S(1)} %neg.11.rates_ref, bf16[128,1536]{1,0:T(8,128)(2,1)S(1)} %copy-done, bf16[256,1536]{1,0:T(8,128)(2,1)S(1)} %constant_dynamic-update-slice_fusion.pair_ref, ...), custom_call_target="tpu_custom_call" | custom-call | flops 1 | bytes 1 | tf_op jit(solution)/shard_map/pallas_call | solution.py:192
  (168 shorter events, 90.6 us)
Async XLA Ops:
  17.6 11.8 %collective-permute-start.5 = (bf16[72,1536]{1,0:T(8,128)(2,1)}, bf16[72,1536]{1,0:T(8,128)(2,1)}, u32[]{:S(2)}, u32[]{:S(2)}) collective-permute-start(bf16[72,1536]{1,0:T(8,128)(2,1)} %copy-done.8), channel_id=1, source_target_pairs={{0,8},{4,12},{8,0},{12,4},{16,24},{20,28},{24,16},{28,20},{1,9},{5... | collective-permute-start | bytes 663560 | tf_op jit(solution)/shard_map/ppermute | solution.py:205
  45.2 11.0 %collective-permute-start.8 = (bf16[144,2304]{1,0:T(8,128)(2,1)}, bf16[144,2304]{1,0:T(8,128)(2,1)}, u32[]{:S(2)}, u32[]{:S(2)}) collective-permute-start(bf16[144,2304]{1,0:T(8,128)(2,1)} %dynamic-slice_bitcast_fusion), channel_id=1, source_target_pairs={{0,1},{1,0},{2,3},{3,2},{4,5},{5,4},{6,7},{7,6},{8,9},{9,8},{10,11... | collective-permute-start | bytes 1990664 | tf_op jit(solution)/shard_map/ppermute | solution.py:205
  45.5 9.6 %collective-permute-start.13 = (bf16[72,1536]{1,0:T(8,128)(2,1)S(1)}, bf16[72,1536]{1,0:T(8,128)(2,1)}, u32[]{:S(2)}, u32[]{:S(2)}) collective-permute-start(bf16[72,1536]{1,0:T(8,128)(2,1)S(1)} %copy-done.7), channel_id=1, source_target_pairs={{0,24},{4,28},{8,16},{12,20},{16,8},{20,12},{24,0},{28,4},{1,25},{... | collective-permute-start | bytes 663560 | tf_op jit(solution)/shard_map/ppermute | solution.py:205
  48.2 9.4 %collective-permute-start.4 = (bf16[6,128,128]{2,1,0:T(8,128)(2,1)}, bf16[6,128,128]{2,1,0:T(8,128)(2,1)S(1)}, u32[]{:S(2)}, u32[]{:S(2)}) collective-permute-start(bf16[6,128,128]{2,1,0:T(8,128)(2,1)} %get-tuple-element.102), channel_id=1, source_target_pairs={{0,4},{4,0},{8,12},{12,8},{16,20},{20,16},{24,28},{28,24},{1,5},{5... | collective-permute-start | bytes 589832 | tf_op jit(solution)/shard_map/ppermute | solution.py:205
  58.9 12.8 %collective-permute-start.15 = (bf16[72,1536]{1,0:T(8,128)(2,1)S(1)}, bf16[72,1536]{1,0:T(8,128)(2,1)S(1)}, u32[]{:S(2)}, u32[]{:S(2)}) collective-permute-start(bf16[72,1536]{1,0:T(8,128)(2,1)S(1)} %get-tuple-element.66), channel_id=1, source_target_pairs={{0,24},{4,28},{8,16},{12,20},{16,8},{20,12},{24,0},{28,4},{1,25},{... | collective-permute-start | bytes 663560 | tf_op jit(solution)/shard_map/ppermute | solution.py:205
  63.2 17.1 %collective-permute-start.11 = (bf16[72,1536]{1,0:T(8,128)(2,1)S(1)}, bf16[72,1536]{1,0:T(8,128)(2,1)S(1)}, u32[]{:S(2)}, u32[]{:S(2)}) collective-permute-start(bf16[72,1536]{1,0:T(8,128)(2,1)S(1)} %get-tuple-element.63), channel_id=1, source_target_pairs={{0,8},{4,12},{8,0},{12,4},{16,24},{20,28},{24,16},{28,20},{1,9},{5... | collective-permute-start | bytes 663560 | tf_op jit(solution)/shard_map/ppermute | solution.py:205
  69.1 11.3 %collective-permute-start.10 = (bf16[72,1536]{1,0:T(8,128)(2,1)S(1)}, bf16[72,1536]{1,0:T(8,128)(2,1)S(1)}, u32[]{:S(2)}, u32[]{:S(2)}) collective-permute-start(bf16[72,1536]{1,0:T(8,128)(2,1)S(1)} %get-tuple-element.62), channel_id=1, source_target_pairs={{0,4},{4,0},{8,12},{12,8},{16,20},{20,16},{24,28},{28,24},{1,5},{5... | collective-permute-start | bytes 663560 | tf_op jit(solution)/shard_map/ppermute | solution.py:205
  70.2 18.8 %collective-permute-start.9 = (bf16[144,2304]{1,0:T(8,128)(2,1)S(1)}, bf16[144,2304]{1,0:T(8,128)(2,1)S(1)}, u32[]{:S(2)}, u32[]{:S(2)}) collective-permute-start(bf16[144,2304]{1,0:T(8,128)(2,1)S(1)} %fusion.91), channel_id=1, source_target_pairs={{0,2},{1,3},{2,0},{3,1},{4,6},{5,7},{6,4},{7,5},{8,10},{9,11},{10,... | collective-permute-start | bytes 1990664 | tf_op jit(solution)/shard_map/ppermute | solution.py:205
  77.3 24.2 %collective-permute-start.22 = (bf16[72,1536]{1,0:T(8,128)(2,1)S(1)}, bf16[72,1536]{1,0:T(8,128)(2,1)S(1)}, u32[]{:S(2)}, u32[]{:S(2)}) collective-permute-start(bf16[72,1536]{1,0:T(8,128)(2,1)S(1)} %copy-done.5), channel_id=1, source_target_pairs={{0,16},{4,20},{8,24},{12,28},{16,0},{20,4},{24,8},{28,12},{1,17},{... | collective-permute-start | bytes 663560 | tf_op jit(solution)/shard_map/ppermute | solution.py:205
  79.8 19.8 %collective-permute-start.28 = (bf16[72,1536]{1,0:T(8,128)(2,1)S(1)}, bf16[72,1536]{1,0:T(8,128)(2,1)S(1)}, u32[]{:S(2)}, u32[]{:S(2)}) collective-permute-start(bf16[72,1536]{1,0:T(8,128)(2,1)S(1)} %get-tuple-element.78), channel_id=1, source_target_pairs={{0,16},{4,20},{8,24},{12,28},{16,0},{20,4},{24,8},{28,12},{1,17},{... | collective-permute-start | bytes 663560 | tf_op jit(solution)/shard_map/ppermute | solution.py:205
  80.3 8.6 %collective-permute-start.16 = (bf16[72,2304]{1,0:T(8,128)(2,1)S(1)}, bf16[72,2304]{1,0:T(8,128)(2,1)S(1)}, u32[]{:S(2)}, u32[]{:S(2)}) collective-permute-start(bf16[72,2304]{1,0:T(8,128)(2,1)S(1)} %dynamic-slice_bitcast_fusion.2), channel_id=1, source_target_pairs={{0,1},{1,0},{2,3},{3,2},{4,5},{5,4},{6,7},{7,6},{8,9},{9,8},{10,11... | collective-permute-start | bytes 995336 | tf_op jit(solution)/shard_map/ppermute | solution.py:205
  90.5 26.3 %collective-permute-start.34 = (bf16[72,2304]{1,0:T(8,128)(2,1)S(1)}, bf16[72,2304]{1,0:T(8,128)(2,1)S(1)}, u32[]{:S(2)}, u32[]{:S(2)}) collective-permute-start(bf16[72,2304]{1,0:T(8,128)(2,1)S(1)} %fusion.113), channel_id=1, source_target_pairs={{0,2},{1,3},{2,0},{3,1},{4,6},{5,7},{6,4},{7,5},{8,10},{9,11},{10,... | collective-permute-start | bytes 995336 | tf_op jit(solution)/shard_map/ppermute | solution.py:205
  96.5 27.6 %collective-permute-start.18 = (bf16[144,2304]{1,0:T(8,128)(2,1)S(1)}, bf16[144,2304]{1,0:T(8,128)(2,1)S(1)}, u32[]{:S(2)}, u32[]{:S(2)}) collective-permute-start(bf16[144,2304]{1,0:T(8,128)(2,1)S(1)} %add_convert_fusion.1), channel_id=1, source_target_pairs={{0,2},{1,3},{2,0},{3,1},{4,6},{5,7},{6,4},{7,5},{8,10},{9,11},{10,... | collective-permute-start | bytes 1990664 | tf_op jit(solution)/shard_map/ppermute | solution.py:205
  101.5 9.7 %collective-permute-start.25 = (bf16[72,2304]{1,0:T(8,128)(2,1)S(1)}, bf16[72,2304]{1,0:T(8,128)(2,1)S(1)}, u32[]{:S(2)}, u32[]{:S(2)}) collective-permute-start(bf16[72,2304]{1,0:T(8,128)(2,1)S(1)} %fusion.42), channel_id=1, source_target_pairs={{0,1},{1,0},{2,3},{3,2},{4,5},{5,4},{6,7},{7,6},{8,9},{9,8},{10,11... | collective-permute-start | bytes 995336 | tf_op jit(solution)/shard_map/ppermute | solution.py:205
  101.6 9.6 %collective-permute-start.23 = (bf16[72,1536]{1,0:T(8,128)(2,1)S(1)}, bf16[72,1536]{1,0:T(8,128)(2,1)S(1)}, u32[]{:S(2)}, u32[]{:S(2)}) collective-permute-start(bf16[72,1536]{1,0:T(8,128)(2,1)S(1)} %collective-permute-done.22), channel_id=1, source_target_pairs={{0,4},{4,0},{8,12},{12,8},{16,20},{20,16},{24,28},{28,24},{1,5},{5... | collective-permute-start | bytes 663560 | tf_op jit(solution)/shard_map/ppermute | solution.py:205
  112.6 9.5 %collective-permute-start.30 = (bf16[72,2304]{1,0:T(8,128)(2,1)S(1)}, bf16[72,2304]{1,0:T(8,128)(2,1)S(1)}, u32[]{:S(2)}, u32[]{:S(2)}) collective-permute-start(bf16[72,2304]{1,0:T(8,128)(2,1)S(1)} %fusion.54), channel_id=1, source_target_pairs={{0,2},{1,3},{2,0},{3,1},{4,6},{5,7},{6,4},{7,5},{8,10},{9,11},{10,... | collective-permute-start | bytes 995336 | tf_op jit(solution)/shard_map/ppermute | solution.py:205
  125.4 10.7 %collective-permute-start.27 = (bf16[72,2304]{1,0:T(8,128)(2,1)S(1)}, bf16[72,2304]{1,0:T(8,128)(2,1)S(1)}, u32[]{:S(2)}, u32[]{:S(2)}) collective-permute-start(bf16[72,2304]{1,0:T(8,128)(2,1)S(1)} %fusion.112), channel_id=1, source_target_pairs={{0,2},{1,3},{2,0},{3,1},{4,6},{5,7},{6,4},{7,5},{8,10},{9,11},{10,... | collective-permute-start | bytes 995336 | tf_op jit(solution)/shard_map/ppermute | solution.py:205
  127.9 14.4 %collective-permute-start.32 = (bf16[72,2304]{1,0:T(8,128)(2,1)S(1)}, bf16[72,2304]{1,0:T(8,128)(2,1)S(1)}, u32[]{:S(2)}, u32[]{:S(2)}) collective-permute-start(bf16[72,2304]{1,0:T(8,128)(2,1)S(1)} %fusion.69), channel_id=1, source_target_pairs={{0,2},{1,3},{2,0},{3,1},{4,6},{5,7},{6,4},{7,5},{8,10},{9,11},{10,... | collective-permute-start | bytes 995336 | tf_op jit(solution)/shard_map/ppermute | solution.py:205
  133.8 10.5 %collective-permute-start.38 = (bf16[72,1536]{1,0:T(8,128)(2,1)S(1)}, bf16[72,1536]{1,0:T(8,128)(2,1)S(1)}, u32[]{:S(2)}, u32[]{:S(2)}) collective-permute-start(bf16[72,1536]{1,0:T(8,128)(2,1)S(1)} %slice.45), channel_id=1, source_target_pairs={{0,4},{4,0},{8,12},{12,8},{16,20},{20,16},{24,28},{28,24},{1,5},{5... | collective-permute-start | bytes 663560 | tf_op jit(solution)/shard_map/ppermute | solution.py:205
  142.8 13.0 %collective-permute-start.20 = (bf16[144,1536]{1,0:T(8,128)(2,1)S(1)}, bf16[144,1536]{1,0:T(8,128)(2,1)S(1)}, u32[]{:S(2)}, u32[]{:S(2)}) collective-permute-start(bf16[144,1536]{1,0:T(8,128)(2,1)S(1)} %slice.39), channel_id=1, source_target_pairs={{0,4},{4,0},{8,12},{12,8},{16,20},{20,16},{24,28},{28,24},{1,5},{5... | collective-permute-start | bytes 1327112 | tf_op jit(solution)/shard_map/ppermute | solution.py:205
  144.4 18.2 %collective-permute-start.39 = (bf16[72,1536]{1,0:T(8,128)(2,1)S(1)}, bf16[72,1536]{1,0:T(8,128)(2,1)S(1)}, u32[]{:S(2)}, u32[]{:S(2)}) collective-permute-start(bf16[72,1536]{1,0:T(8,128)(2,1)S(1)} %add_convert_fusion.8), channel_id=1, source_target_pairs={{0,24},{4,28},{8,16},{12,20},{16,8},{20,12},{24,0},{28,4},{1,25},{... | collective-permute-start | bytes 663560 | tf_op jit(solution)/shard_map/ppermute | solution.py:205
  148.5 11.6 %collective-permute-start.36 = (bf16[72,1536]{1,0:T(8,128)(2,1)S(1)}, bf16[72,1536]{1,0:T(8,128)(2,1)S(1)}, u32[]{:S(2)}, u32[]{:S(2)}) collective-permute-start(bf16[72,1536]{1,0:T(8,128)(2,1)S(1)} %slice.43), channel_id=1, source_target_pairs={{0,4},{4,0},{8,12},{12,8},{16,20},{20,16},{24,28},{28,24},{1,5},{5... | collective-permute-start | bytes 663560 | tf_op jit(solution)/shard_map/ppermute | solution.py:205
  160.1 12.7 %collective-permute-start.37 = (bf16[72,1536]{1,0:T(8,128)(2,1)S(1)}, bf16[72,1536]{1,0:T(8,128)(2,1)S(1)}, u32[]{:S(2)}, u32[]{:S(2)}) collective-permute-start(bf16[72,1536]{1,0:T(8,128)(2,1)S(1)} %add_convert_fusion.9), channel_id=1, source_target_pairs={{0,16},{4,20},{8,24},{12,28},{16,0},{20,4},{24,8},{28,12},{1,17},{... | collective-permute-start | bytes 663560 | tf_op jit(solution)/shard_map/ppermute | solution.py:205
  186.9 9.0 %collective-permute-start.42 = (bf16[6,128,128]{2,1,0:T(8,128)(2,1)S(1)}, bf16[6,128,128]{2,1,0:T(8,128)(2,1)S(1)}, u32[]{:S(2)}, u32[]{:S(2)}) collective-permute-start(bf16[6,128,128]{2,1,0:T(8,128)(2,1)S(1)} %add_convert_fusion.10), channel_id=1, source_target_pairs={{16,0},{20,4},{8,8},{12,12},{0,16},{4,20},{24,24},{28,28},{17,1},{... | collective-permute-start | bytes 589832 | tf_op jit(solution)/shard_map/ppermute | solution.py:209
  (40 other events, 293.5 us)

commit v11 on v10

--- a/solution.py
+++ b/solution.py
@@ -275,15 +275,6 @@
     )
     sent = multiply(after(rows(1 - mine), *events)).astype(BF16)
     return sent, multiply(after(rows(mine), sent)).astype(BF16)
-
-
-def one_product(own, other, part, multiply, *events):
-    mine = lax.axis_index("exp") & 1
-    rows = [side[k] for side in (own, other) for k in part]
-    whole = multiply(after(jnp.concatenate(rows, axis=0), *events)).astype(BF16)
-    whole = whole.reshape(2, whole.shape[0] // 2, whole.shape[1])
-    sent = lax.dynamic_index_in_dim(whole, 1 - mine, 0, False)
-    return sent, lax.dynamic_index_in_dim(whole, mine, 0, False)
 
 
 def over_cores(sent, kept):
@@ -345,21 +336,23 @@
     grad_other = {0: swap(after(send_grad[0], total), "ctx", 1)}
     for k in near_part[1:]:
         grad_own[k] = pairs_of(after(send_grad[k], total), k)
-    for k in near_part[1:]:
-        grad_other[k] = swap(grad_own[k], "ctx", 1)
+    for k in first_far:
+        grad_own[k] = pairs_of(after(send_grad[k], total), k)
     before = None
     for index, reach in enumerate(reaches):
         events = [intra] if index == 1 else []
         before, upto = scan_step(
             before, total, reach, decay_rates, place, block_len, False, *events
         )
+    for k in near_part[1:]:
+        grad_other[k] = swap(after(grad_own[k], upto), "ctx", 1)
+    for k in first_far:
+        grad_other[k] = swap(after(grad_own[k], upto), "ctx", 1)
     keep, give = scan_ends(before, key_mine, partner, decay_rates, place, block_len, False)
-    for k in first_far:
+    for k in second_far:
         grad_own[k] = pairs_of(after(send_grad[k], give), k)
-    for k in first_far:
-        grad_other[k] = swap(grad_own[k], "ctx", 1)
     given = swap(give, "ctx", 1)
-    hidden_near = one_product(grad_own, grad_other, near_part, by_down, give)
+    hidden_near = two_products(grad_own, grad_other, near_part, by_down, give)
     hidden_near_sum = over_cores(*hidden_near)
     hidden_near_all = sum_over_rest(hidden_near_sum, bits)
     given, hidden_near_sum = lax.optimization_barrier((given, hidden_near_sum))
@@ -373,29 +366,27 @@
         in_own[k] = pairs_of(send_in[k], k)
     for k in near_part[1:]:
         in_other[k] = swap(in_own[k], "ctx", 1)
-    hidden_first = one_product(grad_own, grad_other, first_far, by_down, hidden_near_sum, *[in_own[k] for k in first_far])
+    hidden_first = two_products(grad_own, grad_other, first_far, by_down, send_in[0])
     hidden_first_sum = over_cores(*hidden_first)
     hidden_first_all = sum_over_rest(hidden_first_sum, bits)
     for k in second_far:
-        in_own[k] = pairs_of(after(send_in[k], *[in_own[k] for k in first_far]), k)
-    for k in second_far:
-        grad_own[k] = pairs_of(after(send_grad[k], *[in_own[k] for k in first_far]), k)
+        in_own[k] = pairs_of(after(send_in[k], *[in_own[k] for k in first_far], hidden_first_sum), k)
     for k in first_far:
-        in_other[k] = swap(after(in_own[k], *[in_other[k] for k in near_part[1:]]), "ctx", 1)
-    pre_near = two_products(in_own, in_other, near_part, by_up, hidden_first_sum, hidden_near_all)
+        in_other[k] = swap(in_own[k], "ctx", 1)
+    pre_near = two_products(in_own, in_other, near_part, by_up, hidden_first_sum)
     pre_near_sum = over_cores(*pre_near)
     pre_near_all = sum_over_rest(pre_near_sum, bits)
     for k in second_far:
         in_other[k] = swap(after(in_own[k], pre_near_sum), "ctx", 1)
     for k in second_far:
         grad_other[k] = swap(after(grad_own[k], pre_near_sum), "ctx", 1)
-    pre_first = two_products(in_own, in_other, first_far, by_up, pre_near_sum, hidden_near_all)
+    pre_first = two_products(in_own, in_other, first_far, by_up, pre_near_sum)
     pre_first_sum = over_cores(*pre_first)
     pre_first_all = sum_over_rest(pre_first_sum, bits)
-    hidden_second = one_product(grad_own, grad_other, second_far, by_down, pre_first_sum)
+    hidden_second = two_products(grad_own, grad_other, second_far, by_down, pre_first_sum)
     hidden_second_sum = over_cores(*hidden_second)
     hidden_second_all = sum_over_rest(hidden_second_sum, bits)
-    pre_second = two_products(in_own, in_other, second_far, by_up, hidden_second[0], pre_first_all)
+    pre_second = two_products(in_own, in_other, second_far, by_up, hidden_second_sum)
     pre_second_sum = over_cores(*pre_second)
     pre_second_all = sum_over_rest(pre_second_sum, bits)
 

time: 206 us -> 189 us (0.917)
  starting transfers between devices: 61.1 us -> 46.9 us
  matrix products: 28.6 us -> 32.3 us
  other arithmetic: 13.4 us -> 9.75 us
  waiting for transfers between devices: 83.1 us -> 81 us
    ppermute x39, starting transfers between devices: 47.9 us -> 37.4 us  [swap(): return lax.ppermute(array, axis, [(i, i ^ distance) for i in range(size)])]
    dot_general x12 -> x15, matrix products: 28.6 us -> 32.3 us  [dot(): lax.dot_general(left, right, (((left_dim,), (right_dim,)), ((), ())), pre...]
    ppermute x6, starting transfers between devices: 13.2 us -> 9.52 us  [trade(): lax.ppermute(array, 'ctx', [(2 * partner(i) + s, 2 * i + s) for i in rang...]
    concatenate x3 -> x0, other arithmetic: 2.16 us -> none  [one_product(): whole = multiply(after(jnp.concatenate(rows, axis=0), *events)).astype(BF16)]
  transfers between devices with their start and end apart: 45 -> 45, of which waited for: 19 -> 22; matrix products, arithmetic and copies ran while one was open for 16% -> 21% of each run, Pallas kernels for 4% -> 5%
where the time goes in v11:
time: 189 us; the launch traced here: 188 us
  waiting for transfers between devices  81 us (43%)
  starting transfers between devices  46.9 us (25%)
  matrix products  32.3 us (17%)
  Pallas kernels  13.2 us (7%)
  other arithmetic  9.75 us (5%)
  local copies, waits for them, and re-layouts  4.17 us (2%)
    ppermute x39, waiting for transfers between devices, swap(): return lax.ppermute(array, axis, [(i, i ^ distance) for i in range(size)])  69.6 us
    ppermute x39, starting transfers between devices, swap(): return lax.ppermute(array, axis, [(i, i ^ distance) for i in range(size)])  37.4 us
    dot_general x15, matrix products, dot(): lax.dot_general(left, right, (((left_dim,), (right_dim,)), ((), ())), pre...  32.3 us
    pallas_call x7, Pallas kernels, call(): pl.pallas_call(kernel, out_shape=list(out_shapes), in_specs=[SMEM] * len(...  13.2 us
    ppermute x6, waiting for transfers between devices, trade(): lax.ppermute(array, 'ctx', [(2 * partner(i) + s, 2 * i + s) for i in rang...  11.4 us
    ppermute x6, starting transfers between devices, trade(): lax.ppermute(array, 'ctx', [(2 * partner(i) + s, 2 * i + s) for i in rang...  9.52 us
  transfers between devices with their start and end apart: 45, of which 22 were waited for; matrix products, arithmetic and copies ran while one was open for 21% of the time, Pallas kernels for 5%

profile of v11, /device:TPU:0, one launch (start us, length us, event | category | flops | bytes accessed | tf_op | source)
XLA Modules:
  0.0 188.5 jit_solution(9883520559668383782)
XLA Ops:
  4.3 3.0 %collective-permute-start = (bf16[6,128,128]{2,1,0:T(8,128)(2,1)S(1)}, bf16[6,128,128]{2,1,0:T(8,128)(2,1)S(1)}, u32[]{:S(2)}, u32[]{:S(2)}) collective-permute-start(bf16[6,128,128]{2,1,0:T(8,128)(2,1)S(1)} %get-tuple-element.54), channel_id=1, source_target_pairs={{0,4},{4,0},{8,12},{12,8},{16,20},{20,16},{24,28},{28,24},{1,5},{5... | collective-permute-start | bytes 589832 | tf_op jit(solution)/shard_map/ppermute | solution.py:205
  15.9 2.5 %shard_map.114 = (f32[128,1536]{1,0:T(8,128)S(1)}, bf16[12,128,128]{2,1,0:T(8,128)(2,1)S(1)}) custom-call(s32[3]{0:T(128)S(1)} %pad_add_fusion.place_ref, f32[12]{0:T(128)S(1)} %neg.11.rates_ref, bf16[128,1536]{1,0:T(8,128)(2,1)S(1)} %copy-done, bf16[256,1536]{1,0:T(8,128)(2,1)S(1)} %constant_dynamic-update-slice_fusion.pair_ref), custom_call_target="tpu_custom_call" | custom-call | flops 1 | bytes 40000000 | tf_op jit(solution)/shard_map/pallas_call | solution.py:192
  20.4 3.6 %collective-permute-start.13 = (bf16[72,1536]{1,0:T(8,128)(2,1)S(1)}, bf16[72,1536]{1,0:T(8,128)(2,1)S(1)}, u32[]{:S(2)}, u32[]{:S(2)}) collective-permute-start(bf16[72,1536]{1,0:T(8,128)(2,1)S(1)} %get-tuple-element.71), channel_id=1, source_target_pairs={{0,24},{4,28},{8,16},{12,20},{16,8},{20,12},{24,0},{28,4},{1,25},{... | collective-permute-start | bytes 663560 | tf_op jit(solution)/shard_map/ppermute | solution.py:205
  27.1 7.6 %collective-permute-done.13 = bf16[72,1536]{1,0:T(8,128)(2,1)S(1)} collective-permute-done((bf16[72,1536]{1,0:T(8,128)(2,1)S(1)}, bf16[72,1536]{1,0:T(8,128)(2,1)S(1)}, u32[]{:S(2)}, u32[]{:S(2)}) %collective-permute-start.13) | collective-permute-done | bytes 221216 | tf_op jit(solution)/shard_map/ppermute | solution.py:205
  38.6 3.4 %collective-permute-start.21 = (bf16[72,1536]{1,0:T(8,128)(2,1)S(1)}, bf16[72,1536]{1,0:T(8,128)(2,1)S(1)}, u32[]{:S(2)}, u32[]{:S(2)}) collective-permute-start(bf16[72,1536]{1,0:T(8,128)(2,1)S(1)} %get-tuple-element.78), channel_id=1, source_target_pairs={{0,16},{4,20},{8,24},{12,28},{16,0},{20,4},{24,8},{28,12},{1,17},{... | collective-permute-start | bytes 663560 | tf_op jit(solution)/shard_map/ppermute | solution.py:205
  42.1 5.6 %fusion.30 = bf16[144,2304]{1,0:T(8,128)(2,1)S(1)} fusion(bf16[144,1536]{1,0:T(8,128)(2,1)S(1)} %pad_maximum_fusion.1, bf16[1,2304,1536]{2,1,0:T(8,128)(2,1)} %param.14), kind=kOutput, calls=%fused_computation.30 | convolution fusion | flops 1019547648 | bytes 8183808 | tf_op jit(solution)/shard_map/dot_general | solution.py:22
  49.9 2.4 %add_convert_fusion.3 = bf16[144,2304]{1,0:T(8,128)(2,1)S(1)} fusion(bf16[144,2304]{1,0:T(8,128)(2,1)S(1)} %collective-permute-done.8, bf16[144,1536]{1,0:T(8,128)(2,1)S(1)} %pad_maximum_fusion, bf16[1,2304,1536]{2,1,0:T(8,128)(2,1)S(1)} %bitcast.114), kind=kOutput, calls=%fused_computation.74 | convolution fusion | flops 1020874752 | bytes 8847360 | tf_op jit(solution)/shard_map/dot_general | solution.py:22
  55.1 3.0 %collective-permute-start.11 = (bf16[72,1536]{1,0:T(8,128)(2,1)S(1)}, bf16[72,1536]{1,0:T(8,128)(2,1)S(1)}, u32[]{:S(2)}, u32[]{:S(2)}) collective-permute-start(bf16[72,1536]{1,0:T(8,128)(2,1)S(1)} %get-tuple-element.69), channel_id=1, source_target_pairs={{0,8},{4,12},{8,0},{12,4},{16,24},{20,28},{24,16},{28,20},{1,9},{5... | collective-permute-start | bytes 663560 | tf_op jit(solution)/shard_map/ppermute | solution.py:205
  60.8 3.2 %collective-permute-done.11 = bf16[72,1536]{1,0:T(8,128)(2,1)S(1)} collective-permute-done((bf16[72,1536]{1,0:T(8,128)(2,1)S(1)}, bf16[72,1536]{1,0:T(8,128)(2,1)S(1)}, u32[]{:S(2)}, u32[]{:S(2)}) %collective-permute-start.11) | collective-permute-done | bytes 221216 | tf_op jit(solution)/shard_map/ppermute | solution.py:205
  65.5 3.3 %collective-permute-done.23 = bf16[72,1536]{1,0:T(8,128)(2,1)S(1)} collective-permute-done((bf16[72,1536]{1,0:T(8,128)(2,1)S(1)}, bf16[72,1536]{1,0:T(8,128)(2,1)S(1)}, u32[]{:S(2)}, u32[]{:S(2)}) %collective-permute-start.23) | collective-permute-done | bytes 221216 | tf_op jit(solution)/shard_map/ppermute | solution.py:205
  74.7 2.4 %collective-permute-done.12 = bf16[72,1536]{1,0:T(8,128)(2,1)S(1)} collective-permute-done((bf16[72,1536]{1,0:T(8,128)(2,1)S(1)}, bf16[72,1536]{1,0:T(8,128)(2,1)S(1)}, u32[]{:S(2)}, u32[]{:S(2)}) %collective-permute-start.12) | collective-permute-done | bytes 221216 | tf_op jit(solution)/shard_map/ppermute | solution.py:205
  85.5 6.7 %collective-permute-done.28 = bf16[72,1536]{1,0:T(8,128)(2,1)S(1)} collective-permute-done((bf16[72,1536]{1,0:T(8,128)(2,1)S(1)}, bf16[72,1536]{1,0:T(8,128)(2,1)S(1)}, u32[]{:S(2)}, u32[]{:S(2)}) %collective-permute-start.28) | collective-permute-done | bytes 221216 | tf_op jit(solution)/shard_map/ppermute | solution.py:205
  101.6 2.5 %fusion.75 = bf16[72,2304]{1,0:T(8,128)(2,1)S(1)} fusion(bf16[72,1536]{1,0:T(8,128)(2,1)S(1)} %get-tuple-element.84, bf16[1,2304,1536]{2,1,0:T(8,128)(2,1)S(1)} %bitcast.114, bf16[72,2304]{1,0:T(8,128)(2,1)S(1)} %collective-permute-done.26), kind=kOutput, calls=%fused_computation.45 | convolution fusion | flops 510437376 | bytes 7962624 | tf_op jit(solution)/shard_map/dot_general | solution.py:22
  107.3 3.4 %collective-permute-done.34 = bf16[72,2304]{1,0:T(8,128)(2,1)S(1)} collective-permute-done((bf16[72,2304]{1,0:T(8,128)(2,1)S(1)}, bf16[72,2304]{1,0:T(8,128)(2,1)S(1)}, u32[]{:S(2)}, u32[]{:S(2)}) %collective-permute-start.34) | collective-permute-done | bytes 331808 | tf_op jit(solution)/shard_map/ppermute | solution.py:205
  119.8 3.9 %collective-permute-done.31 = bf16[72,2304]{1,0:T(8,128)(2,1)S(1)} collective-permute-done((bf16[72,2304]{1,0:T(8,128)(2,1)S(1)}, bf16[72,2304]{1,0:T(8,128)(2,1)S(1)}, u32[]{:S(2)}, u32[]{:S(2)}) %collective-permute-start.31) | collective-permute-done | bytes 331808 | tf_op jit(solution)/shard_map/ppermute | solution.py:205
  128.1 2.4 %fusion.114 = bf16[144,1536]{1,0:T(8,128)(2,1)S(1)} fusion(bf16[1,1536,2304]{2,1,0:T(8,128)(2,1)S(1)} %bitcast.112, bf16[72,2304]{1,0:T(8,128)(2,1)S(1)} %get-tuple-element.110, bf16[72,2304]{1,0:T(8,128)(2,1)S(1)} %get-tuple-element.109), kind=kOutput, calls=%fused_computation.58 | convolution fusion | flops 1020764160 | bytes 8183808 | tf_op jit(solution)/shard_map/dot_general | solution.py:22
  131.2 6.0 %collective-permute-done.19 = bf16[144,1536]{1,0:T(8,128)(2,1)S(1)} collective-permute-done((bf16[144,1536]{1,0:T(8,128)(2,1)S(1)}, bf16[144,1536]{1,0:T(8,128)(2,1)S(1)}, u32[]{:S(2)}, u32[]{:S(2)}) %collective-permute-start.19) | collective-permute-done | bytes 442400 | tf_op jit(solution)/shard_map/ppermute | solution.py:205
  137.5 4.0 %collective-permute-done.36 = bf16[72,1536]{1,0:T(8,128)(2,1)S(1)} collective-permute-done((bf16[72,1536]{1,0:T(8,128)(2,1)S(1)}, bf16[72,1536]{1,0:T(8,128)(2,1)S(1)}, u32[]{:S(2)}, u32[]{:S(2)}) %collective-permute-start.36) | collective-permute-done | bytes 221216 | tf_op jit(solution)/shard_map/ppermute | solution.py:205
  144.0 9.8 %collective-permute-done.37.refs_2_ = bf16[72,1536]{1,0:T(8,128)(2,1)S(1)} collective-permute-done((bf16[72,1536]{1,0:T(8,128)(2,1)S(1)}, bf16[72,1536]{1,0:T(8,128)(2,1)S(1)}, u32[]{:S(2)}, u32[]{:S(2)}) %collective-permute-start.37) | collective-permute-done | bytes 221216 | tf_op jit(solution)/shard_map/ppermute | solution.py:205
  155.9 6.2 %collective-permute-done.40 = bf16[6,128,128]{2,1,0:T(8,128)(2,1)S(1)} collective-permute-done((bf16[6,128,128]{2,1,0:T(8,128)(2,1)S(1)}, bf16[6,128,128]{2,1,0:T(8,128)(2,1)S(1)}, u32[]{:S(2)}, u32[]{:S(2)}) %collective-permute-start.40) | collective-permute-done | bytes 196640 | tf_op jit(solution)/shard_map/ppermute | solution.py:205
  162.2 6.0 %collective-permute-done.41 = bf16[6,128,128]{2,1,0:T(8,128)(2,1)S(1)} collective-permute-done((bf16[6,128,128]{2,1,0:T(8,128)(2,1)S(1)}, bf16[6,128,128]{2,1,0:T(8,128)(2,1)S(1)}, u32[]{:S(2)}, u32[]{:S(2)}) %collective-permute-start.41) | collective-permute-done | bytes 196640 | tf_op jit(solution)/shard_map/ppermute | solution.py:209
  169.1 5.2 %collective-permute-start.42 = (bf16[6,128,128]{2,1,0:T(8,128)(2,1)S(1)}, bf16[6,128,128]{2,1,0:T(8,128)(2,1)}, u32[]{:S(2)}, u32[]{:S(2)}) collective-permute-start(bf16[6,128,128]{2,1,0:T(8,128)(2,1)S(1)} %add_convert_fusion.11), channel_id=1, source_target_pairs={{16,0},{20,4},{8,8},{12,12},{0,16},{4,20},{24,24},{28,28},{17,1},{... | collective-permute-start | bytes 589832 | tf_op jit(solution)/shard_map/ppermute | solution.py:209
  174.2 5.4 %collective-permute-done.42 = bf16[6,128,128]{2,1,0:T(8,128)(2,1)} collective-permute-done((bf16[6,128,128]{2,1,0:T(8,128)(2,1)S(1)}, bf16[6,128,128]{2,1,0:T(8,128)(2,1)}, u32[]{:S(2)}, u32[]{:S(2)}) %collective-permute-start.42) | collective-permute-done | bytes 196640 | tf_op jit(solution)/shard_map/ppermute | solution.py:209
  181.5 4.0 %shard_map.117 = (bf16[128,1536]{1,0:T(8,128)(2,1)}, f32[128,1536]{1,0:T(8,128)S(1)}, f32[128,1536]{1,0:T(8,128)S(1)}) custom-call(s32[3]{0:T(128)S(1)} %pad_add_fusion.place_ref, f32[12]{0:T(128)S(1)} %neg.11.rates_ref, bf16[128,1536]{1,0:T(8,128)(2,1)S(1)} %copy-done.1, bf16[256,1536]{1,0:T(8,128)(2,1)S(1)} %constant_dynamic-update-slice_fusion.pair_ref, ...), custom_call_target="tpu_custom_call" | custom-call | flops 1 | bytes 1 | tf_op jit(solution)/shard_map/pallas_call | solution.py:192
  (147 shorter events, 81.9 us)
Async XLA Ops:
  13.0 11.0 %collective-permute-start.1 = (bf16[6,128,128]{2,1,0:T(8,128)(2,1)}, bf16[6,128,128]{2,1,0:T(8,128)(2,1)}, u32[]{:S(2)}, u32[]{:S(2)}) collective-permute-start(bf16[6,128,128]{2,1,0:T(8,128)(2,1)} %fusion.148), channel_id=1, source_target_pairs={{8,0},{12,4},{0,8},{4,12},{24,16},{28,20},{16,24},{20,28},{9,1},{1... | collective-permute-start | bytes 589832 | tf_op jit(solution)/shard_map/ppermute | solution.py:209
  18.4 18.3 %collective-permute-start.5 = (bf16[72,1536]{1,0:T(8,128)(2,1)S(1)}, bf16[72,1536]{1,0:T(8,128)(2,1)S(1)}, u32[]{:S(2)}, u32[]{:S(2)}) collective-permute-start(bf16[72,1536]{1,0:T(8,128)(2,1)S(1)} %get-tuple-element.59), channel_id=1, source_target_pairs={{0,4},{4,0},{8,12},{12,8},{16,20},{20,16},{24,28},{28,24},{1,5},{5... | collective-permute-start | bytes 663560 | tf_op jit(solution)/shard_map/ppermute | solution.py:205
  20.0 14.7 %collective-permute-start.6 = (bf16[72,1536]{1,0:T(8,128)(2,1)S(1)}, bf16[72,1536]{1,0:T(8,128)(2,1)S(1)}, u32[]{:S(2)}, u32[]{:S(2)}) collective-permute-start(bf16[72,1536]{1,0:T(8,128)(2,1)S(1)} %get-tuple-element.61), channel_id=1, source_target_pairs={{0,8},{4,12},{8,0},{12,4},{16,24},{20,28},{24,16},{28,20},{1,9},{5... | collective-permute-start | bytes 663560 | tf_op jit(solution)/shard_map/ppermute | solution.py:205
  20.4 14.2 %collective-permute-start.13 = (bf16[72,1536]{1,0:T(8,128)(2,1)S(1)}, bf16[72,1536]{1,0:T(8,128)(2,1)S(1)}, u32[]{:S(2)}, u32[]{:S(2)}) collective-permute-start(bf16[72,1536]{1,0:T(8,128)(2,1)S(1)} %get-tuple-element.71), channel_id=1, source_target_pairs={{0,24},{4,28},{8,16},{12,20},{16,8},{20,12},{24,0},{28,4},{1,25},{... | collective-permute-start | bytes 663560 | tf_op jit(solution)/shard_map/ppermute | solution.py:205
  25.3 11.5 %collective-permute-start.3 = (bf16[6,128,128]{2,1,0:T(8,128)(2,1)S(1)}, bf16[6,128,128]{2,1,0:T(8,128)(2,1)S(1)}, u32[]{:S(2)}, u32[]{:S(2)}) collective-permute-start(bf16[6,128,128]{2,1,0:T(8,128)(2,1)S(1)} %add_convert_fusion.12), channel_id=1, source_target_pairs={{0,0},{4,4},{16,8},{20,12},{8,16},{12,20},{24,24},{28,28},{1,1},{5... | collective-permute-start | bytes 589832 | tf_op jit(solution)/shard_map/ppermute | solution.py:209
  26.1 10.7 %collective-permute-start.2 = (bf16[6,128,128]{2,1,0:T(8,128)(2,1)S(1)}, bf16[6,128,128]{2,1,0:T(8,128)(2,1)S(1)}, u32[]{:S(2)}, u32[]{:S(2)}) collective-permute-start(bf16[6,128,128]{2,1,0:T(8,128)(2,1)S(1)} %add_convert_fusion.12), channel_id=1, source_target_pairs={{0,0},{4,4},{24,8},{28,12},{16,16},{20,20},{8,24},{12,28},{1,1},{5... | collective-permute-start | bytes 589832 | tf_op jit(solution)/shard_map/ppermute | solution.py:209
  35.2 12.6 %collective-permute-start.14 = (bf16[72,1536]{1,0:T(8,128)(2,1)S(1)}, bf16[72,1536]{1,0:T(8,128)(2,1)S(1)}, u32[]{:S(2)}, u32[]{:S(2)}) collective-permute-start(bf16[72,1536]{1,0:T(8,128)(2,1)S(1)} %collective-permute-done.13), channel_id=1, source_target_pairs={{0,4},{4,0},{8,12},{12,8},{16,20},{20,16},{24,28},{28,24},{1,5},{5... | collective-permute-start | bytes 663560 | tf_op jit(solution)/shard_map/ppermute | solution.py:205
  38.0 14.4 %collective-permute-start.4 = (bf16[6,128,128]{2,1,0:T(8,128)(2,1)S(1)}, bf16[6,128,128]{2,1,0:T(8,128)(2,1)S(1)}, u32[]{:S(2)}, u32[]{:S(2)}) collective-permute-start(bf16[6,128,128]{2,1,0:T(8,128)(2,1)S(1)} %get-tuple-element.108), channel_id=1, source_target_pairs={{0,4},{4,0},{8,12},{12,8},{16,20},{20,16},{24,28},{28,24},{1,5},{5... | collective-permute-start | bytes 589832 | tf_op jit(solution)/shard_map/ppermute | solution.py:205
  38.6 44.8 %collective-permute-start.21 = (bf16[72,1536]{1,0:T(8,128)(2,1)S(1)}, bf16[72,1536]{1,0:T(8,128)(2,1)S(1)}, u32[]{:S(2)}, u32[]{:S(2)}) collective-permute-start(bf16[72,1536]{1,0:T(8,128)(2,1)S(1)} %get-tuple-element.78), channel_id=1, source_target_pairs={{0,16},{4,20},{8,24},{12,28},{16,0},{20,4},{24,8},{28,12},{1,17},{... | collective-permute-start | bytes 663560 | tf_op jit(solution)/shard_map/ppermute | solution.py:205
  53.6 15.8 %collective-permute-start.10 = (bf16[72,1536]{1,0:T(8,128)(2,1)S(1)}, bf16[72,1536]{1,0:T(8,128)(2,1)S(1)}, u32[]{:S(2)}, u32[]{:S(2)}) collective-permute-start(bf16[72,1536]{1,0:T(8,128)(2,1)S(1)} %get-tuple-element.68), channel_id=1, source_target_pairs={{0,4},{4,0},{8,12},{12,8},{16,20},{20,16},{24,28},{28,24},{1,5},{5... | collective-permute-start | bytes 663560 | tf_op jit(solution)/shard_map/ppermute | solution.py:205
  58.1 10.7 %collective-permute-start.23 = (bf16[72,1536]{1,0:T(8,128)(2,1)S(1)}, bf16[72,1536]{1,0:T(8,128)(2,1)S(1)}, u32[]{:S(2)}, u32[]{:S(2)}) collective-permute-start(bf16[72,1536]{1,0:T(8,128)(2,1)S(1)} %get-tuple-element.80), channel_id=1, source_target_pairs={{0,24},{4,28},{8,16},{12,20},{16,8},{20,12},{24,0},{28,4},{1,25},{... | collective-permute-start | bytes 663560 | tf_op jit(solution)/shard_map/ppermute | solution.py:205
  64.0 42.0 %collective-permute-start.9 = (bf16[144,2304]{1,0:T(8,128)(2,1)S(1)}, bf16[144,2304]{1,0:T(8,128)(2,1)S(1)}, u32[]{:S(2)}, u32[]{:S(2)}) collective-permute-start(bf16[144,2304]{1,0:T(8,128)(2,1)S(1)} %add_convert_fusion.3), channel_id=1, source_target_pairs={{0,2},{1,3},{2,0},{3,1},{4,6},{5,7},{6,4},{7,5},{8,10},{9,11},{10,... | collective-permute-start | bytes 1990664 | tf_op jit(solution)/shard_map/ppermute | solution.py:205
  69.4 10.7 %collective-permute-start.24 = (bf16[72,1536]{1,0:T(8,128)(2,1)S(1)}, bf16[72,1536]{1,0:T(8,128)(2,1)S(1)}, u32[]{:S(2)}, u32[]{:S(2)}) collective-permute-start(bf16[72,1536]{1,0:T(8,128)(2,1)S(1)} %collective-permute-done.23), channel_id=1, source_target_pairs={{0,4},{4,0},{8,12},{12,8},{16,20},{20,16},{24,28},{28,24},{1,5},{5... | collective-permute-start | bytes 663560 | tf_op jit(solution)/shard_map/ppermute | solution.py:205
  73.1 34.2 %collective-permute-start.33 = (bf16[72,2304]{1,0:T(8,128)(2,1)S(1)}, bf16[72,2304]{1,0:T(8,128)(2,1)S(1)}, u32[]{:S(2)}, u32[]{:S(2)}) collective-permute-start(bf16[72,2304]{1,0:T(8,128)(2,1)S(1)} %fusion.60), channel_id=1, source_target_pairs={{0,2},{1,3},{2,0},{3,1},{4,6},{5,7},{6,4},{7,5},{8,10},{9,11},{10,... | collective-permute-start | bytes 995336 | tf_op jit(solution)/shard_map/ppermute | solution.py:205
  80.1 12.0 %collective-permute-start.28 = (bf16[72,1536]{1,0:T(8,128)(2,1)S(1)}, bf16[72,1536]{1,0:T(8,128)(2,1)S(1)}, u32[]{:S(2)}, u32[]{:S(2)}) collective-permute-start(bf16[72,1536]{1,0:T(8,128)(2,1)S(1)} %get-tuple-element.86), channel_id=1, source_target_pairs={{0,16},{4,20},{8,24},{12,28},{16,0},{20,4},{24,8},{28,12},{1,17},{... | collective-permute-start | bytes 663560 | tf_op jit(solution)/shard_map/ppermute | solution.py:205
  81.8 24.2 %collective-permute-start.17 = (bf16[144,2304]{1,0:T(8,128)(2,1)S(1)}, bf16[144,2304]{1,0:T(8,128)(2,1)S(1)}, u32[]{:S(2)}, u32[]{:S(2)}) collective-permute-start(bf16[144,2304]{1,0:T(8,128)(2,1)S(1)} %add_convert_fusion.1), channel_id=1, source_target_pairs={{0,2},{1,3},{2,0},{3,1},{4,6},{5,7},{6,4},{7,5},{8,10},{9,11},{10,... | collective-permute-start | bytes 1990664 | tf_op jit(solution)/shard_map/ppermute | solution.py:205
  100.0 10.8 %collective-permute-start.34 = (bf16[72,2304]{1,0:T(8,128)(2,1)S(1)}, bf16[72,2304]{1,0:T(8,128)(2,1)S(1)}, u32[]{:S(2)}, u32[]{:S(2)}) collective-permute-start(bf16[72,2304]{1,0:T(8,128)(2,1)S(1)} %fusion.90), channel_id=1, source_target_pairs={{0,2},{1,3},{2,0},{3,1},{4,6},{5,7},{6,4},{7,5},{8,10},{9,11},{10,... | collective-permute-start | bytes 995336 | tf_op jit(solution)/shard_map/ppermute | solution.py:205
  104.1 15.8 %collective-permute-start.27 = (bf16[72,2304]{1,0:T(8,128)(2,1)S(1)}, bf16[72,2304]{1,0:T(8,128)(2,1)S(1)}, u32[]{:S(2)}, u32[]{:S(2)}) collective-permute-start(bf16[72,2304]{1,0:T(8,128)(2,1)S(1)} %fusion.75), channel_id=1, source_target_pairs={{0,2},{1,3},{2,0},{3,1},{4,6},{5,7},{6,4},{7,5},{8,10},{9,11},{10,... | collective-permute-start | bytes 995336 | tf_op jit(solution)/shard_map/ppermute | solution.py:205
  112.6 11.1 %collective-permute-start.31 = (bf16[72,2304]{1,0:T(8,128)(2,1)S(1)}, bf16[72,2304]{1,0:T(8,128)(2,1)S(1)}, u32[]{:S(2)}, u32[]{:S(2)}) collective-permute-start(bf16[72,2304]{1,0:T(8,128)(2,1)S(1)} %fusion.105), channel_id=1, source_target_pairs={{0,2},{1,3},{2,0},{3,1},{4,6},{5,7},{6,4},{7,5},{8,10},{9,11},{10,... | collective-permute-start | bytes 995336 | tf_op jit(solution)/shard_map/ppermute | solution.py:205
  124.2 13.0 %collective-permute-start.19 = (bf16[144,1536]{1,0:T(8,128)(2,1)S(1)}, bf16[144,1536]{1,0:T(8,128)(2,1)S(1)}, u32[]{:S(2)}, u32[]{:S(2)}) collective-permute-start(bf16[144,1536]{1,0:T(8,128)(2,1)S(1)} %slice.39), channel_id=1, source_target_pairs={{0,4},{4,0},{8,12},{12,8},{16,20},{20,16},{24,28},{28,24},{1,5},{5... | collective-permute-start | bytes 1327112 | tf_op jit(solution)/shard_map/ppermute | solution.py:205
  126.8 14.9 %collective-permute-start.39 = (bf16[72,1536]{1,0:T(8,128)(2,1)S(1)}, bf16[72,1536]{1,0:T(8,128)(2,1)S(1)}, u32[]{:S(2)}, u32[]{:S(2)}) collective-permute-start(bf16[72,1536]{1,0:T(8,128)(2,1)S(1)} %add_convert_fusion.9), channel_id=1, source_target_pairs={{0,24},{4,28},{8,16},{12,20},{16,8},{20,12},{24,0},{28,4},{1,25},{... | collective-permute-start | bytes 663560 | tf_op jit(solution)/shard_map/ppermute | solution.py:205
  130.5 11.0 %collective-permute-start.36 = (bf16[72,1536]{1,0:T(8,128)(2,1)S(1)}, bf16[72,1536]{1,0:T(8,128)(2,1)S(1)}, u32[]{:S(2)}, u32[]{:S(2)}) collective-permute-start(bf16[72,1536]{1,0:T(8,128)(2,1)S(1)} %slice.43), channel_id=1, source_target_pairs={{0,4},{4,0},{8,12},{12,8},{16,20},{20,16},{24,28},{28,24},{1,5},{5... | collective-permute-start | bytes 663560 | tf_op jit(solution)/shard_map/ppermute | solution.py:205
  141.6 12.2 %collective-permute-start.37 = (bf16[72,1536]{1,0:T(8,128)(2,1)S(1)}, bf16[72,1536]{1,0:T(8,128)(2,1)S(1)}, u32[]{:S(2)}, u32[]{:S(2)}) collective-permute-start(bf16[72,1536]{1,0:T(8,128)(2,1)S(1)} %add_convert_fusion.10), channel_id=1, source_target_pairs={{0,16},{4,20},{8,24},{12,28},{16,0},{20,4},{24,8},{28,12},{1,17},{... | collective-permute-start | bytes 663560 | tf_op jit(solution)/shard_map/ppermute | solution.py:205
  169.1 10.6 %collective-permute-start.42 = (bf16[6,128,128]{2,1,0:T(8,128)(2,1)S(1)}, bf16[6,128,128]{2,1,0:T(8,128)(2,1)}, u32[]{:S(2)}, u32[]{:S(2)}) collective-permute-start(bf16[6,128,128]{2,1,0:T(8,128)(2,1)S(1)} %add_convert_fusion.11), channel_id=1, source_target_pairs={{16,0},{20,4},{8,8},{12,12},{0,16},{4,20},{24,24},{28,28},{17,1},{... | collective-permute-start | bytes 589832 | tf_op jit(solution)/shard_map/ppermute | solution.py:209
  (30 other events, 224.8 us)

commit v12 on v11

--- a/solution.py
+++ b/solution.py
@@ -372,7 +372,7 @@
     for k in second_far:
         in_own[k] = pairs_of(after(send_in[k], *[in_own[k] for k in first_far], hidden_first_sum), k)
     for k in first_far:
-        in_other[k] = swap(in_own[k], "ctx", 1)
+        in_other[k] = swap(after(in_own[k], *[in_other[k] for k in near_part[1:]]), "ctx", 1)
     pre_near = two_products(in_own, in_other, near_part, by_up, hidden_first_sum)
     pre_near_sum = over_cores(*pre_near)
     pre_near_all = sum_over_rest(pre_near_sum, bits)

time: 189 us -> 187 us (0.989)
  waiting for transfers between devices: 81 us -> 71.7 us
  starting transfers between devices: 46.9 us -> 54.4 us
    ppermute x39, waiting for transfers between devices: 69.6 us -> 61.3 us  [swap(): return lax.ppermute(array, axis, [(i, i ^ distance) for i in range(size)])]
    ppermute x39, starting transfers between devices: 37.4 us -> 43.7 us  [swap(): return lax.ppermute(array, axis, [(i, i ^ distance) for i in range(size)])]
  transfers between devices with their start and end apart: 45 -> 45, of which waited for: 22 -> 21; matrix products, arithmetic and copies ran while one was open for 21% -> 21% of each run, Pallas kernels for 5% -> 5%
where the time goes in v12:
time: 187 us
  waiting for transfers between devices  71.7 us (38%)
  starting transfers between devices  54.4 us (29%)
  matrix products  32.3 us (17%)
  Pallas kernels  13.2 us (7%)
  other arithmetic  9.75 us (5%)
  local copies, waits for them, and re-layouts  4.17 us (2%)
    ppermute x39, waiting for transfers between devices, swap(): return lax.ppermute(array, axis, [(i, i ^ distance) for i in range(size)])  61.3 us
    ppermute x39, starting transfers between devices, swap(): return lax.ppermute(array, axis, [(i, i ^ distance) for i in range(size)])  43.7 us
    dot_general x15, matrix products, dot(): lax.dot_general(left, right, (((left_dim,), (right_dim,)), ((), ())), pre...  32.3 us
    pallas_call x7, Pallas kernels, call(): pl.pallas_call(kernel, out_shape=list(out_shapes), in_specs=[SMEM] * len(...  13.2 us
    ppermute x6, starting transfers between devices, trade(): lax.ppermute(array, 'ctx', [(2 * partner(i) + s, 2 * i + s) for i in rang...  10.6 us
    ppermute x6, waiting for transfers between devices, trade(): lax.ppermute(array, 'ctx', [(2 * partner(i) + s, 2 * i + s) for i in rang...  10.4 us
  transfers between devices with their start and end apart: 45, of which 21 were waited for; matrix products, arithmetic and copies ran while one was open for 21% of the time, Pallas kernels for 5%

profile of v12, /device:TPU:0, one launch (start us, length us, event | category | flops | bytes accessed | tf_op | source)
XLA Modules:
  0.0 186.6 jit_solution(10094962137040157940)
XLA Ops:
  4.3 3.0 %collective-permute-start = (bf16[6,128,128]{2,1,0:T(8,128)(2,1)S(1)}, bf16[6,128,128]{2,1,0:T(8,128)(2,1)S(1)}, u32[]{:S(2)}, u32[]{:S(2)}) collective-permute-start(bf16[6,128,128]{2,1,0:T(8,128)(2,1)S(1)} %get-tuple-element.55), channel_id=1, source_target_pairs={{0,4},{4,0},{8,12},{12,8},{16,20},{20,16},{24,28},{28,24},{1,5},{5... | collective-permute-start | bytes 589832 | tf_op jit(solution)/shard_map/ppermute | solution.py:205
  15.9 2.5 %shard_map.114 = (f32[128,1536]{1,0:T(8,128)S(1)}, bf16[12,128,128]{2,1,0:T(8,128)(2,1)S(1)}) custom-call(s32[3]{0:T(128)S(1)} %pad_add_fusion.place_ref, f32[12]{0:T(128)S(1)} %neg.11.rates_ref, bf16[128,1536]{1,0:T(8,128)(2,1)S(1)} %copy-done, bf16[256,1536]{1,0:T(8,128)(2,1)S(1)} %constant_dynamic-update-slice_fusion.pair_ref), custom_call_target="tpu_custom_call" | custom-call | flops 1 | bytes 40000000 | tf_op jit(solution)/shard_map/pallas_call | solution.py:192
  20.4 3.6 %collective-permute-start.13 = (bf16[72,1536]{1,0:T(8,128)(2,1)S(1)}, bf16[72,1536]{1,0:T(8,128)(2,1)S(1)}, u32[]{:S(2)}, u32[]{:S(2)}) collective-permute-start(bf16[72,1536]{1,0:T(8,128)(2,1)S(1)} %get-tuple-element.72), channel_id=1, source_target_pairs={{0,24},{4,28},{8,16},{12,20},{16,8},{20,12},{24,0},{28,4},{1,25},{... | collective-permute-start | bytes 663560 | tf_op jit(solution)/shard_map/ppermute | solution.py:205
  27.1 7.6 %collective-permute-done.13 = bf16[72,1536]{1,0:T(8,128)(2,1)S(1)} collective-permute-done((bf16[72,1536]{1,0:T(8,128)(2,1)S(1)}, bf16[72,1536]{1,0:T(8,128)(2,1)S(1)}, u32[]{:S(2)}, u32[]{:S(2)}) %collective-permute-start.13) | collective-permute-done | bytes 221216 | tf_op jit(solution)/shard_map/ppermute | solution.py:205
  38.6 3.4 %collective-permute-start.21 = (bf16[72,1536]{1,0:T(8,128)(2,1)S(1)}, bf16[72,1536]{1,0:T(8,128)(2,1)S(1)}, u32[]{:S(2)}, u32[]{:S(2)}) collective-permute-start(bf16[72,1536]{1,0:T(8,128)(2,1)S(1)} %get-tuple-element.79), channel_id=1, source_target_pairs={{0,16},{4,20},{8,24},{12,28},{16,0},{20,4},{24,8},{28,12},{1,17},{... | collective-permute-start | bytes 663560 | tf_op jit(solution)/shard_map/ppermute | solution.py:205
  42.1 5.6 %fusion.30 = bf16[144,2304]{1,0:T(8,128)(2,1)S(1)} fusion(bf16[144,1536]{1,0:T(8,128)(2,1)S(1)} %pad_maximum_fusion.1, bf16[1,2304,1536]{2,1,0:T(8,128)(2,1)} %param.14), kind=kOutput, calls=%fused_computation.30 | convolution fusion | flops 1019547648 | bytes 8183808 | tf_op jit(solution)/shard_map/dot_general | solution.py:22
  49.9 2.4 %add_convert_fusion.3 = bf16[144,2304]{1,0:T(8,128)(2,1)S(1)} fusion(bf16[144,2304]{1,0:T(8,128)(2,1)S(1)} %collective-permute-done.8, bf16[144,1536]{1,0:T(8,128)(2,1)S(1)} %pad_maximum_fusion, bf16[1,2304,1536]{2,1,0:T(8,128)(2,1)S(1)} %bitcast.114), kind=kOutput, calls=%fused_computation.74 | convolution fusion | flops 1020874752 | bytes 8847360 | tf_op jit(solution)/shard_map/dot_general | solution.py:22
  55.1 3.0 %collective-permute-start.11 = (bf16[72,1536]{1,0:T(8,128)(2,1)S(1)}, bf16[72,1536]{1,0:T(8,128)(2,1)S(1)}, u32[]{:S(2)}, u32[]{:S(2)}) collective-permute-start(bf16[72,1536]{1,0:T(8,128)(2,1)S(1)} %get-tuple-element.70), channel_id=1, source_target_pairs={{0,8},{4,12},{8,0},{12,4},{16,24},{20,28},{24,16},{28,20},{1,9},{5... | collective-permute-start | bytes 663560 | tf_op jit(solution)/shard_map/ppermute | solution.py:205
  60.9 3.1 %collective-permute-done.11 = bf16[72,1536]{1,0:T(8,128)(2,1)S(1)} collective-permute-done((bf16[72,1536]{1,0:T(8,128)(2,1)S(1)}, bf16[72,1536]{1,0:T(8,128)(2,1)S(1)}, u32[]{:S(2)}, u32[]{:S(2)}) %collective-permute-start.11) | collective-permute-done | bytes 221216 | tf_op jit(solution)/shard_map/ppermute | solution.py:205
  73.5 3.8 %collective-permute-done.24 = bf16[72,1536]{1,0:T(8,128)(2,1)S(1)} collective-permute-done((bf16[72,1536]{1,0:T(8,128)(2,1)S(1)}, bf16[72,1536]{1,0:T(8,128)(2,1)S(1)}, u32[]{:S(2)}, u32[]{:S(2)}) %collective-permute-start.24) | collective-permute-done | bytes 221216 | tf_op jit(solution)/shard_map/ppermute | solution.py:205
  77.4 3.6 %collective-permute-start.28 = (bf16[72,1536]{1,0:T(8,128)(2,1)S(1)}, bf16[72,1536]{1,0:T(8,128)(2,1)S(1)}, u32[]{:S(2)}, u32[]{:S(2)}) collective-permute-start(bf16[72,1536]{1,0:T(8,128)(2,1)S(1)} %get-tuple-element.88), channel_id=1, source_target_pairs={{0,16},{4,20},{8,24},{12,28},{16,0},{20,4},{24,8},{28,12},{1,17},{... | collective-permute-start | bytes 663560 | tf_op jit(solution)/shard_map/ppermute | solution.py:205
  85.8 4.2 %collective-permute-done.28 = bf16[72,1536]{1,0:T(8,128)(2,1)S(1)} collective-permute-done((bf16[72,1536]{1,0:T(8,128)(2,1)S(1)}, bf16[72,1536]{1,0:T(8,128)(2,1)S(1)}, u32[]{:S(2)}, u32[]{:S(2)}) %collective-permute-start.28) | collective-permute-done | bytes 221216 | tf_op jit(solution)/shard_map/ppermute | solution.py:205
  99.5 2.5 %fusion.75 = bf16[72,2304]{1,0:T(8,128)(2,1)S(1)} fusion(bf16[72,1536]{1,0:T(8,128)(2,1)S(1)} %get-tuple-element.86, bf16[1,2304,1536]{2,1,0:T(8,128)(2,1)S(1)} %bitcast.114, bf16[72,2304]{1,0:T(8,128)(2,1)S(1)} %collective-permute-done.26), kind=kOutput, calls=%fused_computation.45 | convolution fusion | flops 510437376 | bytes 7962624 | tf_op jit(solution)/shard_map/dot_general | solution.py:22
  105.3 3.4 %collective-permute-done.34 = bf16[72,2304]{1,0:T(8,128)(2,1)S(1)} collective-permute-done((bf16[72,2304]{1,0:T(8,128)(2,1)S(1)}, bf16[72,2304]{1,0:T(8,128)(2,1)S(1)}, u32[]{:S(2)}, u32[]{:S(2)}) %collective-permute-start.34) | collective-permute-done | bytes 331808 | tf_op jit(solution)/shard_map/ppermute | solution.py:205
  117.8 4.6 %collective-permute-done.31 = bf16[72,2304]{1,0:T(8,128)(2,1)S(1)} collective-permute-done((bf16[72,2304]{1,0:T(8,128)(2,1)S(1)}, bf16[72,2304]{1,0:T(8,128)(2,1)S(1)}, u32[]{:S(2)}, u32[]{:S(2)}) %collective-permute-start.31) | collective-permute-done | bytes 331808 | tf_op jit(solution)/shard_map/ppermute | solution.py:205
  130.1 5.7 %collective-permute-done.19 = bf16[144,1536]{1,0:T(8,128)(2,1)S(1)} collective-permute-done((bf16[144,1536]{1,0:T(8,128)(2,1)S(1)}, bf16[144,1536]{1,0:T(8,128)(2,1)S(1)}, u32[]{:S(2)}, u32[]{:S(2)}) %collective-permute-start.19) | collective-permute-done | bytes 442400 | tf_op jit(solution)/shard_map/ppermute | solution.py:205
  136.0 2.6 %collective-permute-start.20 = (bf16[72,1536]{1,0:T(8,128)(2,1)S(1)}, bf16[72,1536]{1,0:T(8,128)(2,1)S(1)}, u32[]{:S(2)}, u32[]{:S(2)}) collective-permute-start(bf16[72,1536]{1,0:T(8,128)(2,1)S(1)} %get-tuple-element.121), channel_id=1, source_target_pairs={{0,8},{4,12},{8,0},{12,4},{16,24},{20,28},{24,16},{28,20},{1,9},{5... | collective-permute-start | bytes 663560 | tf_op jit(solution)/shard_map/ppermute | solution.py:205
  141.2 5.1 %collective-permute-done.20.refs_1_ = bf16[72,1536]{1,0:T(8,128)(2,1)S(1)} collective-permute-done((bf16[72,1536]{1,0:T(8,128)(2,1)S(1)}, bf16[72,1536]{1,0:T(8,128)(2,1)S(1)}, u32[]{:S(2)}, u32[]{:S(2)}) %collective-permute-start.20) | collective-permute-done | bytes 221216 | tf_op jit(solution)/shard_map/ppermute | solution.py:205
  146.2 6.7 %collective-permute-done.37.refs_2_ = bf16[72,1536]{1,0:T(8,128)(2,1)S(1)} collective-permute-done((bf16[72,1536]{1,0:T(8,128)(2,1)S(1)}, bf16[72,1536]{1,0:T(8,128)(2,1)S(1)}, u32[]{:S(2)}, u32[]{:S(2)}) %collective-permute-start.37) | collective-permute-done | bytes 221216 | tf_op jit(solution)/shard_map/ppermute | solution.py:205
  155.1 5.0 %collective-permute-done.40 = bf16[6,128,128]{2,1,0:T(8,128)(2,1)S(1)} collective-permute-done((bf16[6,128,128]{2,1,0:T(8,128)(2,1)S(1)}, bf16[6,128,128]{2,1,0:T(8,128)(2,1)S(1)}, u32[]{:S(2)}, u32[]{:S(2)}) %collective-permute-start.40) | collective-permute-done | bytes 196640 | tf_op jit(solution)/shard_map/ppermute | solution.py:205
  160.9 5.0 %collective-permute-done.41 = bf16[6,128,128]{2,1,0:T(8,128)(2,1)S(1)} collective-permute-done((bf16[6,128,128]{2,1,0:T(8,128)(2,1)S(1)}, bf16[6,128,128]{2,1,0:T(8,128)(2,1)S(1)}, u32[]{:S(2)}, u32[]{:S(2)}) %collective-permute-start.41) | collective-permute-done | bytes 196640 | tf_op jit(solution)/shard_map/ppermute | solution.py:209
  166.8 5.7 %collective-permute-start.42 = (bf16[6,128,128]{2,1,0:T(8,128)(2,1)S(1)}, bf16[6,128,128]{2,1,0:T(8,128)(2,1)}, u32[]{:S(2)}, u32[]{:S(2)}) collective-permute-start(bf16[6,128,128]{2,1,0:T(8,128)(2,1)S(1)} %add_convert_fusion.11), channel_id=1, source_target_pairs={{16,0},{20,4},{8,8},{12,12},{0,16},{4,20},{24,24},{28,28},{17,1},{... | collective-permute-start | bytes 589832 | tf_op jit(solution)/shard_map/ppermute | solution.py:209
  172.5 5.4 %collective-permute-done.42 = bf16[6,128,128]{2,1,0:T(8,128)(2,1)} collective-permute-done((bf16[6,128,128]{2,1,0:T(8,128)(2,1)S(1)}, bf16[6,128,128]{2,1,0:T(8,128)(2,1)}, u32[]{:S(2)}, u32[]{:S(2)}) %collective-permute-start.42) | collective-permute-done | bytes 196640 | tf_op jit(solution)/shard_map/ppermute | solution.py:209
  179.7 4.0 %shard_map.117 = (bf16[128,1536]{1,0:T(8,128)(2,1)}, f32[128,1536]{1,0:T(8,128)S(1)}, f32[128,1536]{1,0:T(8,128)S(1)}) custom-call(s32[3]{0:T(128)S(1)} %pad_add_fusion.place_ref, f32[12]{0:T(128)S(1)} %neg.11.rates_ref, bf16[128,1536]{1,0:T(8,128)(2,1)S(1)} %copy-done.1, bf16[256,1536]{1,0:T(8,128)(2,1)S(1)} %constant_dynamic-update-slice_fusion.pair_ref, ...), custom_call_target="tpu_custom_call" | custom-call | flops 1 | bytes 1 | tf_op jit(solution)/shard_map/pallas_call | solution.py:192
  (147 shorter events, 84.0 us)
Async XLA Ops:
  13.0 11.0 %collective-permute-start.1 = (bf16[6,128,128]{2,1,0:T(8,128)(2,1)}, bf16[6,128,128]{2,1,0:T(8,128)(2,1)}, u32[]{:S(2)}, u32[]{:S(2)}) collective-permute-start(bf16[6,128,128]{2,1,0:T(8,128)(2,1)} %fusion.148), channel_id=1, source_target_pairs={{8,0},{12,4},{0,8},{4,12},{24,16},{28,20},{16,24},{20,28},{9,1},{1... | collective-permute-start | bytes 589832 | tf_op jit(solution)/shard_map/ppermute | solution.py:209
  18.4 18.3 %collective-permute-start.5 = (bf16[72,1536]{1,0:T(8,128)(2,1)S(1)}, bf16[72,1536]{1,0:T(8,128)(2,1)S(1)}, u32[]{:S(2)}, u32[]{:S(2)}) collective-permute-start(bf16[72,1536]{1,0:T(8,128)(2,1)S(1)} %get-tuple-element.60), channel_id=1, source_target_pairs={{0,4},{4,0},{8,12},{12,8},{16,20},{20,16},{24,28},{28,24},{1,5},{5... | collective-permute-start | bytes 663560 | tf_op jit(solution)/shard_map/ppermute | solution.py:205
  20.0 14.7 %collective-permute-start.6 = (bf16[72,1536]{1,0:T(8,128)(2,1)S(1)}, bf16[72,1536]{1,0:T(8,128)(2,1)S(1)}, u32[]{:S(2)}, u32[]{:S(2)}) collective-permute-start(bf16[72,1536]{1,0:T(8,128)(2,1)S(1)} %get-tuple-element.62), channel_id=1, source_target_pairs={{0,8},{4,12},{8,0},{12,4},{16,24},{20,28},{24,16},{28,20},{1,9},{5... | collective-permute-start | bytes 663560 | tf_op jit(solution)/shard_map/ppermute | solution.py:205
  20.4 14.2 %collective-permute-start.13 = (bf16[72,1536]{1,0:T(8,128)(2,1)S(1)}, bf16[72,1536]{1,0:T(8,128)(2,1)S(1)}, u32[]{:S(2)}, u32[]{:S(2)}) collective-permute-start(bf16[72,1536]{1,0:T(8,128)(2,1)S(1)} %get-tuple-element.72), channel_id=1, source_target_pairs={{0,24},{4,28},{8,16},{12,20},{16,8},{20,12},{24,0},{28,4},{1,25},{... | collective-permute-start | bytes 663560 | tf_op jit(solution)/shard_map/ppermute | solution.py:205
  25.3 11.5 %collective-permute-start.3 = (bf16[6,128,128]{2,1,0:T(8,128)(2,1)S(1)}, bf16[6,128,128]{2,1,0:T(8,128)(2,1)S(1)}, u32[]{:S(2)}, u32[]{:S(2)}) collective-permute-start(bf16[6,128,128]{2,1,0:T(8,128)(2,1)S(1)} %add_convert_fusion.12), channel_id=1, source_target_pairs={{0,0},{4,4},{16,8},{20,12},{8,16},{12,20},{24,24},{28,28},{1,1},{5... | collective-permute-start | bytes 589832 | tf_op jit(solution)/shard_map/ppermute | solution.py:209
  26.1 10.7 %collective-permute-start.2 = (bf16[6,128,128]{2,1,0:T(8,128)(2,1)S(1)}, bf16[6,128,128]{2,1,0:T(8,128)(2,1)S(1)}, u32[]{:S(2)}, u32[]{:S(2)}) collective-permute-start(bf16[6,128,128]{2,1,0:T(8,128)(2,1)S(1)} %add_convert_fusion.12), channel_id=1, source_target_pairs={{0,0},{4,4},{24,8},{28,12},{16,16},{20,20},{8,24},{12,28},{1,1},{5... | collective-permute-start | bytes 589832 | tf_op jit(solution)/shard_map/ppermute | solution.py:209
  35.2 12.6 %collective-permute-start.14 = (bf16[72,1536]{1,0:T(8,128)(2,1)S(1)}, bf16[72,1536]{1,0:T(8,128)(2,1)S(1)}, u32[]{:S(2)}, u32[]{:S(2)}) collective-permute-start(bf16[72,1536]{1,0:T(8,128)(2,1)S(1)} %collective-permute-done.13), channel_id=1, source_target_pairs={{0,4},{4,0},{8,12},{12,8},{16,20},{20,16},{24,28},{28,24},{1,5},{5... | collective-permute-start | bytes 663560 | tf_op jit(solution)/shard_map/ppermute | solution.py:205
  38.0 14.4 %collective-permute-start.4 = (bf16[6,128,128]{2,1,0:T(8,128)(2,1)S(1)}, bf16[6,128,128]{2,1,0:T(8,128)(2,1)S(1)}, u32[]{:S(2)}, u32[]{:S(2)}) collective-permute-start(bf16[6,128,128]{2,1,0:T(8,128)(2,1)S(1)} %get-tuple-element.110), channel_id=1, source_target_pairs={{0,4},{4,0},{8,12},{12,8},{16,20},{20,16},{24,28},{28,24},{1,5},{5... | collective-permute-start | bytes 589832 | tf_op jit(solution)/shard_map/ppermute | solution.py:205
  38.6 45.2 %collective-permute-start.21 = (bf16[72,1536]{1,0:T(8,128)(2,1)S(1)}, bf16[72,1536]{1,0:T(8,128)(2,1)S(1)}, u32[]{:S(2)}, u32[]{:S(2)}) collective-permute-start(bf16[72,1536]{1,0:T(8,128)(2,1)S(1)} %get-tuple-element.79), channel_id=1, source_target_pairs={{0,16},{4,20},{8,24},{12,28},{16,0},{20,4},{24,8},{28,12},{1,17},{... | collective-permute-start | bytes 663560 | tf_op jit(solution)/shard_map/ppermute | solution.py:205
  53.6 11.8 %collective-permute-start.10 = (bf16[72,1536]{1,0:T(8,128)(2,1)S(1)}, bf16[72,1536]{1,0:T(8,128)(2,1)S(1)}, u32[]{:S(2)}, u32[]{:S(2)}) collective-permute-start(bf16[72,1536]{1,0:T(8,128)(2,1)S(1)} %get-tuple-element.69), channel_id=1, source_target_pairs={{0,4},{4,0},{8,12},{12,8},{16,20},{20,16},{24,28},{28,24},{1,5},{5... | collective-permute-start | bytes 663560 | tf_op jit(solution)/shard_map/ppermute | solution.py:205
  60.4 9.7 %collective-permute-start.23 = (bf16[72,1536]{1,0:T(8,128)(2,1)S(1)}, bf16[72,1536]{1,0:T(8,128)(2,1)S(1)}, u32[]{:S(2)}, u32[]{:S(2)}) collective-permute-start(bf16[72,1536]{1,0:T(8,128)(2,1)S(1)} %get-tuple-element.81), channel_id=1, source_target_pairs={{0,24},{4,28},{8,16},{12,20},{16,8},{20,12},{24,0},{28,4},{1,25},{... | collective-permute-start | bytes 663560 | tf_op jit(solution)/shard_map/ppermute | solution.py:205
  63.9 40.0 %collective-permute-start.9 = (bf16[144,2304]{1,0:T(8,128)(2,1)S(1)}, bf16[144,2304]{1,0:T(8,128)(2,1)S(1)}, u32[]{:S(2)}, u32[]{:S(2)}) collective-permute-start(bf16[144,2304]{1,0:T(8,128)(2,1)S(1)} %add_convert_fusion.3), channel_id=1, source_target_pairs={{0,2},{1,3},{2,0},{3,1},{4,6},{5,7},{6,4},{7,5},{8,10},{9,11},{10,... | collective-permute-start | bytes 1990664 | tf_op jit(solution)/shard_map/ppermute | solution.py:205
  68.4 36.8 %collective-permute-start.33 = (bf16[72,2304]{1,0:T(8,128)(2,1)S(1)}, bf16[72,2304]{1,0:T(8,128)(2,1)S(1)}, u32[]{:S(2)}, u32[]{:S(2)}) collective-permute-start(bf16[72,2304]{1,0:T(8,128)(2,1)S(1)} %fusion.60), channel_id=1, source_target_pairs={{0,2},{1,3},{2,0},{3,1},{4,6},{5,7},{6,4},{7,5},{8,10},{9,11},{10,... | collective-permute-start | bytes 995336 | tf_op jit(solution)/shard_map/ppermute | solution.py:205
  77.4 12.7 %collective-permute-start.28 = (bf16[72,1536]{1,0:T(8,128)(2,1)S(1)}, bf16[72,1536]{1,0:T(8,128)(2,1)S(1)}, u32[]{:S(2)}, u32[]{:S(2)}) collective-permute-start(bf16[72,1536]{1,0:T(8,128)(2,1)S(1)} %get-tuple-element.88), channel_id=1, source_target_pairs={{0,16},{4,20},{8,24},{12,28},{16,0},{20,4},{24,8},{28,12},{1,17},{... | collective-permute-start | bytes 663560 | tf_op jit(solution)/shard_map/ppermute | solution.py:205
  82.2 21.8 %collective-permute-start.17 = (bf16[144,2304]{1,0:T(8,128)(2,1)S(1)}, bf16[144,2304]{1,0:T(8,128)(2,1)S(1)}, u32[]{:S(2)}, u32[]{:S(2)}) collective-permute-start(bf16[144,2304]{1,0:T(8,128)(2,1)S(1)} %add_convert_fusion.1), channel_id=1, source_target_pairs={{0,2},{1,3},{2,0},{3,1},{4,6},{5,7},{6,4},{7,5},{8,10},{9,11},{10,... | collective-permute-start | bytes 1990664 | tf_op jit(solution)/shard_map/ppermute | solution.py:205
  97.9 10.8 %collective-permute-start.34 = (bf16[72,2304]{1,0:T(8,128)(2,1)S(1)}, bf16[72,2304]{1,0:T(8,128)(2,1)S(1)}, u32[]{:S(2)}, u32[]{:S(2)}) collective-permute-start(bf16[72,2304]{1,0:T(8,128)(2,1)S(1)} %fusion.90), channel_id=1, source_target_pairs={{0,2},{1,3},{2,0},{3,1},{4,6},{5,7},{6,4},{7,5},{8,10},{9,11},{10,... | collective-permute-start | bytes 995336 | tf_op jit(solution)/shard_map/ppermute | solution.py:205
  102.0 15.8 %collective-permute-start.27 = (bf16[72,2304]{1,0:T(8,128)(2,1)S(1)}, bf16[72,2304]{1,0:T(8,128)(2,1)S(1)}, u32[]{:S(2)}, u32[]{:S(2)}) collective-permute-start(bf16[72,2304]{1,0:T(8,128)(2,1)S(1)} %fusion.75), channel_id=1, source_target_pairs={{0,2},{1,3},{2,0},{3,1},{4,6},{5,7},{6,4},{7,5},{8,10},{9,11},{10,... | collective-permute-start | bytes 995336 | tf_op jit(solution)/shard_map/ppermute | solution.py:205
  110.5 11.8 %collective-permute-start.31 = (bf16[72,2304]{1,0:T(8,128)(2,1)S(1)}, bf16[72,2304]{1,0:T(8,128)(2,1)S(1)}, u32[]{:S(2)}, u32[]{:S(2)}) collective-permute-start(bf16[72,2304]{1,0:T(8,128)(2,1)S(1)} %fusion.105), channel_id=1, source_target_pairs={{0,2},{1,3},{2,0},{3,1},{4,6},{5,7},{6,4},{7,5},{8,10},{9,11},{10,... | collective-permute-start | bytes 995336 | tf_op jit(solution)/shard_map/ppermute | solution.py:205
  122.8 13.0 %collective-permute-start.19 = (bf16[144,1536]{1,0:T(8,128)(2,1)S(1)}, bf16[144,1536]{1,0:T(8,128)(2,1)S(1)}, u32[]{:S(2)}, u32[]{:S(2)}) collective-permute-start(bf16[144,1536]{1,0:T(8,128)(2,1)S(1)} %slice.39), channel_id=1, source_target_pairs={{0,4},{4,0},{8,12},{12,8},{16,20},{20,16},{24,28},{28,24},{1,5},{5... | collective-permute-start | bytes 1327112 | tf_op jit(solution)/shard_map/ppermute | solution.py:205
  124.7 16.5 %collective-permute-start.39 = (bf16[72,1536]{1,0:T(8,128)(2,1)S(1)}, bf16[72,1536]{1,0:T(8,128)(2,1)S(1)}, u32[]{:S(2)}, u32[]{:S(2)}) collective-permute-start(bf16[72,1536]{1,0:T(8,128)(2,1)S(1)} %add_convert_fusion.9), channel_id=1, source_target_pairs={{0,24},{4,28},{8,16},{12,20},{16,8},{20,12},{24,0},{28,4},{1,25},{... | collective-permute-start | bytes 663560 | tf_op jit(solution)/shard_map/ppermute | solution.py:205
  129.4 10.7 %collective-permute-start.36 = (bf16[72,1536]{1,0:T(8,128)(2,1)S(1)}, bf16[72,1536]{1,0:T(8,128)(2,1)S(1)}, u32[]{:S(2)}, u32[]{:S(2)}) collective-permute-start(bf16[72,1536]{1,0:T(8,128)(2,1)S(1)} %slice.43), channel_id=1, source_target_pairs={{0,4},{4,0},{8,12},{12,8},{16,20},{20,16},{24,28},{28,24},{1,5},{5... | collective-permute-start | bytes 663560 | tf_op jit(solution)/shard_map/ppermute | solution.py:205
  136.0 10.3 %collective-permute-start.20 = (bf16[72,1536]{1,0:T(8,128)(2,1)S(1)}, bf16[72,1536]{1,0:T(8,128)(2,1)S(1)}, u32[]{:S(2)}, u32[]{:S(2)}) collective-permute-start(bf16[72,1536]{1,0:T(8,128)(2,1)S(1)} %get-tuple-element.121), channel_id=1, source_target_pairs={{0,8},{4,12},{8,0},{12,4},{16,24},{20,28},{24,16},{28,20},{1,9},{5... | collective-permute-start | bytes 663560 | tf_op jit(solution)/shard_map/ppermute | solution.py:205
  140.2 12.7 %collective-permute-start.37 = (bf16[72,1536]{1,0:T(8,128)(2,1)S(1)}, bf16[72,1536]{1,0:T(8,128)(2,1)S(1)}, u32[]{:S(2)}, u32[]{:S(2)}) collective-permute-start(bf16[72,1536]{1,0:T(8,128)(2,1)S(1)} %add_convert_fusion.10), channel_id=1, source_target_pairs={{0,16},{4,20},{8,24},{12,28},{16,0},{20,4},{24,8},{28,12},{1,17},{... | collective-permute-start | bytes 663560 | tf_op jit(solution)/shard_map/ppermute | solution.py:205
  166.8 11.0 %collective-permute-start.42 = (bf16[6,128,128]{2,1,0:T(8,128)(2,1)S(1)}, bf16[6,128,128]{2,1,0:T(8,128)(2,1)}, u32[]{:S(2)}, u32[]{:S(2)}) collective-permute-start(bf16[6,128,128]{2,1,0:T(8,128)(2,1)S(1)} %add_convert_fusion.11), channel_id=1, source_target_pairs={{16,0},{20,4},{8,8},{12,12},{0,16},{4,20},{24,24},{28,28},{17,1},{... | collective-permute-start | bytes 589832 | tf_op jit(solution)/shard_map/ppermute | solution.py:209
  (30 other events, 215.2 us)

commit v13 on v12

--- a/solution.py
+++ b/solution.py
@@ -275,6 +275,15 @@
     )
     sent = multiply(after(rows(1 - mine), *events)).astype(BF16)
     return sent, multiply(after(rows(mine), sent)).astype(BF16)
+
+
+def one_product(own, other, part, multiply, *events):
+    mine = lax.axis_index("exp") & 1
+    rows = [side[k] for side in (own, other) for k in part]
+    whole = multiply(after(jnp.concatenate(rows, axis=0), *events)).astype(BF16)
+    whole = whole.reshape(2, whole.shape[0] // 2, whole.shape[1])
+    sent = lax.dynamic_index_in_dim(whole, 1 - mine, 0, False)
+    return sent, lax.dynamic_index_in_dim(whole, mine, 0, False)
 
 
 def over_cores(sent, kept):
@@ -346,13 +355,13 @@
         )
     for k in near_part[1:]:
         grad_other[k] = swap(after(grad_own[k], upto), "ctx", 1)
-    for k in first_far:
-        grad_other[k] = swap(after(grad_own[k], upto), "ctx", 1)
     keep, give = scan_ends(before, key_mine, partner, decay_rates, place, block_len, False)
     for k in second_far:
         grad_own[k] = pairs_of(after(send_grad[k], give), k)
+    for k in first_far:
+        grad_other[k] = swap(grad_own[k], "ctx", 1)
     given = swap(give, "ctx", 1)
-    hidden_near = two_products(grad_own, grad_other, near_part, by_down, give)
+    hidden_near = one_product(grad_own, grad_other, near_part, by_down, give)
     hidden_near_sum = over_cores(*hidden_near)
     hidden_near_all = sum_over_rest(hidden_near_sum, bits)
     given, hidden_near_sum = lax.optimization_barrier((given, hidden_near_sum))

time: 187 us -> 195 us (1.043)
  starting transfers between devices: 54.4 us -> 48.5 us
  other arithmetic: 9.75 us -> 15.5 us
  waiting for transfers between devices: 71.7 us -> 77.4 us
    ppermute x39, starting transfers between devices: 43.7 us -> 34.8 us  [swap(): return lax.ppermute(array, axis, [(i, i ^ distance) for i in range(size)])]
    ppermute x39, waiting for transfers between devices: 61.3 us -> 66.2 us  [swap(): return lax.ppermute(array, axis, [(i, i ^ distance) for i in range(size)])]
    ppermute x6, starting transfers between devices: 10.6 us -> 13.7 us  [trade(): lax.ppermute(array, 'ctx', [(2 * partner(i) + s, 2 * i + s) for i in rang...]
    dot_general x15 -> x14, matrix products: 32.3 us -> 32.8 us  [dot(): lax.dot_general(left, right, (((left_dim,), (right_dim,)), ((), ())), pre...]
  transfers between devices with their start and end apart: 45 -> 45, of which waited for: 21 -> 23; matrix products, arithmetic and copies ran while one was open for 21% -> 24% of each run, Pallas kernels for 5% -> 5%
where the time goes in v13:
time: 195 us; the launch traced here: 194 us
  waiting for transfers between devices  77.4 us (40%)
  starting transfers between devices  48.5 us (25%)
  matrix products  32.8 us (17%)
  other arithmetic  15.5 us (8%)
  Pallas kernels  13.2 us (7%)
  local copies, waits for them, and re-layouts  5.57 us (3%)
    ppermute x39, waiting for transfers between devices, swap(): return lax.ppermute(array, axis, [(i, i ^ distance) for i in range(size)])  66.2 us
    ppermute x39, starting transfers between devices, swap(): return lax.ppermute(array, axis, [(i, i ^ distance) for i in range(size)])  34.8 us
    dot_general x14, matrix products, dot(): lax.dot_general(left, right, (((left_dim,), (right_dim,)), ((), ())), pre...  32.8 us
    ppermute x6, starting transfers between devices, trade(): lax.ppermute(array, 'ctx', [(2 * partner(i) + s, 2 * i + s) for i in rang...  13.7 us
    pallas_call x7, Pallas kernels, call(): pl.pallas_call(kernel, out_shape=list(out_shapes), in_specs=[SMEM] * len(...  13.2 us
    ppermute x6, waiting for transfers between devices, trade(): lax.ppermute(array, 'ctx', [(2 * partner(i) + s, 2 * i + s) for i in rang...  11.2 us
  transfers between devices with their start and end apart: 45, of which 23 were waited for; matrix products, arithmetic and copies ran while one was open for 24% of the time, Pallas kernels for 5%

profile of v13, /device:TPU:0, one launch (start us, length us, event | category | flops | bytes accessed | tf_op | source)
XLA Modules:
  0.0 194.2 jit_solution(6172721050648414009)
XLA Ops:
  4.4 3.0 %collective-permute-start = (bf16[6,128,128]{2,1,0:T(8,128)(2,1)S(1)}, bf16[6,128,128]{2,1,0:T(8,128)(2,1)S(1)}, u32[]{:S(2)}, u32[]{:S(2)}) collective-permute-start(bf16[6,128,128]{2,1,0:T(8,128)(2,1)S(1)} %get-tuple-element.53), channel_id=1, source_target_pairs={{0,4},{4,0},{8,12},{12,8},{16,20},{20,16},{24,28},{28,24},{1,5},{5... | collective-permute-start | bytes 589832 | tf_op jit(solution)/shard_map/ppermute | solution.py:205
  15.0 2.5 %shard_map.114 = (f32[128,1536]{1,0:T(8,128)S(1)}, bf16[12,128,128]{2,1,0:T(8,128)(2,1)S(1)}) custom-call(s32[3]{0:T(128)S(1)} %pad_add_fusion.place_ref, f32[12]{0:T(128)S(1)} %neg.11.rates_ref, bf16[128,1536]{1,0:T(8,128)(2,1)S(1)} %copy-done, bf16[256,1536]{1,0:T(8,128)(2,1)S(1)} %constant_dynamic-update-slice_fusion.pair_ref), custom_call_target="tpu_custom_call" | custom-call | flops 1 | bytes 40000000 | tf_op jit(solution)/shard_map/pallas_call | solution.py:192
  17.8 3.8 %collective-permute-start.13 = (bf16[72,1536]{1,0:T(8,128)(2,1)}, bf16[72,1536]{1,0:T(8,128)(2,1)}, u32[]{:S(2)}, u32[]{:S(2)}) collective-permute-start(bf16[72,1536]{1,0:T(8,128)(2,1)} %copy-done.6), channel_id=1, source_target_pairs={{0,24},{4,28},{8,16},{12,20},{16,8},{20,12},{24,0},{28,4},{1,25},{... | collective-permute-start | bytes 663560 | tf_op jit(solution)/shard_map/ppermute | solution.py:205
  23.5 3.0 %collective-permute-start.3 = (bf16[6,128,128]{2,1,0:T(8,128)(2,1)}, bf16[6,128,128]{2,1,0:T(8,128)(2,1)}, u32[]{:S(2)}, u32[]{:S(2)}) collective-permute-start(bf16[6,128,128]{2,1,0:T(8,128)(2,1)} %add_convert_fusion.11), channel_id=1, source_target_pairs={{0,0},{4,4},{16,8},{20,12},{8,16},{12,20},{24,24},{28,28},{1,1},{5... | collective-permute-start | bytes 589832 | tf_op jit(solution)/shard_map/ppermute | solution.py:209
  26.5 3.0 %collective-permute-start.2 = (bf16[6,128,128]{2,1,0:T(8,128)(2,1)}, bf16[6,128,128]{2,1,0:T(8,128)(2,1)}, u32[]{:S(2)}, u32[]{:S(2)}) collective-permute-start(bf16[6,128,128]{2,1,0:T(8,128)(2,1)} %add_convert_fusion.11), channel_id=1, source_target_pairs={{0,0},{4,4},{24,8},{28,12},{16,16},{20,20},{8,24},{12,28},{1,1},{5... | collective-permute-start | bytes 589832 | tf_op jit(solution)/shard_map/ppermute | solution.py:209
  37.9 4.3 %collective-permute-done.7 = bf16[72,1536]{1,0:T(8,128)(2,1)S(1)} collective-permute-done((bf16[72,1536]{1,0:T(8,128)(2,1)}, bf16[72,1536]{1,0:T(8,128)(2,1)S(1)}, u32[]{:S(2)}, u32[]{:S(2)}) %collective-permute-start.7) | collective-permute-done | bytes 221216 | tf_op jit(solution)/shard_map/ppermute | solution.py:205
  43.2 5.3 %fusion.28 = bf16[288,2304]{1,0:T(8,128)(2,1)S(1)} fusion(bf16[288,1536]{1,0:T(8,128)(2,1)S(1)} %pad_maximum_fusion, bf16[1,2304,1536]{2,1,0:T(8,128)(2,1)} %param.14), kind=kOutput, calls=%fused_computation.28 | convolution fusion | flops 2039095296 | bytes 9289728 | tf_op jit(solution)/shard_map/dot_general | solution.py:22
  54.8 3.2 %collective-permute-done.4.other_ref = bf16[6,128,128]{2,1,0:T(8,128)(2,1)S(1)} collective-permute-done((bf16[6,128,128]{2,1,0:T(8,128)(2,1)}, bf16[6,128,128]{2,1,0:T(8,128)(2,1)S(1)}, u32[]{:S(2)}, u32[]{:S(2)}) %collective-permute-start.4) | collective-permute-done | bytes 196640 | tf_op jit(solution)/shard_map/ppermute | solution.py:205
  61.5 5.4 %fusion.40 = bf16[72,2304]{1,0:T(8,128)(2,1)S(1)} fusion(bf16[72,1536]{1,0:T(8,128)(2,1)S(1)} %get-tuple-element.70, bf16[1,2304,1536]{2,1,0:T(8,128)(2,1)} %param.14), kind=kOutput, calls=%fused_computation.32 | convolution fusion | flops 509773824 | bytes 7630848 | tf_op jit(solution)/shard_map/dot_general | solution.py:22
  67.4 2.4 %collective-permute-done.11 = bf16[72,1536]{1,0:T(8,128)(2,1)S(1)} collective-permute-done((bf16[72,1536]{1,0:T(8,128)(2,1)S(1)}, bf16[72,1536]{1,0:T(8,128)(2,1)S(1)}, u32[]{:S(2)}, u32[]{:S(2)}) %collective-permute-start.11) | collective-permute-done | bytes 221216 | tf_op jit(solution)/shard_map/ppermute | solution.py:205
  80.5 4.1 %collective-permute-done.24 = bf16[72,1536]{1,0:T(8,128)(2,1)S(1)} collective-permute-done((bf16[72,1536]{1,0:T(8,128)(2,1)S(1)}, bf16[72,1536]{1,0:T(8,128)(2,1)S(1)}, u32[]{:S(2)}, u32[]{:S(2)}) %collective-permute-start.24) | collective-permute-done | bytes 221216 | tf_op jit(solution)/shard_map/ppermute | solution.py:205
  84.6 3.1 %collective-permute-start.28 = (bf16[72,1536]{1,0:T(8,128)(2,1)S(1)}, bf16[72,1536]{1,0:T(8,128)(2,1)S(1)}, u32[]{:S(2)}, u32[]{:S(2)}) collective-permute-start(bf16[72,1536]{1,0:T(8,128)(2,1)S(1)} %get-tuple-element.84), channel_id=1, source_target_pairs={{0,16},{4,20},{8,24},{12,28},{16,0},{20,4},{24,8},{28,12},{1,17},{... | collective-permute-start | bytes 663560 | tf_op jit(solution)/shard_map/ppermute | solution.py:205
  92.6 4.3 %collective-permute-done.28 = bf16[72,1536]{1,0:T(8,128)(2,1)S(1)} collective-permute-done((bf16[72,1536]{1,0:T(8,128)(2,1)S(1)}, bf16[72,1536]{1,0:T(8,128)(2,1)S(1)}, u32[]{:S(2)}, u32[]{:S(2)}) %collective-permute-start.28) | collective-permute-done | bytes 221216 | tf_op jit(solution)/shard_map/ppermute | solution.py:205
  106.4 2.5 %fusion.67 = bf16[72,2304]{1,0:T(8,128)(2,1)S(1)} fusion(bf16[72,1536]{1,0:T(8,128)(2,1)S(1)} %get-tuple-element.82, bf16[1,2304,1536]{2,1,0:T(8,128)(2,1)S(1)} %bitcast.111, bf16[72,2304]{1,0:T(8,128)(2,1)S(1)} %collective-permute-done.26), kind=kOutput, calls=%fused_computation.41 | convolution fusion | flops 510437376 | bytes 7962624 | tf_op jit(solution)/shard_map/dot_general | solution.py:22
  112.2 3.7 %collective-permute-done.34 = bf16[72,2304]{1,0:T(8,128)(2,1)S(1)} collective-permute-done((bf16[72,2304]{1,0:T(8,128)(2,1)S(1)}, bf16[72,2304]{1,0:T(8,128)(2,1)S(1)}, u32[]{:S(2)}, u32[]{:S(2)}) %collective-permute-start.34) | collective-permute-done | bytes 331808 | tf_op jit(solution)/shard_map/ppermute | solution.py:205
  124.8 4.5 %collective-permute-done.31 = bf16[72,2304]{1,0:T(8,128)(2,1)S(1)} collective-permute-done((bf16[72,2304]{1,0:T(8,128)(2,1)S(1)}, bf16[72,2304]{1,0:T(8,128)(2,1)S(1)}, u32[]{:S(2)}, u32[]{:S(2)}) %collective-permute-start.31) | collective-permute-done | bytes 331808 | tf_op jit(solution)/shard_map/ppermute | solution.py:205
  137.3 5.6 %collective-permute-done.19 = bf16[144,1536]{1,0:T(8,128)(2,1)S(1)} collective-permute-done((bf16[144,1536]{1,0:T(8,128)(2,1)S(1)}, bf16[144,1536]{1,0:T(8,128)(2,1)S(1)}, u32[]{:S(2)}, u32[]{:S(2)}) %collective-permute-start.19) | collective-permute-done | bytes 442400 | tf_op jit(solution)/shard_map/ppermute | solution.py:205
  143.1 4.1 %collective-permute-done.36 = bf16[72,1536]{1,0:T(8,128)(2,1)S(1)} collective-permute-done((bf16[72,1536]{1,0:T(8,128)(2,1)S(1)}, bf16[72,1536]{1,0:T(8,128)(2,1)S(1)}, u32[]{:S(2)}, u32[]{:S(2)}) %collective-permute-start.36) | collective-permute-done | bytes 221216 | tf_op jit(solution)/shard_map/ppermute | solution.py:205
  149.6 9.3 %collective-permute-done.37.refs_2_ = bf16[72,1536]{1,0:T(8,128)(2,1)S(1)} collective-permute-done((bf16[72,1536]{1,0:T(8,128)(2,1)S(1)}, bf16[72,1536]{1,0:T(8,128)(2,1)S(1)}, u32[]{:S(2)}, u32[]{:S(2)}) %collective-permute-start.37) | collective-permute-done | bytes 221216 | tf_op jit(solution)/shard_map/ppermute | solution.py:205
  161.0 6.2 %collective-permute-done.40 = bf16[6,128,128]{2,1,0:T(8,128)(2,1)S(1)} collective-permute-done((bf16[6,128,128]{2,1,0:T(8,128)(2,1)S(1)}, bf16[6,128,128]{2,1,0:T(8,128)(2,1)S(1)}, u32[]{:S(2)}, u32[]{:S(2)}) %collective-permute-start.40) | collective-permute-done | bytes 196640 | tf_op jit(solution)/shard_map/ppermute | solution.py:205
  167.4 5.9 %collective-permute-done.41 = bf16[6,128,128]{2,1,0:T(8,128)(2,1)S(1)} collective-permute-done((bf16[6,128,128]{2,1,0:T(8,128)(2,1)S(1)}, bf16[6,128,128]{2,1,0:T(8,128)(2,1)S(1)}, u32[]{:S(2)}, u32[]{:S(2)}) %collective-permute-start.41) | collective-permute-done | bytes 196640 | tf_op jit(solution)/shard_map/ppermute | solution.py:209
  174.2 5.2 %collective-permute-start.42 = (bf16[6,128,128]{2,1,0:T(8,128)(2,1)S(1)}, bf16[6,128,128]{2,1,0:T(8,128)(2,1)S(1)}, u32[]{:S(2)}, u32[]{:S(2)}) collective-permute-start(bf16[6,128,128]{2,1,0:T(8,128)(2,1)S(1)} %add_convert_fusion.10), channel_id=1, source_target_pairs={{16,0},{20,4},{8,8},{12,12},{0,16},{4,20},{24,24},{28,28},{17,1},{... | collective-permute-start | bytes 589832 | tf_op jit(solution)/shard_map/ppermute | solution.py:209
  179.4 5.3 %collective-permute-done.42 = bf16[6,128,128]{2,1,0:T(8,128)(2,1)S(1)} collective-permute-done((bf16[6,128,128]{2,1,0:T(8,128)(2,1)S(1)}, bf16[6,128,128]{2,1,0:T(8,128)(2,1)S(1)}, u32[]{:S(2)}, u32[]{:S(2)}) %collective-permute-start.42) | collective-permute-done | bytes 196640 | tf_op jit(solution)/shard_map/ppermute | solution.py:209
  187.3 4.0 %shard_map.117 = (bf16[128,1536]{1,0:T(8,128)(2,1)}, f32[128,1536]{1,0:T(8,128)S(1)}, f32[128,1536]{1,0:T(8,128)S(1)}) custom-call(s32[3]{0:T(128)S(1)} %pad_add_fusion.place_ref, f32[12]{0:T(128)S(1)} %neg.11.rates_ref, bf16[128,1536]{1,0:T(8,128)(2,1)S(1)} %copy-done, bf16[256,1536]{1,0:T(8,128)(2,1)S(1)} %constant_dynamic-update-slice_fusion.pair_ref, ...), custom_call_target="tpu_custom_call" | custom-call | flops 1 | bytes 1 | tf_op jit(solution)/shard_map/pallas_call | solution.py:192
  (157 shorter events, 89.3 us)
Async XLA Ops:
  4.4 7.9 %collective-permute-start = (bf16[6,128,128]{2,1,0:T(8,128)(2,1)S(1)}, bf16[6,128,128]{2,1,0:T(8,128)(2,1)S(1)}, u32[]{:S(2)}, u32[]{:S(2)}) collective-permute-start(bf16[6,128,128]{2,1,0:T(8,128)(2,1)S(1)} %get-tuple-element.53), channel_id=1, source_target_pairs={{0,4},{4,0},{8,12},{12,8},{16,20},{20,16},{24,28},{28,24},{1,5},{5... | collective-permute-start | bytes 589832 | tf_op jit(solution)/shard_map/ppermute | solution.py:205
  13.1 8.5 %collective-permute-start.1 = (bf16[6,128,128]{2,1,0:T(8,128)(2,1)}, bf16[6,128,128]{2,1,0:T(8,128)(2,1)}, u32[]{:S(2)}, u32[]{:S(2)}) collective-permute-start(bf16[6,128,128]{2,1,0:T(8,128)(2,1)} %fusion.141), channel_id=1, source_target_pairs={{8,0},{12,4},{0,8},{4,12},{24,16},{28,20},{16,24},{20,28},{9,1},{1... | collective-permute-start | bytes 589832 | tf_op jit(solution)/shard_map/ppermute | solution.py:209
  17.5 13.5 %collective-permute-start.5 = (bf16[72,1536]{1,0:T(8,128)(2,1)}, bf16[72,1536]{1,0:T(8,128)(2,1)}, u32[]{:S(2)}, u32[]{:S(2)}) collective-permute-start(bf16[72,1536]{1,0:T(8,128)(2,1)} %copy-done.7), channel_id=1, source_target_pairs={{0,8},{4,12},{8,0},{12,4},{16,24},{20,28},{24,16},{28,20},{1,9},{5... | collective-permute-start | bytes 663560 | tf_op jit(solution)/shard_map/ppermute | solution.py:205
  17.8 15.0 %collective-permute-start.13 = (bf16[72,1536]{1,0:T(8,128)(2,1)}, bf16[72,1536]{1,0:T(8,128)(2,1)}, u32[]{:S(2)}, u32[]{:S(2)}) collective-permute-start(bf16[72,1536]{1,0:T(8,128)(2,1)} %copy-done.6), channel_id=1, source_target_pairs={{0,24},{4,28},{8,16},{12,20},{16,8},{20,12},{24,0},{28,4},{1,25},{... | collective-permute-start | bytes 663560 | tf_op jit(solution)/shard_map/ppermute | solution.py:205
  23.5 10.7 %collective-permute-start.3 = (bf16[6,128,128]{2,1,0:T(8,128)(2,1)}, bf16[6,128,128]{2,1,0:T(8,128)(2,1)}, u32[]{:S(2)}, u32[]{:S(2)}) collective-permute-start(bf16[6,128,128]{2,1,0:T(8,128)(2,1)} %add_convert_fusion.11), channel_id=1, source_target_pairs={{0,0},{4,4},{16,8},{20,12},{8,16},{12,20},{24,24},{28,28},{1,1},{5... | collective-permute-start | bytes 589832 | tf_op jit(solution)/shard_map/ppermute | solution.py:209
  29.5 8.4 %collective-permute-start.6 = (bf16[72,1536]{1,0:T(8,128)(2,1)S(1)}, bf16[72,1536]{1,0:T(8,128)(2,1)S(1)}, u32[]{:S(2)}, u32[]{:S(2)}) collective-permute-start(bf16[72,1536]{1,0:T(8,128)(2,1)S(1)} %get-tuple-element.60), channel_id=1, source_target_pairs={{0,4},{4,0},{8,12},{12,8},{16,20},{20,16},{24,28},{28,24},{1,5},{5... | collective-permute-start | bytes 663560 | tf_op jit(solution)/shard_map/ppermute | solution.py:205
  31.0 11.2 %collective-permute-start.7 = (bf16[72,1536]{1,0:T(8,128)(2,1)}, bf16[72,1536]{1,0:T(8,128)(2,1)S(1)}, u32[]{:S(2)}, u32[]{:S(2)}) collective-permute-start(bf16[72,1536]{1,0:T(8,128)(2,1)} %collective-permute-done.5), channel_id=1, source_target_pairs={{0,4},{4,0},{8,12},{12,8},{16,20},{20,16},{24,28},{28,24},{1,5},{5... | collective-permute-start | bytes 663560 | tf_op jit(solution)/shard_map/ppermute | solution.py:205
  32.8 19.1 %collective-permute-start.14 = (bf16[72,1536]{1,0:T(8,128)(2,1)}, bf16[72,1536]{1,0:T(8,128)(2,1)}, u32[]{:S(2)}, u32[]{:S(2)}) collective-permute-start(bf16[72,1536]{1,0:T(8,128)(2,1)} %collective-permute-done.13), channel_id=1, source_target_pairs={{0,4},{4,0},{8,12},{12,8},{16,20},{20,16},{24,28},{28,24},{1,5},{5... | collective-permute-start | bytes 663560 | tf_op jit(solution)/shard_map/ppermute | solution.py:205
  51.9 38.6 %collective-permute-start.21 = (bf16[72,1536]{1,0:T(8,128)(2,1)S(1)}, bf16[72,1536]{1,0:T(8,128)(2,1)S(1)}, u32[]{:S(2)}, u32[]{:S(2)}) collective-permute-start(bf16[72,1536]{1,0:T(8,128)(2,1)S(1)} %copy-done.5), channel_id=1, source_target_pairs={{0,16},{4,20},{8,24},{12,28},{16,0},{20,4},{24,8},{28,12},{1,17},{... | collective-permute-start | bytes 663560 | tf_op jit(solution)/shard_map/ppermute | solution.py:205
  59.3 12.1 %collective-permute-start.10 = (bf16[72,1536]{1,0:T(8,128)(2,1)S(1)}, bf16[72,1536]{1,0:T(8,128)(2,1)S(1)}, u32[]{:S(2)}, u32[]{:S(2)}) collective-permute-start(bf16[72,1536]{1,0:T(8,128)(2,1)S(1)} %get-tuple-element.66), channel_id=1, source_target_pairs={{0,4},{4,0},{8,12},{12,8},{16,20},{20,16},{24,28},{28,24},{1,5},{5... | collective-permute-start | bytes 663560 | tf_op jit(solution)/shard_map/ppermute | solution.py:205
  60.7 9.1 %collective-permute-start.11 = (bf16[72,1536]{1,0:T(8,128)(2,1)S(1)}, bf16[72,1536]{1,0:T(8,128)(2,1)S(1)}, u32[]{:S(2)}, u32[]{:S(2)}) collective-permute-start(bf16[72,1536]{1,0:T(8,128)(2,1)S(1)} %get-tuple-element.67), channel_id=1, source_target_pairs={{0,8},{4,12},{8,0},{12,4},{16,24},{20,28},{24,16},{28,20},{1,9},{5... | collective-permute-start | bytes 663560 | tf_op jit(solution)/shard_map/ppermute | solution.py:205
  67.0 9.7 %collective-permute-start.23 = (bf16[72,1536]{1,0:T(8,128)(2,1)S(1)}, bf16[72,1536]{1,0:T(8,128)(2,1)S(1)}, u32[]{:S(2)}, u32[]{:S(2)}) collective-permute-start(bf16[72,1536]{1,0:T(8,128)(2,1)S(1)} %get-tuple-element.77), channel_id=1, source_target_pairs={{0,24},{4,28},{8,16},{12,20},{16,8},{20,12},{24,0},{28,4},{1,25},{... | collective-permute-start | bytes 663560 | tf_op jit(solution)/shard_map/ppermute | solution.py:205
  69.8 41.0 %collective-permute-start.9 = (bf16[144,2304]{1,0:T(8,128)(2,1)S(1)}, bf16[144,2304]{1,0:T(8,128)(2,1)S(1)}, u32[]{:S(2)}, u32[]{:S(2)}) collective-permute-start(bf16[144,2304]{1,0:T(8,128)(2,1)S(1)} %fusion.119), channel_id=1, source_target_pairs={{0,2},{1,3},{2,0},{3,1},{4,6},{5,7},{6,4},{7,5},{8,10},{9,11},{10,... | collective-permute-start | bytes 1990664 | tf_op jit(solution)/shard_map/ppermute | solution.py:205
  74.4 37.8 %collective-permute-start.33 = (bf16[72,2304]{1,0:T(8,128)(2,1)S(1)}, bf16[72,2304]{1,0:T(8,128)(2,1)S(1)}, u32[]{:S(2)}, u32[]{:S(2)}) collective-permute-start(bf16[72,2304]{1,0:T(8,128)(2,1)S(1)} %fusion.52), channel_id=1, source_target_pairs={{0,2},{1,3},{2,0},{3,1},{4,6},{5,7},{6,4},{7,5},{8,10},{9,11},{10,... | collective-permute-start | bytes 995336 | tf_op jit(solution)/shard_map/ppermute | solution.py:205
  84.6 12.3 %collective-permute-start.28 = (bf16[72,1536]{1,0:T(8,128)(2,1)S(1)}, bf16[72,1536]{1,0:T(8,128)(2,1)S(1)}, u32[]{:S(2)}, u32[]{:S(2)}) collective-permute-start(bf16[72,1536]{1,0:T(8,128)(2,1)S(1)} %get-tuple-element.84), channel_id=1, source_target_pairs={{0,16},{4,20},{8,24},{12,28},{16,0},{20,4},{24,8},{28,12},{1,17},{... | collective-permute-start | bytes 663560 | tf_op jit(solution)/shard_map/ppermute | solution.py:205
  89.0 22.0 %collective-permute-start.17 = (bf16[144,2304]{1,0:T(8,128)(2,1)S(1)}, bf16[144,2304]{1,0:T(8,128)(2,1)S(1)}, u32[]{:S(2)}, u32[]{:S(2)}) collective-permute-start(bf16[144,2304]{1,0:T(8,128)(2,1)S(1)} %add_convert_fusion.1), channel_id=1, source_target_pairs={{0,2},{1,3},{2,0},{3,1},{4,6},{5,7},{6,4},{7,5},{8,10},{9,11},{10,... | collective-permute-start | bytes 1990664 | tf_op jit(solution)/shard_map/ppermute | solution.py:205
  104.8 11.0 %collective-permute-start.34 = (bf16[72,2304]{1,0:T(8,128)(2,1)S(1)}, bf16[72,2304]{1,0:T(8,128)(2,1)S(1)}, u32[]{:S(2)}, u32[]{:S(2)}) collective-permute-start(bf16[72,2304]{1,0:T(8,128)(2,1)S(1)} %fusion.82), channel_id=1, source_target_pairs={{0,2},{1,3},{2,0},{3,1},{4,6},{5,7},{6,4},{7,5},{8,10},{9,11},{10,... | collective-permute-start | bytes 995336 | tf_op jit(solution)/shard_map/ppermute | solution.py:205
  108.9 15.9 %collective-permute-start.27 = (bf16[72,2304]{1,0:T(8,128)(2,1)S(1)}, bf16[72,2304]{1,0:T(8,128)(2,1)S(1)}, u32[]{:S(2)}, u32[]{:S(2)}) collective-permute-start(bf16[72,2304]{1,0:T(8,128)(2,1)S(1)} %fusion.67), channel_id=1, source_target_pairs={{0,2},{1,3},{2,0},{3,1},{4,6},{5,7},{6,4},{7,5},{8,10},{9,11},{10,... | collective-permute-start | bytes 995336 | tf_op jit(solution)/shard_map/ppermute | solution.py:205
  117.7 11.7 %collective-permute-start.31 = (bf16[72,2304]{1,0:T(8,128)(2,1)S(1)}, bf16[72,2304]{1,0:T(8,128)(2,1)S(1)}, u32[]{:S(2)}, u32[]{:S(2)}) collective-permute-start(bf16[72,2304]{1,0:T(8,128)(2,1)S(1)} %fusion.97), channel_id=1, source_target_pairs={{0,2},{1,3},{2,0},{3,1},{4,6},{5,7},{6,4},{7,5},{8,10},{9,11},{10,... | collective-permute-start | bytes 995336 | tf_op jit(solution)/shard_map/ppermute | solution.py:205
  129.8 13.0 %collective-permute-start.19 = (bf16[144,1536]{1,0:T(8,128)(2,1)S(1)}, bf16[144,1536]{1,0:T(8,128)(2,1)S(1)}, u32[]{:S(2)}, u32[]{:S(2)}) collective-permute-start(bf16[144,1536]{1,0:T(8,128)(2,1)S(1)} %slice.39), channel_id=1, source_target_pairs={{0,4},{4,0},{8,12},{12,8},{16,20},{20,16},{24,28},{28,24},{1,5},{5... | collective-permute-start | bytes 1327112 | tf_op jit(solution)/shard_map/ppermute | solution.py:205
  131.9 15.5 %collective-permute-start.39 = (bf16[72,1536]{1,0:T(8,128)(2,1)S(1)}, bf16[72,1536]{1,0:T(8,128)(2,1)S(1)}, u32[]{:S(2)}, u32[]{:S(2)}) collective-permute-start(bf16[72,1536]{1,0:T(8,128)(2,1)S(1)} %add_convert_fusion.8), channel_id=1, source_target_pairs={{0,24},{4,28},{8,16},{12,20},{16,8},{20,12},{24,0},{28,4},{1,25},{... | collective-permute-start | bytes 663560 | tf_op jit(solution)/shard_map/ppermute | solution.py:205
  136.6 10.6 %collective-permute-start.36 = (bf16[72,1536]{1,0:T(8,128)(2,1)S(1)}, bf16[72,1536]{1,0:T(8,128)(2,1)S(1)}, u32[]{:S(2)}, u32[]{:S(2)}) collective-permute-start(bf16[72,1536]{1,0:T(8,128)(2,1)S(1)} %slice.43), channel_id=1, source_target_pairs={{0,4},{4,0},{8,12},{12,8},{16,20},{20,16},{24,28},{28,24},{1,5},{5... | collective-permute-start | bytes 663560 | tf_op jit(solution)/shard_map/ppermute | solution.py:205
  147.2 11.7 %collective-permute-start.37 = (bf16[72,1536]{1,0:T(8,128)(2,1)S(1)}, bf16[72,1536]{1,0:T(8,128)(2,1)S(1)}, u32[]{:S(2)}, u32[]{:S(2)}) collective-permute-start(bf16[72,1536]{1,0:T(8,128)(2,1)S(1)} %add_convert_fusion.9), channel_id=1, source_target_pairs={{0,16},{4,20},{8,24},{12,28},{16,0},{20,4},{24,8},{28,12},{1,17},{... | collective-permute-start | bytes 663560 | tf_op jit(solution)/shard_map/ppermute | solution.py:205
  174.2 10.5 %collective-permute-start.42 = (bf16[6,128,128]{2,1,0:T(8,128)(2,1)S(1)}, bf16[6,128,128]{2,1,0:T(8,128)(2,1)S(1)}, u32[]{:S(2)}, u32[]{:S(2)}) collective-permute-start(bf16[6,128,128]{2,1,0:T(8,128)(2,1)S(1)} %add_convert_fusion.10), channel_id=1, source_target_pairs={{16,0},{20,4},{8,8},{12,12},{0,16},{4,20},{24,24},{28,28},{17,1},{... | collective-permute-start | bytes 589832 | tf_op jit(solution)/shard_map/ppermute | solution.py:209
  (36 other events, 266.2 us)
